TPU v7x, 32 devices: a whole 2x2x4 slice. The times are simulated.
32 devices in a mesh: row: 4 (over z), col: 8 (over y, x, core).
Axes of the slice: x: 2, y: 2, z: 4, core: 2. Of those that a mesh axis runs over, the one named last changes fastest.
Arguments:
- blocks: bfloat16 [4, 8, 128, 4096], P('row', 'col'), may hold values from -0.25 to 0.25
- block_row: int32 [4, 8, 128], P('row', 'col'), may hold values from 0 to 15
- block_col: int32 [4, 8, 128], P('row', 'col'), may hold values from 0 to 7
- counts: int32 [4, 8], P('row', 'col'), may hold values from 0 to 128, as said below
- vectors: float32 [64, 4096], P(('col', 'row')), may hold values from -6 to 6
- row_mass: float32 [64, 64], P(('row', 'col')), may hold values from 0.25 to 4
- col_mass: float32 [64, 64], P(('col', 'row')), may hold values from 0.25 to 4
Outputs:
- subspace: float32 [64, 4096], P(('col', 'row'))
Inputs may be any that keep to these rules, and one draw needn't show every extreme that they name: `counts`: in every row panel one tile uses all 128 slots; every other tile uses at most 8.
All inputs are finite; a program needn't handle non-finite values.
Results may differ from a plain program's by a relative error of at most 0.0085.
Values may be sent and summed in bfloat16 or wider, within the bound.
No kernel may reach another device: no remote copies, remote signals or barrier semaphores. Data moves between devices by JAX's collectives and lax.ppermute only.
A program may use at most 64 MiB of HBM per device.

v0:
```python
import functools

import jax
import jax.numpy as jnp
from jax import lax
from jax.experimental import pallas as pl
from jax.experimental.pallas import tpu as pltpu
from jax.sharding import PartitionSpec as P

ITERS = 4
OFF_CAP = 8
META = 16
UNROLL = 8
VMEM_LIMIT = 56 * 1024 * 1024

NT = (((1,), (1,)), ((), ()))
NN = (((1,), (0,)), ((), ()))


def dot(a, b, dims=NN):
    return lax.dot_general(a, b, dims, preferred_element_type=jnp.float32)


def split2(x):
    hi = x.astype(jnp.bfloat16)
    return hi, (x - hi.astype(jnp.float32)).astype(jnp.bfloat16)


def inverse_factor(gram):
    n = gram.shape[0]
    rows = lax.broadcasted_iota(jnp.int32, (n, n), 0)
    cols = lax.broadcasted_iota(jnp.int32, (n, n), 1)
    eye = (rows == cols).astype(jnp.float32)
    both = jnp.concatenate([gram, eye], axis=1)
    count = n // 8
    tiles = [both[8 * t : 8 * t + 8] for t in range(count)]
    sub = lax.broadcasted_iota(jnp.int32, (8, 2 * n), 0)
    lane = lax.broadcasted_iota(jnp.int32, (8, 2 * n), 1)
    for b in range(count):
        spread = {
            t: [jnp.broadcast_to(tiles[t][:, 8 * b + s : 8 * b + s + 1], (8, 2 * n)) for s in range(8)]
            for t in range(b, count)
        }
        for s in range(8):
            inv = 1.0 / spread[b][s][s : s + 1]
            step = tiles[b][s : s + 1] * inv
            ahead = [spread[b][s2][s : s + 1] * inv for s2 in range(s + 1, 8)]
            for t in range(b, count):
                factor = spread[t][s]
                if t == b:
                    factor = jnp.where(sub > s, factor, 0.0)
                for s2 in range(s + 1, 8):
                    spread[t][s2] = spread[t][s2] - factor * ahead[s2 - s - 1]
                tiles[t] = tiles[t] - factor * step
    out = []
    for t in range(count):
        pivot = jnp.sum(jnp.where(lane == sub + 8 * t, tiles[t], 0.0), axis=1, keepdims=True)
        out.append(tiles[t] * lax.rsqrt(pivot))
    return jnp.concatenate(out, axis=0)[:, n:]


def kernel(
    n_row, n_col, n_cap, total,
    meta, own, *rest,
):
    smalls, fulls, out = rest[:8], rest[8:16], rest[16]
    lv, lw, sems, small, full, tmp, home, blk = rest[17:25]
    vs, vb, w, wb, wt, wtb, y, yb, ph, rm, ic, linv = rest[25:]
    n_dev = n_row * n_col
    group = n_dev // 2
    k = vs.shape[1]
    half = k // 2
    rpairs, cpairs = n_col, n_row
    rblk, cblk = 2 * rpairs, 2 * cpairs
    part = n_cap // n_col
    vec_at = OFF_CAP * half
    meta_at = vec_at + k
    width = cpairs * 128

    here, chip, core = own[0], own[1], own[2]
    piece = n_dev // 8
    waits = []
    for i, (srcs, dst) in enumerate([(smalls, small), (fulls, full)]):
        for j, ref in enumerate(srcs):
            copy = pltpu.make_async_copy(ref, dst.at[pl.ds(j * piece, piece)], sems.at[8 * i + j])
            copy.start()
            waits.append(copy)
    for copy in waits[:8]:
        copy.wait()

    def at_device(r, c):
        dr, dc, dk = here ^ r, chip ^ (c // 2), core ^ (c % 2)
        dx, dy = dc & 1, dc >> 1
        order = jnp.where(dr < 2, 4 * dy + 2 * dx, 8 + 4 * dx + 2 * dy)
        return dk * group + order + (dr & 1)

    def scatter_pair(pair, blocks, q, x):
        pair[q] = x.astype(pair.dtype)
        blocks[2 * q] = x[:, :k].astype(blocks.dtype)
        blocks[2 * q + 1] = x[:, k:].astype(blocks.dtype)

    for r in range(n_row):
        for c in range(n_col):
            q, p, d = c * n_row + r, r * n_col + c, at_device(r, c)
            rows = small[d, meta_at : meta_at + META, :].astype(jnp.float32)
            rm[p] = jnp.broadcast_to(rows[0:1] + rows[1:2] + rows[2:3], (8, 128))
            ic[q] = jnp.broadcast_to(rows[3:4] + rows[4:5] + rows[5:6], (8, 128))
            scatter_pair(vs, vb, q, small[d, vec_at : vec_at + k, :].astype(jnp.float32))

    def device(d, n):
        count = meta[d, 2 * OFF_CAP]
        count = jnp.where(count > OFF_CAP, 0, count)
        near = (d & 8) == 0
        one, two = (d >> 1) & 1, (d >> 2) & 1
        dc = jnp.where(near, 2 * two + one, 2 * one + two)
        c = 2 * (chip ^ dc) + (core ^ (d >> 4))
        r = here ^ (jnp.where(near, 0, 2) + (d & 1))
        for s in range(OFF_CAP):
            lv[n + s] = c * cblk + meta[d, OFF_CAP + s]
            lw[n + s] = r * rblk + meta[d, s]
            x = small[d, s * half : (s + 1) * half, :].astype(jnp.float32)
            blk[n + s] = jnp.concatenate([x[:, :k], x[:, k:]], axis=0).astype(jnp.bfloat16)
        return n + count

    n_live = lax.fori_loop(0, n_dev, device, jnp.int32(0))
    for u in range(UNROLL - 1):
        lv[n_live + u] = 0
        lw[n_live + u] = 0
        blk[n_live + u] = jnp.zeros((k, k), jnp.bfloat16)
    n_group = (n_live + UNROLL - 1) // UNROLL

    for copy in waits[8:]:
        copy.wait()
    left = lax.broadcasted_iota(jnp.int32, (rblk, 128), 1) < 64
    homes = []
    for r in range(n_row):
        h = jnp.int32(0)
        for c in range(n_col):
            h = jnp.where(meta[at_device(r, c), 2 * OFF_CAP] > OFF_CAP, c, h)
        homes.append(h)
        index = small[at_device(r, h), meta_at : meta_at + META, :].astype(jnp.float32)
        place = index[7:8] * float(rblk) + index[6:7]
        want = lax.broadcasted_iota(jnp.int32, (cblk * rblk, n_cap), 0).astype(jnp.float32)
        select = jnp.where(want == place, 1.0, 0.0).astype(jnp.bfloat16)

        parts = [at_device(r, 2 * i + j) for j in range(2) for i in range(n_col // 2)]

        def build(m, carry, parts=parts, select=select):
            at = pl.multiple_of(m * part, part)
            slots = jnp.concatenate(
                [full[d, pl.ds(at, part), :] for d in parts], axis=0
            )
            dense = dot(select, slots)
            for u in range(cpairs):
                a = dense[2 * u * rblk : (2 * u + 1) * rblk]
                b = dense[(2 * u + 1) * rblk : (2 * u + 2) * rblk]
                even = jnp.where(left, a, pltpu.roll(b, 64, 1))
                odd = jnp.where(left, pltpu.roll(a, 64, 1), b)
                tmp[u, pl.ds(m, rblk, stride=k), :] = even
                tmp[u, pl.ds(m + half, rblk, stride=k), :] = odd
            return carry

        lax.fori_loop(0, half, build, 0, unroll=4)

        def cut(i, carry, r=r):
            at = pl.multiple_of(i * k, k)
            for u in range(cpairs):
                hi, lo = split2(tmp[u, pl.ds(at, k), :])
                home[r, pl.ds(at, k), u * 128 : (u + 1) * 128] = hi
                home[r, pl.ds(at, k), width + u * 128 : width + (u + 1) * 128] = lo
            return carry

        lax.fori_loop(0, rblk, cut, 0, unroll=4)

    def iteration(it, carry):
        @pl.when(it > 0)
        def _():
            lh, ll = split2(linv[...])
            turn = jnp.concatenate([lh, lh, ll], axis=1)
            for q in range(0, n_dev, 4):
                hi = jnp.concatenate([ph[q + d, :k, :] for d in range(4)], axis=1)
                lo = jnp.concatenate([ph[q + d, k:, :] for d in range(4)], axis=1)
                current = dot(turn, jnp.concatenate([hi, lo, hi], axis=0))
                for d in range(4):
                    x = current[:, d * 128 : (d + 1) * 128] * ic[q + d, 0:1, :]
                    scatter_pair(vs, vb, q + d, x)

        for b in range(2 * n_dev):
            wb[b] = jnp.zeros_like(wb[b])
        for r in range(n_row):
            base = homes[r] * cpairs
            vec = jnp.concatenate([vs[base + u] for u in range(cpairs)] * 2, axis=1)
            for p in range(0, rpairs, 2):
                prod = dot(vec, home[r, p * 128 : (p + 2) * 128, :], NT)
                w[r * rpairs + p] = prod[:, :128]
                w[r * rpairs + p + 1] = prod[:, 128:]

        def forward(i, carry):
            prods = [dot(vb[lv[i * UNROLL + u]], blk[i * UNROLL + u], NT) for u in range(UNROLL)]
            for u in range(UNROLL):
                b = lw[i * UNROLL + u]
                wb[b] = wb[b] + prods[u]
            return carry

        lax.fori_loop(0, n_group, forward, 0)
        for p in range(n_dev):
            x = w[p] + jnp.concatenate([wb[2 * p], wb[2 * p + 1]], axis=1)
            scatter_pair(wt, wtb, p, x * rm[p, 0:1, :])
            y[p] = jnp.zeros_like(y[p])
            yb[2 * p] = jnp.zeros_like(yb[2 * p])
            yb[2 * p + 1] = jnp.zeros_like(yb[2 * p + 1])

        for r in range(n_row):
            base = homes[r] * cpairs
            vec = jnp.concatenate([wt[r * rpairs + p] for p in range(rpairs)], axis=1)
            for u in range(0, cpairs, 2):
                cols = slice(u * 128, (u + 2) * 128)
                tail = slice(width + u * 128, width + (u + 2) * 128)
                prod = dot(vec, home[r, :, cols]) + dot(vec, home[r, :, tail])
                y[base + u] = y[base + u] + prod[:, :128]
                y[base + u + 1] = y[base + u + 1] + prod[:, 128:]

        def backward(i, carry):
            prods = [dot(wtb[lw[i * UNROLL + u]], blk[i * UNROLL + u]) for u in range(UNROLL)]
            for u in range(UNROLL):
                b = lv[i * UNROLL + u]
                yb[b] = yb[b] + prods[u]
            return carry

        lax.fori_loop(0, n_group, backward, 0)

        both = jnp.zeros((2 * k, k), jnp.float32)
        for q in range(0, n_dev, 4):
            his, los = [], []
            for d in range(q, q + 4):
                x = y[d] + jnp.concatenate([yb[2 * d], yb[2 * d + 1]], axis=1)
                hi, lo = split2(x * ic[d, 0:1, :])
                ph[d, :k, :] = hi
                ph[d, k:, :] = lo
                his.append(hi)
                los.append(lo)
            hi = jnp.concatenate(his, axis=1)
            lo = jnp.concatenate(los, axis=1)
            both = both + dot(jnp.concatenate([hi, lo], axis=0), hi, NT)
        gram = (both[:k] + (both[k:] + both[k:].T)) / total
        linv[...] = inverse_factor(gram)
        return carry

    lax.fori_loop(0, ITERS, iteration, 0)
    lh, ll = split2(linv[...])
    place = (2 * chip + core) * n_row + here
    hi, lo = ph[place, :k, :], ph[place, k:, :]
    x = dot(lh, hi) + dot(ll, hi) + dot(lh, lo)
    out[0] = x[:, :k]
    out[1] = x[:, k:]


def split3(x):
    a = lax.reduce_precision(x, 8, 7)
    b = lax.reduce_precision(x - a, 8, 7)
    return [v.astype(jnp.bfloat16) for v in (a, b, x - a - b)]


def swap(x, axis, distance):
    size = lax.axis_size(axis)
    return lax.ppermute(x, axis, [(i, i ^ distance) for i in range(size)])


def spread(x):
    near, far = jnp.stack([x, swap(x, "row", 1)]), jnp.stack([swap(x, "row", 2), swap(x, "row", 3)])
    near = jnp.concatenate([near, swap(near, "chip", 1)])
    far = jnp.concatenate([far, swap(far, "chip", 2)])
    mine = [near, swap(near, "chip", 2), far, swap(far, "chip", 1)]
    return mine + [swap(v, "core", 1) for v in mine]


def full_part(tile, has_full, n_chip, part, chip, core):
    tile = tile.reshape(2, n_chip, part, tile.shape[1])
    none = jnp.zeros(tile.shape[1:], tile.dtype)
    kept, sent = (
        jnp.where(has_full, lax.dynamic_index_in_dim(tile, i, 0, False), none)
        for i in (core, 1 - core)
    )
    both = kept + swap(sent, "core", 1)
    mine = lax.dynamic_index_in_dim(both, chip, 0, False)
    for s in range(1, n_chip):
        mine = mine + swap(lax.dynamic_index_in_dim(both, chip ^ s, 0, False), "chip", s)
    return mine


def whole_on_each(n_row, n_col, blocks, block_row, block_col, counts, vectors, row_mass, col_mass):
    tile = blocks[0, 0]
    n_cap = tile.shape[0]
    own, bsize = row_mass.shape
    k = vectors.shape[1] // bsize
    half = bsize // 2
    part = n_cap // n_col
    n_dev = n_row * n_col
    count = counts[0, 0]
    has_full = count > OFF_CAP
    bf16 = jnp.bfloat16
    row, chip, core = (lax.axis_index(name) for name in ("row", "chip", "core"))

    off = tile[:OFF_CAP].reshape(OFF_CAP * half, 128)
    inv_col = 1.0 / jnp.sqrt(col_mass)
    scaled = (vectors.reshape(own, k, bsize) * inv_col[:, None, :]).astype(bf16)
    scaled = scaled.transpose(1, 0, 2).reshape(k, own * bsize)
    mass = row_mass.reshape(own, half, 2).transpose(0, 2, 1).reshape(own * bsize)
    rows, cols = block_row[0, 0], block_col[0, 0]
    short = jnp.concatenate(
        [rows[:OFF_CAP], cols[:OFF_CAP], count[None], jnp.zeros(128 - 2 * OFF_CAP - 1, jnp.int32)]
    )
    meta = [v.astype(bf16) for v in (rows, cols, short)]
    meta = split3(mass) + split3(inv_col.reshape(own * bsize)) + meta
    meta = jnp.stack(meta + [jnp.zeros(128, bf16)] * (META - len(meta)))
    small = jnp.concatenate([off, scaled, meta], axis=0)
    smalls = spread(small)

    home = full_part(tile, has_full, n_col // 2, part, chip, core)
    home = home.reshape(part, half, 128).transpose(1, 0, 2).reshape(half * part, 128)
    homes = spread(home)

    at = small.shape[0] - META + 8
    ints = jnp.concatenate([v[:, at, :32] for v in smalls], axis=0).astype(jnp.int32)
    place = jnp.stack([row, chip, core]).astype(jnp.int32)

    height, width = 2 * n_col * bsize, 2 * n_row * bsize
    slots = n_dev * OFF_CAP + UNROLL
    pair_f32 = pltpu.VMEM((n_dev, k, 128), jnp.float32)
    pair_bf16 = pltpu.VMEM((n_dev, k, 128), bf16)
    block_f32 = pltpu.VMEM((2 * n_dev, k, bsize), jnp.float32)
    block_bf16 = pltpu.VMEM((2 * n_dev, k, bsize), bf16)
    mass_f32 = pltpu.VMEM((n_dev, 8, 128), jnp.float32)
    result = pl.pallas_call(
        functools.partial(kernel, n_row, n_col, n_cap, float(n_dev * own * bsize)),
        out_shape=jax.ShapeDtypeStruct((own, k, bsize), jnp.float32),
        in_specs=[pl.BlockSpec(memory_space=pltpu.SMEM)] * 2
        + [pl.BlockSpec(memory_space=pl.ANY)] * 16,
        out_specs=pl.BlockSpec(memory_space=pltpu.VMEM),
        scratch_shapes=[
            pltpu.SMEM((slots,), jnp.int32),
            pltpu.SMEM((slots,), jnp.int32),
            pltpu.SemaphoreType.DMA((16,)),
            pltpu.VMEM((n_dev,) + small.shape, bf16),
            pltpu.VMEM((n_dev,) + home.shape, bf16),
            pltpu.VMEM((n_row, height, 128), jnp.float32),
            pltpu.VMEM((n_row, height, 2 * width), bf16),
            pltpu.VMEM((slots, bsize, bsize), bf16),
            pair_bf16, block_bf16, pair_f32, block_f32,
            pair_bf16, block_bf16, pair_f32, block_f32,
            pltpu.VMEM((n_dev, 2 * k, 128), bf16),
            mass_f32, mass_f32,
            pltpu.VMEM((k, k), jnp.float32),
        ],
        compiler_params=pltpu.CompilerParams(vmem_limit_bytes=VMEM_LIMIT),
        name="iterate",
    )(ints, place, *smalls, *homes)
    return result.reshape(own, k * bsize)


def rotate(projected, gram):
    lower = jnp.linalg.cholesky(gram)
    inverse = lax.linalg.triangular_solve(
        lower, jnp.eye(gram.shape[0], dtype=jnp.float32), left_side=True, lower=True
    )
    return jnp.einsum(
        "kl,bli->bki",
        inverse,
        projected,
        precision=lax.Precision.HIGHEST,
        preferred_element_type=jnp.float32,
    )


def local_gram(projected):
    return jnp.einsum(
        "bki,bli->kl",
        projected,
        projected,
        precision=lax.Precision.HIGHEST,
        preferred_element_type=jnp.float32,
    )


def split_by_tile(blocks, block_row, block_col, counts, vectors, row_mass, col_mass):
    tile = blocks[0, 0]
    n_cap = tile.shape[0]
    bsize = row_mass.shape[1]
    vecs = vectors.shape[1] // bsize
    own = vectors.shape[0]
    n_row = lax.axis_size("row")
    n_col = lax.axis_size("col")
    row_panel = own * n_col
    col_panel = own * n_row
    total_boxes = float(own * bsize * n_row * n_col)
    rows_idx = block_row[0, 0]
    cols_idx = block_col[0, 0]
    live = jnp.arange(n_cap) < counts[0, 0]
    fwd_ids = jnp.where(live, rows_idx, row_panel)
    bwd_ids = jnp.where(live, cols_idx, col_panel)
    square = tile.reshape(n_cap, bsize, bsize)
    inv_col = 1.0 / jnp.sqrt(col_mass)
    current = vectors.reshape(own, vecs, bsize)
    for step in range(ITERS):
        scaled = (current * inv_col[:, None, :]).astype(jnp.bfloat16).reshape(own, vecs * bsize)
        panel = lax.all_gather(scaled, "row", axis=0, tiled=True)
        forward_taken = jnp.take(panel.reshape(col_panel, vecs, bsize), cols_idx, axis=0)
        forward_product = jnp.einsum(
            "bij,bkj->bki", square, forward_taken, preferred_element_type=jnp.float32
        )
        forward_summed = jax.ops.segment_sum(forward_product, fwd_ids, num_segments=row_panel + 1)
        rows_sum = lax.psum_scatter(
            forward_summed[:row_panel].reshape(row_panel, vecs * bsize),
            "col",
            scatter_dimension=0,
            tiled=True,
        )
        weighted = (rows_sum.reshape(own, vecs, bsize) * row_mass[:, None, :]).astype(jnp.bfloat16)
        whole_rows = lax.all_gather(weighted.reshape(own, vecs * bsize), "col", axis=0, tiled=True)
        taken = jnp.take(whole_rows.reshape(row_panel, vecs, bsize), rows_idx, axis=0)
        product = jnp.einsum("bij,bki->bkj", square, taken, preferred_element_type=jnp.float32)
        summed = jax.ops.segment_sum(product, bwd_ids, num_segments=col_panel + 1)
        cols_sum = lax.psum_scatter(
            summed[:col_panel].reshape(col_panel, vecs * bsize),
            "row",
            scatter_dimension=0,
            tiled=True,
        )
        projected = cols_sum.reshape(own, vecs, bsize) * inv_col[:, None, :]
        gram = lax.psum(local_gram(projected), ("row", "col")) / total_boxes
        current = rotate(projected, gram)
    return current.reshape(own, vecs * bsize)


def fits(n_row, n_col, blocks, vectors, row_mass):
    own, bsize = row_mass.shape[0] // (n_row * n_col), row_mass.shape[1]
    n_cap = blocks.shape[2]
    dense = n_row * (own * n_col * bsize) * (own * n_row * bsize) * 4
    shapes = own * bsize == 128 and vectors.shape[1] == bsize * bsize and n_cap == 128
    return dense <= VMEM_LIMIT // 4 and shapes and n_cap % (16 * n_col) == 0 and n_row == 4 and n_col == 8


def solution(mesh):
    n_row, n_col = mesh.shape["row"], mesh.shape["col"]

    def run(blocks, block_row, block_col, counts, vectors, row_mass, col_mass):
        args = (blocks, block_row, block_col, counts, vectors, row_mass, col_mass)
        if fits(n_row, n_col, blocks, vectors, row_mass):
            devices = mesh.devices.reshape(n_row, n_col // 2, 2)
            grid, col = jax.sharding.Mesh(devices, ("row", "chip", "core")), ("chip", "core")
            body = functools.partial(whole_on_each, n_row, n_col)
        else:
            grid, col, body = mesh, ("col",), split_by_tile
        by_row, by_col = P(("row",) + col, None), P(col + ("row",), None)
        in_specs = (
            P("row", col, None, None), P("row", col, None), P("row", col, None), P("row", col),
            by_col, by_row, by_col,
        )
        return jax.shard_map(
            body, mesh=grid, in_specs=in_specs, out_specs=by_col, check_vma=False
        )(*args)

    return run
```

profile of v0, /device:TPU:0, one launch (start us, length us, event | category | flops | bytes accessed | tf_op | source)
XLA Modules:
  0.0 155.8 jit_solution(3496349511282055943)
XLA Ops:
  0.8 1.1 select_bitcast_fusion
  1.9 0.5 collective-permute-start.11
  2.4 0.1 copy-done.16
  2.5 0.7 copy-done.14
  3.3 0.6 copy-done.13
  4.2 0.5 copy-done.12
  4.6 0.1 reshape.204
  4.9 3.0 %collective-permute-start.12 = (bf16[16,4096]{1,0:T(8,128)(2,1)S(1)}, bf16[16,4096]{1,0:T(8,128)(2,1)S(1)}, u32[]{:S(2)}, u32[]{:S(2)}) collective-permute-start(bf16[16,4096]{1,0:T(8,128)(2,1)S(1)} %get-tuple-element.5), channel_id=1, source_target_pairs={{0,2},{2,0},{4,6},{6,4},{1,3},{3,1},{5,7},{7,5},{8,10},{10,8},{12,... | collective-permute-start | bytes 393224 | tf_op jit(solution)/shard_map/ppermute | solution.py:266
  7.9 1.5 collective-permute-start.14
  9.8 2.1 %collective-permute-start = (bf16[336,128]{1,0:T(8,128)(2,1)S(1)}, bf16[336,128]{1,0:T(8,128)(2,1)S(1)}, u32[]{:S(2)}, u32[]{:S(2)}) collective-permute-start(bf16[336,128]{1,0:T(8,128)(2,1)S(1)} %concatenate.48), channel_id=1, source_target_pairs={{0,8},{8,0},{16,24},{24,16},{1,9},{9,1},{17,25},{25,17},{2,10},{10... | collective-permute-start | bytes 258056 | tf_op jit(solution)/shard_map/ppermute | solution.py:266
  11.9 3.7 %collective-permute-done.14 = bf16[16,4096]{1,0:T(8,128)(2,1)S(1)} collective-permute-done((bf16[16,4096]{1,0:T(8,128)(2,1)S(1)}, bf16[16,4096]{1,0:T(8,128)(2,1)S(1)}, u32[]{:S(2)}, u32[]{:S(2)}) %collective-permute-start.14) | collective-permute-done | bytes 131104 | tf_op jit(solution)/shard_map/ppermute | solution.py:266
  15.6 1.4 collective-permute-done.13
  17.1 1.6 %collective-permute-start.15 = (bf16[512,128]{1,0:T(8,128)(2,1)S(1)}, bf16[512,128]{1,0:T(8,128)(2,1)S(1)}, u32[]{:S(2)}, u32[]{:S(2)}) collective-permute-start(bf16[512,128]{1,0:T(8,128)(2,1)S(1)} %bitcast.78), channel_id=1, source_target_pairs={{0,8},{8,0},{16,24},{24,16},{1,9},{9,1},{17,25},{25,17},{2,10},{10... | collective-permute-start | bytes 393224 | tf_op jit(solution)/shard_map/ppermute | solution.py:266
  18.8 2.5 %collective-permute-start.4 = (bf16[336,128]{1,0:T(8,128)(2,1)S(1)}, bf16[336,128]{1,0:T(8,128)(2,1)S(1)}, u32[]{:S(2)}, u32[]{:S(2)}) collective-permute-start(bf16[336,128]{1,0:T(8,128)(2,1)S(1)} %concatenate.48), channel_id=1, source_target_pairs={{0,24},{8,16},{16,8},{24,0},{1,25},{9,17},{17,9},{25,1},{2,26},{10... | collective-permute-start | bytes 258056 | tf_op jit(solution)/shard_map/ppermute | solution.py:266
  21.2 0.1 collective-permute-start.3
  21.4 2.9 %collective-permute-start.19 = (bf16[512,128]{1,0:T(8,128)(2,1)S(1)}, bf16[512,128]{1,0:T(8,128)(2,1)S(1)}, u32[]{:S(2)}, u32[]{:S(2)}) collective-permute-start(bf16[512,128]{1,0:T(8,128)(2,1)S(1)} %bitcast.79), channel_id=1, source_target_pairs={{0,24},{8,16},{16,8},{24,0},{1,25},{9,17},{17,9},{25,1},{2,26},{10... | collective-permute-start | bytes 393224 | tf_op jit(solution)/shard_map/ppermute | solution.py:266
  24.3 0.3 collective-permute-start.18
  24.7 1.6 collective-permute-start.1
  26.2 5.5 %collective-permute-done.19 = bf16[512,128]{1,0:T(8,128)(2,1)S(1)} collective-permute-done((bf16[512,128]{1,0:T(8,128)(2,1)S(1)}, bf16[512,128]{1,0:T(8,128)(2,1)S(1)}, u32[]{:S(2)}, u32[]{:S(2)}) %collective-permute-start.19) | collective-permute-done | bytes 131104 | tf_op jit(solution)/shard_map/ppermute | solution.py:266
  31.7 1.5 collective-permute-start.16
  33.2 6.8 %collective-permute-done.18 = bf16[512,128]{1,0:T(8,128)(2,1)S(1)} collective-permute-done((bf16[512,128]{1,0:T(8,128)(2,1)S(1)}, bf16[512,128]{1,0:T(8,128)(2,1)S(1)}, u32[]{:S(2)}, u32[]{:S(2)}) %collective-permute-start.18) | collective-permute-done | bytes 131104 | tf_op jit(solution)/shard_map/ppermute | solution.py:266
  40.1 0.4 collective-permute-start.20
  40.5 1.8 %collective-permute-start.5 = (bf16[2,336,128]{2,1,0:T(8,128)(2,1)S(1)}, bf16[2,336,128]{2,1,0:T(8,128)(2,1)S(1)}, u32[]{:S(2)}, u32[]{:S(2)}) collective-permute-start(bf16[2,336,128]{2,1,0:T(8,128)(2,1)S(1)} %pad_maximum_fusion.7), channel_id=1, source_target_pairs={{0,4},{2,6},{4,0},{6,2},{1,5},{3,7},{5,1},{7,3},{8,12},{10,14},{12... | collective-permute-start | bytes 516104 | tf_op jit(solution)/shard_map/ppermute | solution.py:266
  42.5 0.4 collective-permute-start.17
  42.8 6.5 %collective-permute-done.20 = bf16[2,512,128]{2,1,0:T(8,128)(2,1)S(1)} collective-permute-done((bf16[2,512,128]{2,1,0:T(8,128)(2,1)S(1)}, bf16[2,512,128]{2,1,0:T(8,128)(2,1)S(1)}, u32[]{:S(2)}, u32[]{:S(2)}) %collective-permute-start.20) | collective-permute-done | bytes 262176 | tf_op jit(solution)/shard_map/ppermute | solution.py:266
  49.4 1.6 collective-permute-start.21
  51.0 0.5 collective-permute-start.2
  51.5 1.6 collective-permute-done.5
  53.2 1.6 collective-permute-start.6
  54.8 15.2 %collective-permute-done.2.rest_1_ = bf16[4,336,128]{2,1,0:T(8,128)(2,1)S(1)} collective-permute-done((bf16[4,336,128]{2,1,0:T(8,128)(2,1)S(1)}, bf16[4,336,128]{2,1,0:T(8,128)(2,1)S(1)}, u32[]{:S(2)}, u32[]{:S(2)}) %collective-permute-start.2) | collective-permute-done | bytes 344096 | tf_op jit(solution)/shard_map/ppermute | solution.py:266
  70.0 0.6 collective-permute-start.22
  70.7 0.4 collective-permute-start.23
  71.1 0.1 collective-permute-start.25
  71.3 0.4 collective-permute-done.8.rest_5_
  71.7 0.7 copy-done.11
  72.4 0.1 collective-permute-start.10
  72.5 0.7 pad_add_fusion.own
  73.2 0.7 slice.53
  73.9 0.7 slice.50
  74.6 0.7 slice.55
  75.3 0.7 slice.52
  76.1 0.7 slice.54
  76.8 0.7 slice.56
  77.5 0.1 concatenate.51
  77.6 0.6 convert_element_type.111.meta
  78.3 0.7 copy-done.7
  79.0 75.2 %iterate.1 = f32[2,64,64]{2,1,0:T(8,128)} custom-call(s32[32,32]{1,0:T(8,128)} %convert_element_type.111.meta, s32[3]{0:T(128)} %pad_add_fusion.own, bf16[4,336,128]{2,1,0:T(8,128)(2,1)} %copy-done.2, bf16[4,336,128]{2,1,0:T(8,128)(2,1)} %copy-done.9, bf16[4,336,128]{2,1,0:T(8,128)(2,1)} %copy-done.3, bf16[4,336,128]{2,1,0:T(8,128)(2,1)} %collective-permute-done.6.rest_3_, ...), custom_call_target="tpu_custom_call" | custom-call | tf_op jit(solution)/shard_map/iterate/pallas_call | solution.py:334
  154.3 1.5 reshape.211
  (94 shorter events, 1.6 us)
Async XLA Ops:
  0.0 4.8 %copy-start.4 = (bf16[1,1,128,4096]{3,2,1,0:T(8,128)(2,1)S(1)}, bf16[1,1,128,4096]{3,2,1,0:T(8,128)(2,1)}, u32[]{:S(2)}) copy-start(bf16[1,1,128,4096]{3,2,1,0:T(8,128)(2,1)} %param.7) | copy-start | bytes 3145732
  0.7 1.6 %copy-start.15 = (s32[1,1,128]{2,1,0:T(1,128)S(1)}, s32[1,1,128]{2,1,0:T(1,128)}, u32[]{:S(2)}) copy-start(s32[1,1,128]{2,1,0:T(1,128)} %param.8) | copy-start | bytes 1540
  1.8 0.7 copy-start.16
  1.9 2.9 %collective-permute-start.11 = (bf16[4,16,4096]{2,1,0:T(8,128)(2,1)S(1)}, bf16[4,16,4096]{2,1,0:T(8,128)(2,1)S(1)}, u32[]{:S(2)}, u32[]{:S(2)}) collective-permute-start(bf16[4,16,4096]{2,1,0:T(8,128)(2,1)S(1)} %select_bitcast_fusion), channel_id=1, source_target_pairs={{0,1},{1,0},{2,3},{3,2},{4,5},{5,4},{6,7},{7,6},{8,9},{9,8},{10,11... | collective-permute-start | bytes 1572872 | tf_op jit(solution)/shard_map/ppermute | solution.py:266
  2.5 0.7 copy-start.14
  3.2 0.7 copy-start.13
  3.9 0.8 copy-start.12
  4.9 7.0 %collective-permute-start.12 = (bf16[16,4096]{1,0:T(8,128)(2,1)S(1)}, bf16[16,4096]{1,0:T(8,128)(2,1)S(1)}, u32[]{:S(2)}, u32[]{:S(2)}) collective-permute-start(bf16[16,4096]{1,0:T(8,128)(2,1)S(1)} %get-tuple-element.5), channel_id=1, source_target_pairs={{0,2},{2,0},{4,6},{6,4},{1,3},{3,1},{5,7},{7,5},{8,10},{10,8},{12,... | collective-permute-start | bytes 393224 | tf_op jit(solution)/shard_map/ppermute | solution.py:266
  7.9 7.7 %collective-permute-start.14 = (bf16[16,4096]{1,0:T(8,128)(2,1)S(1)}, bf16[16,4096]{1,0:T(8,128)(2,1)S(1)}, u32[]{:S(2)}, u32[]{:S(2)}) collective-permute-start(bf16[16,4096]{1,0:T(8,128)(2,1)S(1)} %get-tuple-element.6), channel_id=1, source_target_pairs={{0,6},{2,4},{4,2},{6,0},{1,7},{3,5},{5,3},{7,1},{8,14},{10,12},{12... | collective-permute-start | bytes 393224 | tf_op jit(solution)/shard_map/ppermute | solution.py:266
  9.4 7.6 %collective-permute-start.13 = (bf16[16,4096]{1,0:T(8,128)(2,1)S(1)}, bf16[16,4096]{1,0:T(8,128)(2,1)S(1)}, u32[]{:S(2)}, u32[]{:S(2)}) collective-permute-start(bf16[16,4096]{1,0:T(8,128)(2,1)S(1)} %get-tuple-element.7), channel_id=1, source_target_pairs={{0,4},{2,6},{4,0},{6,2},{1,5},{3,7},{5,1},{7,3},{8,12},{10,14},{12... | collective-permute-start | bytes 393224 | tf_op jit(solution)/shard_map/ppermute | solution.py:266
  9.8 14.4 %collective-permute-start = (bf16[336,128]{1,0:T(8,128)(2,1)S(1)}, bf16[336,128]{1,0:T(8,128)(2,1)S(1)}, u32[]{:S(2)}, u32[]{:S(2)}) collective-permute-start(bf16[336,128]{1,0:T(8,128)(2,1)S(1)} %concatenate.48), channel_id=1, source_target_pairs={{0,8},{8,0},{16,24},{24,16},{1,9},{9,1},{17,25},{25,17},{2,10},{10... | collective-permute-start | bytes 258056 | tf_op jit(solution)/shard_map/ppermute | solution.py:266
  17.1 7.5 %collective-permute-start.15 = (bf16[512,128]{1,0:T(8,128)(2,1)S(1)}, bf16[512,128]{1,0:T(8,128)(2,1)S(1)}, u32[]{:S(2)}, u32[]{:S(2)}) collective-permute-start(bf16[512,128]{1,0:T(8,128)(2,1)S(1)} %bitcast.78), channel_id=1, source_target_pairs={{0,8},{8,0},{16,24},{24,16},{1,9},{9,1},{17,25},{25,17},{2,10},{10... | collective-permute-start | bytes 393224 | tf_op jit(solution)/shard_map/ppermute | solution.py:266
  18.8 21.7 %collective-permute-start.4 = (bf16[336,128]{1,0:T(8,128)(2,1)S(1)}, bf16[336,128]{1,0:T(8,128)(2,1)S(1)}, u32[]{:S(2)}, u32[]{:S(2)}) collective-permute-start(bf16[336,128]{1,0:T(8,128)(2,1)S(1)} %concatenate.48), channel_id=1, source_target_pairs={{0,24},{8,16},{16,8},{24,0},{1,25},{9,17},{17,9},{25,1},{2,26},{10... | collective-permute-start | bytes 258056 | tf_op jit(solution)/shard_map/ppermute | solution.py:266
  21.2 19.2 %collective-permute-start.3 = (bf16[336,128]{1,0:T(8,128)(2,1)S(1)}, bf16[336,128]{1,0:T(8,128)(2,1)S(1)}, u32[]{:S(2)}, u32[]{:S(2)}) collective-permute-start(bf16[336,128]{1,0:T(8,128)(2,1)S(1)} %concatenate.48), channel_id=1, source_target_pairs={{0,16},{8,24},{16,0},{24,8},{1,17},{9,25},{17,1},{25,9},{2,18},{10... | collective-permute-start | bytes 258056 | tf_op jit(solution)/shard_map/ppermute | solution.py:266
  21.4 10.4 %collective-permute-start.19 = (bf16[512,128]{1,0:T(8,128)(2,1)S(1)}, bf16[512,128]{1,0:T(8,128)(2,1)S(1)}, u32[]{:S(2)}, u32[]{:S(2)}) collective-permute-start(bf16[512,128]{1,0:T(8,128)(2,1)S(1)} %bitcast.79), channel_id=1, source_target_pairs={{0,24},{8,16},{16,8},{24,0},{1,25},{9,17},{17,9},{25,1},{2,26},{10... | collective-permute-start | bytes 393224 | tf_op jit(solution)/shard_map/ppermute | solution.py:266
  24.3 15.7 %collective-permute-start.18 = (bf16[512,128]{1,0:T(8,128)(2,1)S(1)}, bf16[512,128]{1,0:T(8,128)(2,1)S(1)}, u32[]{:S(2)}, u32[]{:S(2)}) collective-permute-start(bf16[512,128]{1,0:T(8,128)(2,1)S(1)} %bitcast.80), channel_id=1, source_target_pairs={{0,16},{8,24},{16,0},{24,8},{1,17},{9,25},{17,1},{25,9},{2,18},{10... | collective-permute-start | bytes 393224 | tf_op jit(solution)/shard_map/ppermute | solution.py:266
  24.7 17.6 %collective-permute-start.1 = (bf16[2,336,128]{2,1,0:T(8,128)(2,1)S(1)}, bf16[2,336,128]{2,1,0:T(8,128)(2,1)S(1)}, u32[]{:S(2)}, u32[]{:S(2)}) collective-permute-start(bf16[2,336,128]{2,1,0:T(8,128)(2,1)S(1)} %pad_maximum_fusion.6), channel_id=1, source_target_pairs={{0,2},{2,0},{4,6},{6,4},{1,3},{3,1},{5,7},{7,5},{8,10},{10,8},{12,... | collective-permute-start | bytes 516104 | tf_op jit(solution)/shard_map/ppermute | solution.py:266
  31.7 10.7 %collective-permute-start.16 = (bf16[2,512,128]{2,1,0:T(8,128)(2,1)S(1)}, bf16[2,512,128]{2,1,0:T(8,128)(2,1)S(1)}, u32[]{:S(2)}, u32[]{:S(2)}) collective-permute-start(bf16[2,512,128]{2,1,0:T(8,128)(2,1)S(1)} %pad_maximum_fusion.4), channel_id=1, source_target_pairs={{0,2},{2,0},{4,6},{6,4},{1,3},{3,1},{5,7},{7,5},{8,10},{10,8},{12,... | collective-permute-start | bytes 786440 | tf_op jit(solution)/shard_map/ppermute | solution.py:266
  40.1 9.3 %collective-permute-start.20 = (bf16[2,512,128]{2,1,0:T(8,128)(2,1)S(1)}, bf16[2,512,128]{2,1,0:T(8,128)(2,1)S(1)}, u32[]{:S(2)}, u32[]{:S(2)}) collective-permute-start(bf16[2,512,128]{2,1,0:T(8,128)(2,1)S(1)} %pad_maximum_fusion.5), channel_id=1, source_target_pairs={{0,4},{2,6},{4,0},{6,2},{1,5},{3,7},{5,1},{7,3},{8,12},{10,14},{12... | collective-permute-start | bytes 786440 | tf_op jit(solution)/shard_map/ppermute | solution.py:266
  40.5 12.6 %collective-permute-start.5 = (bf16[2,336,128]{2,1,0:T(8,128)(2,1)S(1)}, bf16[2,336,128]{2,1,0:T(8,128)(2,1)S(1)}, u32[]{:S(2)}, u32[]{:S(2)}) collective-permute-start(bf16[2,336,128]{2,1,0:T(8,128)(2,1)S(1)} %pad_maximum_fusion.7), channel_id=1, source_target_pairs={{0,4},{2,6},{4,0},{6,2},{1,5},{3,7},{5,1},{7,3},{8,12},{10,14},{12... | collective-permute-start | bytes 516104 | tf_op jit(solution)/shard_map/ppermute | solution.py:266
  42.3 30.9 %copy-start.2 = (bf16[4,336,128]{2,1,0:T(8,128)(2,1)}, bf16[4,336,128]{2,1,0:T(8,128)(2,1)S(1)}, u32[]{:S(2)}) copy-start(bf16[4,336,128]{2,1,0:T(8,128)(2,1)S(1)} %pad_maximum_fusion.2.rest_0_) | copy-start | bytes 1032196
  42.3 10.9 %collective-permute-start.7 = (bf16[4,336,128]{2,1,0:T(8,128)(2,1)S(1)}, bf16[4,336,128]{2,1,0:T(8,128)(2,1)S(1)}, u32[]{:S(2)}, u32[]{:S(2)}) collective-permute-start(bf16[4,336,128]{2,1,0:T(8,128)(2,1)S(1)} %pad_maximum_fusion.2.rest_0_), channel_id=1, source_target_pairs={{0,1},{1,0},{2,3},{3,2},{4,5},{5,4},{6,7},{7,6},{8,9},{9,8},{10,11... | collective-permute-start | bytes 1032200 | tf_op jit(solution)/shard_map/ppermute | solution.py:266
  42.4 27.6 %copy-start = (bf16[4,512,128]{2,1,0:T(8,128)(2,1)}, bf16[4,512,128]{2,1,0:T(8,128)(2,1)S(1)}, u32[]{:S(2)}) copy-start(bf16[4,512,128]{2,1,0:T(8,128)(2,1)S(1)} %pad_maximum_fusion.rest_8_) | copy-start | bytes 1572868
  42.5 28.2 %collective-permute-start.17 = (bf16[4,512,128]{2,1,0:T(8,128)(2,1)S(1)}, bf16[4,512,128]{2,1,0:T(8,128)(2,1)S(1)}, u32[]{:S(2)}, u32[]{:S(2)}) collective-permute-start(bf16[4,512,128]{2,1,0:T(8,128)(2,1)S(1)} %pad_maximum_fusion.rest_8_), channel_id=1, source_target_pairs={{0,4},{2,6},{4,0},{6,2},{1,5},{3,7},{5,1},{7,3},{8,12},{10,14},{12... | collective-permute-start | bytes 1572872 | tf_op jit(solution)/shard_map/ppermute | solution.py:266
  49.4 28.8 %copy-start.1 = (bf16[4,512,128]{2,1,0:T(8,128)(2,1)}, bf16[4,512,128]{2,1,0:T(8,128)(2,1)S(1)}, u32[]{:S(2)}) copy-start(bf16[4,512,128]{2,1,0:T(8,128)(2,1)S(1)} %pad_maximum_fusion.1.rest_10_) | copy-start | bytes 1572868
  49.4 21.7 %collective-permute-start.21 = (bf16[4,512,128]{2,1,0:T(8,128)(2,1)S(1)}, bf16[4,512,128]{2,1,0:T(8,128)(2,1)S(1)}, u32[]{:S(2)}, u32[]{:S(2)}) collective-permute-start(bf16[4,512,128]{2,1,0:T(8,128)(2,1)S(1)} %pad_maximum_fusion.1.rest_10_), channel_id=1, source_target_pairs={{0,2},{2,0},{4,6},{6,4},{1,3},{3,1},{5,7},{7,5},{8,10},{10,8},{12,... | collective-permute-start | bytes 1572872 | tf_op jit(solution)/shard_map/ppermute | solution.py:266
  51.0 19.0 %collective-permute-start.2 = (bf16[4,336,128]{2,1,0:T(8,128)(2,1)S(1)}, bf16[4,336,128]{2,1,0:T(8,128)(2,1)S(1)}, u32[]{:S(2)}, u32[]{:S(2)}) collective-permute-start(bf16[4,336,128]{2,1,0:T(8,128)(2,1)S(1)} %pad_maximum_fusion.2.rest_0_), channel_id=1, source_target_pairs={{0,4},{2,6},{4,0},{6,2},{1,5},{3,7},{5,1},{7,3},{8,12},{10,14},{12... | collective-permute-start | bytes 1032200 | tf_op jit(solution)/shard_map/ppermute | solution.py:266
  53.1 25.2 %copy-start.3 = (bf16[4,336,128]{2,1,0:T(8,128)(2,1)}, bf16[4,336,128]{2,1,0:T(8,128)(2,1)S(1)}, u32[]{:S(2)}) copy-start(bf16[4,336,128]{2,1,0:T(8,128)(2,1)S(1)} %pad_maximum_fusion.3.rest_2_) | copy-start | bytes 1032196
  53.1 16.9 %collective-permute-start.9 = (bf16[4,336,128]{2,1,0:T(8,128)(2,1)S(1)}, bf16[4,336,128]{2,1,0:T(8,128)(2,1)S(1)}, u32[]{:S(2)}, u32[]{:S(2)}) collective-permute-start(bf16[4,336,128]{2,1,0:T(8,128)(2,1)S(1)} %pad_maximum_fusion.3.rest_2_), channel_id=1, source_target_pairs={{0,1},{1,0},{2,3},{3,2},{4,5},{5,4},{6,7},{7,6},{8,9},{9,8},{10,11... | collective-permute-start | bytes 1032200 | tf_op jit(solution)/shard_map/ppermute | solution.py:266
  53.2 16.8 %copy-start.8 = (bf16[4,336,128]{2,1,0:T(8,128)(2,1)}, bf16[4,336,128]{2,1,0:T(8,128)(2,1)S(1)}, u32[]{:S(2)}) copy-start(bf16[4,336,128]{2,1,0:T(8,128)(2,1)S(1)} %collective-permute-done.7.rest_4_) | copy-start | bytes 1032196
  53.2 17.4 %collective-permute-start.6 = (bf16[4,336,128]{2,1,0:T(8,128)(2,1)S(1)}, bf16[4,336,128]{2,1,0:T(8,128)(2,1)}, u32[]{:S(2)}, u32[]{:S(2)}) collective-permute-start(bf16[4,336,128]{2,1,0:T(8,128)(2,1)S(1)} %pad_maximum_fusion.3.rest_2_), channel_id=1, source_target_pairs={{0,2},{2,0},{4,6},{6,4},{1,3},{3,1},{5,7},{7,5},{8,10},{10,8},{12,... | collective-permute-start | bytes 1032200 | tf_op jit(solution)/shard_map/ppermute | solution.py:266
  70.0 1.1 copy-start.9
  70.0 1.7 %collective-permute-start.8 = (bf16[4,336,128]{2,1,0:T(8,128)(2,1)S(1)}, bf16[4,336,128]{2,1,0:T(8,128)(2,1)S(1)}, u32[]{:S(2)}, u32[]{:S(2)}) collective-permute-start(bf16[4,336,128]{2,1,0:T(8,128)(2,1)S(1)} %collective-permute-done.2.rest_1_), channel_id=1, source_target_pairs={{0,1},{1,0},{2,3},{3,2},{4,5},{5,4},{6,7},{7,6},{8,9},{9,8},{10,11... | collective-permute-start | bytes 1032200 | tf_op jit(solution)/shard_map/ppermute | solution.py:266
  70.0 1.6 %copy-start.10 = (bf16[4,336,128]{2,1,0:T(8,128)(2,1)}, bf16[4,336,128]{2,1,0:T(8,128)(2,1)S(1)}, u32[]{:S(2)}) copy-start(bf16[4,336,128]{2,1,0:T(8,128)(2,1)S(1)} %collective-permute-done.9.rest_6_) | copy-start | bytes 1032196
  70.0 8.2 %collective-permute-start.22 = (bf16[4,512,128]{2,1,0:T(8,128)(2,1)S(1)}, bf16[4,512,128]{2,1,0:T(8,128)(2,1)S(1)}, u32[]{:S(2)}, u32[]{:S(2)}) collective-permute-start(bf16[4,512,128]{2,1,0:T(8,128)(2,1)S(1)} %pad_maximum_fusion.rest_8_), channel_id=1, source_target_pairs={{0,1},{1,0},{2,3},{3,2},{4,5},{5,4},{6,7},{7,6},{8,9},{9,8},{10,11... | collective-permute-start | bytes 1572872 | tf_op jit(solution)/shard_map/ppermute | solution.py:266
  70.6 7.6 %collective-permute-start.24 = (bf16[4,512,128]{2,1,0:T(8,128)(2,1)S(1)}, bf16[4,512,128]{2,1,0:T(8,128)(2,1)}, u32[]{:S(2)}, u32[]{:S(2)}) collective-permute-start(bf16[4,512,128]{2,1,0:T(8,128)(2,1)S(1)} %pad_maximum_fusion.1.rest_10_), channel_id=1, source_target_pairs={{0,1},{1,0},{2,3},{3,2},{4,5},{5,4},{6,7},{7,6},{8,9},{9,8},{10,11... | collective-permute-start | bytes 1572872 | tf_op jit(solution)/shard_map/ppermute | solution.py:266
  70.7 7.6 %copy-start.5 = (bf16[4,512,128]{2,1,0:T(8,128)(2,1)}, bf16[4,512,128]{2,1,0:T(8,128)(2,1)S(1)}, u32[]{:S(2)}) copy-start(bf16[4,512,128]{2,1,0:T(8,128)(2,1)S(1)} %collective-permute-done.17.rest_9_) | copy-start | bytes 1572868
  70.7 7.5 %collective-permute-start.23 = (bf16[4,512,128]{2,1,0:T(8,128)(2,1)S(1)}, bf16[4,512,128]{2,1,0:T(8,128)(2,1)}, u32[]{:S(2)}, u32[]{:S(2)}) collective-permute-start(bf16[4,512,128]{2,1,0:T(8,128)(2,1)S(1)} %collective-permute-done.17.rest_9_), channel_id=1, source_target_pairs={{0,1},{1,0},{2,3},{3,2},{4,5},{5,4},{6,7},{7,6},{8,9},{9,8},{10,11... | collective-permute-start | bytes 1572872 | tf_op jit(solution)/shard_map/ppermute | solution.py:266
  71.1 7.1 %copy-start.6 = (bf16[4,512,128]{2,1,0:T(8,128)(2,1)}, bf16[4,512,128]{2,1,0:T(8,128)(2,1)S(1)}, u32[]{:S(2)}) copy-start(bf16[4,512,128]{2,1,0:T(8,128)(2,1)S(1)} %collective-permute-done.21.rest_11_) | copy-start | bytes 1572868
  71.1 7.1 %collective-permute-start.25 = (bf16[4,512,128]{2,1,0:T(8,128)(2,1)S(1)}, bf16[4,512,128]{2,1,0:T(8,128)(2,1)}, u32[]{:S(2)}, u32[]{:S(2)}) collective-permute-start(bf16[4,512,128]{2,1,0:T(8,128)(2,1)S(1)} %collective-permute-done.21.rest_11_), channel_id=1, source_target_pairs={{0,1},{1,0},{2,3},{3,2},{4,5},{5,4},{6,7},{7,6},{8,9},{9,8},{10,11... | collective-permute-start | bytes 1572872 | tf_op jit(solution)/shard_map/ppermute | solution.py:266
  71.7 0.7 copy-start.11
  72.4 4.4 %collective-permute-start.10 = (bf16[4,336,128]{2,1,0:T(8,128)(2,1)}, bf16[4,336,128]{2,1,0:T(8,128)(2,1)}, u32[]{:S(2)}, u32[]{:S(2)}) collective-permute-start(bf16[4,336,128]{2,1,0:T(8,128)(2,1)} %collective-permute-done.6.rest_3_), channel_id=1, source_target_pairs={{0,1},{1,0},{2,3},{3,2},{4,5},{5,4},{6,7},{7,6},{8,9},{9,8},{10,11... | collective-permute-start | bytes 1032200 | tf_op jit(solution)/shard_map/ppermute | solution.py:266
  78.2 0.8 copy-start.7
where the time goes:
time: 157 us; the launch traced here: 156 us
  Pallas kernels  75.2 us (48%)
  waiting for transfers between devices  41.1 us (26%)
  starting transfers between devices  25.3 us (16%)
  local copies, waits for them, and re-layouts  10.2 us (6%)
  other arithmetic  2.81 us (2%)
    pallas_call x1, Pallas kernels, whole_on_each(): pl.pallas_call(functools.partial(kernel, n_row, n_col, n_cap, float(n_dev...  75.2 us
    ppermute x26, waiting for transfers between devices, swap(): return lax.ppermute(x, axis, [(i, i ^ distance) for i in range(size)])  41.1 us
    ppermute x26, starting transfers between devices, swap(): return lax.ppermute(x, axis, [(i, i ^ distance) for i in range(size)])  25.3 us
    slice x8, local copies, waits for them, and re-layouts, whole_on_each(): v[:, at, :32]  4.22 us
    unnamed x43, local copies, waits for them, and re-layouts  3.45 us
  transfers between devices with their start and end apart: 26, of which 8 were waited for; matrix products, arithmetic and copies ran while one was open for 4% of the time, Pallas kernels for 0%

commit v1 on v0

--- a/solution.py
+++ b/solution.py
@@ -11,7 +11,7 @@
 OFF_CAP = 8
 META = 16
 UNROLL = 8
-VMEM_LIMIT = 56 * 1024 * 1024
+VMEM_LIMIT = 40 * 1024 * 1024
 
 NT = (((1,), (1,)), ((), ()))
 NN = (((1,), (0,)), ((), ()))
@@ -24,6 +24,13 @@
 def split2(x):
     hi = x.astype(jnp.bfloat16)
     return hi, (x - hi.astype(jnp.float32)).astype(jnp.bfloat16)
+
+
+def reciprocal(x):
+    y = pl.reciprocal(x, approx=True)
+    for _ in range(2):
+        y = y * (2.0 - x * y)
+    return y
 
 
 def inverse_factor(gram):
@@ -42,7 +49,7 @@
             for t in range(b, count)
         }
         for s in range(8):
-            inv = 1.0 / spread[b][s][s : s + 1]
+            inv = reciprocal(spread[b][s][s : s + 1])
             step = tiles[b][s : s + 1] * inv
             ahead = [spread[b][s2][s : s + 1] * inv for s2 in range(s + 1, 8)]
             for t in range(b, count):
@@ -61,11 +68,11 @@
 
 def kernel(
     n_row, n_col, n_cap, total,
-    meta, own, *rest,
+    own, *rest,
 ):
     smalls, fulls, out = rest[:8], rest[8:16], rest[16]
-    lv, lw, sems, small, full, tmp, home, blk = rest[17:25]
-    vs, vb, w, wb, wt, wtb, y, yb, ph, rm, ic, linv = rest[25:]
+    ints, meta, lv, lw, sems, small, full, tmp, home, blk = rest[17:27]
+    vs, vb, w, wb, wt, wtb, y, yb, ph, rm, ic, linv = rest[27:]
     n_dev = n_row * n_col
     group = n_dev // 2
     k = vs.shape[1]
@@ -87,6 +94,11 @@
             waits.append(copy)
     for copy in waits[:8]:
         copy.wait()
+    for d in range(n_dev):
+        rows = small[d, meta_at : meta_at + META, :].astype(jnp.float32)
+        ints[d : d + 1, :] = rows[8:9].astype(jnp.int32)
+    to_scalars = pltpu.make_async_copy(ints, meta, sems.at[16])
+    to_scalars.start()
 
     def at_device(r, c):
         dr, dc, dk = here ^ r, chip ^ (c // 2), core ^ (c % 2)
@@ -106,6 +118,8 @@
             rm[p] = jnp.broadcast_to(rows[0:1] + rows[1:2] + rows[2:3], (8, 128))
             ic[q] = jnp.broadcast_to(rows[3:4] + rows[4:5] + rows[5:6], (8, 128))
             scatter_pair(vs, vb, q, small[d, vec_at : vec_at + k, :].astype(jnp.float32))
+
+    to_scalars.wait()
 
     def device(d, n):
         count = meta[d, 2 * OFF_CAP]
@@ -266,12 +280,19 @@
     return lax.ppermute(x, axis, [(i, i ^ distance) for i in range(size)])
 
 
-def spread(x):
-    near, far = jnp.stack([x, swap(x, "row", 1)]), jnp.stack([swap(x, "row", 2), swap(x, "row", 3)])
+def along_rows(x):
+    return [x] + [swap(x, "row", s) for s in range(1, lax.axis_size("row"))]
+
+
+def along_chips(x):
+    near, far = jnp.stack(x[:2]), jnp.stack(x[2:])
     near = jnp.concatenate([near, swap(near, "chip", 1)])
     far = jnp.concatenate([far, swap(far, "chip", 2)])
-    mine = [near, swap(near, "chip", 2), far, swap(far, "chip", 1)]
-    return mine + [swap(v, "core", 1) for v in mine]
+    return [near, swap(near, "chip", 2), far, swap(far, "chip", 1)]
+
+
+def with_other_core(x):
+    return x + [swap(v, "core", 1) for v in x]
 
 
 def full_part(tile, has_full, n_chip, part, chip, core):
@@ -314,14 +335,15 @@
     meta = split3(mass) + split3(inv_col.reshape(own * bsize)) + meta
     meta = jnp.stack(meta + [jnp.zeros(128, bf16)] * (META - len(meta)))
     small = jnp.concatenate([off, scaled, meta], axis=0)
-    smalls = spread(small)
-
     home = full_part(tile, has_full, n_col // 2, part, chip, core)
     home = home.reshape(part, half, 128).transpose(1, 0, 2).reshape(half * part, 128)
-    homes = spread(home)
-
-    at = small.shape[0] - META + 8
-    ints = jnp.concatenate([v[:, at, :32] for v in smalls], axis=0).astype(jnp.int32)
+
+    smalls = along_rows(small)
+    home, smalls = lax.optimization_barrier((home, smalls))
+    homes, smalls = along_rows(home), along_chips(smalls)
+    homes, smalls = lax.optimization_barrier((homes, smalls))
+    smalls, homes = with_other_core(smalls), with_other_core(along_chips(homes))
+
     place = jnp.stack([row, chip, core]).astype(jnp.int32)
 
     height, width = 2 * n_col * bsize, 2 * n_row * bsize
@@ -334,13 +356,15 @@
     result = pl.pallas_call(
         functools.partial(kernel, n_row, n_col, n_cap, float(n_dev * own * bsize)),
         out_shape=jax.ShapeDtypeStruct((own, k, bsize), jnp.float32),
-        in_specs=[pl.BlockSpec(memory_space=pltpu.SMEM)] * 2
+        in_specs=[pl.BlockSpec(memory_space=pltpu.SMEM)]
         + [pl.BlockSpec(memory_space=pl.ANY)] * 16,
         out_specs=pl.BlockSpec(memory_space=pltpu.VMEM),
         scratch_shapes=[
+            pltpu.VMEM((n_dev, 128), jnp.int32),
+            pltpu.SMEM((n_dev, 128), jnp.int32),
             pltpu.SMEM((slots,), jnp.int32),
             pltpu.SMEM((slots,), jnp.int32),
-            pltpu.SemaphoreType.DMA((16,)),
+            pltpu.SemaphoreType.DMA((17,)),
             pltpu.VMEM((n_dev,) + small.shape, bf16),
             pltpu.VMEM((n_dev,) + home.shape, bf16),
             pltpu.VMEM((n_row, height, 128), jnp.float32),
@@ -354,7 +378,7 @@
         ],
         compiler_params=pltpu.CompilerParams(vmem_limit_bytes=VMEM_LIMIT),
         name="iterate",
-    )(ints, place, *smalls, *homes)
+    )(place, *smalls, *homes)
     return result.reshape(own, k * bsize)
 
 

time: 157 us -> 146 us (0.930)
  waiting for transfers between devices: 41.1 us -> 30.2 us
  Pallas kernels: 75.2 us -> 77.2 us
    ppermute x26, waiting for transfers between devices: 41.1 us -> 30.2 us  [swap(): return lax.ppermute(x, axis, [(i, i ^ distance) for i in range(size)])]
    unnamed x43 -> x29, local copies, waits for them, and re-layouts: 3.45 us -> 7.99 us
    slice x8 -> x0, local copies, waits for them, and re-layouts: 4.22 us -> none  [whole_on_each(): v[:, at, :32]]
    pallas_call x1, Pallas kernels: 75.2 us -> 77.2 us  [whole_on_each(): pl.pallas_call(functools.partial(kernel, n_row, n_col, n_cap, float(n_dev...]
  transfers between devices with their start and end apart: 26 -> 26, of which waited for: 8 -> 13; matrix products, arithmetic and copies ran while one was open for 4% -> 1% of each run, Pallas kernels for 0% -> 0%
where the time goes in v1:
time: 146 us; the launch traced here: 145 us
  Pallas kernels  77.2 us (53%)
  waiting for transfers between devices  30.2 us (21%)
  starting transfers between devices  25.6 us (18%)
  local copies, waits for them, and re-layouts  9.53 us (7%)
  other arithmetic  1.62 us (1%)
    pallas_call x1, Pallas kernels, whole_on_each(): pl.pallas_call(functools.partial(kernel, n_row, n_col, n_cap, float(n_dev...  77.2 us
    ppermute x26, waiting for transfers between devices, swap(): return lax.ppermute(x, axis, [(i, i ^ distance) for i in range(size)])  30.2 us
    ppermute x26, starting transfers between devices, swap(): return lax.ppermute(x, axis, [(i, i ^ distance) for i in range(size)])  25.6 us
    unnamed x29, local copies, waits for them, and re-layouts  7.99 us
  transfers between devices with their start and end apart: 26, of which 13 were waited for; matrix products, arithmetic and copies ran while one was open for 1% of the time, Pallas kernels for 0%

profile of v1, /device:TPU:0, one launch (start us, length us, event | category | flops | bytes accessed | tf_op | source)
XLA Modules:
  0.0 145.1 jit_solution(10616565310040627622)
XLA Ops:
  0.8 1.1 select_bitcast_fusion
  1.9 0.5 collective-permute-start
  2.4 0.1 copy-done.13
  2.5 0.7 copy-done.11
  3.3 0.6 copy-done.10
  3.9 0.1 reshape.208
  4.2 0.5 copy-done.9
  4.6 0.1 reshape.206
  4.9 3.0 %collective-permute-start.1 = (bf16[16,4096]{1,0:T(8,128)(2,1)S(1)}, bf16[16,4096]{1,0:T(8,128)(2,1)S(1)}, u32[]{:S(2)}, u32[]{:S(2)}) collective-permute-start(bf16[16,4096]{1,0:T(8,128)(2,1)S(1)} %get-tuple-element.31), channel_id=1, source_target_pairs={{0,2},{2,0},{4,6},{6,4},{1,3},{3,1},{5,7},{7,5},{8,10},{10,8},{12,... | collective-permute-start | bytes 393224 | tf_op jit(solution)/shard_map/ppermute | solution.py:280
  7.9 1.5 %collective-permute-start.3 = (bf16[16,4096]{1,0:T(8,128)(2,1)S(1)}, bf16[16,4096]{1,0:T(8,128)(2,1)S(1)}, u32[]{:S(2)}, u32[]{:S(2)}) collective-permute-start(bf16[16,4096]{1,0:T(8,128)(2,1)S(1)} %get-tuple-element.32), channel_id=1, source_target_pairs={{0,6},{2,4},{4,2},{6,0},{1,7},{3,5},{5,3},{7,1},{8,14},{10,12},{12... | collective-permute-start | bytes 393224 | tf_op jit(solution)/shard_map/ppermute | solution.py:280
  9.7 0.1 concatenate.45
  9.8 4.1 %collective-permute-start.6 = (bf16[336,128]{1,0:T(8,128)(2,1)S(1)}, bf16[336,128]{1,0:T(8,128)(2,1)S(1)}, u32[]{:S(2)}, u32[]{:S(2)}) collective-permute-start(bf16[336,128]{1,0:T(8,128)(2,1)S(1)} %concatenate.45), channel_id=1, source_target_pairs={{0,24},{8,16},{16,8},{24,0},{1,25},{9,17},{17,9},{25,1},{2,26},{10... | collective-permute-start | bytes 258056 | tf_op jit(solution)/shard_map/ppermute | solution.py:280
  14.0 0.6 collective-permute-start.4
  14.6 1.0 collective-permute-done.3
  15.6 1.4 collective-permute-done.2
  17.1 0.1 collective-permute-done.6
  17.2 3.2 %collective-permute-done.5 = bf16[336,128]{1,0:T(8,128)(2,1)S(1)} collective-permute-done((bf16[336,128]{1,0:T(8,128)(2,1)S(1)}, bf16[336,128]{1,0:T(8,128)(2,1)S(1)}, u32[]{:S(2)}, u32[]{:S(2)}) %collective-permute-start.5) | collective-permute-done | bytes 86048 | tf_op jit(solution)/shard_map/ppermute | solution.py:280
  20.5 1.6 %collective-permute-start.10 = (bf16[2,336,128]{2,1,0:T(8,128)(2,1)S(1)}, bf16[2,336,128]{2,1,0:T(8,128)(2,1)S(1)}, u32[]{:S(2)}, u32[]{:S(2)}) collective-permute-start(bf16[2,336,128]{2,1,0:T(8,128)(2,1)S(1)} %pad_maximum_fusion.6), channel_id=1, source_target_pairs={{0,2},{2,0},{4,6},{6,4},{1,3},{3,1},{5,7},{7,5},{8,10},{10,8},{12,... | collective-permute-start | bytes 516104 | tf_op jit(solution)/shard_map/ppermute | solution.py:280
  22.1 1.6 %collective-permute-start.12 = (bf16[2,336,128]{2,1,0:T(8,128)(2,1)S(1)}, bf16[2,336,128]{2,1,0:T(8,128)(2,1)S(1)}, u32[]{:S(2)}, u32[]{:S(2)}) collective-permute-start(bf16[2,336,128]{2,1,0:T(8,128)(2,1)S(1)} %pad_maximum_fusion.7), channel_id=1, source_target_pairs={{0,4},{2,6},{4,0},{6,2},{1,5},{3,7},{5,1},{7,3},{8,12},{10,14},{12... | collective-permute-start | bytes 516104 | tf_op jit(solution)/shard_map/ppermute | solution.py:280
  23.6 2.8 %collective-permute-done.10 = bf16[2,336,128]{2,1,0:T(8,128)(2,1)S(1)} collective-permute-done((bf16[2,336,128]{2,1,0:T(8,128)(2,1)S(1)}, bf16[2,336,128]{2,1,0:T(8,128)(2,1)S(1)}, u32[]{:S(2)}, u32[]{:S(2)}) %collective-permute-start.10) | collective-permute-done | bytes 172064 | tf_op jit(solution)/shard_map/ppermute | solution.py:280
  26.5 1.6 %collective-permute-start.11 = (bf16[4,336,128]{2,1,0:T(8,128)(2,1)S(1)}, bf16[4,336,128]{2,1,0:T(8,128)(2,1)S(1)}, u32[]{:S(2)}, u32[]{:S(2)}) collective-permute-start(bf16[4,336,128]{2,1,0:T(8,128)(2,1)S(1)} %pad_maximum_fusion.2.rest_0_), channel_id=1, source_target_pairs={{0,4},{2,6},{4,0},{6,2},{1,5},{3,7},{5,1},{7,3},{8,12},{10,14},{12... | collective-permute-start | bytes 1032200 | tf_op jit(solution)/shard_map/ppermute | solution.py:280
  28.1 1.6 %collective-permute-start.13 = (bf16[4,336,128]{2,1,0:T(8,128)(2,1)S(1)}, bf16[4,336,128]{2,1,0:T(8,128)(2,1)}, u32[]{:S(2)}, u32[]{:S(2)}) collective-permute-start(bf16[4,336,128]{2,1,0:T(8,128)(2,1)S(1)} %pad_maximum_fusion.3.rest_2_), channel_id=1, source_target_pairs={{0,2},{2,0},{4,6},{6,4},{1,3},{3,1},{5,7},{7,5},{8,10},{10,8},{12,... | collective-permute-start | bytes 1032200 | tf_op jit(solution)/shard_map/ppermute | solution.py:280
  29.7 3.4 %collective-permute-start.9 = (bf16[512,128]{1,0:T(8,128)(2,1)S(1)}, bf16[512,128]{1,0:T(8,128)(2,1)S(1)}, u32[]{:S(2)}, u32[]{:S(2)}) collective-permute-start(bf16[512,128]{1,0:T(8,128)(2,1)S(1)} %bitcast.54), channel_id=1, source_target_pairs={{0,24},{8,16},{16,8},{24,0},{1,25},{9,17},{17,9},{25,1},{2,26},{10... | collective-permute-start | bytes 393224 | tf_op jit(solution)/shard_map/ppermute | solution.py:280
  33.1 0.9 collective-permute-start.7
  34.1 3.8 %collective-permute-done.9 = bf16[512,128]{1,0:T(8,128)(2,1)S(1)} collective-permute-done((bf16[512,128]{1,0:T(8,128)(2,1)S(1)}, bf16[512,128]{1,0:T(8,128)(2,1)S(1)}, u32[]{:S(2)}, u32[]{:S(2)}) %collective-permute-start.9) | collective-permute-done | bytes 131104 | tf_op jit(solution)/shard_map/ppermute | solution.py:280
  37.9 3.3 %collective-permute-done.8 = bf16[512,128]{1,0:T(8,128)(2,1)S(1)} collective-permute-done((bf16[512,128]{1,0:T(8,128)(2,1)S(1)}, bf16[512,128]{1,0:T(8,128)(2,1)S(1)}, u32[]{:S(2)}, u32[]{:S(2)}) %collective-permute-start.8) | collective-permute-done | bytes 131104 | tf_op jit(solution)/shard_map/ppermute | solution.py:280
  41.3 0.6 collective-permute-start.18
  41.9 1.2 collective-permute-start.20
  43.1 7.1 %collective-permute-done.18 = bf16[2,512,128]{2,1,0:T(8,128)(2,1)S(1)} collective-permute-done((bf16[2,512,128]{2,1,0:T(8,128)(2,1)S(1)}, bf16[2,512,128]{2,1,0:T(8,128)(2,1)S(1)}, u32[]{:S(2)}, u32[]{:S(2)}) %collective-permute-start.18) | collective-permute-done | bytes 262176 | tf_op jit(solution)/shard_map/ppermute | solution.py:280
  50.3 0.7 collective-permute-done.20
  51.1 1.7 %collective-permute-start.21 = (bf16[4,512,128]{2,1,0:T(8,128)(2,1)S(1)}, bf16[4,512,128]{2,1,0:T(8,128)(2,1)S(1)}, u32[]{:S(2)}, u32[]{:S(2)}) collective-permute-start(bf16[4,512,128]{2,1,0:T(8,128)(2,1)S(1)} %pad_maximum_fusion.1.rest_10_), channel_id=1, source_target_pairs={{0,2},{2,0},{4,6},{6,4},{1,3},{3,1},{5,7},{7,5},{8,10},{10,8},{12,... | collective-permute-start | bytes 1572872 | tf_op jit(solution)/shard_map/ppermute | solution.py:280
  52.8 0.5 collective-permute-start.15
  53.3 1.1 collective-permute-done.14.rest_4_
  54.5 0.7 copy-done.2
  55.2 0.1 collective-permute-start.22
  55.3 0.7 copy-done.4
  56.1 0.4 collective-permute-start.24
  56.4 3.1 %collective-permute-done.19.rest_9_ = bf16[4,512,128]{2,1,0:T(8,128)(2,1)S(1)} collective-permute-done((bf16[4,512,128]{2,1,0:T(8,128)(2,1)S(1)}, bf16[4,512,128]{2,1,0:T(8,128)(2,1)S(1)}, u32[]{:S(2)}, u32[]{:S(2)}) %collective-permute-start.19) | collective-permute-done | bytes 524320 | tf_op jit(solution)/shard_map/ppermute | solution.py:280
  59.5 0.9 collective-permute-done.21.rest_11_
  60.4 0.7 copy-done.6
  61.1 0.5 collective-permute-start.17
  61.7 1.5 %collective-permute-done.17.rest_7_ = bf16[4,336,128]{2,1,0:T(8,128)(2,1)} collective-permute-done((bf16[4,336,128]{2,1,0:T(8,128)(2,1)}, bf16[4,336,128]{2,1,0:T(8,128)(2,1)}, u32[]{:S(2)}, u32[]{:S(2)}) %collective-permute-start.17) | collective-permute-done | bytes 344096 | tf_op jit(solution)/shard_map/ppermute | solution.py:280
  63.3 1.0 copy-done.1
  64.2 1.0 copy-done.3
  65.2 1.0 copy-done.5
  66.2 1.0 copy-done.7
  67.2 77.2 %iterate.1 = f32[2,64,64]{2,1,0:T(8,128)S(1)} custom-call(s32[3]{0:T(128)S(1)} %pad_add_fusion.own, bf16[4,336,128]{2,1,0:T(8,128)(2,1)S(1)} %pad_maximum_fusion.2.rest_0_, bf16[4,336,128]{2,1,0:T(8,128)(2,1)S(1)} %copy-done.1, bf16[4,336,128]{2,1,0:T(8,128)(2,1)S(1)} %pad_maximum_fusion.3.rest_2_, bf16[4,336,128]{2,1,0:T(8,128)(2,1)} %collective-permute-done.13.rest_3_, ...), custom_call_target="tpu_custom_call" | custom-call | tf_op jit(solution)/shard_map/iterate/pallas_call | solution.py:356
  144.4 0.7 reshape.211
  (70 shorter events, 1.3 us)
Async XLA Ops:
  0.0 4.8 %copy-start.8 = (bf16[1,1,128,4096]{3,2,1,0:T(8,128)(2,1)S(1)}, bf16[1,1,128,4096]{3,2,1,0:T(8,128)(2,1)}, u32[]{:S(2)}) copy-start(bf16[1,1,128,4096]{3,2,1,0:T(8,128)(2,1)} %param.7) | copy-start | bytes 3145732
  0.7 1.6 %copy-start.12 = (s32[1,1,128]{2,1,0:T(1,128)S(1)}, s32[1,1,128]{2,1,0:T(1,128)}, u32[]{:S(2)}) copy-start(s32[1,1,128]{2,1,0:T(1,128)} %param.8) | copy-start | bytes 1540
  1.8 0.7 copy-start.13
  1.9 2.9 %collective-permute-start = (bf16[4,16,4096]{2,1,0:T(8,128)(2,1)S(1)}, bf16[4,16,4096]{2,1,0:T(8,128)(2,1)S(1)}, u32[]{:S(2)}, u32[]{:S(2)}) collective-permute-start(bf16[4,16,4096]{2,1,0:T(8,128)(2,1)S(1)} %select_bitcast_fusion), channel_id=1, source_target_pairs={{0,1},{1,0},{2,3},{3,2},{4,5},{5,4},{6,7},{7,6},{8,9},{9,8},{10,11... | collective-permute-start | bytes 1572872 | tf_op jit(solution)/shard_map/ppermute | solution.py:280
  2.5 0.7 copy-start.11
  3.2 0.7 copy-start.10
  3.9 0.8 copy-start.9
  4.9 9.1 %collective-permute-start.1 = (bf16[16,4096]{1,0:T(8,128)(2,1)S(1)}, bf16[16,4096]{1,0:T(8,128)(2,1)S(1)}, u32[]{:S(2)}, u32[]{:S(2)}) collective-permute-start(bf16[16,4096]{1,0:T(8,128)(2,1)S(1)} %get-tuple-element.31), channel_id=1, source_target_pairs={{0,2},{2,0},{4,6},{6,4},{1,3},{3,1},{5,7},{7,5},{8,10},{10,8},{12,... | collective-permute-start | bytes 393224 | tf_op jit(solution)/shard_map/ppermute | solution.py:280
  7.9 7.7 %collective-permute-start.3 = (bf16[16,4096]{1,0:T(8,128)(2,1)S(1)}, bf16[16,4096]{1,0:T(8,128)(2,1)S(1)}, u32[]{:S(2)}, u32[]{:S(2)}) collective-permute-start(bf16[16,4096]{1,0:T(8,128)(2,1)S(1)} %get-tuple-element.32), channel_id=1, source_target_pairs={{0,6},{2,4},{4,2},{6,0},{1,7},{3,5},{5,3},{7,1},{8,14},{10,12},{12... | collective-permute-start | bytes 393224 | tf_op jit(solution)/shard_map/ppermute | solution.py:280
  9.4 7.6 %collective-permute-start.2 = (bf16[16,4096]{1,0:T(8,128)(2,1)S(1)}, bf16[16,4096]{1,0:T(8,128)(2,1)S(1)}, u32[]{:S(2)}, u32[]{:S(2)}) collective-permute-start(bf16[16,4096]{1,0:T(8,128)(2,1)S(1)} %get-tuple-element.33), channel_id=1, source_target_pairs={{0,4},{2,6},{4,0},{6,2},{1,5},{3,7},{5,1},{7,3},{8,12},{10,14},{12... | collective-permute-start | bytes 393224 | tf_op jit(solution)/shard_map/ppermute | solution.py:280
  9.8 7.4 %collective-permute-start.6 = (bf16[336,128]{1,0:T(8,128)(2,1)S(1)}, bf16[336,128]{1,0:T(8,128)(2,1)S(1)}, u32[]{:S(2)}, u32[]{:S(2)}) collective-permute-start(bf16[336,128]{1,0:T(8,128)(2,1)S(1)} %concatenate.45), channel_id=1, source_target_pairs={{0,24},{8,16},{16,8},{24,0},{1,25},{9,17},{17,9},{25,1},{2,26},{10... | collective-permute-start | bytes 258056 | tf_op jit(solution)/shard_map/ppermute | solution.py:280
  14.0 6.5 %collective-permute-start.5 = (bf16[336,128]{1,0:T(8,128)(2,1)S(1)}, bf16[336,128]{1,0:T(8,128)(2,1)S(1)}, u32[]{:S(2)}, u32[]{:S(2)}) collective-permute-start(bf16[336,128]{1,0:T(8,128)(2,1)S(1)} %concatenate.45), channel_id=1, source_target_pairs={{0,16},{8,24},{16,0},{24,8},{1,17},{9,25},{17,1},{25,9},{2,18},{10... | collective-permute-start | bytes 258056 | tf_op jit(solution)/shard_map/ppermute | solution.py:280
  14.0 6.5 %collective-permute-start.4 = (bf16[336,128]{1,0:T(8,128)(2,1)S(1)}, bf16[336,128]{1,0:T(8,128)(2,1)S(1)}, u32[]{:S(2)}, u32[]{:S(2)}) collective-permute-start(bf16[336,128]{1,0:T(8,128)(2,1)S(1)} %concatenate.45), channel_id=1, source_target_pairs={{0,8},{8,0},{16,24},{24,16},{1,9},{9,1},{17,25},{25,17},{2,10},{10... | collective-permute-start | bytes 258056 | tf_op jit(solution)/shard_map/ppermute | solution.py:280
  20.5 6.0 %collective-permute-start.10 = (bf16[2,336,128]{2,1,0:T(8,128)(2,1)S(1)}, bf16[2,336,128]{2,1,0:T(8,128)(2,1)S(1)}, u32[]{:S(2)}, u32[]{:S(2)}) collective-permute-start(bf16[2,336,128]{2,1,0:T(8,128)(2,1)S(1)} %pad_maximum_fusion.6), channel_id=1, source_target_pairs={{0,2},{2,0},{4,6},{6,4},{1,3},{3,1},{5,7},{7,5},{8,10},{10,8},{12,... | collective-permute-start | bytes 516104 | tf_op jit(solution)/shard_map/ppermute | solution.py:280
  22.1 6.0 %collective-permute-start.12 = (bf16[2,336,128]{2,1,0:T(8,128)(2,1)S(1)}, bf16[2,336,128]{2,1,0:T(8,128)(2,1)S(1)}, u32[]{:S(2)}, u32[]{:S(2)}) collective-permute-start(bf16[2,336,128]{2,1,0:T(8,128)(2,1)S(1)} %pad_maximum_fusion.7), channel_id=1, source_target_pairs={{0,4},{2,6},{4,0},{6,2},{1,5},{3,7},{5,1},{7,3},{8,12},{10,14},{12... | collective-permute-start | bytes 516104 | tf_op jit(solution)/shard_map/ppermute | solution.py:280
  26.5 14.7 %collective-permute-start.11 = (bf16[4,336,128]{2,1,0:T(8,128)(2,1)S(1)}, bf16[4,336,128]{2,1,0:T(8,128)(2,1)S(1)}, u32[]{:S(2)}, u32[]{:S(2)}) collective-permute-start(bf16[4,336,128]{2,1,0:T(8,128)(2,1)S(1)} %pad_maximum_fusion.2.rest_0_), channel_id=1, source_target_pairs={{0,4},{2,6},{4,0},{6,2},{1,5},{3,7},{5,1},{7,3},{8,12},{10,14},{12... | collective-permute-start | bytes 1032200 | tf_op jit(solution)/shard_map/ppermute | solution.py:280
  28.1 13.1 %collective-permute-start.13 = (bf16[4,336,128]{2,1,0:T(8,128)(2,1)S(1)}, bf16[4,336,128]{2,1,0:T(8,128)(2,1)}, u32[]{:S(2)}, u32[]{:S(2)}) collective-permute-start(bf16[4,336,128]{2,1,0:T(8,128)(2,1)S(1)} %pad_maximum_fusion.3.rest_2_), channel_id=1, source_target_pairs={{0,2},{2,0},{4,6},{6,4},{1,3},{3,1},{5,7},{7,5},{8,10},{10,8},{12,... | collective-permute-start | bytes 1032200 | tf_op jit(solution)/shard_map/ppermute | solution.py:280
  29.7 8.2 %collective-permute-start.9 = (bf16[512,128]{1,0:T(8,128)(2,1)S(1)}, bf16[512,128]{1,0:T(8,128)(2,1)S(1)}, u32[]{:S(2)}, u32[]{:S(2)}) collective-permute-start(bf16[512,128]{1,0:T(8,128)(2,1)S(1)} %bitcast.54), channel_id=1, source_target_pairs={{0,24},{8,16},{16,8},{24,0},{1,25},{9,17},{17,9},{25,1},{2,26},{10... | collective-permute-start | bytes 393224 | tf_op jit(solution)/shard_map/ppermute | solution.py:280
  33.1 8.1 %collective-permute-start.8 = (bf16[512,128]{1,0:T(8,128)(2,1)S(1)}, bf16[512,128]{1,0:T(8,128)(2,1)S(1)}, u32[]{:S(2)}, u32[]{:S(2)}) collective-permute-start(bf16[512,128]{1,0:T(8,128)(2,1)S(1)} %bitcast.55), channel_id=1, source_target_pairs={{0,16},{8,24},{16,0},{24,8},{1,17},{9,25},{17,1},{25,9},{2,18},{10... | collective-permute-start | bytes 393224 | tf_op jit(solution)/shard_map/ppermute | solution.py:280
  33.1 8.1 %collective-permute-start.7 = (bf16[512,128]{1,0:T(8,128)(2,1)S(1)}, bf16[512,128]{1,0:T(8,128)(2,1)S(1)}, u32[]{:S(2)}, u32[]{:S(2)}) collective-permute-start(bf16[512,128]{1,0:T(8,128)(2,1)S(1)} %bitcast.56), channel_id=1, source_target_pairs={{0,8},{8,0},{16,24},{24,16},{1,9},{9,1},{17,25},{25,17},{2,10},{10... | collective-permute-start | bytes 393224 | tf_op jit(solution)/shard_map/ppermute | solution.py:280
  41.2 11.6 %copy-start = (bf16[4,336,128]{2,1,0:T(8,128)(2,1)}, bf16[4,336,128]{2,1,0:T(8,128)(2,1)S(1)}, u32[]{:S(2)}) copy-start(bf16[4,336,128]{2,1,0:T(8,128)(2,1)S(1)} %collective-permute-done.11.rest_1_) | copy-start | bytes 1032196
  41.3 8.9 %collective-permute-start.18 = (bf16[2,512,128]{2,1,0:T(8,128)(2,1)S(1)}, bf16[2,512,128]{2,1,0:T(8,128)(2,1)S(1)}, u32[]{:S(2)}, u32[]{:S(2)}) collective-permute-start(bf16[2,512,128]{2,1,0:T(8,128)(2,1)S(1)} %pad_maximum_fusion.4), channel_id=1, source_target_pairs={{0,2},{2,0},{4,6},{6,4},{1,3},{3,1},{5,7},{7,5},{8,10},{10,8},{12,... | collective-permute-start | bytes 786440 | tf_op jit(solution)/shard_map/ppermute | solution.py:280
  41.9 9.2 %collective-permute-start.20 = (bf16[2,512,128]{2,1,0:T(8,128)(2,1)S(1)}, bf16[2,512,128]{2,1,0:T(8,128)(2,1)S(1)}, u32[]{:S(2)}, u32[]{:S(2)}) collective-permute-start(bf16[2,512,128]{2,1,0:T(8,128)(2,1)S(1)} %pad_maximum_fusion.5), channel_id=1, source_target_pairs={{0,4},{2,6},{4,0},{6,2},{1,5},{3,7},{5,1},{7,3},{8,12},{10,14},{12... | collective-permute-start | bytes 786440 | tf_op jit(solution)/shard_map/ppermute | solution.py:280
  50.3 9.2 %collective-permute-start.19 = (bf16[4,512,128]{2,1,0:T(8,128)(2,1)S(1)}, bf16[4,512,128]{2,1,0:T(8,128)(2,1)S(1)}, u32[]{:S(2)}, u32[]{:S(2)}) collective-permute-start(bf16[4,512,128]{2,1,0:T(8,128)(2,1)S(1)} %pad_maximum_fusion.rest_8_), channel_id=1, source_target_pairs={{0,4},{2,6},{4,0},{6,2},{1,5},{3,7},{5,1},{7,3},{8,12},{10,14},{12... | collective-permute-start | bytes 1572872 | tf_op jit(solution)/shard_map/ppermute | solution.py:280
  51.1 9.2 %collective-permute-start.21 = (bf16[4,512,128]{2,1,0:T(8,128)(2,1)S(1)}, bf16[4,512,128]{2,1,0:T(8,128)(2,1)S(1)}, u32[]{:S(2)}, u32[]{:S(2)}) collective-permute-start(bf16[4,512,128]{2,1,0:T(8,128)(2,1)S(1)} %pad_maximum_fusion.1.rest_10_), channel_id=1, source_target_pairs={{0,2},{2,0},{4,6},{6,4},{1,3},{3,1},{5,7},{7,5},{8,10},{10,8},{12,... | collective-permute-start | bytes 1572872 | tf_op jit(solution)/shard_map/ppermute | solution.py:280
  52.8 1.7 %collective-permute-start.14 = (bf16[4,336,128]{2,1,0:T(8,128)(2,1)S(1)}, bf16[4,336,128]{2,1,0:T(8,128)(2,1)S(1)}, u32[]{:S(2)}, u32[]{:S(2)}) collective-permute-start(bf16[4,336,128]{2,1,0:T(8,128)(2,1)S(1)} %pad_maximum_fusion.2.rest_0_), channel_id=1, source_target_pairs={{0,1},{1,0},{2,3},{3,2},{4,5},{5,4},{6,7},{7,6},{8,9},{9,8},{10,11... | collective-permute-start | bytes 1032200 | tf_op jit(solution)/shard_map/ppermute | solution.py:280
  52.8 2.5 %collective-permute-start.15 = (bf16[4,336,128]{2,1,0:T(8,128)(2,1)S(1)}, bf16[4,336,128]{2,1,0:T(8,128)(2,1)S(1)}, u32[]{:S(2)}, u32[]{:S(2)}) collective-permute-start(bf16[4,336,128]{2,1,0:T(8,128)(2,1)S(1)} %collective-permute-done.11.rest_1_), channel_id=1, source_target_pairs={{0,1},{1,0},{2,3},{3,2},{4,5},{5,4},{6,7},{7,6},{8,9},{9,8},{10,11... | collective-permute-start | bytes 1032200 | tf_op jit(solution)/shard_map/ppermute | solution.py:280
  53.3 7.1 %collective-permute-start.16 = (bf16[4,336,128]{2,1,0:T(8,128)(2,1)S(1)}, bf16[4,336,128]{2,1,0:T(8,128)(2,1)S(1)}, u32[]{:S(2)}, u32[]{:S(2)}) collective-permute-start(bf16[4,336,128]{2,1,0:T(8,128)(2,1)S(1)} %pad_maximum_fusion.3.rest_2_), channel_id=1, source_target_pairs={{0,1},{1,0},{2,3},{3,2},{4,5},{5,4},{6,7},{7,6},{8,9},{9,8},{10,11... | collective-permute-start | bytes 1032200 | tf_op jit(solution)/shard_map/ppermute | solution.py:280
  54.5 0.7 copy-start.2
  55.2 8.1 %collective-permute-start.22 = (bf16[4,512,128]{2,1,0:T(8,128)(2,1)S(1)}, bf16[4,512,128]{2,1,0:T(8,128)(2,1)S(1)}, u32[]{:S(2)}, u32[]{:S(2)}) collective-permute-start(bf16[4,512,128]{2,1,0:T(8,128)(2,1)S(1)} %pad_maximum_fusion.rest_8_), channel_id=1, source_target_pairs={{0,1},{1,0},{2,3},{3,2},{4,5},{5,4},{6,7},{7,6},{8,9},{9,8},{10,11... | collective-permute-start | bytes 1572872 | tf_op jit(solution)/shard_map/ppermute | solution.py:280
  55.3 0.7 copy-start.4
  56.1 7.2 %collective-permute-start.24 = (bf16[4,512,128]{2,1,0:T(8,128)(2,1)S(1)}, bf16[4,512,128]{2,1,0:T(8,128)(2,1)}, u32[]{:S(2)}, u32[]{:S(2)}) collective-permute-start(bf16[4,512,128]{2,1,0:T(8,128)(2,1)S(1)} %pad_maximum_fusion.1.rest_10_), channel_id=1, source_target_pairs={{0,1},{1,0},{2,3},{3,2},{4,5},{5,4},{6,7},{7,6},{8,9},{9,8},{10,11... | collective-permute-start | bytes 1572872 | tf_op jit(solution)/shard_map/ppermute | solution.py:280
  59.5 3.7 %collective-permute-start.23 = (bf16[4,512,128]{2,1,0:T(8,128)(2,1)S(1)}, bf16[4,512,128]{2,1,0:T(8,128)(2,1)}, u32[]{:S(2)}, u32[]{:S(2)}) collective-permute-start(bf16[4,512,128]{2,1,0:T(8,128)(2,1)S(1)} %collective-permute-done.19.rest_9_), channel_id=1, source_target_pairs={{0,1},{1,0},{2,3},{3,2},{4,5},{5,4},{6,7},{7,6},{8,9},{9,8},{10,11... | collective-permute-start | bytes 1572872 | tf_op jit(solution)/shard_map/ppermute | solution.py:280
  60.4 2.9 %collective-permute-start.25 = (bf16[4,512,128]{2,1,0:T(8,128)(2,1)S(1)}, bf16[4,512,128]{2,1,0:T(8,128)(2,1)}, u32[]{:S(2)}, u32[]{:S(2)}) collective-permute-start(bf16[4,512,128]{2,1,0:T(8,128)(2,1)S(1)} %collective-permute-done.21.rest_11_), channel_id=1, source_target_pairs={{0,1},{1,0},{2,3},{3,2},{4,5},{5,4},{6,7},{7,6},{8,9},{9,8},{10,11... | collective-permute-start | bytes 1572872 | tf_op jit(solution)/shard_map/ppermute | solution.py:280
  60.4 0.7 copy-start.6
  61.1 2.1 %collective-permute-start.17 = (bf16[4,336,128]{2,1,0:T(8,128)(2,1)}, bf16[4,336,128]{2,1,0:T(8,128)(2,1)}, u32[]{:S(2)}, u32[]{:S(2)}) collective-permute-start(bf16[4,336,128]{2,1,0:T(8,128)(2,1)} %collective-permute-done.13.rest_3_), channel_id=1, source_target_pairs={{0,1},{1,0},{2,3},{3,2},{4,5},{5,4},{6,7},{7,6},{8,9},{9,8},{10,11... | collective-permute-start | bytes 1032200 | tf_op jit(solution)/shard_map/ppermute | solution.py:280
  63.3 1.0 copy-start.1
  64.2 1.0 copy-start.3
  65.2 1.0 copy-start.5
  66.2 1.0 copy-start.7

commit v2 on v1

--- a/solution.py
+++ b/solution.py
@@ -10,8 +10,9 @@
 ITERS = 4
 OFF_CAP = 8
 META = 16
-UNROLL = 8
-VMEM_LIMIT = 40 * 1024 * 1024
+UNROLL = 16
+BATCH = 8
+VMEM_LIMIT = 56 * 1024 * 1024
 
 NT = (((1,), (1,)), ((), ()))
 NN = (((1,), (0,)), ((), ()))
@@ -186,6 +187,15 @@
 
         lax.fori_loop(0, rblk, cut, 0, unroll=4)
 
+    def clear():
+        for q in range(n_dev):
+            y[q] = jnp.zeros_like(y[q])
+            for ref in (wb, yb):
+                ref[2 * q] = jnp.zeros_like(ref[2 * q])
+                ref[2 * q + 1] = jnp.zeros_like(ref[2 * q + 1])
+
+    clear()
+
     def iteration(it, carry):
         @pl.when(it > 0)
         def _():
@@ -199,8 +209,6 @@
                     x = current[:, d * 128 : (d + 1) * 128] * ic[q + d, 0:1, :]
                     scatter_pair(vs, vb, q + d, x)
 
-        for b in range(2 * n_dev):
-            wb[b] = jnp.zeros_like(wb[b])
         for r in range(n_row):
             base = homes[r] * cpairs
             vec = jnp.concatenate([vs[base + u] for u in range(cpairs)] * 2, axis=1)
@@ -210,19 +218,17 @@
                 w[r * rpairs + p + 1] = prod[:, 128:]
 
         def forward(i, carry):
-            prods = [dot(vb[lv[i * UNROLL + u]], blk[i * UNROLL + u], NT) for u in range(UNROLL)]
-            for u in range(UNROLL):
-                b = lw[i * UNROLL + u]
-                wb[b] = wb[b] + prods[u]
+            for at in range(0, UNROLL, BATCH):
+                slots = [i * UNROLL + at + u for u in range(BATCH)]
+                prods = [dot(vb[lv[s]], blk[s], NT) for s in slots]
+                for s, prod in zip(slots, prods):
+                    wb[lw[s]] = wb[lw[s]] + prod
             return carry
 
         lax.fori_loop(0, n_group, forward, 0)
         for p in range(n_dev):
             x = w[p] + jnp.concatenate([wb[2 * p], wb[2 * p + 1]], axis=1)
             scatter_pair(wt, wtb, p, x * rm[p, 0:1, :])
-            y[p] = jnp.zeros_like(y[p])
-            yb[2 * p] = jnp.zeros_like(yb[2 * p])
-            yb[2 * p + 1] = jnp.zeros_like(yb[2 * p + 1])
 
         for r in range(n_row):
             base = homes[r] * cpairs
@@ -235,10 +241,11 @@
                 y[base + u + 1] = y[base + u + 1] + prod[:, 128:]
 
         def backward(i, carry):
-            prods = [dot(wtb[lw[i * UNROLL + u]], blk[i * UNROLL + u]) for u in range(UNROLL)]
-            for u in range(UNROLL):
-                b = lv[i * UNROLL + u]
-                yb[b] = yb[b] + prods[u]
+            for at in range(0, UNROLL, BATCH):
+                slots = [i * UNROLL + at + u for u in range(BATCH)]
+                prods = [dot(wtb[lw[s]], blk[s]) for s in slots]
+                for s, prod in zip(slots, prods):
+                    yb[lv[s]] = yb[lv[s]] + prod
             return carry
 
         lax.fori_loop(0, n_group, backward, 0)
@@ -257,6 +264,7 @@
             lo = jnp.concatenate(los, axis=1)
             both = both + dot(jnp.concatenate([hi, lo], axis=0), hi, NT)
         gram = (both[:k] + (both[k:] + both[k:].T)) / total
+        clear()
         linv[...] = inverse_factor(gram)
         return carry
 
@@ -284,10 +292,16 @@
     return [x] + [swap(x, "row", s) for s in range(1, lax.axis_size("row"))]
 
 
-def along_chips(x):
+def along_one_chip_axis(x):
     near, far = jnp.stack(x[:2]), jnp.stack(x[2:])
-    near = jnp.concatenate([near, swap(near, "chip", 1)])
-    far = jnp.concatenate([far, swap(far, "chip", 2)])
+    return [
+        jnp.concatenate([near, swap(near, "chip", 1)]),
+        jnp.concatenate([far, swap(far, "chip", 2)]),
+    ]
+
+
+def along_other_chip_axis(x):
+    near, far = x
     return [near, swap(near, "chip", 2), far, swap(far, "chip", 1)]
 
 
@@ -338,11 +352,14 @@
     home = full_part(tile, has_full, n_col // 2, part, chip, core)
     home = home.reshape(part, half, 128).transpose(1, 0, 2).reshape(half * part, 128)
 
+    together = lax.optimization_barrier
     smalls = along_rows(small)
-    home, smalls = lax.optimization_barrier((home, smalls))
-    homes, smalls = along_rows(home), along_chips(smalls)
-    homes, smalls = lax.optimization_barrier((homes, smalls))
-    smalls, homes = with_other_core(smalls), with_other_core(along_chips(homes))
+    home, smalls[1] = together((home, smalls[1]))
+    homes, smalls = along_rows(home), along_one_chip_axis(smalls)
+    smalls, homes[1:3] = together((smalls, homes[1:3]))
+    homes, smalls = together((homes, along_other_chip_axis(smalls)))
+    homes, smalls = together((along_one_chip_axis(homes), with_other_core(smalls)))
+    homes = with_other_core(along_other_chip_axis(homes))
 
     place = jnp.stack([row, chip, core]).astype(jnp.int32)
 

time: 146 us -> 137 us (0.938); the launches traced: 145 us -> 134 us
  Pallas kernels: 77.2 us -> 65.8 us
  local copies, waits for them, and re-layouts: 9.53 us -> 6.22 us
  waiting for transfers between devices: 30.2 us -> 33.1 us
    pallas_call x1, Pallas kernels: 77.2 us -> 65.8 us  [whole_on_each(): pl.pallas_call(functools.partial(kernel, n_row, n_col, n_cap, float(n_dev...]
    unnamed x29 -> x41, local copies, waits for them, and re-layouts: 7.99 us -> 3.84 us
    ppermute x26, waiting for transfers between devices: 30.2 us -> 33.1 us  [swap(): return lax.ppermute(x, axis, [(i, i ^ distance) for i in range(size)])]
  transfers between devices with their start and end apart: 26 -> 26, of which waited for: 13 -> 13; matrix products, arithmetic and copies ran while one was open for 1% -> 2% of each run, Pallas kernels for 0% -> 0%
where the time goes in v2:
time: 137 us; the launch traced here: 134 us
  Pallas kernels  65.8 us (48%)
  waiting for transfers between devices  33.1 us (24%)
  starting transfers between devices  25.7 us (19%)
  local copies, waits for them, and re-layouts  6.22 us (5%)
  other arithmetic  2.27 us (2%)
    pallas_call x1, Pallas kernels, whole_on_each(): pl.pallas_call(functools.partial(kernel, n_row, n_col, n_cap, float(n_dev...  65.8 us
    ppermute x26, waiting for transfers between devices, swap(): return lax.ppermute(x, axis, [(i, i ^ distance) for i in range(size)])  33.1 us
    ppermute x26, starting transfers between devices, swap(): return lax.ppermute(x, axis, [(i, i ^ distance) for i in range(size)])  25.7 us
    unnamed x41, local copies, waits for them, and re-layouts  3.84 us
  transfers between devices with their start and end apart: 26, of which 13 were waited for; matrix products, arithmetic and copies ran while one was open for 2% of the time, Pallas kernels for 0%

profile of v2, /device:TPU:0, one launch (start us, length us, event | category | flops | bytes accessed | tf_op | source)
XLA Modules:
  0.0 134.2 jit_solution(5746798688061997743)
XLA Ops:
  0.7 1.1 select_bitcast_fusion
  1.8 0.5 collective-permute-start
  2.4 0.7 copy-done.17
  3.0 0.1 reshape.210
  3.1 0.6 copy-done.18
  3.7 0.6 copy-done.19
  4.4 0.7 copy-done.16
  5.0 0.1 reshape.208
  5.1 0.1 copy.15
  5.2 0.1 reshape.209
  5.3 0.5 copy-done.15
  5.8 0.1 reshape.206
  6.0 0.1 reshape.207
  6.2 0.1 concatenate.45
  6.3 4.7 %collective-permute-start.7 = (bf16[336,128]{1,0:T(8,128)(2,1)S(1)}, bf16[336,128]{1,0:T(8,128)(2,1)S(1)}, u32[]{:S(2)}, u32[]{:S(2)}) collective-permute-start(bf16[336,128]{1,0:T(8,128)(2,1)S(1)} %concatenate.45), channel_id=1, source_target_pairs={{0,24},{8,16},{16,8},{24,0},{1,25},{9,17},{17,9},{25,1},{2,26},{10... | collective-permute-start | bytes 258056 | tf_op jit(solution)/shard_map/ppermute | solution.py:288
  11.1 1.6 %collective-permute-start.1 = (bf16[16,4096]{1,0:T(8,128)(2,1)S(1)}, bf16[16,4096]{1,0:T(8,128)(2,1)S(1)}, u32[]{:S(2)}, u32[]{:S(2)}) collective-permute-start(bf16[16,4096]{1,0:T(8,128)(2,1)S(1)} %get-tuple-element.53), channel_id=1, source_target_pairs={{0,2},{2,0},{4,6},{6,4},{1,3},{3,1},{5,7},{7,5},{8,10},{10,8},{12,... | collective-permute-start | bytes 393224 | tf_op jit(solution)/shard_map/ppermute | solution.py:288
  12.7 1.5 %collective-permute-start.3 = (bf16[16,4096]{1,0:T(8,128)(2,1)S(1)}, bf16[16,4096]{1,0:T(8,128)(2,1)S(1)}, u32[]{:S(2)}, u32[]{:S(2)}) collective-permute-start(bf16[16,4096]{1,0:T(8,128)(2,1)S(1)} %get-tuple-element.54), channel_id=1, source_target_pairs={{0,6},{2,4},{4,2},{6,0},{1,7},{3,5},{5,3},{7,1},{8,14},{10,12},{12... | collective-permute-start | bytes 393224 | tf_op jit(solution)/shard_map/ppermute | solution.py:288
  14.2 0.5 collective-permute-start.2
  14.7 3.3 %collective-permute-start.4 = (bf16[336,128]{1,0:T(8,128)(2,1)S(1)}, bf16[336,128]{1,0:T(8,128)(2,1)S(1)}, u32[]{:S(2)}, u32[]{:S(2)}) collective-permute-start(bf16[336,128]{1,0:T(8,128)(2,1)S(1)} %concatenate.45), channel_id=1, source_target_pairs={{0,8},{8,0},{16,24},{24,16},{1,9},{9,1},{17,25},{25,17},{2,10},{10... | collective-permute-start | bytes 258056 | tf_op jit(solution)/shard_map/ppermute | solution.py:288
  18.0 0.9 collective-permute-done.6
  19.0 1.6 %collective-permute-start.8 = (bf16[2,336,128]{2,1,0:T(8,128)(2,1)S(1)}, bf16[2,336,128]{2,1,0:T(8,128)(2,1)S(1)}, u32[]{:S(2)}, u32[]{:S(2)}) collective-permute-start(bf16[2,336,128]{2,1,0:T(8,128)(2,1)S(1)} %pad_maximum_fusion.7), channel_id=1, source_target_pairs={{0,4},{2,6},{4,0},{6,2},{1,5},{3,7},{5,1},{7,3},{8,12},{10,14},{12... | collective-permute-start | bytes 516104 | tf_op jit(solution)/shard_map/ppermute | solution.py:288
  20.6 0.1 collective-permute-done.3
  20.7 2.1 %collective-permute-done.2 = bf16[16,4096]{1,0:T(8,128)(2,1)S(1)} collective-permute-done((bf16[16,4096]{1,0:T(8,128)(2,1)S(1)}, bf16[16,4096]{1,0:T(8,128)(2,1)S(1)}, u32[]{:S(2)}, u32[]{:S(2)}) %collective-permute-start.2) | collective-permute-done | bytes 131104 | tf_op jit(solution)/shard_map/ppermute | solution.py:288
  22.9 1.6 %collective-permute-start.5 = (bf16[2,336,128]{2,1,0:T(8,128)(2,1)S(1)}, bf16[2,336,128]{2,1,0:T(8,128)(2,1)S(1)}, u32[]{:S(2)}, u32[]{:S(2)}) collective-permute-start(bf16[2,336,128]{2,1,0:T(8,128)(2,1)S(1)} %pad_maximum_fusion.6), channel_id=1, source_target_pairs={{0,2},{2,0},{4,6},{6,4},{1,3},{3,1},{5,7},{7,5},{8,10},{10,8},{12,... | collective-permute-start | bytes 516104 | tf_op jit(solution)/shard_map/ppermute | solution.py:288
  24.5 2.9 %collective-permute-start.10 = (bf16[512,128]{1,0:T(8,128)(2,1)S(1)}, bf16[512,128]{1,0:T(8,128)(2,1)S(1)}, u32[]{:S(2)}, u32[]{:S(2)}) collective-permute-start(bf16[512,128]{1,0:T(8,128)(2,1)S(1)} %bitcast.54), channel_id=1, source_target_pairs={{0,16},{8,24},{16,0},{24,8},{1,17},{9,25},{17,1},{25,9},{2,18},{10... | collective-permute-start | bytes 393224 | tf_op jit(solution)/shard_map/ppermute | solution.py:288
  27.5 0.9 collective-permute-done.5
  28.5 3.4 %collective-permute-done.10 = bf16[512,128]{1,0:T(8,128)(2,1)S(1)} collective-permute-done((bf16[512,128]{1,0:T(8,128)(2,1)S(1)}, bf16[512,128]{1,0:T(8,128)(2,1)S(1)}, u32[]{:S(2)}, u32[]{:S(2)}) %collective-permute-start.10) | collective-permute-done | bytes 131104 | tf_op jit(solution)/shard_map/ppermute | solution.py:288
  31.8 1.3 collective-permute-done.9
  33.2 0.5 collective-permute-start.12
  33.7 0.6 collective-permute-start.13
  34.3 0.8 collective-permute-start.11
  35.1 6.0 %collective-permute-done.11 = bf16[512,128]{1,0:T(8,128)(2,1)S(1)} collective-permute-done((bf16[512,128]{1,0:T(8,128)(2,1)S(1)}, bf16[512,128]{1,0:T(8,128)(2,1)S(1)}, u32[]{:S(2)}, u32[]{:S(2)}) %collective-permute-start.11) | collective-permute-done | bytes 131104 | tf_op jit(solution)/shard_map/ppermute | solution.py:288
  41.0 0.3 collective-permute-done.12.rest_1_
  41.3 1.7 %collective-permute-start.15 = (bf16[2,512,128]{2,1,0:T(8,128)(2,1)S(1)}, bf16[2,512,128]{2,1,0:T(8,128)(2,1)S(1)}, u32[]{:S(2)}, u32[]{:S(2)}) collective-permute-start(bf16[2,512,128]{2,1,0:T(8,128)(2,1)S(1)} %pad_maximum_fusion.5), channel_id=1, source_target_pairs={{0,4},{2,6},{4,0},{6,2},{1,5},{3,7},{5,1},{7,3},{8,12},{10,14},{12... | collective-permute-start | bytes 786440 | tf_op jit(solution)/shard_map/ppermute | solution.py:288
  43.1 1.1 collective-permute-start.14
  44.2 0.5 collective-permute-start.17
  44.8 3.0 %collective-permute-done.15 = bf16[2,512,128]{2,1,0:T(8,128)(2,1)S(1)} collective-permute-done((bf16[2,512,128]{2,1,0:T(8,128)(2,1)S(1)}, bf16[2,512,128]{2,1,0:T(8,128)(2,1)S(1)}, u32[]{:S(2)}, u32[]{:S(2)}) %collective-permute-start.15) | collective-permute-done | bytes 262176 | tf_op jit(solution)/shard_map/ppermute | solution.py:288
  47.8 1.7 %collective-permute-done.14 = bf16[2,512,128]{2,1,0:T(8,128)(2,1)S(1)} collective-permute-done((bf16[2,512,128]{2,1,0:T(8,128)(2,1)S(1)}, bf16[2,512,128]{2,1,0:T(8,128)(2,1)S(1)}, u32[]{:S(2)}, u32[]{:S(2)}) %collective-permute-start.14) | collective-permute-done | bytes 262176 | tf_op jit(solution)/shard_map/ppermute | solution.py:288
  49.6 0.7 copy-done.11
  50.4 0.7 collective-permute-start.20
  51.1 1.1 collective-permute-start.21
  52.2 0.5 collective-permute-start.24
  52.7 10.7 %collective-permute-done.20.rest_9_ = bf16[4,512,128]{2,1,0:T(8,128)(2,1)S(1)} collective-permute-done((bf16[4,512,128]{2,1,0:T(8,128)(2,1)S(1)}, bf16[4,512,128]{2,1,0:T(8,128)(2,1)S(1)}, u32[]{:S(2)}, u32[]{:S(2)}) %collective-permute-start.20) | collective-permute-done | bytes 524320 | tf_op jit(solution)/shard_map/ppermute | solution.py:288
  63.4 1.4 %collective-permute-done.21.rest_11_ = bf16[4,512,128]{2,1,0:T(8,128)(2,1)S(1)} collective-permute-done((bf16[4,512,128]{2,1,0:T(8,128)(2,1)S(1)}, bf16[4,512,128]{2,1,0:T(8,128)(2,1)S(1)}, u32[]{:S(2)}, u32[]{:S(2)}) %collective-permute-start.21) | collective-permute-done | bytes 524320 | tf_op jit(solution)/shard_map/ppermute | solution.py:288
  64.8 0.7 pad_add_fusion.own
  65.5 1.3 collective-permute-done.25.rest_15_
  66.8 65.8 %iterate.1 = f32[2,64,64]{2,1,0:T(8,128)} custom-call(s32[3]{0:T(128)} %pad_add_fusion.own, bf16[4,336,128]{2,1,0:T(8,128)(2,1)} %copy-done.3, bf16[4,336,128]{2,1,0:T(8,128)(2,1)} %copy-done.9, bf16[4,336,128]{2,1,0:T(8,128)(2,1)} %copy-done.2, bf16[4,336,128]{2,1,0:T(8,128)(2,1)} %copy-done.10, bf16[4,336,128]{2,1,0:T(8,128)(2,1)} %copy-done.11, ...), custom_call_target="tpu_custom_call" | custom-call | tf_op jit(solution)/shard_map/iterate/pallas_call | solution.py:373
  132.6 1.5 %reshape.211 = f32[2,4096]{1,0:T(2,128)} reshape(f32[2,64,64]{2,1,0:T(8,128)} %iterate.1) | data formatting | bytes 65536 | tf_op jit(solution)/shard_map/reshape | solution.py:399
  (82 shorter events, 0.9 us)
Async XLA Ops:
  0.0 2.4 %copy-start.4 = (bf16[1,1,128,4096]{3,2,1,0:T(8,128)(2,1)S(1)}, bf16[1,1,128,4096]{3,2,1,0:T(8,128)(2,1)}, u32[]{:S(2)}) copy-start(bf16[1,1,128,4096]{3,2,1,0:T(8,128)(2,1)} %param.7) | copy-start | bytes 3145732
  1.8 9.2 %collective-permute-start = (bf16[4,16,4096]{2,1,0:T(8,128)(2,1)S(1)}, bf16[4,16,4096]{2,1,0:T(8,128)(2,1)S(1)}, u32[]{:S(2)}, u32[]{:S(2)}) collective-permute-start(bf16[4,16,4096]{2,1,0:T(8,128)(2,1)S(1)} %select_bitcast_fusion), channel_id=1, source_target_pairs={{0,1},{1,0},{2,3},{3,2},{4,5},{5,4},{6,7},{7,6},{8,9},{9,8},{10,11... | collective-permute-start | bytes 1572872 | tf_op jit(solution)/shard_map/ppermute | solution.py:288
  2.4 0.7 copy-start.17
  3.0 0.7 copy-start.18
  3.7 0.7 copy-start.19
  4.4 0.7 copy-start.16
  5.0 0.8 copy-start.15
  6.3 8.4 %collective-permute-start.7 = (bf16[336,128]{1,0:T(8,128)(2,1)S(1)}, bf16[336,128]{1,0:T(8,128)(2,1)S(1)}, u32[]{:S(2)}, u32[]{:S(2)}) collective-permute-start(bf16[336,128]{1,0:T(8,128)(2,1)S(1)} %concatenate.45), channel_id=1, source_target_pairs={{0,24},{8,16},{16,8},{24,0},{1,25},{9,17},{17,9},{25,1},{2,26},{10... | collective-permute-start | bytes 258056 | tf_op jit(solution)/shard_map/ppermute | solution.py:288
  11.0 7.9 %collective-permute-start.6 = (bf16[336,128]{1,0:T(8,128)(2,1)S(1)}, bf16[336,128]{1,0:T(8,128)(2,1)S(1)}, u32[]{:S(2)}, u32[]{:S(2)}) collective-permute-start(bf16[336,128]{1,0:T(8,128)(2,1)S(1)} %concatenate.45), channel_id=1, source_target_pairs={{0,16},{8,24},{16,0},{24,8},{1,17},{9,25},{17,1},{25,9},{2,18},{10... | collective-permute-start | bytes 258056 | tf_op jit(solution)/shard_map/ppermute | solution.py:288
  11.1 9.4 %collective-permute-start.1 = (bf16[16,4096]{1,0:T(8,128)(2,1)S(1)}, bf16[16,4096]{1,0:T(8,128)(2,1)S(1)}, u32[]{:S(2)}, u32[]{:S(2)}) collective-permute-start(bf16[16,4096]{1,0:T(8,128)(2,1)S(1)} %get-tuple-element.53), channel_id=1, source_target_pairs={{0,2},{2,0},{4,6},{6,4},{1,3},{3,1},{5,7},{7,5},{8,10},{10,8},{12,... | collective-permute-start | bytes 393224 | tf_op jit(solution)/shard_map/ppermute | solution.py:288
  12.7 8.0 %collective-permute-start.3 = (bf16[16,4096]{1,0:T(8,128)(2,1)S(1)}, bf16[16,4096]{1,0:T(8,128)(2,1)S(1)}, u32[]{:S(2)}, u32[]{:S(2)}) collective-permute-start(bf16[16,4096]{1,0:T(8,128)(2,1)S(1)} %get-tuple-element.54), channel_id=1, source_target_pairs={{0,6},{2,4},{4,2},{6,0},{1,7},{3,5},{5,3},{7,1},{8,14},{10,12},{12... | collective-permute-start | bytes 393224 | tf_op jit(solution)/shard_map/ppermute | solution.py:288
  14.2 8.6 %collective-permute-start.2 = (bf16[16,4096]{1,0:T(8,128)(2,1)S(1)}, bf16[16,4096]{1,0:T(8,128)(2,1)S(1)}, u32[]{:S(2)}, u32[]{:S(2)}) collective-permute-start(bf16[16,4096]{1,0:T(8,128)(2,1)S(1)} %get-tuple-element.55), channel_id=1, source_target_pairs={{0,4},{2,6},{4,0},{6,2},{1,5},{3,7},{5,1},{7,3},{8,12},{10,14},{12... | collective-permute-start | bytes 393224 | tf_op jit(solution)/shard_map/ppermute | solution.py:288
  14.7 8.2 %collective-permute-start.4 = (bf16[336,128]{1,0:T(8,128)(2,1)S(1)}, bf16[336,128]{1,0:T(8,128)(2,1)S(1)}, u32[]{:S(2)}, u32[]{:S(2)}) collective-permute-start(bf16[336,128]{1,0:T(8,128)(2,1)S(1)} %concatenate.45), channel_id=1, source_target_pairs={{0,8},{8,0},{16,24},{24,16},{1,9},{9,1},{17,25},{25,17},{2,10},{10... | collective-permute-start | bytes 258056 | tf_op jit(solution)/shard_map/ppermute | solution.py:288
  19.0 8.4 %collective-permute-start.8 = (bf16[2,336,128]{2,1,0:T(8,128)(2,1)S(1)}, bf16[2,336,128]{2,1,0:T(8,128)(2,1)S(1)}, u32[]{:S(2)}, u32[]{:S(2)}) collective-permute-start(bf16[2,336,128]{2,1,0:T(8,128)(2,1)S(1)} %pad_maximum_fusion.7), channel_id=1, source_target_pairs={{0,4},{2,6},{4,0},{6,2},{1,5},{3,7},{5,1},{7,3},{8,12},{10,14},{12... | collective-permute-start | bytes 516104 | tf_op jit(solution)/shard_map/ppermute | solution.py:288
  22.9 5.5 %collective-permute-start.5 = (bf16[2,336,128]{2,1,0:T(8,128)(2,1)S(1)}, bf16[2,336,128]{2,1,0:T(8,128)(2,1)S(1)}, u32[]{:S(2)}, u32[]{:S(2)}) collective-permute-start(bf16[2,336,128]{2,1,0:T(8,128)(2,1)S(1)} %pad_maximum_fusion.6), channel_id=1, source_target_pairs={{0,2},{2,0},{4,6},{6,4},{1,3},{3,1},{5,7},{7,5},{8,10},{10,8},{12,... | collective-permute-start | bytes 516104 | tf_op jit(solution)/shard_map/ppermute | solution.py:288
  24.5 7.4 %collective-permute-start.10 = (bf16[512,128]{1,0:T(8,128)(2,1)S(1)}, bf16[512,128]{1,0:T(8,128)(2,1)S(1)}, u32[]{:S(2)}, u32[]{:S(2)}) collective-permute-start(bf16[512,128]{1,0:T(8,128)(2,1)S(1)} %bitcast.54), channel_id=1, source_target_pairs={{0,16},{8,24},{16,0},{24,8},{1,17},{9,25},{17,1},{25,9},{2,18},{10... | collective-permute-start | bytes 393224 | tf_op jit(solution)/shard_map/ppermute | solution.py:288
  27.4 5.8 %collective-permute-start.9 = (bf16[512,128]{1,0:T(8,128)(2,1)S(1)}, bf16[512,128]{1,0:T(8,128)(2,1)S(1)}, u32[]{:S(2)}, u32[]{:S(2)}) collective-permute-start(bf16[512,128]{1,0:T(8,128)(2,1)S(1)} %bitcast.55), channel_id=1, source_target_pairs={{0,8},{8,0},{16,24},{24,16},{1,9},{9,1},{17,25},{25,17},{2,10},{10... | collective-permute-start | bytes 393224 | tf_op jit(solution)/shard_map/ppermute | solution.py:288
  27.5 17.3 %copy-start.2 = (bf16[4,336,128]{2,1,0:T(8,128)(2,1)}, bf16[4,336,128]{2,1,0:T(8,128)(2,1)S(1)}, u32[]{:S(2)}) copy-start(bf16[4,336,128]{2,1,0:T(8,128)(2,1)S(1)} %pad_maximum_fusion.3.rest_2_) | copy-start | bytes 1032196
  28.4 15.8 %copy-start.3 = (bf16[4,336,128]{2,1,0:T(8,128)(2,1)}, bf16[4,336,128]{2,1,0:T(8,128)(2,1)S(1)}, u32[]{:S(2)}) copy-start(bf16[4,336,128]{2,1,0:T(8,128)(2,1)S(1)} %pad_maximum_fusion.2.rest_0_) | copy-start | bytes 1032196
  33.2 8.1 %collective-permute-start.12 = (bf16[4,336,128]{2,1,0:T(8,128)(2,1)S(1)}, bf16[4,336,128]{2,1,0:T(8,128)(2,1)S(1)}, u32[]{:S(2)}, u32[]{:S(2)}) collective-permute-start(bf16[4,336,128]{2,1,0:T(8,128)(2,1)S(1)} %pad_maximum_fusion.2.rest_0_), channel_id=1, source_target_pairs={{0,4},{2,6},{4,0},{6,2},{1,5},{3,7},{5,1},{7,3},{8,12},{10,14},{12... | collective-permute-start | bytes 1032200 | tf_op jit(solution)/shard_map/ppermute | solution.py:288
  33.7 7.6 %collective-permute-start.13 = (bf16[4,336,128]{2,1,0:T(8,128)(2,1)S(1)}, bf16[4,336,128]{2,1,0:T(8,128)(2,1)S(1)}, u32[]{:S(2)}, u32[]{:S(2)}) collective-permute-start(bf16[4,336,128]{2,1,0:T(8,128)(2,1)S(1)} %pad_maximum_fusion.3.rest_2_), channel_id=1, source_target_pairs={{0,2},{2,0},{4,6},{6,4},{1,3},{3,1},{5,7},{7,5},{8,10},{10,8},{12,... | collective-permute-start | bytes 1032200 | tf_op jit(solution)/shard_map/ppermute | solution.py:288
  34.3 6.8 %collective-permute-start.11 = (bf16[512,128]{1,0:T(8,128)(2,1)S(1)}, bf16[512,128]{1,0:T(8,128)(2,1)S(1)}, u32[]{:S(2)}, u32[]{:S(2)}) collective-permute-start(bf16[512,128]{1,0:T(8,128)(2,1)S(1)} %bitcast.56), channel_id=1, source_target_pairs={{0,24},{8,16},{16,8},{24,0},{1,25},{9,17},{17,9},{25,1},{2,26},{10... | collective-permute-start | bytes 393224 | tf_op jit(solution)/shard_map/ppermute | solution.py:288
  41.3 2.9 %copy-start.9 = (bf16[4,336,128]{2,1,0:T(8,128)(2,1)}, bf16[4,336,128]{2,1,0:T(8,128)(2,1)S(1)}, u32[]{:S(2)}) copy-start(bf16[4,336,128]{2,1,0:T(8,128)(2,1)S(1)} %collective-permute-done.12.rest_1_) | copy-start | bytes 1032196
  41.3 6.5 %copy-start.10 = (bf16[4,336,128]{2,1,0:T(8,128)(2,1)}, bf16[4,336,128]{2,1,0:T(8,128)(2,1)S(1)}, u32[]{:S(2)}) copy-start(bf16[4,336,128]{2,1,0:T(8,128)(2,1)S(1)} %collective-permute-done.13.rest_3_) | copy-start | bytes 1032196
  41.3 6.4 %collective-permute-start.15 = (bf16[2,512,128]{2,1,0:T(8,128)(2,1)S(1)}, bf16[2,512,128]{2,1,0:T(8,128)(2,1)S(1)}, u32[]{:S(2)}, u32[]{:S(2)}) collective-permute-start(bf16[2,512,128]{2,1,0:T(8,128)(2,1)S(1)} %pad_maximum_fusion.5), channel_id=1, source_target_pairs={{0,4},{2,6},{4,0},{6,2},{1,5},{3,7},{5,1},{7,3},{8,12},{10,14},{12... | collective-permute-start | bytes 786440 | tf_op jit(solution)/shard_map/ppermute | solution.py:288
  43.1 6.4 %collective-permute-start.14 = (bf16[2,512,128]{2,1,0:T(8,128)(2,1)S(1)}, bf16[2,512,128]{2,1,0:T(8,128)(2,1)S(1)}, u32[]{:S(2)}, u32[]{:S(2)}) collective-permute-start(bf16[2,512,128]{2,1,0:T(8,128)(2,1)S(1)} %pad_maximum_fusion.4), channel_id=1, source_target_pairs={{0,2},{2,0},{4,6},{6,4},{1,3},{3,1},{5,7},{7,5},{8,10},{10,8},{12,... | collective-permute-start | bytes 786440 | tf_op jit(solution)/shard_map/ppermute | solution.py:288
  44.2 5.4 %collective-permute-start.16 = (bf16[4,336,128]{2,1,0:T(8,128)(2,1)S(1)}, bf16[4,336,128]{2,1,0:T(8,128)(2,1)S(1)}, u32[]{:S(2)}, u32[]{:S(2)}) collective-permute-start(bf16[4,336,128]{2,1,0:T(8,128)(2,1)S(1)} %pad_maximum_fusion.2.rest_0_), channel_id=1, source_target_pairs={{0,1},{1,0},{2,3},{3,2},{4,5},{5,4},{6,7},{7,6},{8,9},{9,8},{10,11... | collective-permute-start | bytes 1032200 | tf_op jit(solution)/shard_map/ppermute | solution.py:288
  44.2 5.4 %collective-permute-start.17 = (bf16[4,336,128]{2,1,0:T(8,128)(2,1)S(1)}, bf16[4,336,128]{2,1,0:T(8,128)(2,1)S(1)}, u32[]{:S(2)}, u32[]{:S(2)}) collective-permute-start(bf16[4,336,128]{2,1,0:T(8,128)(2,1)S(1)} %collective-permute-done.12.rest_1_), channel_id=1, source_target_pairs={{0,1},{1,0},{2,3},{3,2},{4,5},{5,4},{6,7},{7,6},{8,9},{9,8},{10,11... | collective-permute-start | bytes 1032200 | tf_op jit(solution)/shard_map/ppermute | solution.py:288
  44.7 4.9 %collective-permute-start.18 = (bf16[4,336,128]{2,1,0:T(8,128)(2,1)S(1)}, bf16[4,336,128]{2,1,0:T(8,128)(2,1)S(1)}, u32[]{:S(2)}, u32[]{:S(2)}) collective-permute-start(bf16[4,336,128]{2,1,0:T(8,128)(2,1)S(1)} %pad_maximum_fusion.3.rest_2_), channel_id=1, source_target_pairs={{0,1},{1,0},{2,3},{3,2},{4,5},{5,4},{6,7},{7,6},{8,9},{9,8},{10,11... | collective-permute-start | bytes 1032200 | tf_op jit(solution)/shard_map/ppermute | solution.py:288
  47.8 1.9 %collective-permute-start.19 = (bf16[4,336,128]{2,1,0:T(8,128)(2,1)S(1)}, bf16[4,336,128]{2,1,0:T(8,128)(2,1)S(1)}, u32[]{:S(2)}, u32[]{:S(2)}) collective-permute-start(bf16[4,336,128]{2,1,0:T(8,128)(2,1)S(1)} %collective-permute-done.13.rest_3_), channel_id=1, source_target_pairs={{0,1},{1,0},{2,3},{3,2},{4,5},{5,4},{6,7},{7,6},{8,9},{9,8},{10,11... | collective-permute-start | bytes 1032200 | tf_op jit(solution)/shard_map/ppermute | solution.py:288
  47.8 4.3 %copy-start = (bf16[4,512,128]{2,1,0:T(8,128)(2,1)}, bf16[4,512,128]{2,1,0:T(8,128)(2,1)S(1)}, u32[]{:S(2)}) copy-start(bf16[4,512,128]{2,1,0:T(8,128)(2,1)S(1)} %pad_maximum_fusion.1.rest_10_) | copy-start | bytes 1572868
  49.6 17.2 %copy-start.1 = (bf16[4,512,128]{2,1,0:T(8,128)(2,1)}, bf16[4,512,128]{2,1,0:T(8,128)(2,1)S(1)}, u32[]{:S(2)}) copy-start(bf16[4,512,128]{2,1,0:T(8,128)(2,1)S(1)} %pad_maximum_fusion.rest_8_) | copy-start | bytes 1572868
  49.6 0.8 copy-start.11
  49.6 1.5 %copy-start.12 = (bf16[4,336,128]{2,1,0:T(8,128)(2,1)}, bf16[4,336,128]{2,1,0:T(8,128)(2,1)S(1)}, u32[]{:S(2)}) copy-start(bf16[4,336,128]{2,1,0:T(8,128)(2,1)S(1)} %collective-permute-done.17.rest_5_) | copy-start | bytes 1032196
  49.6 2.5 %copy-start.13 = (bf16[4,336,128]{2,1,0:T(8,128)(2,1)}, bf16[4,336,128]{2,1,0:T(8,128)(2,1)S(1)}, u32[]{:S(2)}) copy-start(bf16[4,336,128]{2,1,0:T(8,128)(2,1)S(1)} %collective-permute-done.18.rest_6_) | copy-start | bytes 1032196
  50.4 14.4 %copy-start.14 = (bf16[4,336,128]{2,1,0:T(8,128)(2,1)}, bf16[4,336,128]{2,1,0:T(8,128)(2,1)S(1)}, u32[]{:S(2)}) copy-start(bf16[4,336,128]{2,1,0:T(8,128)(2,1)S(1)} %collective-permute-done.19.rest_7_) | copy-start | bytes 1032196
  50.4 13.0 %collective-permute-start.20 = (bf16[4,512,128]{2,1,0:T(8,128)(2,1)S(1)}, bf16[4,512,128]{2,1,0:T(8,128)(2,1)S(1)}, u32[]{:S(2)}, u32[]{:S(2)}) collective-permute-start(bf16[4,512,128]{2,1,0:T(8,128)(2,1)S(1)} %pad_maximum_fusion.rest_8_), channel_id=1, source_target_pairs={{0,4},{2,6},{4,0},{6,2},{1,5},{3,7},{5,1},{7,3},{8,12},{10,14},{12... | collective-permute-start | bytes 1572872 | tf_op jit(solution)/shard_map/ppermute | solution.py:288
  51.1 13.7 %collective-permute-start.21 = (bf16[4,512,128]{2,1,0:T(8,128)(2,1)S(1)}, bf16[4,512,128]{2,1,0:T(8,128)(2,1)S(1)}, u32[]{:S(2)}, u32[]{:S(2)}) collective-permute-start(bf16[4,512,128]{2,1,0:T(8,128)(2,1)S(1)} %pad_maximum_fusion.1.rest_10_), channel_id=1, source_target_pairs={{0,2},{2,0},{4,6},{6,4},{1,3},{3,1},{5,7},{7,5},{8,10},{10,8},{12,... | collective-permute-start | bytes 1572872 | tf_op jit(solution)/shard_map/ppermute | solution.py:288
  52.2 13.3 %collective-permute-start.22 = (bf16[4,512,128]{2,1,0:T(8,128)(2,1)S(1)}, bf16[4,512,128]{2,1,0:T(8,128)(2,1)S(1)}, u32[]{:S(2)}, u32[]{:S(2)}) collective-permute-start(bf16[4,512,128]{2,1,0:T(8,128)(2,1)S(1)} %pad_maximum_fusion.rest_8_), channel_id=1, source_target_pairs={{0,1},{1,0},{2,3},{3,2},{4,5},{5,4},{6,7},{7,6},{8,9},{9,8},{10,11... | collective-permute-start | bytes 1572872 | tf_op jit(solution)/shard_map/ppermute | solution.py:288
  52.2 13.3 %collective-permute-start.24 = (bf16[4,512,128]{2,1,0:T(8,128)(2,1)S(1)}, bf16[4,512,128]{2,1,0:T(8,128)(2,1)S(1)}, u32[]{:S(2)}, u32[]{:S(2)}) collective-permute-start(bf16[4,512,128]{2,1,0:T(8,128)(2,1)S(1)} %pad_maximum_fusion.1.rest_10_), channel_id=1, source_target_pairs={{0,1},{1,0},{2,3},{3,2},{4,5},{5,4},{6,7},{7,6},{8,9},{9,8},{10,11... | collective-permute-start | bytes 1572872 | tf_op jit(solution)/shard_map/ppermute | solution.py:288
  63.4 3.4 %copy-start.5 = (bf16[4,512,128]{2,1,0:T(8,128)(2,1)}, bf16[4,512,128]{2,1,0:T(8,128)(2,1)S(1)}, u32[]{:S(2)}) copy-start(bf16[4,512,128]{2,1,0:T(8,128)(2,1)S(1)} %collective-permute-done.20.rest_9_) | copy-start | bytes 1572868
  63.4 2.1 %collective-permute-start.23 = (bf16[4,512,128]{2,1,0:T(8,128)(2,1)S(1)}, bf16[4,512,128]{2,1,0:T(8,128)(2,1)}, u32[]{:S(2)}, u32[]{:S(2)}) collective-permute-start(bf16[4,512,128]{2,1,0:T(8,128)(2,1)S(1)} %collective-permute-done.20.rest_9_), channel_id=1, source_target_pairs={{0,1},{1,0},{2,3},{3,2},{4,5},{5,4},{6,7},{7,6},{8,9},{9,8},{10,11... | collective-permute-start | bytes 1572872 | tf_op jit(solution)/shard_map/ppermute | solution.py:288
  64.8 2.1 %copy-start.6 = (bf16[4,512,128]{2,1,0:T(8,128)(2,1)}, bf16[4,512,128]{2,1,0:T(8,128)(2,1)S(1)}, u32[]{:S(2)}) copy-start(bf16[4,512,128]{2,1,0:T(8,128)(2,1)S(1)} %collective-permute-done.21.rest_11_) | copy-start | bytes 1572868
  64.8 2.0 %collective-permute-start.25 = (bf16[4,512,128]{2,1,0:T(8,128)(2,1)S(1)}, bf16[4,512,128]{2,1,0:T(8,128)(2,1)}, u32[]{:S(2)}, u32[]{:S(2)}) collective-permute-start(bf16[4,512,128]{2,1,0:T(8,128)(2,1)S(1)} %collective-permute-done.21.rest_11_), channel_id=1, source_target_pairs={{0,1},{1,0},{2,3},{3,2},{4,5},{5,4},{6,7},{7,6},{8,9},{9,8},{10,11... | collective-permute-start | bytes 1572872 | tf_op jit(solution)/shard_map/ppermute | solution.py:288
  65.5 1.3 %copy-start.7 = (bf16[4,512,128]{2,1,0:T(8,128)(2,1)}, bf16[4,512,128]{2,1,0:T(8,128)(2,1)S(1)}, u32[]{:S(2)}) copy-start(bf16[4,512,128]{2,1,0:T(8,128)(2,1)S(1)} %collective-permute-done.22.rest_12_) | copy-start | bytes 1572868
  65.5 1.3 %copy-start.8 = (bf16[4,512,128]{2,1,0:T(8,128)(2,1)}, bf16[4,512,128]{2,1,0:T(8,128)(2,1)S(1)}, u32[]{:S(2)}) copy-start(bf16[4,512,128]{2,1,0:T(8,128)(2,1)S(1)} %collective-permute-done.24.rest_14_) | copy-start | bytes 1572868

commit v3 on v2

--- a/solution.py
+++ b/solution.py
@@ -67,50 +67,74 @@
     return jnp.concatenate(out, axis=0)[:, n:]
 
 
-def kernel(
-    n_row, n_col, n_cap, total,
-    own, *rest,
+def place_of(own, n_row, n_dev):
+    here, chip, core = own[0], own[1], own[2]
+
+    def at_device(r, c):
+        dr, dc, dk = here ^ r, chip ^ (c // 2), core ^ (c % 2)
+        dx, dy = dc & 1, dc >> 1
+        order = jnp.where(dr < 2, 2 * dx, 4 + 2 * dy) + jnp.where(
+            jnp.where(dr < 2, dy, dx) > 0, n_dev // 4, 0
+        )
+        return dk * (n_dev // 2) + order + (dr & 1)
+
+    def device_at(d):
+        far, second = (d >> 2) & 1, (d >> 3) & 1
+        first = (d >> 1) & 1
+        dc = jnp.where(far == 0, 2 * second + first, 2 * first + second)
+        return here ^ (2 * far + (d & 1)), 2 * (chip ^ dc) + (core ^ (d >> 4))
+
+    return at_device, device_at
+
+
+def copy_in(pairs, sems):
+    copies = [pltpu.make_async_copy(src, dst, sems.at[i]) for i, (src, dst) in enumerate(pairs)]
+    for copy in copies:
+        copy.start()
+    return copies
+
+
+def scatter_pair(pair, blocks, q, x):
+    k = x.shape[0]
+    if pair is not None:
+        pair[q] = x.astype(pair.dtype)
+    blocks[2 * q] = x[:, :k].astype(blocks.dtype)
+    blocks[2 * q + 1] = x[:, k:].astype(blocks.dtype)
+
+
+def add_products(n_group, blk, dims, from_list, source, to_list, total):
+    def group(i, carry):
+        for at in range(0, UNROLL, BATCH):
+            slots = [i * UNROLL + at + u for u in range(BATCH)]
+            prods = [dot(source[from_list[s]], blk[s], dims) for s in slots]
+            for s, prod in zip(slots, prods):
+                total[to_list[s]] = total[to_list[s]] + prod
+        return carry
+
+    lax.fori_loop(0, n_group, group, 0)
+
+
+def unpack(
+    n_row, n_col, own, mine, other,
+    lv, lw, nums, place, blk, vs, rm, ic, wb,
+    ints, meta, sems, small, vb,
 ):
-    smalls, fulls, out = rest[:8], rest[8:16], rest[16]
-    ints, meta, lv, lw, sems, small, full, tmp, home, blk = rest[17:27]
-    vs, vb, w, wb, wt, wtb, y, yb, ph, rm, ic, linv = rest[27:]
     n_dev = n_row * n_col
-    group = n_dev // 2
     k = vs.shape[1]
     half = k // 2
-    rpairs, cpairs = n_col, n_row
-    rblk, cblk = 2 * rpairs, 2 * cpairs
-    part = n_cap // n_col
+    rblk, cblk = 2 * n_col, 2 * n_row
     vec_at = OFF_CAP * half
     meta_at = vec_at + k
-    width = cpairs * 128
-
-    here, chip, core = own[0], own[1], own[2]
-    piece = n_dev // 8
-    waits = []
-    for i, (srcs, dst) in enumerate([(smalls, small), (fulls, full)]):
-        for j, ref in enumerate(srcs):
-            copy = pltpu.make_async_copy(ref, dst.at[pl.ds(j * piece, piece)], sems.at[8 * i + j])
-            copy.start()
-            waits.append(copy)
-    for copy in waits[:8]:
+    at_device, device_at = place_of(own, n_row, n_dev)
+
+    first, second = pl.ds(0, n_dev // 2), pl.ds(n_dev // 2, n_dev // 2)
+    for copy in copy_in([(mine, small.at[first]), (other, small.at[second])], sems):
         copy.wait()
     for d in range(n_dev):
         rows = small[d, meta_at : meta_at + META, :].astype(jnp.float32)
         ints[d : d + 1, :] = rows[8:9].astype(jnp.int32)
-    to_scalars = pltpu.make_async_copy(ints, meta, sems.at[16])
+    to_scalars = pltpu.make_async_copy(ints, meta, sems.at[2])
     to_scalars.start()
-
-    def at_device(r, c):
-        dr, dc, dk = here ^ r, chip ^ (c // 2), core ^ (c % 2)
-        dx, dy = dc & 1, dc >> 1
-        order = jnp.where(dr < 2, 4 * dy + 2 * dx, 8 + 4 * dx + 2 * dy)
-        return dk * group + order + (dr & 1)
-
-    def scatter_pair(pair, blocks, q, x):
-        pair[q] = x.astype(pair.dtype)
-        blocks[2 * q] = x[:, :k].astype(blocks.dtype)
-        blocks[2 * q + 1] = x[:, k:].astype(blocks.dtype)
 
     for r in range(n_row):
         for c in range(n_col):
@@ -119,17 +143,14 @@
             rm[p] = jnp.broadcast_to(rows[0:1] + rows[1:2] + rows[2:3], (8, 128))
             ic[q] = jnp.broadcast_to(rows[3:4] + rows[4:5] + rows[5:6], (8, 128))
             scatter_pair(vs, vb, q, small[d, vec_at : vec_at + k, :].astype(jnp.float32))
-
+            wb[2 * p] = jnp.zeros_like(wb[2 * p])
+            wb[2 * p + 1] = jnp.zeros_like(wb[2 * p + 1])
     to_scalars.wait()
 
     def device(d, n):
         count = meta[d, 2 * OFF_CAP]
         count = jnp.where(count > OFF_CAP, 0, count)
-        near = (d & 8) == 0
-        one, two = (d >> 1) & 1, (d >> 2) & 1
-        dc = jnp.where(near, 2 * two + one, 2 * one + two)
-        c = 2 * (chip ^ dc) + (core ^ (d >> 4))
-        r = here ^ (jnp.where(near, 0, 2) + (d & 1))
+        r, c = device_at(d)
         for s in range(OFF_CAP):
             lv[n + s] = c * cblk + meta[d, OFF_CAP + s]
             lw[n + s] = r * rblk + meta[d, s]
@@ -143,20 +164,47 @@
         lw[n_live + u] = 0
         blk[n_live + u] = jnp.zeros((k, k), jnp.bfloat16)
     n_group = (n_live + UNROLL - 1) // UNROLL
-
-    for copy in waits[8:]:
-        copy.wait()
-    left = lax.broadcasted_iota(jnp.int32, (rblk, 128), 1) < 64
-    homes = []
+    nums[0] = n_group
+
     for r in range(n_row):
         h = jnp.int32(0)
         for c in range(n_col):
             h = jnp.where(meta[at_device(r, c), 2 * OFF_CAP] > OFF_CAP, c, h)
-        homes.append(h)
+        nums[1 + r] = h
         index = small[at_device(r, h), meta_at : meta_at + META, :].astype(jnp.float32)
-        place = index[7:8] * float(rblk) + index[6:7]
+        place[r : r + 1, :] = index[7:8] * float(rblk) + index[6:7]
+
+    add_products(n_group, blk, NT, lv, vb, lw, wb)
+
+
+def iterate(n_row, n_col, n_cap, total, own, lv, lw, nums, place, *rest):
+    sources, fulls, out = rest[:5], rest[5:9], rest[9]
+    sems, full, tmp, home, blk, vs, rm, ic, wb = rest[10:19]
+    vb, w, wt, wtb, y, yb, ph, linv = rest[19:]
+    n_dev = n_row * n_col
+    k = vs.shape[1]
+    half = k // 2
+    rpairs, cpairs = n_col, n_row
+    rblk, cblk = 2 * rpairs, 2 * cpairs
+    part = n_cap // n_col
+    width = cpairs * 128
+    at_device, _ = place_of(own, n_row, n_dev)
+
+    at, pairs = 0, []
+    for ref in fulls:
+        pairs.append((ref, full.at[pl.ds(at, ref.shape[0])]))
+        at += ref.shape[0]
+    copies = copy_in(pairs + list(zip(sources, (blk, vs, rm, ic, wb))), sems)
+    for copy in copies[: len(fulls)]:
+        copy.wait()
+    n_group = nums[0]
+
+    left = lax.broadcasted_iota(jnp.int32, (rblk, 128), 1) < 64
+    homes = []
+    for r in range(n_row):
+        homes.append(nums[1 + r])
         want = lax.broadcasted_iota(jnp.int32, (cblk * rblk, n_cap), 0).astype(jnp.float32)
-        select = jnp.where(want == place, 1.0, 0.0).astype(jnp.bfloat16)
+        select = jnp.where(want == place[r : r + 1, :], 1.0, 0.0).astype(jnp.bfloat16)
 
         parts = [at_device(r, 2 * i + j) for j in range(2) for i in range(n_col // 2)]
 
@@ -187,14 +235,14 @@
 
         lax.fori_loop(0, rblk, cut, 0, unroll=4)
 
-    def clear():
-        for q in range(n_dev):
-            y[q] = jnp.zeros_like(y[q])
-            for ref in (wb, yb):
-                ref[2 * q] = jnp.zeros_like(ref[2 * q])
-                ref[2 * q + 1] = jnp.zeros_like(ref[2 * q + 1])
-
-    clear()
+    def clear(refs):
+        for ref in refs:
+            for q in range(ref.shape[0]):
+                ref[q] = jnp.zeros_like(ref[q])
+
+    clear([y, yb])
+    for copy in copies[len(fulls) :]:
+        copy.wait()
 
     def iteration(it, carry):
         @pl.when(it > 0)
@@ -217,15 +265,10 @@
                 w[r * rpairs + p] = prod[:, :128]
                 w[r * rpairs + p + 1] = prod[:, 128:]
 
-        def forward(i, carry):
-            for at in range(0, UNROLL, BATCH):
-                slots = [i * UNROLL + at + u for u in range(BATCH)]
-                prods = [dot(vb[lv[s]], blk[s], NT) for s in slots]
-                for s, prod in zip(slots, prods):
-                    wb[lw[s]] = wb[lw[s]] + prod
-            return carry
-
-        lax.fori_loop(0, n_group, forward, 0)
+        @pl.when(it > 0)
+        def _():
+            add_products(n_group, blk, NT, lv, vb, lw, wb)
+
         for p in range(n_dev):
             x = w[p] + jnp.concatenate([wb[2 * p], wb[2 * p + 1]], axis=1)
             scatter_pair(wt, wtb, p, x * rm[p, 0:1, :])
@@ -240,15 +283,7 @@
                 y[base + u] = y[base + u] + prod[:, :128]
                 y[base + u + 1] = y[base + u + 1] + prod[:, 128:]
 
-        def backward(i, carry):
-            for at in range(0, UNROLL, BATCH):
-                slots = [i * UNROLL + at + u for u in range(BATCH)]
-                prods = [dot(wtb[lw[s]], blk[s]) for s in slots]
-                for s, prod in zip(slots, prods):
-                    yb[lv[s]] = yb[lv[s]] + prod
-            return carry
-
-        lax.fori_loop(0, n_group, backward, 0)
+        add_products(n_group, blk, NN, lw, wtb, lv, yb)
 
         both = jnp.zeros((2 * k, k), jnp.float32)
         for q in range(0, n_dev, 4):
@@ -264,14 +299,14 @@
             lo = jnp.concatenate(los, axis=1)
             both = both + dot(jnp.concatenate([hi, lo], axis=0), hi, NT)
         gram = (both[:k] + (both[k:] + both[k:].T)) / total
-        clear()
+        clear([y, yb, wb])
         linv[...] = inverse_factor(gram)
         return carry
 
     lax.fori_loop(0, ITERS, iteration, 0)
     lh, ll = split2(linv[...])
-    place = (2 * chip + core) * n_row + here
-    hi, lo = ph[place, :k, :], ph[place, k:, :]
+    q = (2 * own[1] + own[2]) * n_row + own[0]
+    hi, lo = ph[q, :k, :], ph[q, k:, :]
     x = dot(lh, hi) + dot(ll, hi) + dot(lh, lo)
     out[0] = x[:, :k]
     out[1] = x[:, k:]
@@ -302,11 +337,7 @@
 
 def along_other_chip_axis(x):
     near, far = x
-    return [near, swap(near, "chip", 2), far, swap(far, "chip", 1)]
-
-
-def with_other_core(x):
-    return x + [swap(v, "core", 1) for v in x]
+    return [swap(near, "chip", 2), swap(far, "chip", 1)]
 
 
 def full_part(tile, has_full, n_chip, part, chip, core):
@@ -357,45 +388,68 @@
     home, smalls[1] = together((home, smalls[1]))
     homes, smalls = along_rows(home), along_one_chip_axis(smalls)
     smalls, homes[1:3] = together((smalls, homes[1:3]))
-    homes, smalls = together((homes, along_other_chip_axis(smalls)))
-    homes, smalls = together((along_one_chip_axis(homes), with_other_core(smalls)))
-    homes = with_other_core(along_other_chip_axis(homes))
-
-    place = jnp.stack([row, chip, core]).astype(jnp.int32)
+    smalls = jnp.concatenate(smalls + along_other_chip_axis(smalls))
+    homes, smalls = together((homes, smalls))
+    homes, others = together((along_one_chip_axis(homes), swap(smalls, "core", 1)))
+    last = along_other_chip_axis(homes)
+    homes = jnp.concatenate(homes)
+    other_homes = swap(homes, "core", 1)
+
+    where = jnp.stack([row, chip, core]).astype(jnp.int32)
 
     height, width = 2 * n_col * bsize, 2 * n_row * bsize
     slots = n_dev * OFF_CAP + UNROLL
-    pair_f32 = pltpu.VMEM((n_dev, k, 128), jnp.float32)
-    pair_bf16 = pltpu.VMEM((n_dev, k, 128), bf16)
-    block_f32 = pltpu.VMEM((2 * n_dev, k, bsize), jnp.float32)
-    block_bf16 = pltpu.VMEM((2 * n_dev, k, bsize), bf16)
-    mass_f32 = pltpu.VMEM((n_dev, 8, 128), jnp.float32)
+    f32, i32 = jnp.float32, jnp.int32
+    pair, block, mass = (n_dev, k, 128), (2 * n_dev, k, bsize), (n_dev, 8, 128)
+    smem, anywhere = (pl.BlockSpec(memory_space=m) for m in (pltpu.SMEM, pl.ANY))
+    vmem = pl.BlockSpec(memory_space=pltpu.VMEM)
+    lists = [((slots,), i32), ((slots,), i32), ((1 + n_row,), i32)]
+    arrays = [
+        ((8, 128), f32), ((slots, bsize, bsize), bf16), (pair, bf16), (mass, f32), (mass, f32), (block, f32),
+    ]
+    unpacked = pl.pallas_call(
+        functools.partial(unpack, n_row, n_col),
+        out_shape=[jax.ShapeDtypeStruct(*v) for v in lists + arrays],
+        in_specs=[smem, anywhere, anywhere],
+        out_specs=[smem] * len(lists) + [vmem] * len(arrays),
+        scratch_shapes=[
+            pltpu.VMEM((n_dev, 128), i32),
+            pltpu.SMEM((n_dev, 128), i32),
+            pltpu.SemaphoreType.DMA((3,)),
+            pltpu.VMEM((n_dev,) + small.shape, bf16),
+            pltpu.VMEM(block, bf16),
+        ],
+        compiler_params=pltpu.CompilerParams(vmem_limit_bytes=VMEM_LIMIT // 2),
+        cost_estimate=pl.CostEstimate(
+            flops=2 * slots * bsize**3, bytes_accessed=2 * n_dev * small.size * 2, transcendentals=0
+        ),
+        name="unpack",
+    )(where, smalls, others)
+    last, unpacked = together((last, unpacked))
+    last = jnp.concatenate(last)
+    fulls = [homes, last, other_homes, swap(last, "core", 1)]
     result = pl.pallas_call(
-        functools.partial(kernel, n_row, n_col, n_cap, float(n_dev * own * bsize)),
-        out_shape=jax.ShapeDtypeStruct((own, k, bsize), jnp.float32),
-        in_specs=[pl.BlockSpec(memory_space=pltpu.SMEM)]
-        + [pl.BlockSpec(memory_space=pl.ANY)] * 16,
-        out_specs=pl.BlockSpec(memory_space=pltpu.VMEM),
+        functools.partial(iterate, n_row, n_col, n_cap, float(n_dev * own * bsize)),
+        out_shape=jax.ShapeDtypeStruct((own, k, bsize), f32),
+        in_specs=[smem] * 4 + [vmem] + [anywhere] * (5 + len(fulls)),
+        out_specs=vmem,
         scratch_shapes=[
-            pltpu.VMEM((n_dev, 128), jnp.int32),
-            pltpu.SMEM((n_dev, 128), jnp.int32),
-            pltpu.SMEM((slots,), jnp.int32),
-            pltpu.SMEM((slots,), jnp.int32),
-            pltpu.SemaphoreType.DMA((17,)),
-            pltpu.VMEM((n_dev,) + small.shape, bf16),
+            pltpu.SemaphoreType.DMA((5 + len(fulls),)),
             pltpu.VMEM((n_dev,) + home.shape, bf16),
-            pltpu.VMEM((n_row, height, 128), jnp.float32),
+            pltpu.VMEM((n_row, height, 128), f32),
             pltpu.VMEM((n_row, height, 2 * width), bf16),
-            pltpu.VMEM((slots, bsize, bsize), bf16),
-            pair_bf16, block_bf16, pair_f32, block_f32,
-            pair_bf16, block_bf16, pair_f32, block_f32,
-            pltpu.VMEM((n_dev, 2 * k, 128), bf16),
-            mass_f32, mass_f32,
-            pltpu.VMEM((k, k), jnp.float32),
+            *[pltpu.VMEM(*v) for v in arrays[1:]],
+            *[
+                pltpu.VMEM(*v)
+                for v in [
+                    (block, bf16), (pair, f32), (pair, bf16), (block, bf16), (pair, f32), (block, f32),
+                    ((n_dev, 2 * k, 128), bf16), ((k, k), f32),
+                ]
+            ],
         ],
         compiler_params=pltpu.CompilerParams(vmem_limit_bytes=VMEM_LIMIT),
         name="iterate",
-    )(place, *smalls, *homes)
+    )(where, *unpacked, *fulls)
     return result.reshape(own, k * bsize)
 
 

time: 137 us -> 144 us (1.051); the launches traced: 134 us -> 143 us
  local copies, waits for them, and re-layouts: 6.22 us -> 17.4 us
  waiting for transfers between devices: 33.1 us -> 24.1 us
  Pallas kernels: 65.8 us -> 71.8 us
  other arithmetic: 2.27 us -> 3.97 us
    ppermute x26 -> x21, waiting for transfers between devices: 33.1 us -> 24.1 us  [swap(): return lax.ppermute(x, axis, [(i, i ^ distance) for i in range(size)])]
    unnamed x41 -> x33, local copies, waits for them, and re-layouts: 3.84 us -> 10.9 us
    pallas_call x1 -> x2, Pallas kernels: 65.8 us -> 71.8 us  [the longest x1 64.1 us: whole_on_each(): pl.pallas_call(functools.partial(iterate, n_row, n_col, n_cap, float(n_de...]
    ppermute x26 -> x21, starting transfers between devices: 25.7 us -> 25.1 us  [swap(): return lax.ppermute(x, axis, [(i, i ^ distance) for i in range(size)])]
  transfers between devices with their start and end apart: 26 -> 21, of which waited for: 13 -> 10; matrix products, arithmetic and copies ran while one was open for 2% -> 7% of each run, Pallas kernels for 0% -> 5%
where the time goes in v3:
time: 144 us; the launch traced here: 143 us
  Pallas kernels  71.8 us (50%)
  starting transfers between devices  25.1 us (17%)
  waiting for transfers between devices  24.1 us (17%)
  local copies, waits for them, and re-layouts  17.4 us (12%)
  other arithmetic  3.97 us (3%)
    pallas_call x1, Pallas kernels, whole_on_each(): pl.pallas_call(functools.partial(iterate, n_row, n_col, n_cap, float(n_de...  64.1 us
    ppermute x21, starting transfers between devices, swap(): return lax.ppermute(x, axis, [(i, i ^ distance) for i in range(size)])  25.1 us
    ppermute x21, waiting for transfers between devices, swap(): return lax.ppermute(x, axis, [(i, i ^ distance) for i in range(size)])  24.1 us
    unnamed x33, local copies, waits for them, and re-layouts  10.9 us
    pallas_call x1, Pallas kernels, whole_on_each(): pl.pallas_call(functools.partial(unpack, n_row, n_col), out_shape=[jax.Sh...  7.67 us
  transfers between devices with their start and end apart: 21, of which 10 were waited for; matrix products, arithmetic and copies ran while one was open for 7% of the time, Pallas kernels for 5%

profile of v3, /device:TPU:0, one launch (start us, length us, event | category | flops | bytes accessed | tf_op | source)
XLA Modules:
  0.0 143.4 jit_solution(4623857234653194562)
XLA Ops:
  0.7 1.1 select_bitcast_fusion
  2.4 0.8 slice.14
  3.2 0.7 fusion.6
  3.9 0.7 fusion.7
  4.5 0.7 sqrt.3
  5.3 0.8 reshape.208
  6.2 0.9 reshape.206
  7.5 3.7 %collective-permute-start.6 = (bf16[336,128]{1,0:T(8,128)(2,1)S(1)}, bf16[336,128]{1,0:T(8,128)(2,1)S(1)}, u32[]{:S(2)}, u32[]{:S(2)}) collective-permute-start(bf16[336,128]{1,0:T(8,128)(2,1)S(1)} %concatenate.54), channel_id=1, source_target_pairs={{0,16},{8,24},{16,0},{24,8},{1,17},{9,25},{17,1},{25,9},{2,18},{10... | collective-permute-start | bytes 258056 | tf_op jit(solution)/shard_map/ppermute | solution.py:323
  11.2 1.3 collective-permute-start.7
  12.7 1.6 %collective-permute-start.1 = (bf16[16,4096]{1,0:T(8,128)(2,1)S(1)}, bf16[16,4096]{1,0:T(8,128)(2,1)S(1)}, u32[]{:S(2)}, u32[]{:S(2)}) collective-permute-start(bf16[16,4096]{1,0:T(8,128)(2,1)S(1)} %get-tuple-element.73), channel_id=1, source_target_pairs={{0,2},{2,0},{4,6},{6,4},{1,3},{3,1},{5,7},{7,5},{8,10},{10,8},{12,... | collective-permute-start | bytes 393224 | tf_op jit(solution)/shard_map/ppermute | solution.py:323
  14.2 1.5 %collective-permute-start.2 = (bf16[16,4096]{1,0:T(8,128)(2,1)S(1)}, bf16[16,4096]{1,0:T(8,128)(2,1)S(1)}, u32[]{:S(2)}, u32[]{:S(2)}) collective-permute-start(bf16[16,4096]{1,0:T(8,128)(2,1)S(1)} %get-tuple-element.75), channel_id=1, source_target_pairs={{0,4},{2,6},{4,0},{6,2},{1,5},{3,7},{5,1},{7,3},{8,12},{10,14},{12... | collective-permute-start | bytes 393224 | tf_op jit(solution)/shard_map/ppermute | solution.py:323
  16.2 2.0 %collective-permute-done.6 = bf16[336,128]{1,0:T(8,128)(2,1)S(1)} collective-permute-done((bf16[336,128]{1,0:T(8,128)(2,1)S(1)}, bf16[336,128]{1,0:T(8,128)(2,1)S(1)}, u32[]{:S(2)}, u32[]{:S(2)}) %collective-permute-start.6) | collective-permute-done | bytes 86048 | tf_op jit(solution)/shard_map/ppermute | solution.py:323
  18.3 0.6 collective-permute-start.4
  18.9 1.6 %collective-permute-start.8 = (bf16[2,336,128]{2,1,0:T(8,128)(2,1)S(1)}, bf16[2,336,128]{2,1,0:T(8,128)(2,1)S(1)}, u32[]{:S(2)}, u32[]{:S(2)}) collective-permute-start(bf16[2,336,128]{2,1,0:T(8,128)(2,1)S(1)} %pad_maximum_fusion.8), channel_id=1, source_target_pairs={{0,4},{2,6},{4,0},{6,2},{1,5},{3,7},{5,1},{7,3},{8,12},{10,14},{12... | collective-permute-start | bytes 516104 | tf_op jit(solution)/shard_map/ppermute | solution.py:323
  20.4 1.8 %collective-permute-done.2 = bf16[16,4096]{1,0:T(8,128)(2,1)S(1)} collective-permute-done((bf16[16,4096]{1,0:T(8,128)(2,1)S(1)}, bf16[16,4096]{1,0:T(8,128)(2,1)S(1)}, u32[]{:S(2)}, u32[]{:S(2)}) %collective-permute-start.2) | collective-permute-done | bytes 131104 | tf_op jit(solution)/shard_map/ppermute | solution.py:323
  22.8 1.8 %collective-permute-start.5 = (bf16[2,336,128]{2,1,0:T(8,128)(2,1)S(1)}, bf16[2,336,128]{2,1,0:T(8,128)(2,1)S(1)}, u32[]{:S(2)}, u32[]{:S(2)}) collective-permute-start(bf16[2,336,128]{2,1,0:T(8,128)(2,1)S(1)} %pad_maximum_fusion.7), channel_id=1, source_target_pairs={{0,2},{2,0},{4,6},{6,4},{1,3},{3,1},{5,7},{7,5},{8,10},{10,8},{12,... | collective-permute-start | bytes 516104 | tf_op jit(solution)/shard_map/ppermute | solution.py:323
  24.6 1.9 %collective-permute-start.10 = (bf16[512,128]{1,0:T(8,128)(2,1)S(1)}, bf16[512,128]{1,0:T(8,128)(2,1)S(1)}, u32[]{:S(2)}, u32[]{:S(2)}) collective-permute-start(bf16[512,128]{1,0:T(8,128)(2,1)S(1)} %bitcast.54), channel_id=1, source_target_pairs={{0,16},{8,24},{16,0},{24,8},{1,17},{9,25},{17,1},{25,9},{2,18},{10... | collective-permute-start | bytes 393224 | tf_op jit(solution)/shard_map/ppermute | solution.py:323
  26.5 1.8 %collective-permute-start.9 = (bf16[512,128]{1,0:T(8,128)(2,1)S(1)}, bf16[512,128]{1,0:T(8,128)(2,1)S(1)}, u32[]{:S(2)}, u32[]{:S(2)}) collective-permute-start(bf16[512,128]{1,0:T(8,128)(2,1)S(1)} %bitcast.55), channel_id=1, source_target_pairs={{0,8},{8,0},{16,24},{24,16},{1,9},{9,1},{17,25},{25,17},{2,10},{10... | collective-permute-start | bytes 393224 | tf_op jit(solution)/shard_map/ppermute | solution.py:323
  28.4 3.9 %collective-permute-done.10 = bf16[512,128]{1,0:T(8,128)(2,1)S(1)} collective-permute-done((bf16[512,128]{1,0:T(8,128)(2,1)S(1)}, bf16[512,128]{1,0:T(8,128)(2,1)S(1)}, u32[]{:S(2)}, u32[]{:S(2)}) %collective-permute-start.10) | collective-permute-done | bytes 131104 | tf_op jit(solution)/shard_map/ppermute | solution.py:323
  32.3 0.7 collective-permute-done.9
  33.0 1.5 %collective-permute-start.12 = (bf16[4,336,128]{2,1,0:T(8,128)(2,1)S(1)}, bf16[4,336,128]{2,1,0:T(8,128)(2,1)S(1)}, u32[]{:S(2)}, u32[]{:S(2)}) collective-permute-start(bf16[4,336,128]{2,1,0:T(8,128)(2,1)S(1)} %pad_maximum_fusion.3), channel_id=1, source_target_pairs={{0,4},{2,6},{4,0},{6,2},{1,5},{3,7},{5,1},{7,3},{8,12},{10,14},{12... | collective-permute-start | bytes 1032200 | tf_op jit(solution)/shard_map/ppermute | solution.py:323
  34.5 0.5 collective-permute-start.13
  35.1 2.4 %collective-permute-start.11 = (bf16[512,128]{1,0:T(8,128)(2,1)S(1)}, bf16[512,128]{1,0:T(8,128)(2,1)S(1)}, u32[]{:S(2)}, u32[]{:S(2)}) collective-permute-start(bf16[512,128]{1,0:T(8,128)(2,1)S(1)} %bitcast.56), channel_id=1, source_target_pairs={{0,24},{8,16},{16,8},{24,0},{1,25},{9,17},{17,9},{25,1},{2,26},{10... | collective-permute-start | bytes 393224 | tf_op jit(solution)/shard_map/ppermute | solution.py:323
  37.5 3.8 %collective-permute-done.12 = bf16[4,336,128]{2,1,0:T(8,128)(2,1)S(1)} collective-permute-done((bf16[4,336,128]{2,1,0:T(8,128)(2,1)S(1)}, bf16[4,336,128]{2,1,0:T(8,128)(2,1)S(1)}, u32[]{:S(2)}, u32[]{:S(2)}) %collective-permute-start.12) | collective-permute-done | bytes 344096 | tf_op jit(solution)/shard_map/ppermute | solution.py:323
  41.3 1.2 collective-permute-done.13
  42.9 0.6 collective-permute-start.15
  43.5 0.6 collective-permute-start.14
  44.1 7.6 %collective-permute-done.15 = bf16[2,512,128]{2,1,0:T(8,128)(2,1)S(1)} collective-permute-done((bf16[2,512,128]{2,1,0:T(8,128)(2,1)S(1)}, bf16[2,512,128]{2,1,0:T(8,128)(2,1)S(1)}, u32[]{:S(2)}, u32[]{:S(2)}) %collective-permute-start.15) | collective-permute-done | bytes 262176 | tf_op jit(solution)/shard_map/ppermute | solution.py:323
  52.0 0.9 pad_maximum_fusion.1
  52.9 1.5 %collective-permute-start.17 = (bf16[4,512,128]{2,1,0:T(8,128)(2,1)}, bf16[4,512,128]{2,1,0:T(8,128)(2,1)}, u32[]{:S(2)}, u32[]{:S(2)}) collective-permute-start(bf16[4,512,128]{2,1,0:T(8,128)(2,1)} %pad_maximum_fusion.1), channel_id=1, source_target_pairs={{0,4},{2,6},{4,0},{6,2},{1,5},{3,7},{5,1},{7,3},{8,12},{10,14},{12... | collective-permute-start | bytes 1572872 | tf_op jit(solution)/shard_map/ppermute | solution.py:323
  55.0 1.1 constant_dynamic-update-slice_fusion.1
  56.3 7.7 %unpack.1 = (s32[272]{0:T(512)S(1)}, s32[272]{0:T(512)S(1)}, s32[5]{0:T(128)S(1)}, f32[8,128]{1,0:T(8,128)S(1)}, bf16[272,64,64]{2,1,0:T(8,128)(2,1)S(1)}, /*ind...) custom-call(s32[3]{0:T(128)S(1)} %pad_add_fusion.own, ...), custom_call_target="tpu_custom_call" | custom-call | flops 142606336 | bytes 5505024 | tf_op jit(solution)/shard_map/unpack/pallas_call | solution.py:410
  64.0 2.1 %copy-done = bf16[272,64,64]{2,1,0:T(8,128)(2,1)} copy-done((bf16[272,64,64]{2,1,0:T(8,128)(2,1)}, bf16[272,64,64]{2,1,0:T(8,128)(2,1)S(1)}, u32[]{:S(2)}) %copy-start) | copy-done | bytes 2228248
  66.0 1.4 copy-done.1
  67.4 0.8 copy-done.2
  68.2 0.6 copy-done.3
  68.8 0.6 copy-done.4
  69.5 0.6 copy-done.6
  70.1 0.5 copy-done.7
  70.6 0.5 copy-done.8
  71.1 0.6 copy-done.9
  71.7 1.1 constant_dynamic-update-slice_fusion.3
  72.8 1.1 constant_dynamic-update-slice_fusion.2.rest_6_
  73.9 0.6 collective-permute-start.20
  74.5 2.3 %collective-permute-done.20.rest_8_ = bf16[8,512,128]{2,1,0:T(8,128)(2,1)S(1)} collective-permute-done((bf16[8,512,128]{2,1,0:T(8,128)(2,1)S(1)}, bf16[8,512,128]{2,1,0:T(8,128)(2,1)S(1)}, u32[]{:S(2)}, u32[]{:S(2)}) %collective-permute-start.20) | collective-permute-done | bytes 1048608 | tf_op jit(solution)/shard_map/ppermute | solution.py:323
  76.8 1.0 copy-done.14
  77.7 64.1 %iterate.1 = f32[2,64,64]{2,1,0:T(8,128)} custom-call(s32[3]{0:T(128)} %copy-done.5, s32[272]{0:T(512)} %copy-done.7, s32[272]{0:T(512)} %copy-done.8, s32[5]{0:T(128)} %copy-done.9, f32[8,128]{1,0:T(8,128)} %copy-done.6, bf16[272,64,64]{2,1,0:T(8,128)(2,1)} %copy-done, bf16[32,64,128]{2,1,0:T(8,128)(2,1)} %copy-done.2, f32[32,8,128]{2,1,0:T(8,128)} %copy-done.3, ...), custom_call_target="tpu_custom_call" | custom-call | tf_op jit(solution)/shard_map/iterate/pallas_call | solution.py:431
  141.9 1.5 %reshape.211 = f32[2,4096]{1,0:T(2,128)} reshape(f32[2,64,64]{2,1,0:T(8,128)} %iterate.1) | data formatting | bytes 65536 | tf_op jit(solution)/shard_map/reshape | solution.py:453
  (68 shorter events, 3.8 us)
Async XLA Ops:
  0.0 12.6 %copy-start.12 = (bf16[1,1,128,4096]{3,2,1,0:T(8,128)(2,1)S(1)}, bf16[1,1,128,4096]{3,2,1,0:T(8,128)(2,1)}, u32[]{:S(2)}) copy-start(bf16[1,1,128,4096]{3,2,1,0:T(8,128)(2,1)} %param.7) | copy-start | bytes 3145732
  1.8 10.7 %collective-permute-start = (bf16[4,16,4096]{2,1,0:T(8,128)(2,1)S(1)}, bf16[4,16,4096]{2,1,0:T(8,128)(2,1)S(1)}, u32[]{:S(2)}, u32[]{:S(2)}) collective-permute-start(bf16[4,16,4096]{2,1,0:T(8,128)(2,1)S(1)} %select_bitcast_fusion), channel_id=1, source_target_pairs={{0,1},{1,0},{2,3},{3,2},{4,5},{5,4},{6,7},{7,6},{8,9},{9,8},{10,11... | collective-permute-start | bytes 1572872 | tf_op jit(solution)/shard_map/ppermute | solution.py:323
  7.5 10.7 %collective-permute-start.6 = (bf16[336,128]{1,0:T(8,128)(2,1)S(1)}, bf16[336,128]{1,0:T(8,128)(2,1)S(1)}, u32[]{:S(2)}, u32[]{:S(2)}) collective-permute-start(bf16[336,128]{1,0:T(8,128)(2,1)S(1)} %concatenate.54), channel_id=1, source_target_pairs={{0,16},{8,24},{16,0},{24,8},{1,17},{9,25},{17,1},{25,9},{2,18},{10... | collective-permute-start | bytes 258056 | tf_op jit(solution)/shard_map/ppermute | solution.py:323
  11.2 7.6 %collective-permute-start.7 = (bf16[336,128]{1,0:T(8,128)(2,1)S(1)}, bf16[336,128]{1,0:T(8,128)(2,1)S(1)}, u32[]{:S(2)}, u32[]{:S(2)}) collective-permute-start(bf16[336,128]{1,0:T(8,128)(2,1)S(1)} %concatenate.54), channel_id=1, source_target_pairs={{0,24},{8,16},{16,8},{24,0},{1,25},{9,17},{17,9},{25,1},{2,26},{10... | collective-permute-start | bytes 258056 | tf_op jit(solution)/shard_map/ppermute | solution.py:323
  12.7 7.8 %collective-permute-start.1 = (bf16[16,4096]{1,0:T(8,128)(2,1)S(1)}, bf16[16,4096]{1,0:T(8,128)(2,1)S(1)}, u32[]{:S(2)}, u32[]{:S(2)}) collective-permute-start(bf16[16,4096]{1,0:T(8,128)(2,1)S(1)} %get-tuple-element.73), channel_id=1, source_target_pairs={{0,2},{2,0},{4,6},{6,4},{1,3},{3,1},{5,7},{7,5},{8,10},{10,8},{12,... | collective-permute-start | bytes 393224 | tf_op jit(solution)/shard_map/ppermute | solution.py:323
  14.2 8.0 %collective-permute-start.2 = (bf16[16,4096]{1,0:T(8,128)(2,1)S(1)}, bf16[16,4096]{1,0:T(8,128)(2,1)S(1)}, u32[]{:S(2)}, u32[]{:S(2)}) collective-permute-start(bf16[16,4096]{1,0:T(8,128)(2,1)S(1)} %get-tuple-element.75), channel_id=1, source_target_pairs={{0,4},{2,6},{4,0},{6,2},{1,5},{3,7},{5,1},{7,3},{8,12},{10,14},{12... | collective-permute-start | bytes 393224 | tf_op jit(solution)/shard_map/ppermute | solution.py:323
  15.8 6.4 %collective-permute-start.3 = (bf16[16,4096]{1,0:T(8,128)(2,1)S(1)}, bf16[16,4096]{1,0:T(8,128)(2,1)S(1)}, u32[]{:S(2)}, u32[]{:S(2)}) collective-permute-start(bf16[16,4096]{1,0:T(8,128)(2,1)S(1)} %get-tuple-element.74), channel_id=1, source_target_pairs={{0,6},{2,4},{4,2},{6,0},{1,7},{3,5},{5,3},{7,1},{8,14},{10,12},{12... | collective-permute-start | bytes 393224 | tf_op jit(solution)/shard_map/ppermute | solution.py:323
  18.3 4.5 %collective-permute-start.4 = (bf16[336,128]{1,0:T(8,128)(2,1)S(1)}, bf16[336,128]{1,0:T(8,128)(2,1)S(1)}, u32[]{:S(2)}, u32[]{:S(2)}) collective-permute-start(bf16[336,128]{1,0:T(8,128)(2,1)S(1)} %concatenate.54), channel_id=1, source_target_pairs={{0,8},{8,0},{16,24},{24,16},{1,9},{9,1},{17,25},{25,17},{2,10},{10... | collective-permute-start | bytes 258056 | tf_op jit(solution)/shard_map/ppermute | solution.py:323
  18.9 9.4 %collective-permute-start.8 = (bf16[2,336,128]{2,1,0:T(8,128)(2,1)S(1)}, bf16[2,336,128]{2,1,0:T(8,128)(2,1)S(1)}, u32[]{:S(2)}, u32[]{:S(2)}) collective-permute-start(bf16[2,336,128]{2,1,0:T(8,128)(2,1)S(1)} %pad_maximum_fusion.8), channel_id=1, source_target_pairs={{0,4},{2,6},{4,0},{6,2},{1,5},{3,7},{5,1},{7,3},{8,12},{10,14},{12... | collective-permute-start | bytes 516104 | tf_op jit(solution)/shard_map/ppermute | solution.py:323
  22.8 5.5 %collective-permute-start.5 = (bf16[2,336,128]{2,1,0:T(8,128)(2,1)S(1)}, bf16[2,336,128]{2,1,0:T(8,128)(2,1)S(1)}, u32[]{:S(2)}, u32[]{:S(2)}) collective-permute-start(bf16[2,336,128]{2,1,0:T(8,128)(2,1)S(1)} %pad_maximum_fusion.7), channel_id=1, source_target_pairs={{0,2},{2,0},{4,6},{6,4},{1,3},{3,1},{5,7},{7,5},{8,10},{10,8},{12,... | collective-permute-start | bytes 516104 | tf_op jit(solution)/shard_map/ppermute | solution.py:323
  24.6 7.7 %collective-permute-start.10 = (bf16[512,128]{1,0:T(8,128)(2,1)S(1)}, bf16[512,128]{1,0:T(8,128)(2,1)S(1)}, u32[]{:S(2)}, u32[]{:S(2)}) collective-permute-start(bf16[512,128]{1,0:T(8,128)(2,1)S(1)} %bitcast.54), channel_id=1, source_target_pairs={{0,16},{8,24},{16,0},{24,8},{1,17},{9,25},{17,1},{25,9},{2,18},{10... | collective-permute-start | bytes 393224 | tf_op jit(solution)/shard_map/ppermute | solution.py:323
  26.5 6.5 %collective-permute-start.9 = (bf16[512,128]{1,0:T(8,128)(2,1)S(1)}, bf16[512,128]{1,0:T(8,128)(2,1)S(1)}, u32[]{:S(2)}, u32[]{:S(2)}) collective-permute-start(bf16[512,128]{1,0:T(8,128)(2,1)S(1)} %bitcast.55), channel_id=1, source_target_pairs={{0,8},{8,0},{16,24},{24,16},{1,9},{9,1},{17,25},{25,17},{2,10},{10... | collective-permute-start | bytes 393224 | tf_op jit(solution)/shard_map/ppermute | solution.py:323
  33.0 8.3 %collective-permute-start.12 = (bf16[4,336,128]{2,1,0:T(8,128)(2,1)S(1)}, bf16[4,336,128]{2,1,0:T(8,128)(2,1)S(1)}, u32[]{:S(2)}, u32[]{:S(2)}) collective-permute-start(bf16[4,336,128]{2,1,0:T(8,128)(2,1)S(1)} %pad_maximum_fusion.3), channel_id=1, source_target_pairs={{0,4},{2,6},{4,0},{6,2},{1,5},{3,7},{5,1},{7,3},{8,12},{10,14},{12... | collective-permute-start | bytes 1032200 | tf_op jit(solution)/shard_map/ppermute | solution.py:323
  34.5 8.1 %collective-permute-start.13 = (bf16[4,336,128]{2,1,0:T(8,128)(2,1)S(1)}, bf16[4,336,128]{2,1,0:T(8,128)(2,1)S(1)}, u32[]{:S(2)}, u32[]{:S(2)}) collective-permute-start(bf16[4,336,128]{2,1,0:T(8,128)(2,1)S(1)} %pad_maximum_fusion.4), channel_id=1, source_target_pairs={{0,2},{2,0},{4,6},{6,4},{1,3},{3,1},{5,7},{7,5},{8,10},{10,8},{12,... | collective-permute-start | bytes 1032200 | tf_op jit(solution)/shard_map/ppermute | solution.py:323
  35.1 7.7 %collective-permute-start.11 = (bf16[512,128]{1,0:T(8,128)(2,1)S(1)}, bf16[512,128]{1,0:T(8,128)(2,1)S(1)}, u32[]{:S(2)}, u32[]{:S(2)}) collective-permute-start(bf16[512,128]{1,0:T(8,128)(2,1)S(1)} %bitcast.56), channel_id=1, source_target_pairs={{0,24},{8,16},{16,8},{24,0},{1,25},{9,17},{17,9},{25,1},{2,26},{10... | collective-permute-start | bytes 393224 | tf_op jit(solution)/shard_map/ppermute | solution.py:323
  42.8 10.1 %collective-permute-start.16 = (bf16[16,336,128]{2,1,0:T(8,128)(2,1)S(1)}, bf16[16,336,128]{2,1,0:T(8,128)(2,1)S(1)}, u32[]{:S(2)}, u32[]{:S(2)}) collective-permute-start(bf16[16,336,128]{2,1,0:T(8,128)(2,1)S(1)} %pad_maximum_fusion.mine), channel_id=1, source_target_pairs={{0,1},{1,0},{2,3},{3,2},{4,5},{5,4},{6,7},{7,6},{8,9},{9,8},{10,11... | collective-permute-start | bytes 4128776 | tf_op jit(solution)/shard_map/ppermute | solution.py:323
  42.9 8.8 %collective-permute-start.15 = (bf16[2,512,128]{2,1,0:T(8,128)(2,1)S(1)}, bf16[2,512,128]{2,1,0:T(8,128)(2,1)S(1)}, u32[]{:S(2)}, u32[]{:S(2)}) collective-permute-start(bf16[2,512,128]{2,1,0:T(8,128)(2,1)S(1)} %pad_maximum_fusion.6), channel_id=1, source_target_pairs={{0,4},{2,6},{4,0},{6,2},{1,5},{3,7},{5,1},{7,3},{8,12},{10,14},{12... | collective-permute-start | bytes 786440 | tf_op jit(solution)/shard_map/ppermute | solution.py:323
  43.5 8.5 %collective-permute-start.14 = (bf16[2,512,128]{2,1,0:T(8,128)(2,1)S(1)}, bf16[2,512,128]{2,1,0:T(8,128)(2,1)S(1)}, u32[]{:S(2)}, u32[]{:S(2)}) collective-permute-start(bf16[2,512,128]{2,1,0:T(8,128)(2,1)S(1)} %pad_maximum_fusion.5), channel_id=1, source_target_pairs={{0,2},{2,0},{4,6},{6,4},{1,3},{3,1},{5,7},{7,5},{8,10},{10,8},{12,... | collective-permute-start | bytes 786440 | tf_op jit(solution)/shard_map/ppermute | solution.py:323
  52.9 18.8 %collective-permute-start.17 = (bf16[4,512,128]{2,1,0:T(8,128)(2,1)}, bf16[4,512,128]{2,1,0:T(8,128)(2,1)}, u32[]{:S(2)}, u32[]{:S(2)}) collective-permute-start(bf16[4,512,128]{2,1,0:T(8,128)(2,1)} %pad_maximum_fusion.1), channel_id=1, source_target_pairs={{0,4},{2,6},{4,0},{6,2},{1,5},{3,7},{5,1},{7,3},{8,12},{10,14},{12... | collective-permute-start | bytes 1572872 | tf_op jit(solution)/shard_map/ppermute | solution.py:323
  54.4 17.3 %collective-permute-start.18 = (bf16[4,512,128]{2,1,0:T(8,128)(2,1)S(1)}, bf16[4,512,128]{2,1,0:T(8,128)(2,1)}, u32[]{:S(2)}, u32[]{:S(2)}) collective-permute-start(bf16[4,512,128]{2,1,0:T(8,128)(2,1)S(1)} %pad_maximum_fusion.2), channel_id=1, source_target_pairs={{0,2},{2,0},{4,6},{6,4},{1,3},{3,1},{5,7},{7,5},{8,10},{10,8},{12,... | collective-permute-start | bytes 1572872 | tf_op jit(solution)/shard_map/ppermute | solution.py:323
  55.0 8.9 %copy-start.5 = (s32[3]{0:T(128)}, s32[3]{0:T(128)S(1)}, u32[]{:S(2)}) copy-start(s32[3]{0:T(128)S(1)} %pad_add_fusion.own) | copy-start | bytes 40
  56.2 7.8 %copy-start.11 = (bf16[8,512,128]{2,1,0:T(8,128)(2,1)}, bf16[8,512,128]{2,1,0:T(8,128)(2,1)S(1)}, u32[]{:S(2)}) copy-start(bf16[8,512,128]{2,1,0:T(8,128)(2,1)S(1)} %constant_dynamic-update-slice_fusion.rest_5_) | copy-start | bytes 3145732
  56.2 18.3 %collective-permute-start.19 = (bf16[8,512,128]{2,1,0:T(8,128)(2,1)S(1)}, bf16[8,512,128]{2,1,0:T(8,128)(2,1)S(1)}, u32[]{:S(2)}, u32[]{:S(2)}) collective-permute-start(bf16[8,512,128]{2,1,0:T(8,128)(2,1)S(1)} %constant_dynamic-update-slice_fusion.rest_5_), channel_id=1, source_target_pairs={{0,1},{1,0},{2,3},{3,2},{4,5},{5,4},{6,7},{7,6},{8,9},{9,8},{10,11... | collective-permute-start | bytes 3145736 | tf_op jit(solution)/shard_map/ppermute | solution.py:323
  64.0 2.1 %copy-start = (bf16[272,64,64]{2,1,0:T(8,128)(2,1)}, bf16[272,64,64]{2,1,0:T(8,128)(2,1)S(1)}, u32[]{:S(2)}) copy-start(bf16[272,64,64]{2,1,0:T(8,128)(2,1)S(1)} %get-tuple-element.66.rest_0_) | copy-start | bytes 6684676
  66.0 1.4 copy-start.1
  67.4 0.8 copy-start.2
  68.2 0.6 copy-start.3
  68.8 0.6 copy-start.4
  69.5 0.6 copy-start.6
  70.1 0.5 copy-start.7
  70.6 0.5 copy-start.8
  71.1 0.6 copy-start.9
  73.9 2.9 %copy-start.10 = (bf16[8,512,128]{2,1,0:T(8,128)(2,1)}, bf16[8,512,128]{2,1,0:T(8,128)(2,1)S(1)}, u32[]{:S(2)}) copy-start(bf16[8,512,128]{2,1,0:T(8,128)(2,1)S(1)} %constant_dynamic-update-slice_fusion.2.rest_6_) | copy-start | bytes 3145732
  73.9 2.8 %collective-permute-start.20 = (bf16[8,512,128]{2,1,0:T(8,128)(2,1)S(1)}, bf16[8,512,128]{2,1,0:T(8,128)(2,1)S(1)}, u32[]{:S(2)}, u32[]{:S(2)}) collective-permute-start(bf16[8,512,128]{2,1,0:T(8,128)(2,1)S(1)} %constant_dynamic-update-slice_fusion.2.rest_6_), channel_id=1, source_target_pairs={{0,1},{1,0},{2,3},{3,2},{4,5},{5,4},{6,7},{7,6},{8,9},{9,8},{10,11... | collective-permute-start | bytes 3145736 | tf_op jit(solution)/shard_map/ppermute | solution.py:323
  74.5 2.3 %copy-start.13 = (bf16[8,512,128]{2,1,0:T(8,128)(2,1)}, bf16[8,512,128]{2,1,0:T(8,128)(2,1)S(1)}, u32[]{:S(2)}) copy-start(bf16[8,512,128]{2,1,0:T(8,128)(2,1)S(1)} %collective-permute-done.19.rest_7_) | copy-start | bytes 3145732
  76.8 1.0 copy-start.14

commit v4 on v3

--- a/solution.py
+++ b/solution.py
@@ -11,7 +11,7 @@
 OFF_CAP = 8
 META = 16
 UNROLL = 16
-BATCH = 8
+BATCH = 4
 VMEM_LIMIT = 56 * 1024 * 1024
 
 NT = (((1,), (1,)), ((), ()))
@@ -94,21 +94,41 @@
     return copies
 
 
-def scatter_pair(pair, blocks, q, x):
-    k = x.shape[0]
-    if pair is not None:
-        pair[q] = x.astype(pair.dtype)
-    blocks[2 * q] = x[:, :k].astype(blocks.dtype)
-    blocks[2 * q + 1] = x[:, k:].astype(blocks.dtype)
-
-
-def add_products(n_group, blk, dims, from_list, source, to_list, total):
+def left_half(shape):
+    return lax.broadcasted_iota(jnp.int32, shape, len(shape) - 1) < 64
+
+
+def store_twice(pair, twice, q, x):
+    pair[q] = x.astype(pair.dtype)
+    turned, left = pltpu.roll(x, 64, 1), left_half(x.shape)
+    twice[2 * q] = jnp.where(left, x, turned).astype(twice.dtype)
+    twice[2 * q + 1] = jnp.where(left, turned, x).astype(twice.dtype)
+
+
+def gather_pair(q, first, second):
+    left = left_half(first.shape[1:])
+    apart = jnp.where(left, first[2 * q + 1], second[2 * q])
+    return jnp.where(left, first[2 * q], second[2 * q + 1]) + pltpu.roll(apart, 64, 1)
+
+
+def add_products(n_group, blk, dims, from_list, source, to_list, first, second):
+    left = left_half(source.shape[1:])
+
     def group(i, carry):
         for at in range(0, UNROLL, BATCH):
-            slots = [i * UNROLL + at + u for u in range(BATCH)]
-            prods = [dot(source[from_list[s]], blk[s], dims) for s in slots]
-            for s, prod in zip(slots, prods):
-                total[to_list[s]] = total[to_list[s]] + prod
+            pairs = [i * UNROLL + at + u for u in range(BATCH)]
+            prods = [
+                dot(
+                    jnp.where(left, source[from_list[2 * p]], source[from_list[2 * p + 1]]),
+                    blk[p],
+                    dims,
+                )
+                for p in pairs
+            ]
+            for p, prod in zip(pairs, prods):
+                a, b = to_list[2 * p], to_list[2 * p + 1]
+                first[a] = first[a] + prod
+                second[b] = second[b] + prod
         return carry
 
     lax.fori_loop(0, n_group, group, 0)
@@ -116,8 +136,8 @@
 
 def unpack(
     n_row, n_col, own, mine, other,
-    lv, lw, nums, place, blk, vs, rm, ic, wb,
-    ints, meta, sems, small, vb,
+    lv, lw, nums, place, blk, vs, vd, rm, ic,
+    ints, meta, sems, small,
 ):
     n_dev = n_row * n_col
     k = vs.shape[1]
@@ -142,10 +162,10 @@
             rows = small[d, meta_at : meta_at + META, :].astype(jnp.float32)
             rm[p] = jnp.broadcast_to(rows[0:1] + rows[1:2] + rows[2:3], (8, 128))
             ic[q] = jnp.broadcast_to(rows[3:4] + rows[4:5] + rows[5:6], (8, 128))
-            scatter_pair(vs, vb, q, small[d, vec_at : vec_at + k, :].astype(jnp.float32))
-            wb[2 * p] = jnp.zeros_like(wb[2 * p])
-            wb[2 * p + 1] = jnp.zeros_like(wb[2 * p + 1])
+            store_twice(vs, vd, q, small[d, vec_at : vec_at + k, :].astype(jnp.float32))
     to_scalars.wait()
+
+    lanes = lax.broadcasted_iota(jnp.int32, (half, 128), 1)
 
     def device(d, n):
         count = meta[d, 2 * OFF_CAP]
@@ -155,16 +175,23 @@
             lv[n + s] = c * cblk + meta[d, OFF_CAP + s]
             lw[n + s] = r * rblk + meta[d, s]
             x = small[d, s * half : (s + 1) * half, :].astype(jnp.float32)
-            blk[n + s] = jnp.concatenate([x[:, :k], x[:, k:]], axis=0).astype(jnp.bfloat16)
+            turned = pltpu.roll(x, 64, 1)
+            side = (n + s) % 2
+            here = (lanes // 64) == side
+            even = jnp.where(here, jnp.where(side == 0, x, turned), 0.0)
+            odd = jnp.where(here, jnp.where(side == 0, turned, x), 0.0)
+            at = pl.multiple_of(side * k, k)
+            both = jnp.concatenate([even, odd], axis=0).astype(jnp.bfloat16)
+            blk[(n + s) // 2, pl.ds(at, k), :] = both
         return n + count
 
     n_live = lax.fori_loop(0, n_dev, device, jnp.int32(0))
-    for u in range(UNROLL - 1):
+    for u in range(2 * UNROLL - 1):
         lv[n_live + u] = 0
         lw[n_live + u] = 0
-        blk[n_live + u] = jnp.zeros((k, k), jnp.bfloat16)
-    n_group = (n_live + UNROLL - 1) // UNROLL
-    nums[0] = n_group
+        at = pl.multiple_of((n_live + u) % 2 * k, k)
+        blk[(n_live + u) // 2, pl.ds(at, k), :] = jnp.zeros((k, 128), jnp.bfloat16)
+    nums[0] = (n_live + 2 * UNROLL - 1) // (2 * UNROLL)
 
     for r in range(n_row):
         h = jnp.int32(0)
@@ -174,13 +201,11 @@
         index = small[at_device(r, h), meta_at : meta_at + META, :].astype(jnp.float32)
         place[r : r + 1, :] = index[7:8] * float(rblk) + index[6:7]
 
-    add_products(n_group, blk, NT, lv, vb, lw, wb)
-
 
 def iterate(n_row, n_col, n_cap, total, own, lv, lw, nums, place, *rest):
-    sources, fulls, out = rest[:5], rest[5:9], rest[9]
-    sems, full, tmp, home, blk, vs, rm, ic, wb = rest[10:19]
-    vb, w, wt, wtb, y, yb, ph, linv = rest[19:]
+    sources, fulls, out = rest[:5], rest[5:11], rest[11]
+    sems, full, tmp, home, blk, vs, vd, rm, ic = rest[12:21]
+    w, w1, w2, wt, wd, y, y1, y2, ph, linv = rest[21:]
     n_dev = n_row * n_col
     k = vs.shape[1]
     half = k // 2
@@ -194,7 +219,7 @@
     for ref in fulls:
         pairs.append((ref, full.at[pl.ds(at, ref.shape[0])]))
         at += ref.shape[0]
-    copies = copy_in(pairs + list(zip(sources, (blk, vs, rm, ic, wb))), sems)
+    copies = copy_in(pairs + list(zip(sources, (blk, vs, vd, rm, ic))), sems)
     for copy in copies[: len(fulls)]:
         copy.wait()
     n_group = nums[0]
@@ -206,7 +231,7 @@
         want = lax.broadcasted_iota(jnp.int32, (cblk * rblk, n_cap), 0).astype(jnp.float32)
         select = jnp.where(want == place[r : r + 1, :], 1.0, 0.0).astype(jnp.bfloat16)
 
-        parts = [at_device(r, 2 * i + j) for j in range(2) for i in range(n_col // 2)]
+        parts = [at_device(r, c) for c in range(n_col)]
 
         def build(m, carry, parts=parts, select=select):
             at = pl.multiple_of(m * part, part)
@@ -240,7 +265,7 @@
             for q in range(ref.shape[0]):
                 ref[q] = jnp.zeros_like(ref[q])
 
-    clear([y, yb])
+    clear([y, y1, y2, w1, w2])
     for copy in copies[len(fulls) :]:
         copy.wait()
 
@@ -255,7 +280,7 @@
                 current = dot(turn, jnp.concatenate([hi, lo, hi], axis=0))
                 for d in range(4):
                     x = current[:, d * 128 : (d + 1) * 128] * ic[q + d, 0:1, :]
-                    scatter_pair(vs, vb, q + d, x)
+                    store_twice(vs, vd, q + d, x)
 
         for r in range(n_row):
             base = homes[r] * cpairs
@@ -265,13 +290,10 @@
                 w[r * rpairs + p] = prod[:, :128]
                 w[r * rpairs + p + 1] = prod[:, 128:]
 
-        @pl.when(it > 0)
-        def _():
-            add_products(n_group, blk, NT, lv, vb, lw, wb)
-
+        add_products(n_group, blk, NT, lv, vd, lw, w1, w2)
         for p in range(n_dev):
-            x = w[p] + jnp.concatenate([wb[2 * p], wb[2 * p + 1]], axis=1)
-            scatter_pair(wt, wtb, p, x * rm[p, 0:1, :])
+            x = w[p] + gather_pair(p, w1, w2)
+            store_twice(wt, wd, p, x * rm[p, 0:1, :])
 
         for r in range(n_row):
             base = homes[r] * cpairs
@@ -283,13 +305,13 @@
                 y[base + u] = y[base + u] + prod[:, :128]
                 y[base + u + 1] = y[base + u + 1] + prod[:, 128:]
 
-        add_products(n_group, blk, NN, lw, wtb, lv, yb)
+        add_products(n_group, blk, NN, lw, wd, lv, y1, y2)
 
         both = jnp.zeros((2 * k, k), jnp.float32)
         for q in range(0, n_dev, 4):
             his, los = [], []
             for d in range(q, q + 4):
-                x = y[d] + jnp.concatenate([yb[2 * d], yb[2 * d + 1]], axis=1)
+                x = y[d] + gather_pair(d, y1, y2)
                 hi, lo = split2(x * ic[d, 0:1, :])
                 ph[d, :k, :] = hi
                 ph[d, k:, :] = lo
@@ -299,7 +321,7 @@
             lo = jnp.concatenate(los, axis=1)
             both = both + dot(jnp.concatenate([hi, lo], axis=0), hi, NT)
         gram = (both[:k] + (both[k:] + both[k:].T)) / total
-        clear([y, yb, wb])
+        clear([y, y1, y2, w1, w2])
         linv[...] = inverse_factor(gram)
         return carry
 
@@ -338,20 +360,6 @@
 def along_other_chip_axis(x):
     near, far = x
     return [swap(near, "chip", 2), swap(far, "chip", 1)]
-
-
-def full_part(tile, has_full, n_chip, part, chip, core):
-    tile = tile.reshape(2, n_chip, part, tile.shape[1])
-    none = jnp.zeros(tile.shape[1:], tile.dtype)
-    kept, sent = (
-        jnp.where(has_full, lax.dynamic_index_in_dim(tile, i, 0, False), none)
-        for i in (core, 1 - core)
-    )
-    both = kept + swap(sent, "core", 1)
-    mine = lax.dynamic_index_in_dim(both, chip, 0, False)
-    for s in range(1, n_chip):
-        mine = mine + swap(lax.dynamic_index_in_dim(both, chip ^ s, 0, False), "chip", s)
-    return mine
 
 
 def whole_on_each(n_row, n_col, blocks, block_row, block_col, counts, vectors, row_mass, col_mass):
@@ -380,7 +388,9 @@
     meta = split3(mass) + split3(inv_col.reshape(own * bsize)) + meta
     meta = jnp.stack(meta + [jnp.zeros(128, bf16)] * (META - len(meta)))
     small = jnp.concatenate([off, scaled, meta], axis=0)
-    home = full_part(tile, has_full, n_col // 2, part, chip, core)
+    sent = jnp.where(has_full, tile, jnp.zeros_like(tile)).reshape(n_col, part, bsize * bsize)
+    got = lax.all_to_all(sent, ("chip", "core"), split_axis=0, concat_axis=0)
+    home = jnp.sum(got.astype(jnp.float32), axis=0).astype(bf16)
     home = home.reshape(part, half, 128).transpose(1, 0, 2).reshape(half * part, 128)
 
     together = lax.optimization_barrier
@@ -398,14 +408,14 @@
     where = jnp.stack([row, chip, core]).astype(jnp.int32)
 
     height, width = 2 * n_col * bsize, 2 * n_row * bsize
-    slots = n_dev * OFF_CAP + UNROLL
+    slots = n_dev * OFF_CAP + 2 * UNROLL
     f32, i32 = jnp.float32, jnp.int32
-    pair, block, mass = (n_dev, k, 128), (2 * n_dev, k, bsize), (n_dev, 8, 128)
+    pair, twice, mass = (n_dev, k, 128), (2 * n_dev, k, 128), (n_dev, 8, 128)
     smem, anywhere = (pl.BlockSpec(memory_space=m) for m in (pltpu.SMEM, pl.ANY))
     vmem = pl.BlockSpec(memory_space=pltpu.VMEM)
     lists = [((slots,), i32), ((slots,), i32), ((1 + n_row,), i32)]
     arrays = [
-        ((8, 128), f32), ((slots, bsize, bsize), bf16), (pair, bf16), (mass, f32), (mass, f32), (block, f32),
+        ((8, 128), f32), ((slots // 2, 128, 128), bf16), (pair, bf16), (twice, bf16), (mass, f32), (mass, f32),
     ]
     unpacked = pl.pallas_call(
         functools.partial(unpack, n_row, n_col),
@@ -417,7 +427,6 @@
             pltpu.SMEM((n_dev, 128), i32),
             pltpu.SemaphoreType.DMA((3,)),
             pltpu.VMEM((n_dev,) + small.shape, bf16),
-            pltpu.VMEM(block, bf16),
         ],
         compiler_params=pltpu.CompilerParams(vmem_limit_bytes=VMEM_LIMIT // 2),
         cost_estimate=pl.CostEstimate(
@@ -425,9 +434,9 @@
         ),
         name="unpack",
     )(where, smalls, others)
-    last, unpacked = together((last, unpacked))
-    last = jnp.concatenate(last)
-    fulls = [homes, last, other_homes, swap(last, "core", 1)]
+    last, nums = together((last, unpacked[2]))
+    unpacked = (*unpacked[:2], nums, *unpacked[3:])
+    fulls = [homes, *last, other_homes, *(swap(v, "core", 1) for v in last)]
     result = pl.pallas_call(
         functools.partial(iterate, n_row, n_col, n_cap, float(n_dev * own * bsize)),
         out_shape=jax.ShapeDtypeStruct((own, k, bsize), f32),
@@ -442,8 +451,8 @@
             *[
                 pltpu.VMEM(*v)
                 for v in [
-                    (block, bf16), (pair, f32), (pair, bf16), (block, bf16), (pair, f32), (block, f32),
-                    ((n_dev, 2 * k, 128), bf16), ((k, k), f32),
+                    (pair, f32), (twice, f32), (twice, f32), (pair, bf16), (twice, bf16),
+                    (pair, f32), (twice, f32), (twice, f32), ((n_dev, 2 * k, 128), bf16), ((k, k), f32),
                 ]
             ],
         ],

time: 144 us -> 143 us (level); the launches traced: 143 us -> 141 us
  local copies, waits for them, and re-layouts: 17.4 us -> 13.4 us
  waiting for transfers between devices: 24.1 us -> 27.1 us
    all_to_all x0 -> x1, starting transfers between devices: none -> 5.31 us  [whole_on_each(): got = lax.all_to_all(sent, ('chip', 'core'), split_axis=0, concat_axis=0)]
    ppermute x21 -> x18, starting transfers between devices: 25.1 us -> 21.1 us  [swap(): return lax.ppermute(x, axis, [(i, i ^ distance) for i in range(size)])]
    ppermute x21 -> x18, waiting for transfers between devices: 24.1 us -> 26 us  [swap(): return lax.ppermute(x, axis, [(i, i ^ distance) for i in range(size)])]
    concatenate x1, local copies, waits for them, and re-layouts: 0.07 us -> 1.95 us  [whole_on_each(): homes = jnp.concatenate(homes)]
    unnamed x33 -> x36, local copies, waits for them, and re-layouts: 10.9 us -> 9.12 us
  transfers between devices with their start and end apart: 21 -> 19, of which waited for: 10 -> 11; matrix products, arithmetic and copies ran while one was open for 7% -> 4% of each run, Pallas kernels for 5% -> 5%
where the time goes in v4:
time: 143 us; the launch traced here: 141 us
  Pallas kernels  70.4 us (49%)
  waiting for transfers between devices  27.1 us (19%)
  starting transfers between devices  26.4 us (18%)
  local copies, waits for them, and re-layouts  13.4 us (9%)
  other arithmetic  2.64 us (2%)
    pallas_call x1, Pallas kernels, whole_on_each(): pl.pallas_call(functools.partial(iterate, n_row, n_col, n_cap, float(n_de...  63.9 us
    ppermute x18, waiting for transfers between devices, swap(): return lax.ppermute(x, axis, [(i, i ^ distance) for i in range(size)])  26 us
    ppermute x18, starting transfers between devices, swap(): return lax.ppermute(x, axis, [(i, i ^ distance) for i in range(size)])  21.1 us
    unnamed x36, local copies, waits for them, and re-layouts  9.12 us
    pallas_call x1, Pallas kernels, whole_on_each(): pl.pallas_call(functools.partial(unpack, n_row, n_col), out_shape=[jax.Sh...  6.41 us
    all_to_all x1, starting transfers between devices, whole_on_each(): got = lax.all_to_all(sent, ('chip', 'core'), split_axis=0, concat_axis=0)  5.31 us
  transfers between devices with their start and end apart: 19, of which 11 were waited for; matrix products, arithmetic and copies ran while one was open for 4% of the time, Pallas kernels for 5%

profile of v4, /device:TPU:0, one launch (start us, length us, event | category | flops | bytes accessed | tf_op | source)
XLA Modules:
  0.0 140.9 jit_solution(17704460507363701394)
XLA Ops:
  0.7 1.1 broadcast_select_fusion
  1.8 5.3 %all-to-all-start = ((bf16[8,16,4096]{2,1,0:T(8,128)(2,1)}), bf16[8,16,4096]{2,1,0:T(8,128)(2,1)S(1)}, u32[]{:S(2)}, u32[]{:S(2)}) async-start(bf16[8,16,4096]{2,1,0:T(8,128)(2,1)} %bitcast.4), calls=%async_computation | async-start | bytes 2097152 | tf_op jit(solution)/shard_map/all_to_all | solution.py:392
  7.1 0.1 reshape.205
  7.5 0.1 reshape.207
  8.0 0.1 concatenate.51
  8.1 4.3 %collective-permute-start.3 = (bf16[336,128]{1,0:T(8,128)(2,1)S(1)}, bf16[336,128]{1,0:T(8,128)(2,1)S(1)}, u32[]{:S(2)}, u32[]{:S(2)}) collective-permute-start(bf16[336,128]{1,0:T(8,128)(2,1)S(1)} %concatenate.51), channel_id=1, source_target_pairs={{0,24},{8,16},{16,8},{24,0},{1,25},{9,17},{17,9},{25,1},{2,26},{10... | collective-permute-start | bytes 258056 | tf_op jit(solution)/shard_map/ppermute | solution.py:345
  12.4 0.6 collective-permute-start
  13.0 2.8 %collective-permute-done.3 = bf16[336,128]{1,0:T(8,128)(2,1)S(1)} collective-permute-done((bf16[336,128]{1,0:T(8,128)(2,1)S(1)}, bf16[336,128]{1,0:T(8,128)(2,1)S(1)}, u32[]{:S(2)}, u32[]{:S(2)}) %collective-permute-start.3) | collective-permute-done | bytes 86048 | tf_op jit(solution)/shard_map/ppermute | solution.py:345
  15.9 3.7 %collective-permute-done.2 = bf16[336,128]{1,0:T(8,128)(2,1)S(1)} collective-permute-done((bf16[336,128]{1,0:T(8,128)(2,1)S(1)}, bf16[336,128]{1,0:T(8,128)(2,1)S(1)}, u32[]{:S(2)}, u32[]{:S(2)}) %collective-permute-start.2) | collective-permute-done | bytes 86048 | tf_op jit(solution)/shard_map/ppermute | solution.py:345
  19.6 1.8 %collective-permute-start.4 = (bf16[2,336,128]{2,1,0:T(8,128)(2,1)S(1)}, bf16[2,336,128]{2,1,0:T(8,128)(2,1)S(1)}, u32[]{:S(2)}, u32[]{:S(2)}) collective-permute-start(bf16[2,336,128]{2,1,0:T(8,128)(2,1)S(1)} %pad_maximum_fusion.8), channel_id=1, source_target_pairs={{0,4},{2,6},{4,0},{6,2},{1,5},{3,7},{5,1},{7,3},{8,12},{10,14},{12... | collective-permute-start | bytes 516104 | tf_op jit(solution)/shard_map/ppermute | solution.py:345
  21.4 1.1 all-to-all-done
  22.5 0.1 reduce_sum.12
  22.8 0.6 collective-permute-start.1
  23.3 1.6 %collective-permute-start.5 = (bf16[512,128]{1,0:T(8,128)(2,1)S(1)}, bf16[512,128]{1,0:T(8,128)(2,1)S(1)}, u32[]{:S(2)}, u32[]{:S(2)}) collective-permute-start(bf16[512,128]{1,0:T(8,128)(2,1)S(1)} %bitcast.33), channel_id=1, source_target_pairs={{0,8},{8,0},{16,24},{24,16},{1,9},{9,1},{17,25},{25,17},{2,10},{10... | collective-permute-start | bytes 393224 | tf_op jit(solution)/shard_map/ppermute | solution.py:345
  25.0 3.2 %collective-permute-start.6 = (bf16[512,128]{1,0:T(8,128)(2,1)S(1)}, bf16[512,128]{1,0:T(8,128)(2,1)S(1)}, u32[]{:S(2)}, u32[]{:S(2)}) collective-permute-start(bf16[512,128]{1,0:T(8,128)(2,1)S(1)} %bitcast.34), channel_id=1, source_target_pairs={{0,16},{8,24},{16,0},{24,8},{1,17},{9,25},{17,1},{25,9},{2,18},{10... | collective-permute-start | bytes 393224 | tf_op jit(solution)/shard_map/ppermute | solution.py:345
  28.3 0.2 collective-permute-done.5
  28.5 5.6 %collective-permute-done.6 = bf16[512,128]{1,0:T(8,128)(2,1)S(1)} collective-permute-done((bf16[512,128]{1,0:T(8,128)(2,1)S(1)}, bf16[512,128]{1,0:T(8,128)(2,1)S(1)}, u32[]{:S(2)}, u32[]{:S(2)}) %collective-permute-start.6) | collective-permute-done | bytes 131104 | tf_op jit(solution)/shard_map/ppermute | solution.py:345
  34.1 0.4 collective-permute-start.9
  34.5 0.4 collective-permute-start.8
  34.9 2.8 %collective-permute-start.7 = (bf16[512,128]{1,0:T(8,128)(2,1)S(1)}, bf16[512,128]{1,0:T(8,128)(2,1)S(1)}, u32[]{:S(2)}, u32[]{:S(2)}) collective-permute-start(bf16[512,128]{1,0:T(8,128)(2,1)S(1)} %bitcast.35), channel_id=1, source_target_pairs={{0,24},{8,16},{16,8},{24,0},{1,25},{9,17},{17,9},{25,1},{2,26},{10... | collective-permute-start | bytes 393224 | tf_op jit(solution)/shard_map/ppermute | solution.py:345
  37.7 3.7 %collective-permute-done.9 = bf16[4,336,128]{2,1,0:T(8,128)(2,1)S(1)} collective-permute-done((bf16[4,336,128]{2,1,0:T(8,128)(2,1)S(1)}, bf16[4,336,128]{2,1,0:T(8,128)(2,1)S(1)}, u32[]{:S(2)}, u32[]{:S(2)}) %collective-permute-start.9) | collective-permute-done | bytes 344096 | tf_op jit(solution)/shard_map/ppermute | solution.py:345
  41.4 0.4 collective-permute-done.8
  41.8 0.2 pad_maximum_fusion.mine
  42.1 1.7 %collective-permute-start.10 = (bf16[2,512,128]{2,1,0:T(8,128)(2,1)S(1)}, bf16[2,512,128]{2,1,0:T(8,128)(2,1)S(1)}, u32[]{:S(2)}, u32[]{:S(2)}) collective-permute-start(bf16[2,512,128]{2,1,0:T(8,128)(2,1)S(1)} %pad_maximum_fusion.5), channel_id=1, source_target_pairs={{0,2},{2,0},{4,6},{6,4},{1,3},{3,1},{5,7},{7,5},{8,10},{10,8},{12,... | collective-permute-start | bytes 786440 | tf_op jit(solution)/shard_map/ppermute | solution.py:345
  43.8 1.3 collective-permute-start.11
  45.2 5.7 %collective-permute-done.10 = bf16[2,512,128]{2,1,0:T(8,128)(2,1)S(1)} collective-permute-done((bf16[2,512,128]{2,1,0:T(8,128)(2,1)S(1)}, bf16[2,512,128]{2,1,0:T(8,128)(2,1)S(1)}, u32[]{:S(2)}, u32[]{:S(2)}) %collective-permute-start.10) | collective-permute-done | bytes 262176 | tf_op jit(solution)/shard_map/ppermute | solution.py:345
  50.9 1.4 collective-permute-done.11
  52.3 0.9 pad_maximum_fusion.2
  53.2 1.3 collective-permute-start.13
  54.4 0.8 constant_dynamic-update-slice_fusion.1
  55.3 0.4 collective-permute-start.14
  55.7 1.9 %constant_dynamic-update-slice_fusion.rest_5_ = bf16[8,512,128]{2,1,0:T(8,128)(2,1)} fusion(bf16[8,512,128]{2,1,0:T(8,128)(2,1)} %constant_dynamic-update-slice_fusion.1, bf16[4,512,128]{2,1,0:T(8,128)(2,1)} %pad_maximum_fusion.2), kind=kLoop, calls=%fused_computation.12 | loop fusion | bytes 1048576 | tf_op jit(solution)/shard_map/concatenate | solution.py:405
  57.7 6.4 %unpack.1 = (s32[288]{0:T(512)S(1)}, s32[288]{0:T(512)S(1)}, s32[5]{0:T(128)S(1)}, f32[8,128]{1,0:T(8,128)S(1)}, bf16[144,128,128]{2,1,0:T(8,128)(2,1)S(1)}, /*i...) custom-call(s32[3]{0:T(128)S(1)} %pad_add_fusion.own, ...), custom_call_target="tpu_custom_call" | custom-call | flops 150994944 | bytes 5505024 | tf_op jit(solution)/shard_map/unpack/pallas_call | solution.py:420
  64.2 2.1 %copy-done = bf16[144,128,128]{2,1,0:T(8,128)(2,1)} copy-done((bf16[144,128,128]{2,1,0:T(8,128)(2,1)}, bf16[144,128,128]{2,1,0:T(8,128)(2,1)S(1)}, u32[]{:S(2)}) %copy-start) | copy-done | bytes 4718616
  66.3 1.0 copy-done.1
  67.3 0.8 copy-done.2
  68.1 0.7 copy-done.3
  68.7 0.6 copy-done.4
  69.4 0.6 copy-done.6
  70.0 0.5 copy-done.7
  70.5 0.5 copy-done.8
  71.0 0.6 copy-done.9
  71.6 0.5 collective-permute-start.16
  72.2 1.7 %collective-permute-done.16.rest_9_ = bf16[4,512,128]{2,1,0:T(8,128)(2,1)S(1)} collective-permute-done((bf16[4,512,128]{2,1,0:T(8,128)(2,1)}, bf16[4,512,128]{2,1,0:T(8,128)(2,1)S(1)}, u32[]{:S(2)}, u32[]{:S(2)}) %collective-permute-start.16) | collective-permute-done | bytes 524320 | tf_op jit(solution)/shard_map/ppermute | solution.py:345
  73.9 0.7 collective-permute-done.17.rest_10_
  74.7 0.8 copy-done.11
  75.4 63.9 %iterate.1 = f32[2,64,64]{2,1,0:T(8,128)} custom-call(s32[3]{0:T(128)} %copy-done.5, s32[288]{0:T(512)} %copy-done.7, s32[288]{0:T(512)} %copy-done.8, s32[5]{0:T(128)} %copy-done.9, f32[8,128]{1,0:T(8,128)} %copy-done.6, bf16[144,128,128]{2,1,0:T(8,128)(2,1)} %copy-done, bf16[32,64,128]{2,1,0:T(8,128)(2,1)} %copy-done.2, bf16[64,64,128]{2,1,0:T(8,128)(2,1)} %copy-done.1, ...), custom_call_target="tpu_custom_call" | custom-call | tf_op jit(solution)/shard_map/iterate/pallas_call | solution.py:440
  139.4 1.5 %reshape.210 = f32[2,4096]{1,0:T(2,128)} reshape(f32[2,64,64]{2,1,0:T(8,128)} %iterate.1) | data formatting | bytes 65536 | tf_op jit(solution)/shard_map/reshape | solution.py:462
  (65 shorter events, 1.2 us)
Async XLA Ops:
  1.7 5.4 %slice-start = ((bf16[1,1,128,4096]{3,2,1,0:T(8,128)(2,1)}), bf16[1,1,8,4096]{3,2,1,0:T(8,128)(2,1)S(1)}, s32[]{:S(2)}) async-start(bf16[1,1,128,4096]{3,2,1,0:T(8,128)(2,1)} %param.7), calls=%async_computation.1 | async-start | bytes 131072 | tf_op jit(solution)/shard_map/slice | solution.py:378
  1.7 5.4 %copy-start.12 = (f32[2,4096]{1,0:T(2,128)S(1)}, f32[2,4096]{1,0:T(2,128)}, u32[]{:S(2)}) copy-start(f32[2,4096]{1,0:T(2,128)} %param.11) | copy-start | bytes 98308
  1.7 5.5 %copy-start.14 = (f32[2,64]{1,0:T(2,128)S(1)}, f32[2,64]{1,0:T(2,128)}, u32[]{:S(2)}) copy-start(f32[2,64]{1,0:T(2,128)} %param.13) | copy-start | bytes 1540
  1.7 5.8 %copy-start.13 = (f32[2,64]{1,0:T(2,128)S(1)}, f32[2,64]{1,0:T(2,128)}, u32[]{:S(2)}) copy-start(f32[2,64]{1,0:T(2,128)} %param.12) | copy-start | bytes 1540
  1.7 6.0 %copy-start.15 = (s32[1,1,128]{2,1,0:T(1,128)S(1)}, s32[1,1,128]{2,1,0:T(1,128)}, u32[]{:S(2)}) copy-start(s32[1,1,128]{2,1,0:T(1,128)} %param.8) | copy-start | bytes 1540
  1.7 6.0 %copy-start.16 = (s32[1,1,128]{2,1,0:T(1,128)S(1)}, s32[1,1,128]{2,1,0:T(1,128)}, u32[]{:S(2)}) copy-start(s32[1,1,128]{2,1,0:T(1,128)} %param.9) | copy-start | bytes 1540
  1.8 20.8 %all-to-all-start = ((bf16[8,16,4096]{2,1,0:T(8,128)(2,1)}), bf16[8,16,4096]{2,1,0:T(8,128)(2,1)S(1)}, u32[]{:S(2)}, u32[]{:S(2)}) async-start(bf16[8,16,4096]{2,1,0:T(8,128)(2,1)} %bitcast.4), calls=%async_computation | async-start | bytes 2097152 | tf_op jit(solution)/shard_map/all_to_all | solution.py:392
  8.1 7.8 %collective-permute-start.3 = (bf16[336,128]{1,0:T(8,128)(2,1)S(1)}, bf16[336,128]{1,0:T(8,128)(2,1)S(1)}, u32[]{:S(2)}, u32[]{:S(2)}) collective-permute-start(bf16[336,128]{1,0:T(8,128)(2,1)S(1)} %concatenate.51), channel_id=1, source_target_pairs={{0,24},{8,16},{16,8},{24,0},{1,25},{9,17},{17,9},{25,1},{2,26},{10... | collective-permute-start | bytes 258056 | tf_op jit(solution)/shard_map/ppermute | solution.py:345
  12.4 7.2 %collective-permute-start.2 = (bf16[336,128]{1,0:T(8,128)(2,1)S(1)}, bf16[336,128]{1,0:T(8,128)(2,1)S(1)}, u32[]{:S(2)}, u32[]{:S(2)}) collective-permute-start(bf16[336,128]{1,0:T(8,128)(2,1)S(1)} %concatenate.51), channel_id=1, source_target_pairs={{0,16},{8,24},{16,0},{24,8},{1,17},{9,25},{17,1},{25,9},{2,18},{10... | collective-permute-start | bytes 258056 | tf_op jit(solution)/shard_map/ppermute | solution.py:345
  12.4 10.4 %collective-permute-start = (bf16[336,128]{1,0:T(8,128)(2,1)S(1)}, bf16[336,128]{1,0:T(8,128)(2,1)S(1)}, u32[]{:S(2)}, u32[]{:S(2)}) collective-permute-start(bf16[336,128]{1,0:T(8,128)(2,1)S(1)} %concatenate.51), channel_id=1, source_target_pairs={{0,8},{8,0},{16,24},{24,16},{1,9},{9,1},{17,25},{25,17},{2,10},{10... | collective-permute-start | bytes 258056 | tf_op jit(solution)/shard_map/ppermute | solution.py:345
  19.6 8.6 %collective-permute-start.4 = (bf16[2,336,128]{2,1,0:T(8,128)(2,1)S(1)}, bf16[2,336,128]{2,1,0:T(8,128)(2,1)S(1)}, u32[]{:S(2)}, u32[]{:S(2)}) collective-permute-start(bf16[2,336,128]{2,1,0:T(8,128)(2,1)S(1)} %pad_maximum_fusion.8), channel_id=1, source_target_pairs={{0,4},{2,6},{4,0},{6,2},{1,5},{3,7},{5,1},{7,3},{8,12},{10,14},{12... | collective-permute-start | bytes 516104 | tf_op jit(solution)/shard_map/ppermute | solution.py:345
  22.8 5.5 %collective-permute-start.1 = (bf16[2,336,128]{2,1,0:T(8,128)(2,1)S(1)}, bf16[2,336,128]{2,1,0:T(8,128)(2,1)S(1)}, u32[]{:S(2)}, u32[]{:S(2)}) collective-permute-start(bf16[2,336,128]{2,1,0:T(8,128)(2,1)S(1)} %pad_maximum_fusion.7), channel_id=1, source_target_pairs={{0,2},{2,0},{4,6},{6,4},{1,3},{3,1},{5,7},{7,5},{8,10},{10,8},{12,... | collective-permute-start | bytes 516104 | tf_op jit(solution)/shard_map/ppermute | solution.py:345
  23.3 5.2 %collective-permute-start.5 = (bf16[512,128]{1,0:T(8,128)(2,1)S(1)}, bf16[512,128]{1,0:T(8,128)(2,1)S(1)}, u32[]{:S(2)}, u32[]{:S(2)}) collective-permute-start(bf16[512,128]{1,0:T(8,128)(2,1)S(1)} %bitcast.33), channel_id=1, source_target_pairs={{0,8},{8,0},{16,24},{24,16},{1,9},{9,1},{17,25},{25,17},{2,10},{10... | collective-permute-start | bytes 393224 | tf_op jit(solution)/shard_map/ppermute | solution.py:345
  25.0 9.2 %collective-permute-start.6 = (bf16[512,128]{1,0:T(8,128)(2,1)S(1)}, bf16[512,128]{1,0:T(8,128)(2,1)S(1)}, u32[]{:S(2)}, u32[]{:S(2)}) collective-permute-start(bf16[512,128]{1,0:T(8,128)(2,1)S(1)} %bitcast.34), channel_id=1, source_target_pairs={{0,16},{8,24},{16,0},{24,8},{1,17},{9,25},{17,1},{25,9},{2,18},{10... | collective-permute-start | bytes 393224 | tf_op jit(solution)/shard_map/ppermute | solution.py:345
  34.1 7.2 %collective-permute-start.9 = (bf16[4,336,128]{2,1,0:T(8,128)(2,1)S(1)}, bf16[4,336,128]{2,1,0:T(8,128)(2,1)S(1)}, u32[]{:S(2)}, u32[]{:S(2)}) collective-permute-start(bf16[4,336,128]{2,1,0:T(8,128)(2,1)S(1)} %pad_maximum_fusion.4), channel_id=1, source_target_pairs={{0,2},{2,0},{4,6},{6,4},{1,3},{3,1},{5,7},{7,5},{8,10},{10,8},{12,... | collective-permute-start | bytes 1032200 | tf_op jit(solution)/shard_map/ppermute | solution.py:345
  34.5 7.2 %collective-permute-start.8 = (bf16[4,336,128]{2,1,0:T(8,128)(2,1)S(1)}, bf16[4,336,128]{2,1,0:T(8,128)(2,1)S(1)}, u32[]{:S(2)}, u32[]{:S(2)}) collective-permute-start(bf16[4,336,128]{2,1,0:T(8,128)(2,1)S(1)} %pad_maximum_fusion.3), channel_id=1, source_target_pairs={{0,4},{2,6},{4,0},{6,2},{1,5},{3,7},{5,1},{7,3},{8,12},{10,14},{12... | collective-permute-start | bytes 1032200 | tf_op jit(solution)/shard_map/ppermute | solution.py:345
  34.9 7.1 %collective-permute-start.7 = (bf16[512,128]{1,0:T(8,128)(2,1)S(1)}, bf16[512,128]{1,0:T(8,128)(2,1)S(1)}, u32[]{:S(2)}, u32[]{:S(2)}) collective-permute-start(bf16[512,128]{1,0:T(8,128)(2,1)S(1)} %bitcast.35), channel_id=1, source_target_pairs={{0,24},{8,16},{16,8},{24,0},{1,25},{9,17},{17,9},{25,1},{2,26},{10... | collective-permute-start | bytes 393224 | tf_op jit(solution)/shard_map/ppermute | solution.py:345
  42.0 11.2 %collective-permute-start.12 = (bf16[16,336,128]{2,1,0:T(8,128)(2,1)S(1)}, bf16[16,336,128]{2,1,0:T(8,128)(2,1)S(1)}, u32[]{:S(2)}, u32[]{:S(2)}) collective-permute-start(bf16[16,336,128]{2,1,0:T(8,128)(2,1)S(1)} %pad_maximum_fusion.mine), channel_id=1, source_target_pairs={{0,1},{1,0},{2,3},{3,2},{4,5},{5,4},{6,7},{7,6},{8,9},{9,8},{10,11... | collective-permute-start | bytes 4128776 | tf_op jit(solution)/shard_map/ppermute | solution.py:345
  42.1 8.8 %collective-permute-start.10 = (bf16[2,512,128]{2,1,0:T(8,128)(2,1)S(1)}, bf16[2,512,128]{2,1,0:T(8,128)(2,1)S(1)}, u32[]{:S(2)}, u32[]{:S(2)}) collective-permute-start(bf16[2,512,128]{2,1,0:T(8,128)(2,1)S(1)} %pad_maximum_fusion.5), channel_id=1, source_target_pairs={{0,2},{2,0},{4,6},{6,4},{1,3},{3,1},{5,7},{7,5},{8,10},{10,8},{12,... | collective-permute-start | bytes 786440 | tf_op jit(solution)/shard_map/ppermute | solution.py:345
  43.8 8.5 %collective-permute-start.11 = (bf16[2,512,128]{2,1,0:T(8,128)(2,1)S(1)}, bf16[2,512,128]{2,1,0:T(8,128)(2,1)S(1)}, u32[]{:S(2)}, u32[]{:S(2)}) collective-permute-start(bf16[2,512,128]{2,1,0:T(8,128)(2,1)S(1)} %pad_maximum_fusion.6), channel_id=1, source_target_pairs={{0,4},{2,6},{4,0},{6,2},{1,5},{3,7},{5,1},{7,3},{8,12},{10,14},{12... | collective-permute-start | bytes 786440 | tf_op jit(solution)/shard_map/ppermute | solution.py:345
  53.2 18.4 %collective-permute-start.13 = (bf16[4,512,128]{2,1,0:T(8,128)(2,1)S(1)}, bf16[4,512,128]{2,1,0:T(8,128)(2,1)}, u32[]{:S(2)}, u32[]{:S(2)}) collective-permute-start(bf16[4,512,128]{2,1,0:T(8,128)(2,1)S(1)} %pad_maximum_fusion.1), channel_id=1, source_target_pairs={{0,4},{2,6},{4,0},{6,2},{1,5},{3,7},{5,1},{7,3},{8,12},{10,14},{12... | collective-permute-start | bytes 1572872 | tf_op jit(solution)/shard_map/ppermute | solution.py:345
  55.3 16.3 %collective-permute-start.14 = (bf16[4,512,128]{2,1,0:T(8,128)(2,1)}, bf16[4,512,128]{2,1,0:T(8,128)(2,1)}, u32[]{:S(2)}, u32[]{:S(2)}) collective-permute-start(bf16[4,512,128]{2,1,0:T(8,128)(2,1)} %pad_maximum_fusion.2), channel_id=1, source_target_pairs={{0,2},{2,0},{4,6},{6,4},{1,3},{3,1},{5,7},{7,5},{8,10},{10,8},{12,... | collective-permute-start | bytes 1572872 | tf_op jit(solution)/shard_map/ppermute | solution.py:345
  57.6 14.6 %collective-permute-start.15 = (bf16[8,512,128]{2,1,0:T(8,128)(2,1)}, bf16[8,512,128]{2,1,0:T(8,128)(2,1)}, u32[]{:S(2)}, u32[]{:S(2)}) collective-permute-start(bf16[8,512,128]{2,1,0:T(8,128)(2,1)} %constant_dynamic-update-slice_fusion.rest_5_), channel_id=1, source_target_pairs={{0,1},{1,0},{2,3},{3,2},{4,5},{5,4},{6,7},{7,6},{8,9},{9,8},{10,11... | collective-permute-start | bytes 3145736 | tf_op jit(solution)/shard_map/ppermute | solution.py:345
  57.7 6.4 %copy-start.5 = (s32[3]{0:T(128)}, s32[3]{0:T(128)S(1)}, u32[]{:S(2)}) copy-start(s32[3]{0:T(128)S(1)} %pad_add_fusion.own) | copy-start | bytes 40
  64.1 2.1 %copy-start = (bf16[144,128,128]{2,1,0:T(8,128)(2,1)}, bf16[144,128,128]{2,1,0:T(8,128)(2,1)S(1)}, u32[]{:S(2)}) copy-start(bf16[144,128,128]{2,1,0:T(8,128)(2,1)S(1)} %get-tuple-element.50.rest_0_) | copy-start | bytes 14155780
  66.3 1.0 copy-start.1
  67.3 0.8 copy-start.2
  68.1 0.7 copy-start.3
  68.7 0.6 copy-start.4
  69.4 0.6 copy-start.6
  69.9 0.5 copy-start.7
  70.5 0.5 copy-start.8
  71.0 0.6 copy-start.9
  71.6 2.3 %collective-permute-start.16 = (bf16[4,512,128]{2,1,0:T(8,128)(2,1)}, bf16[4,512,128]{2,1,0:T(8,128)(2,1)S(1)}, u32[]{:S(2)}, u32[]{:S(2)}) collective-permute-start(bf16[4,512,128]{2,1,0:T(8,128)(2,1)} %collective-permute-done.13.rest_6_), channel_id=1, source_target_pairs={{0,1},{1,0},{2,3},{3,2},{4,5},{5,4},{6,7},{7,6},{8,9},{9,8},{10,11... | collective-permute-start | bytes 1572872 | tf_op jit(solution)/shard_map/ppermute | solution.py:345
  72.1 2.5 %collective-permute-start.17 = (bf16[4,512,128]{2,1,0:T(8,128)(2,1)}, bf16[4,512,128]{2,1,0:T(8,128)(2,1)S(1)}, u32[]{:S(2)}, u32[]{:S(2)}) collective-permute-start(bf16[4,512,128]{2,1,0:T(8,128)(2,1)} %collective-permute-done.14.rest_7_), channel_id=1, source_target_pairs={{0,1},{1,0},{2,3},{3,2},{4,5},{5,4},{6,7},{7,6},{8,9},{9,8},{10,11... | collective-permute-start | bytes 1572872 | tf_op jit(solution)/shard_map/ppermute | solution.py:345
  73.9 0.8 copy-start.10
  74.6 0.8 copy-start.11

commit v5 on v4

--- a/solution.py
+++ b/solution.py
@@ -27,43 +27,43 @@
     return hi, (x - hi.astype(jnp.float32)).astype(jnp.bfloat16)
 
 
-def reciprocal(x):
-    y = pl.reciprocal(x, approx=True)
-    for _ in range(2):
-        y = y * (2.0 - x * y)
-    return y
-
-
 def inverse_factor(gram):
     n = gram.shape[0]
     rows = lax.broadcasted_iota(jnp.int32, (n, n), 0)
     cols = lax.broadcasted_iota(jnp.int32, (n, n), 1)
     eye = (rows == cols).astype(jnp.float32)
     both = jnp.concatenate([gram, eye], axis=1)
-    count = n // 8
+    count, shape = n // 8, (8, 2 * n)
     tiles = [both[8 * t : 8 * t + 8] for t in range(count)]
-    sub = lax.broadcasted_iota(jnp.int32, (8, 2 * n), 0)
-    lane = lax.broadcasted_iota(jnp.int32, (8, 2 * n), 1)
+    sub = lax.broadcasted_iota(jnp.int32, shape, 0)
+    out = []
     for b in range(count):
-        spread = {
-            t: [jnp.broadcast_to(tiles[t][:, 8 * b + s : 8 * b + s + 1], (8, 2 * n)) for s in range(8)]
+        column = {
+            t: [jnp.broadcast_to(tiles[t][:, 8 * b + s : 8 * b + s + 1], shape) for s in range(8)]
             for t in range(b, count)
         }
+        row = [jnp.broadcast_to(tiles[b][s : s + 1], shape) for s in range(8)]
+        a = [
+            [jnp.broadcast_to(column[b][j][s : s + 1], shape) if j >= s else None for j in range(8)]
+            for s in range(8)
+        ]
+        done = jnp.zeros(shape, jnp.float32)
         for s in range(8):
-            inv = reciprocal(spread[b][s][s : s + 1])
-            step = tiles[b][s : s + 1] * inv
-            ahead = [spread[b][s2][s : s + 1] * inv for s2 in range(s + 1, 8)]
-            for t in range(b, count):
-                factor = spread[t][s]
-                if t == b:
-                    factor = jnp.where(sub > s, factor, 0.0)
-                for s2 in range(s + 1, 8):
-                    spread[t][s2] = spread[t][s2] - factor * ahead[s2 - s - 1]
-                tiles[t] = tiles[t] - factor * step
-    out = []
-    for t in range(count):
-        pivot = jnp.sum(jnp.where(lane == sub + 8 * t, tiles[t], 0.0), axis=1, keepdims=True)
-        out.append(tiles[t] * lax.rsqrt(pivot))
+            root = lax.rsqrt(a[s][s])
+            inv = root * root
+            inv = inv * (2.0 - a[s][s] * inv)
+            step = row[s] * inv
+            done = jnp.where(sub == s, row[s] * root, done)
+            for i in range(s + 1, 8):
+                part = a[s][i] * inv
+                for j in range(i, 8):
+                    a[i][j] = a[i][j] - part * a[s][j]
+                row[i] = row[i] - a[s][i] * step
+                for t in range(b + 1, count):
+                    column[t][i] = column[t][i] - column[t][s] * part
+            for t in range(b + 1, count):
+                tiles[t] = tiles[t] - column[t][s] * step
+        out.append(done)
     return jnp.concatenate(out, axis=0)[:, n:]
 
 
@@ -134,11 +134,7 @@
     lax.fori_loop(0, n_group, group, 0)
 
 
-def unpack(
-    n_row, n_col, own, mine, other,
-    lv, lw, nums, place, blk, vs, vd, rm, ic,
-    ints, meta, sems, small,
-):
+def unpack(n_row, n_col, own, copies, lv, lw, nums, place, blk, vs, vd, rm, ic, ints, meta, sem, small):
     n_dev = n_row * n_col
     k = vs.shape[1]
     half = k // 2
@@ -147,13 +143,12 @@
     meta_at = vec_at + k
     at_device, device_at = place_of(own, n_row, n_dev)
 
-    first, second = pl.ds(0, n_dev // 2), pl.ds(n_dev // 2, n_dev // 2)
-    for copy in copy_in([(mine, small.at[first]), (other, small.at[second])], sems):
+    for copy in copies:
         copy.wait()
     for d in range(n_dev):
         rows = small[d, meta_at : meta_at + META, :].astype(jnp.float32)
         ints[d : d + 1, :] = rows[8:9].astype(jnp.int32)
-    to_scalars = pltpu.make_async_copy(ints, meta, sems.at[2])
+    to_scalars = pltpu.make_async_copy(ints, meta, sem)
     to_scalars.start()
 
     for r in range(n_row):
@@ -202,10 +197,12 @@
         place[r : r + 1, :] = index[7:8] * float(rblk) + index[6:7]
 
 
-def iterate(n_row, n_col, n_cap, total, own, lv, lw, nums, place, *rest):
-    sources, fulls, out = rest[:5], rest[5:11], rest[11]
-    sems, full, tmp, home, blk, vs, vd, rm, ic = rest[12:21]
-    w, w1, w2, wt, wd, y, y1, y2, ph, linv = rest[21:]
+def iterate(n_row, n_col, n_cap, total, own, mine, other, *rest):
+    fulls, out = rest[:6], rest[6]
+    sems, full, tmp, home = rest[7:11]
+    unpacked, rest = rest[11:23], rest[23:]
+    lv, lw, nums, place, blk, vs, vd, rm, ic, ints, meta, small = unpacked
+    w, w1, w2, wt, wd, y, y1, y2, ph, linv = rest
     n_dev = n_row * n_col
     k = vs.shape[1]
     half = k // 2
@@ -215,14 +212,21 @@
     width = cpairs * 128
     at_device, _ = place_of(own, n_row, n_dev)
 
-    at, pairs = 0, []
-    for ref in fulls:
-        pairs.append((ref, full.at[pl.ds(at, ref.shape[0])]))
-        at += ref.shape[0]
-    copies = copy_in(pairs + list(zip(sources, (blk, vs, vd, rm, ic))), sems)
-    for copy in copies[: len(fulls)]:
+    def laid_out(refs, whole):
+        at, pairs = 0, []
+        for ref in refs:
+            pairs.append((ref, whole.at[pl.ds(at, ref.shape[0])]))
+            at += ref.shape[0]
+        return pairs
+
+    copies = copy_in(laid_out([mine, other], small) + laid_out(fulls, full), sems)
+    unpack(
+        n_row, n_col, own, copies[:2],
+        lv, lw, nums, place, blk, vs, vd, rm, ic, ints, meta, sems.at[len(copies)], small,
+    )
+    n_group = nums[0]
+    for copy in copies[2:]:
         copy.wait()
-    n_group = nums[0]
 
     left = lax.broadcasted_iota(jnp.int32, (rblk, 128), 1) < 64
     homes = []
@@ -266,8 +270,6 @@
                 ref[q] = jnp.zeros_like(ref[q])
 
     clear([y, y1, y2, w1, w2])
-    for copy in copies[len(fulls) :]:
-        copy.wait()
 
     def iteration(it, carry):
         @pl.when(it > 0)
@@ -405,60 +407,41 @@
     homes = jnp.concatenate(homes)
     other_homes = swap(homes, "core", 1)
 
+    fulls = [homes, *last, other_homes, *(swap(v, "core", 1) for v in last)]
+
     where = jnp.stack([row, chip, core]).astype(jnp.int32)
-
     height, width = 2 * n_col * bsize, 2 * n_row * bsize
     slots = n_dev * OFF_CAP + 2 * UNROLL
-    f32, i32 = jnp.float32, jnp.int32
+    f32, i32, vmem, smem = jnp.float32, jnp.int32, pltpu.VMEM, pltpu.SMEM
     pair, twice, mass = (n_dev, k, 128), (2 * n_dev, k, 128), (n_dev, 8, 128)
-    smem, anywhere = (pl.BlockSpec(memory_space=m) for m in (pltpu.SMEM, pl.ANY))
-    vmem = pl.BlockSpec(memory_space=pltpu.VMEM)
-    lists = [((slots,), i32), ((slots,), i32), ((1 + n_row,), i32)]
-    arrays = [
-        ((8, 128), f32), ((slots // 2, 128, 128), bf16), (pair, bf16), (twice, bf16), (mass, f32), (mass, f32),
-    ]
-    unpacked = pl.pallas_call(
-        functools.partial(unpack, n_row, n_col),
-        out_shape=[jax.ShapeDtypeStruct(*v) for v in lists + arrays],
-        in_specs=[smem, anywhere, anywhere],
-        out_specs=[smem] * len(lists) + [vmem] * len(arrays),
-        scratch_shapes=[
-            pltpu.VMEM((n_dev, 128), i32),
-            pltpu.SMEM((n_dev, 128), i32),
-            pltpu.SemaphoreType.DMA((3,)),
-            pltpu.VMEM((n_dev,) + small.shape, bf16),
-        ],
-        compiler_params=pltpu.CompilerParams(vmem_limit_bytes=VMEM_LIMIT // 2),
-        cost_estimate=pl.CostEstimate(
-            flops=2 * slots * bsize**3, bytes_accessed=2 * n_dev * small.size * 2, transcendentals=0
-        ),
-        name="unpack",
-    )(where, smalls, others)
-    last, nums = together((last, unpacked[2]))
-    unpacked = (*unpacked[:2], nums, *unpacked[3:])
-    fulls = [homes, *last, other_homes, *(swap(v, "core", 1) for v in last)]
     result = pl.pallas_call(
         functools.partial(iterate, n_row, n_col, n_cap, float(n_dev * own * bsize)),
         out_shape=jax.ShapeDtypeStruct((own, k, bsize), f32),
-        in_specs=[smem] * 4 + [vmem] + [anywhere] * (5 + len(fulls)),
-        out_specs=vmem,
+        in_specs=[pl.BlockSpec(memory_space=smem)]
+        + [pl.BlockSpec(memory_space=pl.ANY)] * (2 + len(fulls)),
+        out_specs=pl.BlockSpec(memory_space=vmem),
         scratch_shapes=[
-            pltpu.SemaphoreType.DMA((5 + len(fulls),)),
-            pltpu.VMEM((n_dev,) + home.shape, bf16),
-            pltpu.VMEM((n_row, height, 128), f32),
-            pltpu.VMEM((n_row, height, 2 * width), bf16),
-            *[pltpu.VMEM(*v) for v in arrays[1:]],
-            *[
-                pltpu.VMEM(*v)
-                for v in [
-                    (pair, f32), (twice, f32), (twice, f32), (pair, bf16), (twice, bf16),
-                    (pair, f32), (twice, f32), (twice, f32), ((n_dev, 2 * k, 128), bf16), ((k, k), f32),
-                ]
-            ],
+            pltpu.SemaphoreType.DMA((3 + len(fulls),)),
+            vmem((n_dev,) + home.shape, bf16),
+            vmem((n_row, height, 128), f32),
+            vmem((n_row, height, 2 * width), bf16),
+            smem((slots,), i32),
+            smem((slots,), i32),
+            smem((1 + n_row,), i32),
+            vmem((8, 128), f32),
+            vmem((slots // 2, 128, 128), bf16),
+            vmem(pair, bf16), vmem(twice, bf16), vmem(mass, f32), vmem(mass, f32),
+            vmem((n_dev, 128), i32),
+            smem((n_dev, 128), i32),
+            vmem((n_dev,) + small.shape, bf16),
+            vmem(pair, f32), vmem(twice, f32), vmem(twice, f32), vmem(pair, bf16), vmem(twice, bf16),
+            vmem(pair, f32), vmem(twice, f32), vmem(twice, f32),
+            vmem((n_dev, 2 * k, 128), bf16),
+            vmem((k, k), f32),
         ],
         compiler_params=pltpu.CompilerParams(vmem_limit_bytes=VMEM_LIMIT),
         name="iterate",
-    )(where, *unpacked, *fulls)
+    )(where, smalls, others, *fulls)
     return result.reshape(own, k * bsize)
 
 

time: 143 us -> 144 us (level)
  waiting for transfers between devices: 27.1 us -> 39.3 us
  local copies, waits for them, and re-layouts: 13.4 us -> 2.51 us
  Pallas kernels: 70.4 us -> 72 us
    ppermute x18, waiting for transfers between devices: 26 us -> 36.7 us  [swap(): return lax.ppermute(x, axis, [(i, i ^ distance) for i in range(size)])]
    unnamed x36 -> x20, local copies, waits for them, and re-layouts: 9.12 us -> 0.09 us
    pallas_call x1, Pallas kernels: 63.9 us -> 72 us  [whole_on_each(): pl.pallas_call(functools.partial(iterate, n_row, n_col, n_cap, float(n_de...]
    pallas_call x1 -> x0, Pallas kernels: 6.41 us -> none  [whole_on_each(): pl.pallas_call(functools.partial(unpack, n_row, n_col), out_shape=[jax.Sh...]
    concatenate x1, local copies, waits for them, and re-layouts: 1.95 us -> 0.07 us  [whole_on_each(): homes = jnp.concatenate(homes)]
    all_to_all x1, waiting for transfers between devices: 1.12 us -> 2.58 us  [whole_on_each(): got = lax.all_to_all(sent, ('chip', 'core'), split_axis=0, concat_axis=0)]
  transfers between devices with their start and end apart: 19 -> 19, of which waited for: 11 -> 13; matrix products, arithmetic and copies ran while one was open for 4% -> 2% of each run, Pallas kernels for 5% -> 0%
where the time goes in v5:
time: 144 us; the launch traced here: 143 us
  Pallas kernels  72 us (50%)
  waiting for transfers between devices  39.3 us (27%)
  starting transfers between devices  26.1 us (18%)
  local copies, waits for them, and re-layouts  2.51 us (2%)
  other arithmetic  2.41 us (2%)
    pallas_call x1, Pallas kernels, whole_on_each(): pl.pallas_call(functools.partial(iterate, n_row, n_col, n_cap, float(n_de...  72 us
    ppermute x18, waiting for transfers between devices, swap(): return lax.ppermute(x, axis, [(i, i ^ distance) for i in range(size)])  36.7 us
    ppermute x18, starting transfers between devices, swap(): return lax.ppermute(x, axis, [(i, i ^ distance) for i in range(size)])  20.8 us
    all_to_all x1, starting transfers between devices, whole_on_each(): got = lax.all_to_all(sent, ('chip', 'core'), split_axis=0, concat_axis=0)  5.31 us
  transfers between devices with their start and end apart: 19, of which 13 were waited for; matrix products, arithmetic and copies ran while one was open for 2% of the time, Pallas kernels for 0%

profile of v5, /device:TPU:0, one launch (start us, length us, event | category | flops | bytes accessed | tf_op | source)
XLA Modules:
  0.0 143.3 jit_solution(4329174781257168706)
XLA Ops:
  0.7 1.1 broadcast_select_fusion
  1.8 5.3 %all-to-all-start = ((bf16[8,16,4096]{2,1,0:T(8,128)(2,1)}), bf16[8,16,4096]{2,1,0:T(8,128)(2,1)S(1)}, u32[]{:S(2)}, u32[]{:S(2)}) async-start(bf16[8,16,4096]{2,1,0:T(8,128)(2,1)} %bitcast.4), calls=%async_computation | async-start | bytes 2097152 | tf_op jit(solution)/shard_map/all_to_all | solution.py:394
  7.1 0.1 reshape.209
  7.2 0.1 reshape.207
  7.3 0.1 copy.15
  7.4 0.1 reshape.208
  7.5 0.1 reshape.205
  7.6 0.1 reshape.206
  7.8 0.1 bitcast_maximum_fusion
  8.0 0.1 concatenate.51
  8.1 2.6 %collective-permute-start.2 = (bf16[336,128]{1,0:T(8,128)(2,1)S(1)}, bf16[336,128]{1,0:T(8,128)(2,1)S(1)}, u32[]{:S(2)}, u32[]{:S(2)}) collective-permute-start(bf16[336,128]{1,0:T(8,128)(2,1)S(1)} %concatenate.51), channel_id=1, source_target_pairs={{0,16},{8,24},{16,0},{24,8},{1,17},{9,25},{17,1},{25,9},{2,18},{10... | collective-permute-start | bytes 258056 | tf_op jit(solution)/shard_map/ppermute | solution.py:347
  10.7 1.8 %collective-permute-start.3 = (bf16[336,128]{1,0:T(8,128)(2,1)S(1)}, bf16[336,128]{1,0:T(8,128)(2,1)S(1)}, u32[]{:S(2)}, u32[]{:S(2)}) collective-permute-start(bf16[336,128]{1,0:T(8,128)(2,1)S(1)} %concatenate.51), channel_id=1, source_target_pairs={{0,24},{8,16},{16,8},{24,0},{1,25},{9,17},{17,9},{25,1},{2,26},{10... | collective-permute-start | bytes 258056 | tf_op jit(solution)/shard_map/ppermute | solution.py:347
  12.4 0.5 collective-permute-start
  12.9 4.6 %collective-permute-done.2 = bf16[336,128]{1,0:T(8,128)(2,1)S(1)} collective-permute-done((bf16[336,128]{1,0:T(8,128)(2,1)S(1)}, bf16[336,128]{1,0:T(8,128)(2,1)S(1)}, u32[]{:S(2)}, u32[]{:S(2)}) %collective-permute-start.2) | collective-permute-done | bytes 86048 | tf_op jit(solution)/shard_map/ppermute | solution.py:347
  17.5 0.5 collective-permute-done.3
  18.0 2.0 %collective-permute-start.4 = (bf16[2,336,128]{2,1,0:T(8,128)(2,1)S(1)}, bf16[2,336,128]{2,1,0:T(8,128)(2,1)S(1)}, u32[]{:S(2)}, u32[]{:S(2)}) collective-permute-start(bf16[2,336,128]{2,1,0:T(8,128)(2,1)S(1)} %pad_maximum_fusion.8), channel_id=1, source_target_pairs={{0,4},{2,6},{4,0},{6,2},{1,5},{3,7},{5,1},{7,3},{8,12},{10,14},{12... | collective-permute-start | bytes 516104 | tf_op jit(solution)/shard_map/ppermute | solution.py:347
  20.0 2.6 %all-to-all-done = bf16[8,16,4096]{2,1,0:T(8,128)(2,1)S(1)} async-done(((bf16[8,16,4096]{2,1,0:T(8,128)(2,1)}), bf16[8,16,4096]{2,1,0:T(8,128)(2,1)S(1)}, u32[]{:S(2)}, u32[]{:S(2)}) %all-to-all-start) | async-done | bytes 1048608 | tf_op jit(solution)/shard_map/all_to_all | solution.py:394
  22.6 0.1 reduce_sum.12
  22.8 0.1 copy.13
  22.9 0.5 collective-permute-start.1
  23.4 1.5 %collective-permute-start.5 = (bf16[512,128]{1,0:T(8,128)(2,1)S(1)}, bf16[512,128]{1,0:T(8,128)(2,1)S(1)}, u32[]{:S(2)}, u32[]{:S(2)}) collective-permute-start(bf16[512,128]{1,0:T(8,128)(2,1)S(1)} %bitcast.33), channel_id=1, source_target_pairs={{0,8},{8,0},{16,24},{24,16},{1,9},{9,1},{17,25},{25,17},{2,10},{10... | collective-permute-start | bytes 393224 | tf_op jit(solution)/shard_map/ppermute | solution.py:347
  24.9 3.3 %collective-permute-start.6 = (bf16[512,128]{1,0:T(8,128)(2,1)S(1)}, bf16[512,128]{1,0:T(8,128)(2,1)S(1)}, u32[]{:S(2)}, u32[]{:S(2)}) collective-permute-start(bf16[512,128]{1,0:T(8,128)(2,1)S(1)} %bitcast.34), channel_id=1, source_target_pairs={{0,16},{8,24},{16,0},{24,8},{1,17},{9,25},{17,1},{25,9},{2,18},{10... | collective-permute-start | bytes 393224 | tf_op jit(solution)/shard_map/ppermute | solution.py:347
  28.2 0.1 collective-permute-done.1
  28.4 0.2 collective-permute-done.5
  28.5 5.6 %collective-permute-done.6 = bf16[512,128]{1,0:T(8,128)(2,1)S(1)} collective-permute-done((bf16[512,128]{1,0:T(8,128)(2,1)S(1)}, bf16[512,128]{1,0:T(8,128)(2,1)S(1)}, u32[]{:S(2)}, u32[]{:S(2)}) %collective-permute-start.6) | collective-permute-done | bytes 131104 | tf_op jit(solution)/shard_map/ppermute | solution.py:347
  34.1 0.4 collective-permute-start.8
  34.5 0.4 collective-permute-start.9
  34.9 2.8 %collective-permute-start.7 = (bf16[512,128]{1,0:T(8,128)(2,1)S(1)}, bf16[512,128]{1,0:T(8,128)(2,1)S(1)}, u32[]{:S(2)}, u32[]{:S(2)}) collective-permute-start(bf16[512,128]{1,0:T(8,128)(2,1)S(1)} %bitcast.35), channel_id=1, source_target_pairs={{0,24},{8,16},{16,8},{24,0},{1,25},{9,17},{17,9},{25,1},{2,26},{10... | collective-permute-start | bytes 393224 | tf_op jit(solution)/shard_map/ppermute | solution.py:347
  37.7 3.7 %collective-permute-done.8 = bf16[4,336,128]{2,1,0:T(8,128)(2,1)S(1)} collective-permute-done((bf16[4,336,128]{2,1,0:T(8,128)(2,1)S(1)}, bf16[4,336,128]{2,1,0:T(8,128)(2,1)S(1)}, u32[]{:S(2)}, u32[]{:S(2)}) %collective-permute-start.8) | collective-permute-done | bytes 344096 | tf_op jit(solution)/shard_map/ppermute | solution.py:347
  41.4 0.4 collective-permute-done.9
  41.8 0.2 pad_maximum_fusion.mine
  42.0 0.1 collective-permute-start.12
  42.1 1.7 %collective-permute-start.11 = (bf16[2,512,128]{2,1,0:T(8,128)(2,1)S(1)}, bf16[2,512,128]{2,1,0:T(8,128)(2,1)S(1)}, u32[]{:S(2)}, u32[]{:S(2)}) collective-permute-start(bf16[2,512,128]{2,1,0:T(8,128)(2,1)S(1)} %pad_maximum_fusion.6), channel_id=1, source_target_pairs={{0,4},{2,6},{4,0},{6,2},{1,5},{3,7},{5,1},{7,3},{8,12},{10,14},{12... | collective-permute-start | bytes 786440 | tf_op jit(solution)/shard_map/ppermute | solution.py:347
  43.8 1.3 collective-permute-start.10
  45.1 5.7 %collective-permute-done.11 = bf16[2,512,128]{2,1,0:T(8,128)(2,1)S(1)} collective-permute-done((bf16[2,512,128]{2,1,0:T(8,128)(2,1)S(1)}, bf16[2,512,128]{2,1,0:T(8,128)(2,1)S(1)}, u32[]{:S(2)}, u32[]{:S(2)}) %collective-permute-start.11) | collective-permute-done | bytes 262176 | tf_op jit(solution)/shard_map/ppermute | solution.py:347
  50.8 0.1 pad_maximum_fusion.2
  50.9 1.4 collective-permute-done.10
  52.3 0.1 pad_maximum_fusion.1
  52.4 0.4 collective-permute-start.13
  52.9 0.1 constant_dynamic-update-slice_fusion.rest_0_
  53.0 0.1 collective-permute-start.15
  53.0 1.3 collective-permute-start.14
  54.4 11.3 %collective-permute-done.13.rest_1_ = bf16[4,512,128]{2,1,0:T(8,128)(2,1)S(1)} collective-permute-done((bf16[4,512,128]{2,1,0:T(8,128)(2,1)S(1)}, bf16[4,512,128]{2,1,0:T(8,128)(2,1)S(1)}, u32[]{:S(2)}, u32[]{:S(2)}) %collective-permute-start.13) | collective-permute-done | bytes 524320 | tf_op jit(solution)/shard_map/ppermute | solution.py:347
  65.7 1.8 %collective-permute-done.14.rest_2_ = bf16[4,512,128]{2,1,0:T(8,128)(2,1)} collective-permute-done((bf16[4,512,128]{2,1,0:T(8,128)(2,1)S(1)}, bf16[4,512,128]{2,1,0:T(8,128)(2,1)}, u32[]{:S(2)}, u32[]{:S(2)}) %collective-permute-start.14) | collective-permute-done | bytes 524320 | tf_op jit(solution)/shard_map/ppermute | solution.py:347
  67.5 0.7 pad_add_fusion.own
  68.1 1.6 %collective-permute-done.17.rest_5_ = bf16[4,512,128]{2,1,0:T(8,128)(2,1)} collective-permute-done((bf16[4,512,128]{2,1,0:T(8,128)(2,1)}, bf16[4,512,128]{2,1,0:T(8,128)(2,1)}, u32[]{:S(2)}, u32[]{:S(2)}) %collective-permute-start.17) | collective-permute-done | bytes 524320 | tf_op jit(solution)/shard_map/ppermute | solution.py:347
  69.8 72.0 %iterate.1 = f32[2,64,64]{2,1,0:T(8,128)} custom-call(s32[3]{0:T(128)} %pad_add_fusion.own, bf16[16,336,128]{2,1,0:T(8,128)(2,1)} %copy-done, bf16[16,336,128]{2,1,0:T(8,128)(2,1)} %copy-done.2, bf16[8,512,128]{2,1,0:T(8,128)(2,1)} %copy-done.1, bf16[4,512,128]{2,1,0:T(8,128)(2,1)} %copy-done.3, bf16[4,512,128]{2,1,0:T(8,128)(2,1)} %collective-permute-done.14.rest_2_, ...), custom_call_target="tpu_custom_call" | custom-call | tf_op jit(solution)/shard_map/iterate/pallas_call | solution.py:417
  141.8 1.5 %reshape.210 = f32[2,4096]{1,0:T(2,128)} reshape(f32[2,64,64]{2,1,0:T(8,128)} %iterate.1) | data formatting | bytes 65536 | tf_op jit(solution)/shard_map/reshape | solution.py:445
  (48 shorter events, 0.4 us)
Async XLA Ops:
  1.7 5.4 %copy-start.7 = (s32[1,1,128]{2,1,0:T(1,128)S(1)}, s32[1,1,128]{2,1,0:T(1,128)}, u32[]{:S(2)}) copy-start(s32[1,1,128]{2,1,0:T(1,128)} %param.8) | copy-start | bytes 1540
  1.7 5.4 %copy-start.6 = (f32[2,64]{1,0:T(2,128)S(1)}, f32[2,64]{1,0:T(2,128)}, u32[]{:S(2)}) copy-start(f32[2,64]{1,0:T(2,128)} %param.13) | copy-start | bytes 1540
  1.7 5.5 %copy-start.5 = (f32[2,64]{1,0:T(2,128)S(1)}, f32[2,64]{1,0:T(2,128)}, u32[]{:S(2)}) copy-start(f32[2,64]{1,0:T(2,128)} %param.12) | copy-start | bytes 1540
  1.7 5.7 %copy-start.4 = (f32[2,4096]{1,0:T(2,128)S(1)}, f32[2,4096]{1,0:T(2,128)}, u32[]{:S(2)}) copy-start(f32[2,4096]{1,0:T(2,128)} %param.11) | copy-start | bytes 98308
  1.7 6.0 %slice-start = ((bf16[1,1,128,4096]{3,2,1,0:T(8,128)(2,1)}), bf16[1,1,8,4096]{3,2,1,0:T(8,128)(2,1)S(1)}, s32[]{:S(2)}) async-start(bf16[1,1,128,4096]{3,2,1,0:T(8,128)(2,1)} %param.7), calls=%async_computation.1 | async-start | bytes 131072 | tf_op jit(solution)/shard_map/slice | solution.py:380
  1.7 6.0 %copy-start.8 = (s32[1,1,128]{2,1,0:T(1,128)S(1)}, s32[1,1,128]{2,1,0:T(1,128)}, u32[]{:S(2)}) copy-start(s32[1,1,128]{2,1,0:T(1,128)} %param.9) | copy-start | bytes 1540
  1.8 20.8 %all-to-all-start = ((bf16[8,16,4096]{2,1,0:T(8,128)(2,1)}), bf16[8,16,4096]{2,1,0:T(8,128)(2,1)S(1)}, u32[]{:S(2)}, u32[]{:S(2)}) async-start(bf16[8,16,4096]{2,1,0:T(8,128)(2,1)} %bitcast.4), calls=%async_computation | async-start | bytes 2097152 | tf_op jit(solution)/shard_map/all_to_all | solution.py:394
  8.1 9.4 %collective-permute-start.2 = (bf16[336,128]{1,0:T(8,128)(2,1)S(1)}, bf16[336,128]{1,0:T(8,128)(2,1)S(1)}, u32[]{:S(2)}, u32[]{:S(2)}) collective-permute-start(bf16[336,128]{1,0:T(8,128)(2,1)S(1)} %concatenate.51), channel_id=1, source_target_pairs={{0,16},{8,24},{16,0},{24,8},{1,17},{9,25},{17,1},{25,9},{2,18},{10... | collective-permute-start | bytes 258056 | tf_op jit(solution)/shard_map/ppermute | solution.py:347
  10.7 7.3 %collective-permute-start.3 = (bf16[336,128]{1,0:T(8,128)(2,1)S(1)}, bf16[336,128]{1,0:T(8,128)(2,1)S(1)}, u32[]{:S(2)}, u32[]{:S(2)}) collective-permute-start(bf16[336,128]{1,0:T(8,128)(2,1)S(1)} %concatenate.51), channel_id=1, source_target_pairs={{0,24},{8,16},{16,8},{24,0},{1,25},{9,17},{17,9},{25,1},{2,26},{10... | collective-permute-start | bytes 258056 | tf_op jit(solution)/shard_map/ppermute | solution.py:347
  12.4 10.4 %collective-permute-start = (bf16[336,128]{1,0:T(8,128)(2,1)S(1)}, bf16[336,128]{1,0:T(8,128)(2,1)S(1)}, u32[]{:S(2)}, u32[]{:S(2)}) collective-permute-start(bf16[336,128]{1,0:T(8,128)(2,1)S(1)} %concatenate.51), channel_id=1, source_target_pairs={{0,8},{8,0},{16,24},{24,16},{1,9},{9,1},{17,25},{25,17},{2,10},{10... | collective-permute-start | bytes 258056 | tf_op jit(solution)/shard_map/ppermute | solution.py:347
  18.0 10.2 %collective-permute-start.4 = (bf16[2,336,128]{2,1,0:T(8,128)(2,1)S(1)}, bf16[2,336,128]{2,1,0:T(8,128)(2,1)S(1)}, u32[]{:S(2)}, u32[]{:S(2)}) collective-permute-start(bf16[2,336,128]{2,1,0:T(8,128)(2,1)S(1)} %pad_maximum_fusion.8), channel_id=1, source_target_pairs={{0,4},{2,6},{4,0},{6,2},{1,5},{3,7},{5,1},{7,3},{8,12},{10,14},{12... | collective-permute-start | bytes 516104 | tf_op jit(solution)/shard_map/ppermute | solution.py:347
  22.9 5.5 %collective-permute-start.1 = (bf16[2,336,128]{2,1,0:T(8,128)(2,1)S(1)}, bf16[2,336,128]{2,1,0:T(8,128)(2,1)S(1)}, u32[]{:S(2)}, u32[]{:S(2)}) collective-permute-start(bf16[2,336,128]{2,1,0:T(8,128)(2,1)S(1)} %pad_maximum_fusion.7), channel_id=1, source_target_pairs={{0,2},{2,0},{4,6},{6,4},{1,3},{3,1},{5,7},{7,5},{8,10},{10,8},{12,... | collective-permute-start | bytes 516104 | tf_op jit(solution)/shard_map/ppermute | solution.py:347
  23.4 5.2 %collective-permute-start.5 = (bf16[512,128]{1,0:T(8,128)(2,1)S(1)}, bf16[512,128]{1,0:T(8,128)(2,1)S(1)}, u32[]{:S(2)}, u32[]{:S(2)}) collective-permute-start(bf16[512,128]{1,0:T(8,128)(2,1)S(1)} %bitcast.33), channel_id=1, source_target_pairs={{0,8},{8,0},{16,24},{24,16},{1,9},{9,1},{17,25},{25,17},{2,10},{10... | collective-permute-start | bytes 393224 | tf_op jit(solution)/shard_map/ppermute | solution.py:347
  24.9 9.2 %collective-permute-start.6 = (bf16[512,128]{1,0:T(8,128)(2,1)S(1)}, bf16[512,128]{1,0:T(8,128)(2,1)S(1)}, u32[]{:S(2)}, u32[]{:S(2)}) collective-permute-start(bf16[512,128]{1,0:T(8,128)(2,1)S(1)} %bitcast.34), channel_id=1, source_target_pairs={{0,16},{8,24},{16,0},{24,8},{1,17},{9,25},{17,1},{25,9},{2,18},{10... | collective-permute-start | bytes 393224 | tf_op jit(solution)/shard_map/ppermute | solution.py:347
  34.1 7.2 %collective-permute-start.8 = (bf16[4,336,128]{2,1,0:T(8,128)(2,1)S(1)}, bf16[4,336,128]{2,1,0:T(8,128)(2,1)S(1)}, u32[]{:S(2)}, u32[]{:S(2)}) collective-permute-start(bf16[4,336,128]{2,1,0:T(8,128)(2,1)S(1)} %pad_maximum_fusion.3), channel_id=1, source_target_pairs={{0,4},{2,6},{4,0},{6,2},{1,5},{3,7},{5,1},{7,3},{8,12},{10,14},{12... | collective-permute-start | bytes 1032200 | tf_op jit(solution)/shard_map/ppermute | solution.py:347
  34.5 7.2 %collective-permute-start.9 = (bf16[4,336,128]{2,1,0:T(8,128)(2,1)S(1)}, bf16[4,336,128]{2,1,0:T(8,128)(2,1)S(1)}, u32[]{:S(2)}, u32[]{:S(2)}) collective-permute-start(bf16[4,336,128]{2,1,0:T(8,128)(2,1)S(1)} %pad_maximum_fusion.4), channel_id=1, source_target_pairs={{0,2},{2,0},{4,6},{6,4},{1,3},{3,1},{5,7},{7,5},{8,10},{10,8},{12,... | collective-permute-start | bytes 1032200 | tf_op jit(solution)/shard_map/ppermute | solution.py:347
  34.9 7.1 %collective-permute-start.7 = (bf16[512,128]{1,0:T(8,128)(2,1)S(1)}, bf16[512,128]{1,0:T(8,128)(2,1)S(1)}, u32[]{:S(2)}, u32[]{:S(2)}) collective-permute-start(bf16[512,128]{1,0:T(8,128)(2,1)S(1)} %bitcast.35), channel_id=1, source_target_pairs={{0,24},{8,16},{16,8},{24,0},{1,25},{9,17},{17,9},{25,1},{2,26},{10... | collective-permute-start | bytes 393224 | tf_op jit(solution)/shard_map/ppermute | solution.py:347
  41.9 10.4 %copy-start = (bf16[16,336,128]{2,1,0:T(8,128)(2,1)}, bf16[16,336,128]{2,1,0:T(8,128)(2,1)S(1)}, u32[]{:S(2)}) copy-start(bf16[16,336,128]{2,1,0:T(8,128)(2,1)S(1)} %pad_maximum_fusion.mine) | copy-start | bytes 4128772
  42.0 10.4 %collective-permute-start.12 = (bf16[16,336,128]{2,1,0:T(8,128)(2,1)S(1)}, bf16[16,336,128]{2,1,0:T(8,128)(2,1)S(1)}, u32[]{:S(2)}, u32[]{:S(2)}) collective-permute-start(bf16[16,336,128]{2,1,0:T(8,128)(2,1)S(1)} %pad_maximum_fusion.mine), channel_id=1, source_target_pairs={{0,1},{1,0},{2,3},{3,2},{4,5},{5,4},{6,7},{7,6},{8,9},{9,8},{10,11... | collective-permute-start | bytes 4128776 | tf_op jit(solution)/shard_map/ppermute | solution.py:347
  42.1 8.8 %collective-permute-start.11 = (bf16[2,512,128]{2,1,0:T(8,128)(2,1)S(1)}, bf16[2,512,128]{2,1,0:T(8,128)(2,1)S(1)}, u32[]{:S(2)}, u32[]{:S(2)}) collective-permute-start(bf16[2,512,128]{2,1,0:T(8,128)(2,1)S(1)} %pad_maximum_fusion.6), channel_id=1, source_target_pairs={{0,4},{2,6},{4,0},{6,2},{1,5},{3,7},{5,1},{7,3},{8,12},{10,14},{12... | collective-permute-start | bytes 786440 | tf_op jit(solution)/shard_map/ppermute | solution.py:347
  43.8 8.5 %collective-permute-start.10 = (bf16[2,512,128]{2,1,0:T(8,128)(2,1)S(1)}, bf16[2,512,128]{2,1,0:T(8,128)(2,1)S(1)}, u32[]{:S(2)}, u32[]{:S(2)}) collective-permute-start(bf16[2,512,128]{2,1,0:T(8,128)(2,1)S(1)} %pad_maximum_fusion.5), channel_id=1, source_target_pairs={{0,2},{2,0},{4,6},{6,4},{1,3},{3,1},{5,7},{7,5},{8,10},{10,8},{12,... | collective-permute-start | bytes 786440 | tf_op jit(solution)/shard_map/ppermute | solution.py:347
  52.4 17.4 %copy-start.2 = (bf16[16,336,128]{2,1,0:T(8,128)(2,1)}, bf16[16,336,128]{2,1,0:T(8,128)(2,1)S(1)}, u32[]{:S(2)}) copy-start(bf16[16,336,128]{2,1,0:T(8,128)(2,1)S(1)} %collective-permute-done.12.other) | copy-start | bytes 4128772
  52.4 13.3 %collective-permute-start.13 = (bf16[4,512,128]{2,1,0:T(8,128)(2,1)S(1)}, bf16[4,512,128]{2,1,0:T(8,128)(2,1)S(1)}, u32[]{:S(2)}, u32[]{:S(2)}) collective-permute-start(bf16[4,512,128]{2,1,0:T(8,128)(2,1)S(1)} %pad_maximum_fusion.1), channel_id=1, source_target_pairs={{0,4},{2,6},{4,0},{6,2},{1,5},{3,7},{5,1},{7,3},{8,12},{10,14},{12... | collective-permute-start | bytes 1572872 | tf_op jit(solution)/shard_map/ppermute | solution.py:347
  53.0 16.8 %copy-start.1 = (bf16[8,512,128]{2,1,0:T(8,128)(2,1)}, bf16[8,512,128]{2,1,0:T(8,128)(2,1)S(1)}, u32[]{:S(2)}) copy-start(bf16[8,512,128]{2,1,0:T(8,128)(2,1)S(1)} %constant_dynamic-update-slice_fusion.rest_0_) | copy-start | bytes 3145732
  53.0 15.2 %collective-permute-start.15 = (bf16[8,512,128]{2,1,0:T(8,128)(2,1)S(1)}, bf16[8,512,128]{2,1,0:T(8,128)(2,1)}, u32[]{:S(2)}, u32[]{:S(2)}) collective-permute-start(bf16[8,512,128]{2,1,0:T(8,128)(2,1)S(1)} %constant_dynamic-update-slice_fusion.rest_0_), channel_id=1, source_target_pairs={{0,1},{1,0},{2,3},{3,2},{4,5},{5,4},{6,7},{7,6},{8,9},{9,8},{10,11... | collective-permute-start | bytes 3145736 | tf_op jit(solution)/shard_map/ppermute | solution.py:347
  53.0 14.4 %collective-permute-start.14 = (bf16[4,512,128]{2,1,0:T(8,128)(2,1)S(1)}, bf16[4,512,128]{2,1,0:T(8,128)(2,1)}, u32[]{:S(2)}, u32[]{:S(2)}) collective-permute-start(bf16[4,512,128]{2,1,0:T(8,128)(2,1)S(1)} %pad_maximum_fusion.2), channel_id=1, source_target_pairs={{0,2},{2,0},{4,6},{6,4},{1,3},{3,1},{5,7},{7,5},{8,10},{10,8},{12,... | collective-permute-start | bytes 1572872 | tf_op jit(solution)/shard_map/ppermute | solution.py:347
  65.7 4.0 %copy-start.3 = (bf16[4,512,128]{2,1,0:T(8,128)(2,1)}, bf16[4,512,128]{2,1,0:T(8,128)(2,1)S(1)}, u32[]{:S(2)}) copy-start(bf16[4,512,128]{2,1,0:T(8,128)(2,1)S(1)} %collective-permute-done.13.rest_1_) | copy-start | bytes 1572868
  65.7 2.4 %collective-permute-start.16 = (bf16[4,512,128]{2,1,0:T(8,128)(2,1)S(1)}, bf16[4,512,128]{2,1,0:T(8,128)(2,1)}, u32[]{:S(2)}, u32[]{:S(2)}) collective-permute-start(bf16[4,512,128]{2,1,0:T(8,128)(2,1)S(1)} %collective-permute-done.13.rest_1_), channel_id=1, source_target_pairs={{0,1},{1,0},{2,3},{3,2},{4,5},{5,4},{6,7},{7,6},{8,9},{9,8},{10,11... | collective-permute-start | bytes 1572872 | tf_op jit(solution)/shard_map/ppermute | solution.py:347
  67.5 2.3 %collective-permute-start.17 = (bf16[4,512,128]{2,1,0:T(8,128)(2,1)}, bf16[4,512,128]{2,1,0:T(8,128)(2,1)}, u32[]{:S(2)}, u32[]{:S(2)}) collective-permute-start(bf16[4,512,128]{2,1,0:T(8,128)(2,1)} %collective-permute-done.14.rest_2_), channel_id=1, source_target_pairs={{0,1},{1,0},{2,3},{3,2},{4,5},{5,4},{6,7},{7,6},{8,9},{9,8},{10,11... | collective-permute-start | bytes 1572872 | tf_op jit(solution)/shard_map/ppermute | solution.py:347

commit v6 on v5

--- a/solution.py
+++ b/solution.py
@@ -197,10 +197,10 @@
         place[r : r + 1, :] = index[7:8] * float(rblk) + index[6:7]
 
 
-def iterate(n_row, n_col, n_cap, total, own, mine, other, *rest):
-    fulls, out = rest[:6], rest[6]
-    sems, full, tmp, home = rest[7:11]
-    unpacked, rest = rest[11:23], rest[23:]
+def iterate(n_row, n_col, n_cap, total, own, *rest):
+    smalls, fulls, out = rest[:8], rest[8:16], rest[16]
+    sems, full, tmp, home = rest[17:21]
+    unpacked, rest = rest[21:33], rest[33:]
     lv, lw, nums, place, blk, vs, vd, rm, ic, ints, meta, small = unpacked
     w, w1, w2, wt, wd, y, y1, y2, ph, linv = rest
     n_dev = n_row * n_col
@@ -219,13 +219,13 @@
             at += ref.shape[0]
         return pairs
 
-    copies = copy_in(laid_out([mine, other], small) + laid_out(fulls, full), sems)
+    copies = copy_in(laid_out(smalls, small) + laid_out(fulls, full), sems)
     unpack(
-        n_row, n_col, own, copies[:2],
+        n_row, n_col, own, copies[:8],
         lv, lw, nums, place, blk, vs, vd, rm, ic, ints, meta, sems.at[len(copies)], small,
     )
     n_group = nums[0]
-    for copy in copies[2:]:
+    for copy in copies[8:]:
         copy.wait()
 
     left = lax.broadcasted_iota(jnp.int32, (rblk, 128), 1) < 64
@@ -235,7 +235,7 @@
         want = lax.broadcasted_iota(jnp.int32, (cblk * rblk, n_cap), 0).astype(jnp.float32)
         select = jnp.where(want == place[r : r + 1, :], 1.0, 0.0).astype(jnp.bfloat16)
 
-        parts = [at_device(r, c) for c in range(n_col)]
+        parts = [at_device(r, 2 * i + j) for j in range(2) for i in range(n_col // 2)]
 
         def build(m, carry, parts=parts, select=select):
             at = pl.multiple_of(m * part, part)
@@ -364,6 +364,20 @@
     return [swap(near, "chip", 2), swap(far, "chip", 1)]
 
 
+def full_part(tile, has_full, n_chip, part, chip, core):
+    tile = tile.reshape(2, n_chip, part, tile.shape[1])
+    none = jnp.zeros(tile.shape[1:], tile.dtype)
+    kept, sent = (
+        jnp.where(has_full, lax.dynamic_index_in_dim(tile, i, 0, False), none)
+        for i in (core, 1 - core)
+    )
+    both = kept + swap(sent, "core", 1)
+    mine = lax.dynamic_index_in_dim(both, chip, 0, False)
+    for s in range(1, n_chip):
+        mine = mine + swap(lax.dynamic_index_in_dim(both, chip ^ s, 0, False), "chip", s)
+    return mine
+
+
 def whole_on_each(n_row, n_col, blocks, block_row, block_col, counts, vectors, row_mass, col_mass):
     tile = blocks[0, 0]
     n_cap = tile.shape[0]
@@ -390,24 +404,17 @@
     meta = split3(mass) + split3(inv_col.reshape(own * bsize)) + meta
     meta = jnp.stack(meta + [jnp.zeros(128, bf16)] * (META - len(meta)))
     small = jnp.concatenate([off, scaled, meta], axis=0)
-    sent = jnp.where(has_full, tile, jnp.zeros_like(tile)).reshape(n_col, part, bsize * bsize)
-    got = lax.all_to_all(sent, ("chip", "core"), split_axis=0, concat_axis=0)
-    home = jnp.sum(got.astype(jnp.float32), axis=0).astype(bf16)
+    home = full_part(tile, has_full, n_col // 2, part, chip, core)
     home = home.reshape(part, half, 128).transpose(1, 0, 2).reshape(half * part, 128)
 
     together = lax.optimization_barrier
-    smalls = along_rows(small)
-    home, smalls[1] = together((home, smalls[1]))
+    home, smalls = together((home, along_rows(small)))
     homes, smalls = along_rows(home), along_one_chip_axis(smalls)
-    smalls, homes[1:3] = together((smalls, homes[1:3]))
-    smalls = jnp.concatenate(smalls + along_other_chip_axis(smalls))
-    homes, smalls = together((homes, smalls))
-    homes, others = together((along_one_chip_axis(homes), swap(smalls, "core", 1)))
-    last = along_other_chip_axis(homes)
-    homes = jnp.concatenate(homes)
-    other_homes = swap(homes, "core", 1)
-
-    fulls = [homes, *last, other_homes, *(swap(v, "core", 1) for v in last)]
+    smalls, homes[1] = together((smalls, homes[1]))
+    homes, smalls = together((homes, smalls + along_other_chip_axis(smalls)))
+    homes = along_one_chip_axis(homes)
+    homes = homes + along_other_chip_axis(homes)
+    smalls, homes = ([*v, *(swap(x, "core", 1) for x in v)] for v in (smalls, homes))
 
     where = jnp.stack([row, chip, core]).astype(jnp.int32)
     height, width = 2 * n_col * bsize, 2 * n_row * bsize
@@ -418,10 +425,10 @@
         functools.partial(iterate, n_row, n_col, n_cap, float(n_dev * own * bsize)),
         out_shape=jax.ShapeDtypeStruct((own, k, bsize), f32),
         in_specs=[pl.BlockSpec(memory_space=smem)]
-        + [pl.BlockSpec(memory_space=pl.ANY)] * (2 + len(fulls)),
+        + [pl.BlockSpec(memory_space=pl.ANY)] * (len(smalls) + len(homes)),
         out_specs=pl.BlockSpec(memory_space=vmem),
         scratch_shapes=[
-            pltpu.SemaphoreType.DMA((3 + len(fulls),)),
+            pltpu.SemaphoreType.DMA((len(smalls) + len(homes) + 1,)),
             vmem((n_dev,) + home.shape, bf16),
             vmem((n_row, height, 128), f32),
             vmem((n_row, height, 2 * width), bf16),
@@ -441,7 +448,7 @@
         ],
         compiler_params=pltpu.CompilerParams(vmem_limit_bytes=VMEM_LIMIT),
         name="iterate",
-    )(where, smalls, others, *fulls)
+    )(where, *smalls, *homes)
     return result.reshape(own, k * bsize)
 
 

time: 144 us -> 140 us (0.972)
  waiting for transfers between devices: 39.3 us -> 32.4 us
  local copies, waits for them, and re-layouts: 2.51 us -> 6.03 us
  starting transfers between devices: 26.1 us -> 24.6 us
    all_to_all x1 -> x0, starting transfers between devices: 5.31 us -> none  [whole_on_each(): got = lax.all_to_all(sent, ('chip', 'core'), split_axis=0, concat_axis=0)]
    ppermute x18 -> x26, waiting for transfers between devices: 36.7 us -> 32.4 us  [swap(): return lax.ppermute(x, axis, [(i, i ^ distance) for i in range(size)])]
    ppermute x18 -> x26, starting transfers between devices: 20.8 us -> 24.6 us  [swap(): return lax.ppermute(x, axis, [(i, i ^ distance) for i in range(size)])]
    unnamed x20 -> x37, local copies, waits for them, and re-layouts: 0.09 us -> 3.65 us
    all_to_all x1 -> x0, waiting for transfers between devices: 2.58 us -> none  [whole_on_each(): got = lax.all_to_all(sent, ('chip', 'core'), split_axis=0, concat_axis=0)]
  transfers between devices with their start and end apart: 19 -> 26, of which waited for: 13 -> 16; matrix products, arithmetic and copies ran while one was open for 2% -> 1% of each run, Pallas kernels for 0% -> 0%
where the time goes in v6:
time: 140 us; the launch traced here: 138 us
  Pallas kernels  72 us (51%)
  waiting for transfers between devices  32.4 us (23%)
  starting transfers between devices  24.6 us (18%)
  local copies, waits for them, and re-layouts  6.03 us (4%)
  other arithmetic  2.14 us (2%)
    pallas_call x1, Pallas kernels, whole_on_each(): pl.pallas_call(functools.partial(iterate, n_row, n_col, n_cap, float(n_de...  72 us
    ppermute x26, waiting for transfers between devices, swap(): return lax.ppermute(x, axis, [(i, i ^ distance) for i in range(size)])  32.4 us
    ppermute x26, starting transfers between devices, swap(): return lax.ppermute(x, axis, [(i, i ^ distance) for i in range(size)])  24.6 us
    unnamed x37, local copies, waits for them, and re-layouts  3.65 us
  transfers between devices with their start and end apart: 26, of which 16 were waited for; matrix products, arithmetic and copies ran while one was open for 1% of the time, Pallas kernels for 0%

profile of v6, /device:TPU:0, one launch (start us, length us, event | category | flops | bytes accessed | tf_op | source)
XLA Modules:
  0.0 138.2 jit_solution(18213655156848554035)
XLA Ops:
  0.8 1.1 select_bitcast_fusion
  1.9 0.5 collective-permute-start
  2.4 0.1 copy-done.17
  2.5 0.7 copy-done.15
  3.3 0.6 copy-done.14
  3.9 0.1 reshape.208
  4.2 0.5 copy-done.13
  4.6 0.1 reshape.206
  4.9 3.0 %collective-permute-start.1 = (bf16[16,4096]{1,0:T(8,128)(2,1)S(1)}, bf16[16,4096]{1,0:T(8,128)(2,1)S(1)}, u32[]{:S(2)}, u32[]{:S(2)}) collective-permute-start(bf16[16,4096]{1,0:T(8,128)(2,1)S(1)} %get-tuple-element.37), channel_id=1, source_target_pairs={{0,2},{2,0},{4,6},{6,4},{1,3},{3,1},{5,7},{7,5},{8,10},{10,8},{12,... | collective-permute-start | bytes 393224 | tf_op jit(solution)/shard_map/ppermute | solution.py:347
  7.9 1.5 %collective-permute-start.3 = (bf16[16,4096]{1,0:T(8,128)(2,1)S(1)}, bf16[16,4096]{1,0:T(8,128)(2,1)S(1)}, u32[]{:S(2)}, u32[]{:S(2)}) collective-permute-start(bf16[16,4096]{1,0:T(8,128)(2,1)S(1)} %get-tuple-element.38), channel_id=1, source_target_pairs={{0,6},{2,4},{4,2},{6,0},{1,7},{3,5},{5,3},{7,1},{8,14},{10,12},{12... | collective-permute-start | bytes 393224 | tf_op jit(solution)/shard_map/ppermute | solution.py:347
  9.8 4.1 %collective-permute-start.6 = (bf16[336,128]{1,0:T(8,128)(2,1)S(1)}, bf16[336,128]{1,0:T(8,128)(2,1)S(1)}, u32[]{:S(2)}, u32[]{:S(2)}) collective-permute-start(bf16[336,128]{1,0:T(8,128)(2,1)S(1)} %concatenate.45), channel_id=1, source_target_pairs={{0,24},{8,16},{16,8},{24,0},{1,25},{9,17},{17,9},{25,1},{2,26},{10... | collective-permute-start | bytes 258056 | tf_op jit(solution)/shard_map/ppermute | solution.py:347
  14.0 0.6 collective-permute-start.4
  14.6 1.0 collective-permute-done.3
  15.6 1.4 collective-permute-done.2
  17.1 0.1 collective-permute-done.6
  17.2 3.2 %collective-permute-done.5 = bf16[336,128]{1,0:T(8,128)(2,1)S(1)} collective-permute-done((bf16[336,128]{1,0:T(8,128)(2,1)S(1)}, bf16[336,128]{1,0:T(8,128)(2,1)S(1)}, u32[]{:S(2)}, u32[]{:S(2)}) %collective-permute-start.5) | collective-permute-done | bytes 86048 | tf_op jit(solution)/shard_map/ppermute | solution.py:347
  20.5 1.6 %collective-permute-start.8 = (bf16[2,336,128]{2,1,0:T(8,128)(2,1)S(1)}, bf16[2,336,128]{2,1,0:T(8,128)(2,1)S(1)}, u32[]{:S(2)}, u32[]{:S(2)}) collective-permute-start(bf16[2,336,128]{2,1,0:T(8,128)(2,1)S(1)} %pad_maximum_fusion.7), channel_id=1, source_target_pairs={{0,4},{2,6},{4,0},{6,2},{1,5},{3,7},{5,1},{7,3},{8,12},{10,14},{12... | collective-permute-start | bytes 516104 | tf_op jit(solution)/shard_map/ppermute | solution.py:347
  22.1 1.6 %collective-permute-start.7 = (bf16[2,336,128]{2,1,0:T(8,128)(2,1)S(1)}, bf16[2,336,128]{2,1,0:T(8,128)(2,1)S(1)}, u32[]{:S(2)}, u32[]{:S(2)}) collective-permute-start(bf16[2,336,128]{2,1,0:T(8,128)(2,1)S(1)} %pad_maximum_fusion.6), channel_id=1, source_target_pairs={{0,2},{2,0},{4,6},{6,4},{1,3},{3,1},{5,7},{7,5},{8,10},{10,8},{12,... | collective-permute-start | bytes 516104 | tf_op jit(solution)/shard_map/ppermute | solution.py:347
  23.6 0.8 collective-permute-start.9
  24.4 2.0 %collective-permute-done.8 = bf16[2,336,128]{2,1,0:T(8,128)(2,1)S(1)} collective-permute-done((bf16[2,336,128]{2,1,0:T(8,128)(2,1)S(1)}, bf16[2,336,128]{2,1,0:T(8,128)(2,1)S(1)}, u32[]{:S(2)}, u32[]{:S(2)}) %collective-permute-start.8) | collective-permute-done | bytes 172064 | tf_op jit(solution)/shard_map/ppermute | solution.py:347
  26.5 1.3 collective-permute-done.7
  27.8 0.8 collective-permute-done.9
  28.6 0.5 collective-permute-start.12
  29.1 0.8 collective-permute-start.13
  29.9 3.6 %collective-permute-start.11 = (bf16[512,128]{1,0:T(8,128)(2,1)S(1)}, bf16[512,128]{1,0:T(8,128)(2,1)S(1)}, u32[]{:S(2)}, u32[]{:S(2)}) collective-permute-start(bf16[512,128]{1,0:T(8,128)(2,1)S(1)} %bitcast.55), channel_id=1, source_target_pairs={{0,24},{8,16},{16,8},{24,0},{1,25},{9,17},{17,9},{25,1},{2,26},{10... | collective-permute-start | bytes 393224 | tf_op jit(solution)/shard_map/ppermute | solution.py:347
  33.5 3.2 %collective-permute-done.11 = bf16[512,128]{1,0:T(8,128)(2,1)S(1)} collective-permute-done((bf16[512,128]{1,0:T(8,128)(2,1)S(1)}, bf16[512,128]{1,0:T(8,128)(2,1)S(1)}, u32[]{:S(2)}, u32[]{:S(2)}) %collective-permute-start.11) | collective-permute-done | bytes 131104 | tf_op jit(solution)/shard_map/ppermute | solution.py:347
  36.7 4.5 %collective-permute-done.10 = bf16[512,128]{1,0:T(8,128)(2,1)S(1)} collective-permute-done((bf16[512,128]{1,0:T(8,128)(2,1)S(1)}, bf16[512,128]{1,0:T(8,128)(2,1)S(1)}, u32[]{:S(2)}, u32[]{:S(2)}) %collective-permute-start.10) | collective-permute-done | bytes 131104 | tf_op jit(solution)/shard_map/ppermute | solution.py:347
  41.2 1.2 collective-permute-start.18
  42.5 1.6 %collective-permute-start.19 = (bf16[2,512,128]{2,1,0:T(8,128)(2,1)S(1)}, bf16[2,512,128]{2,1,0:T(8,128)(2,1)S(1)}, u32[]{:S(2)}, u32[]{:S(2)}) collective-permute-start(bf16[2,512,128]{2,1,0:T(8,128)(2,1)S(1)} %pad_maximum_fusion.5), channel_id=1, source_target_pairs={{0,4},{2,6},{4,0},{6,2},{1,5},{3,7},{5,1},{7,3},{8,12},{10,14},{12... | collective-permute-start | bytes 786440 | tf_op jit(solution)/shard_map/ppermute | solution.py:347
  44.1 3.6 %collective-permute-done.18 = bf16[2,512,128]{2,1,0:T(8,128)(2,1)S(1)} collective-permute-done((bf16[2,512,128]{2,1,0:T(8,128)(2,1)S(1)}, bf16[2,512,128]{2,1,0:T(8,128)(2,1)S(1)}, u32[]{:S(2)}, u32[]{:S(2)}) %collective-permute-start.18) | collective-permute-done | bytes 262176 | tf_op jit(solution)/shard_map/ppermute | solution.py:347
  47.7 1.5 %collective-permute-start.20 = (bf16[4,512,128]{2,1,0:T(8,128)(2,1)S(1)}, bf16[4,512,128]{2,1,0:T(8,128)(2,1)S(1)}, u32[]{:S(2)}, u32[]{:S(2)}) collective-permute-start(bf16[4,512,128]{2,1,0:T(8,128)(2,1)S(1)} %pad_maximum_fusion.rest_8_), channel_id=1, source_target_pairs={{0,4},{2,6},{4,0},{6,2},{1,5},{3,7},{5,1},{7,3},{8,12},{10,14},{12... | collective-permute-start | bytes 1572872 | tf_op jit(solution)/shard_map/ppermute | solution.py:347
  49.3 2.1 %collective-permute-done.19 = bf16[2,512,128]{2,1,0:T(8,128)(2,1)S(1)} collective-permute-done((bf16[2,512,128]{2,1,0:T(8,128)(2,1)S(1)}, bf16[2,512,128]{2,1,0:T(8,128)(2,1)S(1)}, u32[]{:S(2)}, u32[]{:S(2)}) %collective-permute-start.19) | collective-permute-done | bytes 262176 | tf_op jit(solution)/shard_map/ppermute | solution.py:347
  51.4 0.3 collective-permute-start.21
  51.7 0.5 collective-permute-start.15
  52.3 1.1 collective-permute-done.14.rest_4_
  53.4 0.1 collective-permute-start.22
  53.5 0.3 collective-permute-done.15.rest_5_
  53.8 0.1 collective-permute-start.23
  54.0 6.2 %collective-permute-done.20.rest_10_ = bf16[4,512,128]{2,1,0:T(8,128)(2,1)S(1)} collective-permute-done((bf16[4,512,128]{2,1,0:T(8,128)(2,1)S(1)}, bf16[4,512,128]{2,1,0:T(8,128)(2,1)S(1)}, u32[]{:S(2)}, u32[]{:S(2)}) %collective-permute-start.20) | collective-permute-done | bytes 524320 | tf_op jit(solution)/shard_map/ppermute | solution.py:347
  60.2 0.5 collective-permute-done.21.rest_11_
  60.7 0.8 copy-done.12
  61.5 0.5 collective-permute-start.17
  62.0 0.6 pad_add_fusion.own
  62.6 1.1 collective-permute-done.17.rest_7_
  63.7 0.7 copy-done.7
  64.5 0.2 copy-done.8
  64.7 72.0 %iterate.1 = f32[2,64,64]{2,1,0:T(8,128)} custom-call(s32[3]{0:T(128)} %pad_add_fusion.own, bf16[4,336,128]{2,1,0:T(8,128)(2,1)} %copy-done.3, bf16[4,336,128]{2,1,0:T(8,128)(2,1)} %copy-done.2, bf16[4,336,128]{2,1,0:T(8,128)(2,1)} %copy-done.9, bf16[4,336,128]{2,1,0:T(8,128)(2,1)} %collective-permute-done.13.rest_3_, bf16[4,336,128]{2,1,0:T(8,128)(2,1)} %copy-done.10, ...), custom_call_target="tpu_custom_call" | custom-call | tf_op jit(solution)/shard_map/iterate/pallas_call | solution.py:424
  136.7 1.5 %reshape.211 = f32[2,4096]{1,0:T(2,128)} reshape(f32[2,64,64]{2,1,0:T(8,128)} %iterate.1) | data formatting | bytes 65536 | tf_op jit(solution)/shard_map/reshape | solution.py:452
  (78 shorter events, 1.3 us)
Async XLA Ops:
  0.0 4.8 %copy-start.4 = (bf16[1,1,128,4096]{3,2,1,0:T(8,128)(2,1)S(1)}, bf16[1,1,128,4096]{3,2,1,0:T(8,128)(2,1)}, u32[]{:S(2)}) copy-start(bf16[1,1,128,4096]{3,2,1,0:T(8,128)(2,1)} %param.7) | copy-start | bytes 3145732
  0.7 1.6 %copy-start.16 = (s32[1,1,128]{2,1,0:T(1,128)S(1)}, s32[1,1,128]{2,1,0:T(1,128)}, u32[]{:S(2)}) copy-start(s32[1,1,128]{2,1,0:T(1,128)} %param.8) | copy-start | bytes 1540
  1.8 0.7 copy-start.17
  1.9 2.9 %collective-permute-start = (bf16[4,16,4096]{2,1,0:T(8,128)(2,1)S(1)}, bf16[4,16,4096]{2,1,0:T(8,128)(2,1)S(1)}, u32[]{:S(2)}, u32[]{:S(2)}) collective-permute-start(bf16[4,16,4096]{2,1,0:T(8,128)(2,1)S(1)} %select_bitcast_fusion), channel_id=1, source_target_pairs={{0,1},{1,0},{2,3},{3,2},{4,5},{5,4},{6,7},{7,6},{8,9},{9,8},{10,11... | collective-permute-start | bytes 1572872 | tf_op jit(solution)/shard_map/ppermute | solution.py:347
  2.5 0.7 copy-start.15
  3.2 0.7 copy-start.14
  3.9 0.8 copy-start.13
  4.9 9.1 %collective-permute-start.1 = (bf16[16,4096]{1,0:T(8,128)(2,1)S(1)}, bf16[16,4096]{1,0:T(8,128)(2,1)S(1)}, u32[]{:S(2)}, u32[]{:S(2)}) collective-permute-start(bf16[16,4096]{1,0:T(8,128)(2,1)S(1)} %get-tuple-element.37), channel_id=1, source_target_pairs={{0,2},{2,0},{4,6},{6,4},{1,3},{3,1},{5,7},{7,5},{8,10},{10,8},{12,... | collective-permute-start | bytes 393224 | tf_op jit(solution)/shard_map/ppermute | solution.py:347
  7.9 7.7 %collective-permute-start.3 = (bf16[16,4096]{1,0:T(8,128)(2,1)S(1)}, bf16[16,4096]{1,0:T(8,128)(2,1)S(1)}, u32[]{:S(2)}, u32[]{:S(2)}) collective-permute-start(bf16[16,4096]{1,0:T(8,128)(2,1)S(1)} %get-tuple-element.38), channel_id=1, source_target_pairs={{0,6},{2,4},{4,2},{6,0},{1,7},{3,5},{5,3},{7,1},{8,14},{10,12},{12... | collective-permute-start | bytes 393224 | tf_op jit(solution)/shard_map/ppermute | solution.py:347
  9.4 7.6 %collective-permute-start.2 = (bf16[16,4096]{1,0:T(8,128)(2,1)S(1)}, bf16[16,4096]{1,0:T(8,128)(2,1)S(1)}, u32[]{:S(2)}, u32[]{:S(2)}) collective-permute-start(bf16[16,4096]{1,0:T(8,128)(2,1)S(1)} %get-tuple-element.39), channel_id=1, source_target_pairs={{0,4},{2,6},{4,0},{6,2},{1,5},{3,7},{5,1},{7,3},{8,12},{10,14},{12... | collective-permute-start | bytes 393224 | tf_op jit(solution)/shard_map/ppermute | solution.py:347
  9.8 7.4 %collective-permute-start.6 = (bf16[336,128]{1,0:T(8,128)(2,1)S(1)}, bf16[336,128]{1,0:T(8,128)(2,1)S(1)}, u32[]{:S(2)}, u32[]{:S(2)}) collective-permute-start(bf16[336,128]{1,0:T(8,128)(2,1)S(1)} %concatenate.45), channel_id=1, source_target_pairs={{0,24},{8,16},{16,8},{24,0},{1,25},{9,17},{17,9},{25,1},{2,26},{10... | collective-permute-start | bytes 258056 | tf_op jit(solution)/shard_map/ppermute | solution.py:347
  14.0 6.5 %collective-permute-start.5 = (bf16[336,128]{1,0:T(8,128)(2,1)S(1)}, bf16[336,128]{1,0:T(8,128)(2,1)S(1)}, u32[]{:S(2)}, u32[]{:S(2)}) collective-permute-start(bf16[336,128]{1,0:T(8,128)(2,1)S(1)} %concatenate.45), channel_id=1, source_target_pairs={{0,16},{8,24},{16,0},{24,8},{1,17},{9,25},{17,1},{25,9},{2,18},{10... | collective-permute-start | bytes 258056 | tf_op jit(solution)/shard_map/ppermute | solution.py:347
  14.0 6.5 %collective-permute-start.4 = (bf16[336,128]{1,0:T(8,128)(2,1)S(1)}, bf16[336,128]{1,0:T(8,128)(2,1)S(1)}, u32[]{:S(2)}, u32[]{:S(2)}) collective-permute-start(bf16[336,128]{1,0:T(8,128)(2,1)S(1)} %concatenate.45), channel_id=1, source_target_pairs={{0,8},{8,0},{16,24},{24,16},{1,9},{9,1},{17,25},{25,17},{2,10},{10... | collective-permute-start | bytes 258056 | tf_op jit(solution)/shard_map/ppermute | solution.py:347
  20.5 6.0 %collective-permute-start.8 = (bf16[2,336,128]{2,1,0:T(8,128)(2,1)S(1)}, bf16[2,336,128]{2,1,0:T(8,128)(2,1)S(1)}, u32[]{:S(2)}, u32[]{:S(2)}) collective-permute-start(bf16[2,336,128]{2,1,0:T(8,128)(2,1)S(1)} %pad_maximum_fusion.7), channel_id=1, source_target_pairs={{0,4},{2,6},{4,0},{6,2},{1,5},{3,7},{5,1},{7,3},{8,12},{10,14},{12... | collective-permute-start | bytes 516104 | tf_op jit(solution)/shard_map/ppermute | solution.py:347
  22.1 5.7 %collective-permute-start.7 = (bf16[2,336,128]{2,1,0:T(8,128)(2,1)S(1)}, bf16[2,336,128]{2,1,0:T(8,128)(2,1)S(1)}, u32[]{:S(2)}, u32[]{:S(2)}) collective-permute-start(bf16[2,336,128]{2,1,0:T(8,128)(2,1)S(1)} %pad_maximum_fusion.6), channel_id=1, source_target_pairs={{0,2},{2,0},{4,6},{6,4},{1,3},{3,1},{5,7},{7,5},{8,10},{10,8},{12,... | collective-permute-start | bytes 516104 | tf_op jit(solution)/shard_map/ppermute | solution.py:347
  23.6 5.0 %collective-permute-start.9 = (bf16[512,128]{1,0:T(8,128)(2,1)S(1)}, bf16[512,128]{1,0:T(8,128)(2,1)S(1)}, u32[]{:S(2)}, u32[]{:S(2)}) collective-permute-start(bf16[512,128]{1,0:T(8,128)(2,1)S(1)} %bitcast.54), channel_id=1, source_target_pairs={{0,8},{8,0},{16,24},{24,16},{1,9},{9,1},{17,25},{25,17},{2,10},{10... | collective-permute-start | bytes 393224 | tf_op jit(solution)/shard_map/ppermute | solution.py:347
  26.5 25.2 %copy-start.2 = (bf16[4,336,128]{2,1,0:T(8,128)(2,1)}, bf16[4,336,128]{2,1,0:T(8,128)(2,1)S(1)}, u32[]{:S(2)}) copy-start(bf16[4,336,128]{2,1,0:T(8,128)(2,1)S(1)} %pad_maximum_fusion.3.rest_1_) | copy-start | bytes 1032196
  27.8 23.9 %copy-start.3 = (bf16[4,336,128]{2,1,0:T(8,128)(2,1)}, bf16[4,336,128]{2,1,0:T(8,128)(2,1)S(1)}, u32[]{:S(2)}) copy-start(bf16[4,336,128]{2,1,0:T(8,128)(2,1)S(1)} %pad_maximum_fusion.2.rest_0_) | copy-start | bytes 1032196
  28.6 12.6 %collective-permute-start.12 = (bf16[4,336,128]{2,1,0:T(8,128)(2,1)S(1)}, bf16[4,336,128]{2,1,0:T(8,128)(2,1)S(1)}, u32[]{:S(2)}, u32[]{:S(2)}) collective-permute-start(bf16[4,336,128]{2,1,0:T(8,128)(2,1)S(1)} %pad_maximum_fusion.2.rest_0_), channel_id=1, source_target_pairs={{0,4},{2,6},{4,0},{6,2},{1,5},{3,7},{5,1},{7,3},{8,12},{10,14},{12... | collective-permute-start | bytes 1032200 | tf_op jit(solution)/shard_map/ppermute | solution.py:347
  29.1 12.1 %collective-permute-start.13 = (bf16[4,336,128]{2,1,0:T(8,128)(2,1)S(1)}, bf16[4,336,128]{2,1,0:T(8,128)(2,1)}, u32[]{:S(2)}, u32[]{:S(2)}) collective-permute-start(bf16[4,336,128]{2,1,0:T(8,128)(2,1)S(1)} %pad_maximum_fusion.3.rest_1_), channel_id=1, source_target_pairs={{0,2},{2,0},{4,6},{6,4},{1,3},{3,1},{5,7},{7,5},{8,10},{10,8},{12,... | collective-permute-start | bytes 1032200 | tf_op jit(solution)/shard_map/ppermute | solution.py:347
  29.9 6.8 %collective-permute-start.11 = (bf16[512,128]{1,0:T(8,128)(2,1)S(1)}, bf16[512,128]{1,0:T(8,128)(2,1)S(1)}, u32[]{:S(2)}, u32[]{:S(2)}) collective-permute-start(bf16[512,128]{1,0:T(8,128)(2,1)S(1)} %bitcast.55), channel_id=1, source_target_pairs={{0,24},{8,16},{16,8},{24,0},{1,25},{9,17},{17,9},{25,1},{2,26},{10... | collective-permute-start | bytes 393224 | tf_op jit(solution)/shard_map/ppermute | solution.py:347
  33.5 7.7 %collective-permute-start.10 = (bf16[512,128]{1,0:T(8,128)(2,1)S(1)}, bf16[512,128]{1,0:T(8,128)(2,1)S(1)}, u32[]{:S(2)}, u32[]{:S(2)}) collective-permute-start(bf16[512,128]{1,0:T(8,128)(2,1)S(1)} %bitcast.56), channel_id=1, source_target_pairs={{0,16},{8,24},{16,0},{24,8},{1,17},{9,25},{17,1},{25,9},{2,18},{10... | collective-permute-start | bytes 393224 | tf_op jit(solution)/shard_map/ppermute | solution.py:347
  41.2 11.0 %copy-start.9 = (bf16[4,336,128]{2,1,0:T(8,128)(2,1)}, bf16[4,336,128]{2,1,0:T(8,128)(2,1)S(1)}, u32[]{:S(2)}) copy-start(bf16[4,336,128]{2,1,0:T(8,128)(2,1)S(1)} %collective-permute-done.12.rest_2_) | copy-start | bytes 1032196
  41.2 6.4 %collective-permute-start.18 = (bf16[2,512,128]{2,1,0:T(8,128)(2,1)S(1)}, bf16[2,512,128]{2,1,0:T(8,128)(2,1)S(1)}, u32[]{:S(2)}, u32[]{:S(2)}) collective-permute-start(bf16[2,512,128]{2,1,0:T(8,128)(2,1)S(1)} %pad_maximum_fusion.4), channel_id=1, source_target_pairs={{0,2},{2,0},{4,6},{6,4},{1,3},{3,1},{5,7},{7,5},{8,10},{10,8},{12,... | collective-permute-start | bytes 786440 | tf_op jit(solution)/shard_map/ppermute | solution.py:347
  42.5 8.9 %collective-permute-start.19 = (bf16[2,512,128]{2,1,0:T(8,128)(2,1)S(1)}, bf16[2,512,128]{2,1,0:T(8,128)(2,1)S(1)}, u32[]{:S(2)}, u32[]{:S(2)}) collective-permute-start(bf16[2,512,128]{2,1,0:T(8,128)(2,1)S(1)} %pad_maximum_fusion.5), channel_id=1, source_target_pairs={{0,4},{2,6},{4,0},{6,2},{1,5},{3,7},{5,1},{7,3},{8,12},{10,14},{12... | collective-permute-start | bytes 786440 | tf_op jit(solution)/shard_map/ppermute | solution.py:347
  47.7 5.6 %copy-start = (bf16[4,512,128]{2,1,0:T(8,128)(2,1)}, bf16[4,512,128]{2,1,0:T(8,128)(2,1)S(1)}, u32[]{:S(2)}) copy-start(bf16[4,512,128]{2,1,0:T(8,128)(2,1)S(1)} %pad_maximum_fusion.rest_8_) | copy-start | bytes 1572868
  47.7 12.4 %collective-permute-start.20 = (bf16[4,512,128]{2,1,0:T(8,128)(2,1)S(1)}, bf16[4,512,128]{2,1,0:T(8,128)(2,1)S(1)}, u32[]{:S(2)}, u32[]{:S(2)}) collective-permute-start(bf16[4,512,128]{2,1,0:T(8,128)(2,1)S(1)} %pad_maximum_fusion.rest_8_), channel_id=1, source_target_pairs={{0,4},{2,6},{4,0},{6,2},{1,5},{3,7},{5,1},{7,3},{8,12},{10,14},{12... | collective-permute-start | bytes 1572872 | tf_op jit(solution)/shard_map/ppermute | solution.py:347
  51.4 12.3 %copy-start.1 = (bf16[4,512,128]{2,1,0:T(8,128)(2,1)}, bf16[4,512,128]{2,1,0:T(8,128)(2,1)S(1)}, u32[]{:S(2)}) copy-start(bf16[4,512,128]{2,1,0:T(8,128)(2,1)S(1)} %pad_maximum_fusion.1.rest_9_) | copy-start | bytes 1572868
  51.4 9.2 %collective-permute-start.21 = (bf16[4,512,128]{2,1,0:T(8,128)(2,1)S(1)}, bf16[4,512,128]{2,1,0:T(8,128)(2,1)S(1)}, u32[]{:S(2)}, u32[]{:S(2)}) collective-permute-start(bf16[4,512,128]{2,1,0:T(8,128)(2,1)S(1)} %pad_maximum_fusion.1.rest_9_), channel_id=1, source_target_pairs={{0,2},{2,0},{4,6},{6,4},{1,3},{3,1},{5,7},{7,5},{8,10},{10,8},{12,... | collective-permute-start | bytes 1572872 | tf_op jit(solution)/shard_map/ppermute | solution.py:347
  51.7 1.7 %collective-permute-start.14 = (bf16[4,336,128]{2,1,0:T(8,128)(2,1)S(1)}, bf16[4,336,128]{2,1,0:T(8,128)(2,1)S(1)}, u32[]{:S(2)}, u32[]{:S(2)}) collective-permute-start(bf16[4,336,128]{2,1,0:T(8,128)(2,1)S(1)} %pad_maximum_fusion.2.rest_0_), channel_id=1, source_target_pairs={{0,1},{1,0},{2,3},{3,2},{4,5},{5,4},{6,7},{7,6},{8,9},{9,8},{10,11... | collective-permute-start | bytes 1032200 | tf_op jit(solution)/shard_map/ppermute | solution.py:347
  51.7 2.1 %collective-permute-start.15 = (bf16[4,336,128]{2,1,0:T(8,128)(2,1)S(1)}, bf16[4,336,128]{2,1,0:T(8,128)(2,1)S(1)}, u32[]{:S(2)}, u32[]{:S(2)}) collective-permute-start(bf16[4,336,128]{2,1,0:T(8,128)(2,1)S(1)} %pad_maximum_fusion.3.rest_1_), channel_id=1, source_target_pairs={{0,1},{1,0},{2,3},{3,2},{4,5},{5,4},{6,7},{7,6},{8,9},{9,8},{10,11... | collective-permute-start | bytes 1032200 | tf_op jit(solution)/shard_map/ppermute | solution.py:347
  52.2 8.5 %collective-permute-start.16 = (bf16[4,336,128]{2,1,0:T(8,128)(2,1)S(1)}, bf16[4,336,128]{2,1,0:T(8,128)(2,1)S(1)}, u32[]{:S(2)}, u32[]{:S(2)}) collective-permute-start(bf16[4,336,128]{2,1,0:T(8,128)(2,1)S(1)} %collective-permute-done.12.rest_2_), channel_id=1, source_target_pairs={{0,1},{1,0},{2,3},{3,2},{4,5},{5,4},{6,7},{7,6},{8,9},{9,8},{10,11... | collective-permute-start | bytes 1032200 | tf_op jit(solution)/shard_map/ppermute | solution.py:347
  53.4 7.3 %copy-start.10 = (bf16[4,336,128]{2,1,0:T(8,128)(2,1)}, bf16[4,336,128]{2,1,0:T(8,128)(2,1)S(1)}, u32[]{:S(2)}) copy-start(bf16[4,336,128]{2,1,0:T(8,128)(2,1)S(1)} %collective-permute-done.14.rest_4_) | copy-start | bytes 1032196
  53.4 10.3 %collective-permute-start.22 = (bf16[4,512,128]{2,1,0:T(8,128)(2,1)S(1)}, bf16[4,512,128]{2,1,0:T(8,128)(2,1)S(1)}, u32[]{:S(2)}, u32[]{:S(2)}) collective-permute-start(bf16[4,512,128]{2,1,0:T(8,128)(2,1)S(1)} %pad_maximum_fusion.rest_8_), channel_id=1, source_target_pairs={{0,1},{1,0},{2,3},{3,2},{4,5},{5,4},{6,7},{7,6},{8,9},{9,8},{10,11... | collective-permute-start | bytes 1572872 | tf_op jit(solution)/shard_map/ppermute | solution.py:347
  53.8 6.9 %copy-start.11 = (bf16[4,336,128]{2,1,0:T(8,128)(2,1)}, bf16[4,336,128]{2,1,0:T(8,128)(2,1)S(1)}, u32[]{:S(2)}) copy-start(bf16[4,336,128]{2,1,0:T(8,128)(2,1)S(1)} %collective-permute-done.15.rest_5_) | copy-start | bytes 1032196
  53.8 9.8 %collective-permute-start.23 = (bf16[4,512,128]{2,1,0:T(8,128)(2,1)S(1)}, bf16[4,512,128]{2,1,0:T(8,128)(2,1)S(1)}, u32[]{:S(2)}, u32[]{:S(2)}) collective-permute-start(bf16[4,512,128]{2,1,0:T(8,128)(2,1)S(1)} %pad_maximum_fusion.1.rest_9_), channel_id=1, source_target_pairs={{0,1},{1,0},{2,3},{3,2},{4,5},{5,4},{6,7},{7,6},{8,9},{9,8},{10,11... | collective-permute-start | bytes 1572872 | tf_op jit(solution)/shard_map/ppermute | solution.py:347
  60.2 3.6 %copy-start.5 = (bf16[4,512,128]{2,1,0:T(8,128)(2,1)}, bf16[4,512,128]{2,1,0:T(8,128)(2,1)S(1)}, u32[]{:S(2)}) copy-start(bf16[4,512,128]{2,1,0:T(8,128)(2,1)S(1)} %collective-permute-done.20.rest_10_) | copy-start | bytes 1572868
  60.2 3.5 %collective-permute-start.24 = (bf16[4,512,128]{2,1,0:T(8,128)(2,1)S(1)}, bf16[4,512,128]{2,1,0:T(8,128)(2,1)}, u32[]{:S(2)}, u32[]{:S(2)}) collective-permute-start(bf16[4,512,128]{2,1,0:T(8,128)(2,1)S(1)} %collective-permute-done.20.rest_10_), channel_id=1, source_target_pairs={{0,1},{1,0},{2,3},{3,2},{4,5},{5,4},{6,7},{7,6},{8,9},{9,8},{10,11... | collective-permute-start | bytes 1572872 | tf_op jit(solution)/shard_map/ppermute | solution.py:347
  60.7 3.1 %copy-start.6 = (bf16[4,512,128]{2,1,0:T(8,128)(2,1)}, bf16[4,512,128]{2,1,0:T(8,128)(2,1)S(1)}, u32[]{:S(2)}) copy-start(bf16[4,512,128]{2,1,0:T(8,128)(2,1)S(1)} %collective-permute-done.21.rest_11_) | copy-start | bytes 1572868
  60.7 3.0 %collective-permute-start.25 = (bf16[4,512,128]{2,1,0:T(8,128)(2,1)S(1)}, bf16[4,512,128]{2,1,0:T(8,128)(2,1)}, u32[]{:S(2)}, u32[]{:S(2)}) collective-permute-start(bf16[4,512,128]{2,1,0:T(8,128)(2,1)S(1)} %collective-permute-done.21.rest_11_), channel_id=1, source_target_pairs={{0,1},{1,0},{2,3},{3,2},{4,5},{5,4},{6,7},{7,6},{8,9},{9,8},{10,11... | collective-permute-start | bytes 1572872 | tf_op jit(solution)/shard_map/ppermute | solution.py:347
  60.7 0.8 copy-start.12
  61.5 2.2 %collective-permute-start.17 = (bf16[4,336,128]{2,1,0:T(8,128)(2,1)}, bf16[4,336,128]{2,1,0:T(8,128)(2,1)}, u32[]{:S(2)}, u32[]{:S(2)}) collective-permute-start(bf16[4,336,128]{2,1,0:T(8,128)(2,1)} %collective-permute-done.13.rest_3_), channel_id=1, source_target_pairs={{0,1},{1,0},{2,3},{3,2},{4,5},{5,4},{6,7},{7,6},{8,9},{9,8},{10,11... | collective-permute-start | bytes 1032200 | tf_op jit(solution)/shard_map/ppermute | solution.py:347
  63.7 0.8 copy-start.7
  63.7 1.0 copy-start.8

commit v7 on v6

--- a/solution.py
+++ b/solution.py
@@ -111,7 +111,7 @@
     return jnp.where(left, first[2 * q], second[2 * q + 1]) + pltpu.roll(apart, 64, 1)
 
 
-def add_products(n_group, blk, dims, from_list, source, to_list, first, second):
+def add_products(n_group, blk, dims, lists, from_at, source, to_at, first, second):
     left = left_half(source.shape[1:])
 
     def group(i, carry):
@@ -119,14 +119,14 @@
             pairs = [i * UNROLL + at + u for u in range(BATCH)]
             prods = [
                 dot(
-                    jnp.where(left, source[from_list[2 * p]], source[from_list[2 * p + 1]]),
+                    jnp.where(left, source[lists[from_at + 2 * p]], source[lists[from_at + 2 * p + 1]]),
                     blk[p],
                     dims,
                 )
                 for p in pairs
             ]
             for p, prod in zip(pairs, prods):
-                a, b = to_list[2 * p], to_list[2 * p + 1]
+                a, b = lists[to_at + 2 * p], lists[to_at + 2 * p + 1]
                 first[a] = first[a] + prod
                 second[b] = second[b] + prod
         return carry
@@ -134,7 +134,9 @@
     lax.fori_loop(0, n_group, group, 0)
 
 
-def unpack(n_row, n_col, own, copies, lv, lw, nums, place, blk, vs, vd, rm, ic, ints, meta, sem, small):
+def unpack(
+    n_row, n_col, own, mine, other, lists, place, blk, vs, vd, rm, ic, ints, meta, sems, small
+):
     n_dev = n_row * n_col
     k = vs.shape[1]
     half = k // 2
@@ -142,13 +144,15 @@
     vec_at = OFF_CAP * half
     meta_at = vec_at + k
     at_device, device_at = place_of(own, n_row, n_dev)
-
-    for copy in copies:
+    slots = 2 * blk.shape[0]
+
+    first, second = pl.ds(0, n_dev // 2), pl.ds(n_dev // 2, n_dev // 2)
+    for copy in copy_in([(mine, small.at[first]), (other, small.at[second])], sems):
         copy.wait()
     for d in range(n_dev):
         rows = small[d, meta_at : meta_at + META, :].astype(jnp.float32)
         ints[d : d + 1, :] = rows[8:9].astype(jnp.int32)
-    to_scalars = pltpu.make_async_copy(ints, meta, sem)
+    to_scalars = pltpu.make_async_copy(ints, meta, sems.at[2])
     to_scalars.start()
 
     for r in range(n_row):
@@ -167,8 +171,8 @@
         count = jnp.where(count > OFF_CAP, 0, count)
         r, c = device_at(d)
         for s in range(OFF_CAP):
-            lv[n + s] = c * cblk + meta[d, OFF_CAP + s]
-            lw[n + s] = r * rblk + meta[d, s]
+            lists[n + s] = c * cblk + meta[d, OFF_CAP + s]
+            lists[slots + n + s] = r * rblk + meta[d, s]
             x = small[d, s * half : (s + 1) * half, :].astype(jnp.float32)
             turned = pltpu.roll(x, 64, 1)
             side = (n + s) % 2
@@ -182,27 +186,26 @@
 
     n_live = lax.fori_loop(0, n_dev, device, jnp.int32(0))
     for u in range(2 * UNROLL - 1):
-        lv[n_live + u] = 0
-        lw[n_live + u] = 0
+        lists[n_live + u] = 0
+        lists[slots + n_live + u] = 0
         at = pl.multiple_of((n_live + u) % 2 * k, k)
         blk[(n_live + u) // 2, pl.ds(at, k), :] = jnp.zeros((k, 128), jnp.bfloat16)
-    nums[0] = (n_live + 2 * UNROLL - 1) // (2 * UNROLL)
+    lists[2 * slots] = (n_live + 2 * UNROLL - 1) // (2 * UNROLL)
 
     for r in range(n_row):
         h = jnp.int32(0)
         for c in range(n_col):
             h = jnp.where(meta[at_device(r, c), 2 * OFF_CAP] > OFF_CAP, c, h)
-        nums[1 + r] = h
+        lists[2 * slots + 1 + r] = h
         index = small[at_device(r, h), meta_at : meta_at + META, :].astype(jnp.float32)
         place[r : r + 1, :] = index[7:8] * float(rblk) + index[6:7]
 
 
-def iterate(n_row, n_col, n_cap, total, own, *rest):
-    smalls, fulls, out = rest[:8], rest[8:16], rest[16]
-    sems, full, tmp, home = rest[17:21]
-    unpacked, rest = rest[21:33], rest[33:]
-    lv, lw, nums, place, blk, vs, vd, rm, ic, ints, meta, small = unpacked
-    w, w1, w2, wt, wd, y, y1, y2, ph, linv = rest
+def iterate(n_row, n_col, n_cap, total, own, lists, place, *rest):
+    sources, fulls, out = rest[:5], rest[5:13], rest[13]
+    sems, full, tmp, home, blk, vs, vd, rm, ic = rest[14:23]
+    w, w1, w2, wt, wd, y, y1, y2, ph, linv = rest[23:]
+    slots = 2 * blk.shape[0]
     n_dev = n_row * n_col
     k = vs.shape[1]
     half = k // 2
@@ -219,19 +222,15 @@
             at += ref.shape[0]
         return pairs
 
-    copies = copy_in(laid_out(smalls, small) + laid_out(fulls, full), sems)
-    unpack(
-        n_row, n_col, own, copies[:8],
-        lv, lw, nums, place, blk, vs, vd, rm, ic, ints, meta, sems.at[len(copies)], small,
-    )
-    n_group = nums[0]
-    for copy in copies[8:]:
+    copies = copy_in(laid_out(fulls, full) + list(zip(sources, (blk, vs, vd, rm, ic))), sems)
+    for copy in copies[: len(fulls)]:
         copy.wait()
+    n_group = lists[2 * slots]
 
     left = lax.broadcasted_iota(jnp.int32, (rblk, 128), 1) < 64
     homes = []
     for r in range(n_row):
-        homes.append(nums[1 + r])
+        homes.append(lists[2 * slots + 1 + r])
         want = lax.broadcasted_iota(jnp.int32, (cblk * rblk, n_cap), 0).astype(jnp.float32)
         select = jnp.where(want == place[r : r + 1, :], 1.0, 0.0).astype(jnp.bfloat16)
 
@@ -252,7 +251,7 @@
                 tmp[u, pl.ds(m + half, rblk, stride=k), :] = odd
             return carry
 
-        lax.fori_loop(0, half, build, 0, unroll=4)
+        lax.fori_loop(0, half, build, 0, unroll=8)
 
         def cut(i, carry, r=r):
             at = pl.multiple_of(i * k, k)
@@ -262,7 +261,7 @@
                 home[r, pl.ds(at, k), width + u * 128 : width + (u + 1) * 128] = lo
             return carry
 
-        lax.fori_loop(0, rblk, cut, 0, unroll=4)
+        lax.fori_loop(0, rblk, cut, 0, unroll=8)
 
     def clear(refs):
         for ref in refs:
@@ -270,6 +269,8 @@
                 ref[q] = jnp.zeros_like(ref[q])
 
     clear([y, y1, y2, w1, w2])
+    for copy in copies[len(fulls) :]:
+        copy.wait()
 
     def iteration(it, carry):
         @pl.when(it > 0)
@@ -292,7 +293,7 @@
                 w[r * rpairs + p] = prod[:, :128]
                 w[r * rpairs + p + 1] = prod[:, 128:]
 
-        add_products(n_group, blk, NT, lv, vd, lw, w1, w2)
+        add_products(n_group, blk, NT, lists, 0, vd, slots, w1, w2)
         for p in range(n_dev):
             x = w[p] + gather_pair(p, w1, w2)
             store_twice(wt, wd, p, x * rm[p, 0:1, :])
@@ -307,7 +308,7 @@
                 y[base + u] = y[base + u] + prod[:, :128]
                 y[base + u + 1] = y[base + u + 1] + prod[:, 128:]
 
-        add_products(n_group, blk, NN, lw, wd, lv, y1, y2)
+        add_products(n_group, blk, NN, lists, slots, wd, 0, y1, y2)
 
         both = jnp.zeros((2 * k, k), jnp.float32)
         for q in range(0, n_dev, 4):
@@ -331,9 +332,14 @@
     lh, ll = split2(linv[...])
     q = (2 * own[1] + own[2]) * n_row + own[0]
     hi, lo = ph[q, :k, :], ph[q, k:, :]
-    x = dot(lh, hi) + dot(ll, hi) + dot(lh, lo)
-    out[0] = x[:, :k]
-    out[1] = x[:, k:]
+    w[0] = dot(lh, hi) + dot(ll, hi) + dot(lh, lo)
+    even, odd = w[0, pl.ds(0, half, stride=2), :], w[0, pl.ds(1, half, stride=2), :]
+    left = left_half(even.shape)
+    first = jnp.where(left, even, pltpu.roll(odd, 64, 1))
+    second = jnp.where(left, pltpu.roll(even, 64, 1), odd)
+    for i in range(half):
+        out[0:1, i * 128 : (i + 1) * 128] = first[i : i + 1]
+        out[1:2, i * 128 : (i + 1) * 128] = second[i : i + 1]
 
 
 def split3(x):
@@ -411,36 +417,52 @@
     home, smalls = together((home, along_rows(small)))
     homes, smalls = along_rows(home), along_one_chip_axis(smalls)
     smalls, homes[1] = together((smalls, homes[1]))
-    homes, smalls = together((homes, smalls + along_other_chip_axis(smalls)))
-    homes = along_one_chip_axis(homes)
-    homes = homes + along_other_chip_axis(homes)
-    smalls, homes = ([*v, *(swap(x, "core", 1) for x in v)] for v in (smalls, homes))
+    smalls = jnp.concatenate(smalls + along_other_chip_axis(smalls))
+    homes, smalls = together((homes, smalls))
+    homes, others = together((along_one_chip_axis(homes), swap(smalls, "core", 1)))
+    last = along_other_chip_axis(homes)
 
     where = jnp.stack([row, chip, core]).astype(jnp.int32)
     height, width = 2 * n_col * bsize, 2 * n_row * bsize
     slots = n_dev * OFF_CAP + 2 * UNROLL
     f32, i32, vmem, smem = jnp.float32, jnp.int32, pltpu.VMEM, pltpu.SMEM
     pair, twice, mass = (n_dev, k, 128), (2 * n_dev, k, 128), (n_dev, 8, 128)
-    result = pl.pallas_call(
+    smem_spec, vmem_spec, any_spec = (pl.BlockSpec(memory_space=m) for m in (smem, vmem, pl.ANY))
+    arrays = [
+        ((8, 128), f32), ((slots // 2, 128, 128), bf16), (pair, bf16), (twice, bf16), (mass, f32), (mass, f32),
+    ]
+    lists, *unpacked = pl.pallas_call(
+        functools.partial(unpack, n_row, n_col),
+        out_shape=[jax.ShapeDtypeStruct((2 * slots + 8,), i32)]
+        + [jax.ShapeDtypeStruct(*v) for v in arrays],
+        in_specs=[smem_spec, any_spec, any_spec],
+        out_specs=[smem_spec] + [vmem_spec] * len(arrays),
+        scratch_shapes=[
+            vmem((n_dev, 128), i32),
+            smem((n_dev, 128), i32),
+            pltpu.SemaphoreType.DMA((3,)),
+            vmem((n_dev,) + small.shape, bf16),
+        ],
+        compiler_params=pltpu.CompilerParams(vmem_limit_bytes=VMEM_LIMIT),
+        cost_estimate=pl.CostEstimate(
+            flops=0, bytes_accessed=4 * n_dev * small.size * 2, transcendentals=0
+        ),
+        name="unpack",
+    )(where, smalls, others)
+    last, lists = together((last, lists))
+    mine = homes + last
+    fulls = mine + [swap(v, "core", 1) for v in mine]
+    return pl.pallas_call(
         functools.partial(iterate, n_row, n_col, n_cap, float(n_dev * own * bsize)),
-        out_shape=jax.ShapeDtypeStruct((own, k, bsize), f32),
-        in_specs=[pl.BlockSpec(memory_space=smem)]
-        + [pl.BlockSpec(memory_space=pl.ANY)] * (len(smalls) + len(homes)),
-        out_specs=pl.BlockSpec(memory_space=vmem),
+        out_shape=jax.ShapeDtypeStruct((own, k * bsize), f32),
+        in_specs=[smem_spec] * 2 + [vmem_spec] + [any_spec] * (5 + len(fulls)),
+        out_specs=vmem_spec,
         scratch_shapes=[
-            pltpu.SemaphoreType.DMA((len(smalls) + len(homes) + 1,)),
+            pltpu.SemaphoreType.DMA((5 + len(fulls),)),
             vmem((n_dev,) + home.shape, bf16),
             vmem((n_row, height, 128), f32),
             vmem((n_row, height, 2 * width), bf16),
-            smem((slots,), i32),
-            smem((slots,), i32),
-            smem((1 + n_row,), i32),
-            vmem((8, 128), f32),
-            vmem((slots // 2, 128, 128), bf16),
-            vmem(pair, bf16), vmem(twice, bf16), vmem(mass, f32), vmem(mass, f32),
-            vmem((n_dev, 128), i32),
-            smem((n_dev, 128), i32),
-            vmem((n_dev,) + small.shape, bf16),
+            *[vmem(*v) for v in arrays[1:]],
             vmem(pair, f32), vmem(twice, f32), vmem(twice, f32), vmem(pair, bf16), vmem(twice, bf16),
             vmem(pair, f32), vmem(twice, f32), vmem(twice, f32),
             vmem((n_dev, 2 * k, 128), bf16),
@@ -448,8 +470,7 @@
         ],
         compiler_params=pltpu.CompilerParams(vmem_limit_bytes=VMEM_LIMIT),
         name="iterate",
-    )(where, *smalls, *homes)
-    return result.reshape(own, k * bsize)
+    )(where, lists, *unpacked, *fulls)
 
 
 def rotate(projected, gram):

time: 140 us -> 135 us (0.964); the launches traced: 138 us -> 135 us
  waiting for transfers between devices: 32.4 us -> 24.2 us
  Pallas kernels: 72 us -> 74.3 us
  starting transfers between devices: 24.6 us -> 26.4 us
  other arithmetic: 2.14 us -> 3.64 us
    pallas_call x0 -> x1, Pallas kernels: none -> 9.95 us  [whole_on_each(): pl.pallas_call(functools.partial(unpack, n_row, n_col), out_shape=[jax.Sh...]
    ppermute x26 -> x23, waiting for transfers between devices: 32.4 us -> 24.2 us  [swap(): return lax.ppermute(x, axis, [(i, i ^ distance) for i in range(size)])]
    pallas_call x1, Pallas kernels: 72 us -> 64.4 us  [whole_on_each(): pl.pallas_call(functools.partial(iterate, n_row, n_col, n_cap, float(n_de...]
    ppermute x26 -> x23, starting transfers between devices: 24.6 us -> 26.4 us  [swap(): return lax.ppermute(x, axis, [(i, i ^ distance) for i in range(size)])]
    unnamed x37 -> x23, local copies, waits for them, and re-layouts: 3.65 us -> 2.01 us
    reshape x1 -> x0, local copies, waits for them, and re-layouts: 1.55 us -> none  [whole_on_each(): return result.reshape(own, k * bsize)]
  transfers between devices with their start and end apart: 26 -> 23, of which waited for: 16 -> 13; matrix products, arithmetic and copies ran while one was open for 1% -> 4% of each run, Pallas kernels for 0% -> 7%
where the time goes in v7:
time: 135 us
  Pallas kernels  74.3 us (55%)
  starting transfers between devices  26.4 us (20%)
  waiting for transfers between devices  24.2 us (18%)
  local copies, waits for them, and re-layouts  4.97 us (4%)
  other arithmetic  3.64 us (3%)
    pallas_call x1, Pallas kernels, whole_on_each(): pl.pallas_call(functools.partial(iterate, n_row, n_col, n_cap, float(n_de...  64.4 us
    ppermute x23, starting transfers between devices, swap(): return lax.ppermute(x, axis, [(i, i ^ distance) for i in range(size)])  26.4 us
    ppermute x23, waiting for transfers between devices, swap(): return lax.ppermute(x, axis, [(i, i ^ distance) for i in range(size)])  24.2 us
    pallas_call x1, Pallas kernels, whole_on_each(): pl.pallas_call(functools.partial(unpack, n_row, n_col), out_shape=[jax.Sh...  9.95 us
  transfers between devices with their start and end apart: 23, of which 13 were waited for; matrix products, arithmetic and copies ran while one was open for 4% of the time, Pallas kernels for 7%

profile of v7, /device:TPU:0, one launch (start us, length us, event | category | flops | bytes accessed | tf_op | source)
XLA Modules:
  0.0 134.7 jit_solution(1762324562664468611)
XLA Ops:
  0.7 1.1 select_bitcast_fusion
  1.8 0.5 collective-permute-start
  2.4 0.7 fusion.6
  3.0 0.7 fusion.7
  3.7 0.7 sqrt.3
  4.4 0.8 reshape.205
  5.2 0.1 copy.15
  5.3 0.1 reshape.206
  5.4 0.9 reshape.203
  6.4 2.6 %collective-permute-start.1 = (bf16[16,4096]{1,0:T(8,128)(2,1)S(1)}, bf16[16,4096]{1,0:T(8,128)(2,1)S(1)}, u32[]{:S(2)}, u32[]{:S(2)}) collective-permute-start(bf16[16,4096]{1,0:T(8,128)(2,1)S(1)} %get-tuple-element.57), channel_id=1, source_target_pairs={{0,2},{2,0},{4,6},{6,4},{1,3},{3,1},{5,7},{7,5},{8,10},{10,8},{12,... | collective-permute-start | bytes 393224 | tf_op jit(solution)/shard_map/ppermute | solution.py:353
  9.0 1.5 %collective-permute-start.2 = (bf16[16,4096]{1,0:T(8,128)(2,1)S(1)}, bf16[16,4096]{1,0:T(8,128)(2,1)S(1)}, u32[]{:S(2)}, u32[]{:S(2)}) collective-permute-start(bf16[16,4096]{1,0:T(8,128)(2,1)S(1)} %get-tuple-element.59), channel_id=1, source_target_pairs={{0,4},{2,6},{4,0},{6,2},{1,5},{3,7},{5,1},{7,3},{8,12},{10,14},{12... | collective-permute-start | bytes 393224 | tf_op jit(solution)/shard_map/ppermute | solution.py:353
  10.6 0.1 reshape.204
  10.8 0.1 concatenate.48
  10.9 2.1 %collective-permute-start.4 = (bf16[336,128]{1,0:T(8,128)(2,1)S(1)}, bf16[336,128]{1,0:T(8,128)(2,1)S(1)}, u32[]{:S(2)}, u32[]{:S(2)}) collective-permute-start(bf16[336,128]{1,0:T(8,128)(2,1)S(1)} %concatenate.48), channel_id=1, source_target_pairs={{0,8},{8,0},{16,24},{24,16},{1,9},{9,1},{17,25},{25,17},{2,10},{10... | collective-permute-start | bytes 258056 | tf_op jit(solution)/shard_map/ppermute | solution.py:353
  13.0 2.6 %collective-permute-start.5 = (bf16[336,128]{1,0:T(8,128)(2,1)S(1)}, bf16[336,128]{1,0:T(8,128)(2,1)S(1)}, u32[]{:S(2)}, u32[]{:S(2)}) collective-permute-start(bf16[336,128]{1,0:T(8,128)(2,1)S(1)} %concatenate.48), channel_id=1, source_target_pairs={{0,16},{8,24},{16,0},{24,8},{1,17},{9,25},{17,1},{25,9},{2,18},{10... | collective-permute-start | bytes 258056 | tf_op jit(solution)/shard_map/ppermute | solution.py:353
  15.6 1.8 %collective-permute-start.6 = (bf16[336,128]{1,0:T(8,128)(2,1)S(1)}, bf16[336,128]{1,0:T(8,128)(2,1)S(1)}, u32[]{:S(2)}, u32[]{:S(2)}) collective-permute-start(bf16[336,128]{1,0:T(8,128)(2,1)S(1)} %concatenate.48), channel_id=1, source_target_pairs={{0,24},{8,16},{16,8},{24,0},{1,25},{9,17},{17,9},{25,1},{2,26},{10... | collective-permute-start | bytes 258056 | tf_op jit(solution)/shard_map/ppermute | solution.py:353
  17.6 4.8 %collective-permute-done.5 = bf16[336,128]{1,0:T(8,128)(2,1)S(1)} collective-permute-done((bf16[336,128]{1,0:T(8,128)(2,1)S(1)}, bf16[336,128]{1,0:T(8,128)(2,1)S(1)}, u32[]{:S(2)}, u32[]{:S(2)}) %collective-permute-start.5) | collective-permute-done | bytes 86048 | tf_op jit(solution)/shard_map/ppermute | solution.py:353
  22.4 1.6 %collective-permute-start.8 = (bf16[2,336,128]{2,1,0:T(8,128)(2,1)S(1)}, bf16[2,336,128]{2,1,0:T(8,128)(2,1)S(1)}, u32[]{:S(2)}, u32[]{:S(2)}) collective-permute-start(bf16[2,336,128]{2,1,0:T(8,128)(2,1)S(1)} %pad_maximum_fusion.8), channel_id=1, source_target_pairs={{0,4},{2,6},{4,0},{6,2},{1,5},{3,7},{5,1},{7,3},{8,12},{10,14},{12... | collective-permute-start | bytes 516104 | tf_op jit(solution)/shard_map/ppermute | solution.py:353
  24.0 1.6 %collective-permute-start.7 = (bf16[2,336,128]{2,1,0:T(8,128)(2,1)S(1)}, bf16[2,336,128]{2,1,0:T(8,128)(2,1)S(1)}, u32[]{:S(2)}, u32[]{:S(2)}) collective-permute-start(bf16[2,336,128]{2,1,0:T(8,128)(2,1)S(1)} %pad_maximum_fusion.7), channel_id=1, source_target_pairs={{0,2},{2,0},{4,6},{6,4},{1,3},{3,1},{5,7},{7,5},{8,10},{10,8},{12,... | collective-permute-start | bytes 516104 | tf_op jit(solution)/shard_map/ppermute | solution.py:353
  25.5 1.5 %collective-permute-start.9 = (bf16[512,128]{1,0:T(8,128)(2,1)S(1)}, bf16[512,128]{1,0:T(8,128)(2,1)S(1)}, u32[]{:S(2)}, u32[]{:S(2)}) collective-permute-start(bf16[512,128]{1,0:T(8,128)(2,1)S(1)} %bitcast.54), channel_id=1, source_target_pairs={{0,8},{8,0},{16,24},{24,16},{1,9},{9,1},{17,25},{25,17},{2,10},{10... | collective-permute-start | bytes 393224 | tf_op jit(solution)/shard_map/ppermute | solution.py:353
  27.0 0.8 collective-permute-done.8
  27.9 1.6 %collective-permute-done.7 = bf16[2,336,128]{2,1,0:T(8,128)(2,1)S(1)} collective-permute-done((bf16[2,336,128]{2,1,0:T(8,128)(2,1)S(1)}, bf16[2,336,128]{2,1,0:T(8,128)(2,1)S(1)}, u32[]{:S(2)}, u32[]{:S(2)}) %collective-permute-start.7) | collective-permute-done | bytes 172064 | tf_op jit(solution)/shard_map/ppermute | solution.py:353
  29.5 1.0 collective-permute-done.9
  30.5 0.5 collective-permute-start.12
  31.0 0.6 collective-permute-start.13
  31.6 2.5 %collective-permute-start.10 = (bf16[512,128]{1,0:T(8,128)(2,1)S(1)}, bf16[512,128]{1,0:T(8,128)(2,1)S(1)}, u32[]{:S(2)}, u32[]{:S(2)}) collective-permute-start(bf16[512,128]{1,0:T(8,128)(2,1)S(1)} %bitcast.55), channel_id=1, source_target_pairs={{0,16},{8,24},{16,0},{24,8},{1,17},{9,25},{17,1},{25,9},{2,18},{10... | collective-permute-start | bytes 393224 | tf_op jit(solution)/shard_map/ppermute | solution.py:353
  34.1 1.3 %collective-permute-start.11 = (bf16[512,128]{1,0:T(8,128)(2,1)S(1)}, bf16[512,128]{1,0:T(8,128)(2,1)S(1)}, u32[]{:S(2)}, u32[]{:S(2)}) collective-permute-start(bf16[512,128]{1,0:T(8,128)(2,1)S(1)} %bitcast.56), channel_id=1, source_target_pairs={{0,24},{8,16},{16,8},{24,0},{1,25},{9,17},{17,9},{25,1},{2,26},{10... | collective-permute-start | bytes 393224 | tf_op jit(solution)/shard_map/ppermute | solution.py:353
  35.4 2.3 %collective-permute-done.12 = bf16[4,336,128]{2,1,0:T(8,128)(2,1)S(1)} collective-permute-done((bf16[4,336,128]{2,1,0:T(8,128)(2,1)S(1)}, bf16[4,336,128]{2,1,0:T(8,128)(2,1)S(1)}, u32[]{:S(2)}, u32[]{:S(2)}) %collective-permute-start.12) | collective-permute-done | bytes 344096 | tf_op jit(solution)/shard_map/ppermute | solution.py:353
  37.7 0.5 collective-permute-done.13
  38.3 0.2 pad_maximum_fusion.mine
  38.4 3.1 %collective-permute-done.10 = bf16[512,128]{1,0:T(8,128)(2,1)S(1)} collective-permute-done((bf16[512,128]{1,0:T(8,128)(2,1)S(1)}, bf16[512,128]{1,0:T(8,128)(2,1)S(1)}, u32[]{:S(2)}, u32[]{:S(2)}) %collective-permute-start.10) | collective-permute-done | bytes 131104 | tf_op jit(solution)/shard_map/ppermute | solution.py:353
  41.6 1.7 %collective-permute-start.15 = (bf16[2,512,128]{2,1,0:T(8,128)(2,1)S(1)}, bf16[2,512,128]{2,1,0:T(8,128)(2,1)S(1)}, u32[]{:S(2)}, u32[]{:S(2)}) collective-permute-start(bf16[2,512,128]{2,1,0:T(8,128)(2,1)S(1)} %pad_maximum_fusion.6), channel_id=1, source_target_pairs={{0,4},{2,6},{4,0},{6,2},{1,5},{3,7},{5,1},{7,3},{8,12},{10,14},{12... | collective-permute-start | bytes 786440 | tf_op jit(solution)/shard_map/ppermute | solution.py:353
  43.3 1.3 collective-permute-start.14
  44.6 5.7 %collective-permute-done.15 = bf16[2,512,128]{2,1,0:T(8,128)(2,1)S(1)} collective-permute-done((bf16[2,512,128]{2,1,0:T(8,128)(2,1)S(1)}, bf16[2,512,128]{2,1,0:T(8,128)(2,1)S(1)}, u32[]{:S(2)}, u32[]{:S(2)}) %collective-permute-start.15) | collective-permute-done | bytes 262176 | tf_op jit(solution)/shard_map/ppermute | solution.py:353
  50.4 1.4 %collective-permute-done.14 = bf16[2,512,128]{2,1,0:T(8,128)(2,1)S(1)} collective-permute-done((bf16[2,512,128]{2,1,0:T(8,128)(2,1)S(1)}, bf16[2,512,128]{2,1,0:T(8,128)(2,1)S(1)}, u32[]{:S(2)}, u32[]{:S(2)}) %collective-permute-start.14) | collective-permute-done | bytes 262176 | tf_op jit(solution)/shard_map/ppermute | solution.py:353
  51.9 1.2 copy-done.3
  53.1 0.4 collective-permute-start.17
  53.4 1.4 %collective-permute-start.18 = (bf16[4,512,128]{2,1,0:T(8,128)(2,1)S(1)}, bf16[4,512,128]{2,1,0:T(8,128)(2,1)S(1)}, u32[]{:S(2)}, u32[]{:S(2)}) collective-permute-start(bf16[4,512,128]{2,1,0:T(8,128)(2,1)S(1)} %pad_maximum_fusion.2.rest_6_), channel_id=1, source_target_pairs={{0,2},{2,0},{4,6},{6,4},{1,3},{3,1},{5,7},{7,5},{8,10},{10,8},{12,... | collective-permute-start | bytes 1572872 | tf_op jit(solution)/shard_map/ppermute | solution.py:353
  54.8 0.6 pad_add_fusion.own
  55.4 0.5 collective-permute-start.20
  56.0 10.0 %unpack.1 = (s32[584]{0:T(1024)}, f32[8,128]{1,0:T(8,128)}, bf16[144,128,128]{2,1,0:T(8,128)(2,1)}, bf16[32,64,128]{2,1,0:T(8,128)(2,1)}, bf16[64,64,128]{2,1,0:...) custom-call(s32[3]{0:T(128)} %pad_add_fusion.own, bf16[16,336,128]{2,1,0:T(8,128)(2,1)} %copy-done, ...), custom_call_target="tpu_custom_call" | custom-call | bytes 11010048 | tf_op jit(solution)/shard_map/unpack/pallas_call | solution.py:434
  65.9 0.4 collective-permute-done.17.rest_7_
  66.3 0.4 collective-permute-done.18.rest_8_
  66.7 0.5 collective-permute-start.22
  67.2 1.4 %collective-permute-done.21.rest_11_ = bf16[4,512,128]{2,1,0:T(8,128)(2,1)S(1)} collective-permute-done((bf16[4,512,128]{2,1,0:T(8,128)(2,1)S(1)}, bf16[4,512,128]{2,1,0:T(8,128)(2,1)S(1)}, u32[]{:S(2)}, u32[]{:S(2)}) %collective-permute-start.21) | collective-permute-done | bytes 524320 | tf_op jit(solution)/shard_map/ppermute | solution.py:353
  68.6 0.7 collective-permute-done.22.rest_12_
  69.4 0.7 copy-done.10
  70.2 64.4 %iterate.1 = f32[2,4096]{1,0:T(2,128)} custom-call(s32[3]{0:T(128)} %pad_add_fusion.own, s32[584]{0:T(1024)} %get-tuple-element.48.lists, f32[8,128]{1,0:T(8,128)} %get-tuple-element.49.place, bf16[144,128,128]{2,1,0:T(8,128)(2,1)} %get-tuple-element.50.rest_0_, bf16[32,64,128]{2,1,0:T(8,128)(2,1)} %get-tuple-element.51.rest_1_, ...), custom_call_target="tpu_custom_call" | custom-call | tf_op jit(solution)/shard_map/iterate/pallas_call | solution.py:455
  (59 shorter events, 0.9 us)
Async XLA Ops:
  0.0 6.3 %copy-start.4 = (bf16[1,1,128,4096]{3,2,1,0:T(8,128)(2,1)S(1)}, bf16[1,1,128,4096]{3,2,1,0:T(8,128)(2,1)}, u32[]{:S(2)}) copy-start(bf16[1,1,128,4096]{3,2,1,0:T(8,128)(2,1)} %param.7) | copy-start | bytes 3145732
  1.8 4.5 %collective-permute-start = (bf16[4,16,4096]{2,1,0:T(8,128)(2,1)S(1)}, bf16[4,16,4096]{2,1,0:T(8,128)(2,1)S(1)}, u32[]{:S(2)}, u32[]{:S(2)}) collective-permute-start(bf16[4,16,4096]{2,1,0:T(8,128)(2,1)S(1)} %select_bitcast_fusion), channel_id=1, source_target_pairs={{0,1},{1,0},{2,3},{3,2},{4,5},{5,4},{6,7},{7,6},{8,9},{9,8},{10,11... | collective-permute-start | bytes 1572872 | tf_op jit(solution)/shard_map/ppermute | solution.py:353
  6.4 9.2 %collective-permute-start.1 = (bf16[16,4096]{1,0:T(8,128)(2,1)S(1)}, bf16[16,4096]{1,0:T(8,128)(2,1)S(1)}, u32[]{:S(2)}, u32[]{:S(2)}) collective-permute-start(bf16[16,4096]{1,0:T(8,128)(2,1)S(1)} %get-tuple-element.57), channel_id=1, source_target_pairs={{0,2},{2,0},{4,6},{6,4},{1,3},{3,1},{5,7},{7,5},{8,10},{10,8},{12,... | collective-permute-start | bytes 393224 | tf_op jit(solution)/shard_map/ppermute | solution.py:353
  9.0 8.4 %collective-permute-start.2 = (bf16[16,4096]{1,0:T(8,128)(2,1)S(1)}, bf16[16,4096]{1,0:T(8,128)(2,1)S(1)}, u32[]{:S(2)}, u32[]{:S(2)}) collective-permute-start(bf16[16,4096]{1,0:T(8,128)(2,1)S(1)} %get-tuple-element.59), channel_id=1, source_target_pairs={{0,4},{2,6},{4,0},{6,2},{1,5},{3,7},{5,1},{7,3},{8,12},{10,14},{12... | collective-permute-start | bytes 393224 | tf_op jit(solution)/shard_map/ppermute | solution.py:353
  10.5 6.9 %collective-permute-start.3 = (bf16[16,4096]{1,0:T(8,128)(2,1)S(1)}, bf16[16,4096]{1,0:T(8,128)(2,1)S(1)}, u32[]{:S(2)}, u32[]{:S(2)}) collective-permute-start(bf16[16,4096]{1,0:T(8,128)(2,1)S(1)} %get-tuple-element.58), channel_id=1, source_target_pairs={{0,6},{2,4},{4,2},{6,0},{1,7},{3,5},{5,3},{7,1},{8,14},{10,12},{12... | collective-permute-start | bytes 393224 | tf_op jit(solution)/shard_map/ppermute | solution.py:353
  10.9 6.6 %collective-permute-start.4 = (bf16[336,128]{1,0:T(8,128)(2,1)S(1)}, bf16[336,128]{1,0:T(8,128)(2,1)S(1)}, u32[]{:S(2)}, u32[]{:S(2)}) collective-permute-start(bf16[336,128]{1,0:T(8,128)(2,1)S(1)} %concatenate.48), channel_id=1, source_target_pairs={{0,8},{8,0},{16,24},{24,16},{1,9},{9,1},{17,25},{25,17},{2,10},{10... | collective-permute-start | bytes 258056 | tf_op jit(solution)/shard_map/ppermute | solution.py:353
  13.0 9.3 %collective-permute-start.5 = (bf16[336,128]{1,0:T(8,128)(2,1)S(1)}, bf16[336,128]{1,0:T(8,128)(2,1)S(1)}, u32[]{:S(2)}, u32[]{:S(2)}) collective-permute-start(bf16[336,128]{1,0:T(8,128)(2,1)S(1)} %concatenate.48), channel_id=1, source_target_pairs={{0,16},{8,24},{16,0},{24,8},{1,17},{9,25},{17,1},{25,9},{2,18},{10... | collective-permute-start | bytes 258056 | tf_op jit(solution)/shard_map/ppermute | solution.py:353
  15.6 6.7 %collective-permute-start.6 = (bf16[336,128]{1,0:T(8,128)(2,1)S(1)}, bf16[336,128]{1,0:T(8,128)(2,1)S(1)}, u32[]{:S(2)}, u32[]{:S(2)}) collective-permute-start(bf16[336,128]{1,0:T(8,128)(2,1)S(1)} %concatenate.48), channel_id=1, source_target_pairs={{0,24},{8,16},{16,8},{24,0},{1,25},{9,17},{17,9},{25,1},{2,26},{10... | collective-permute-start | bytes 258056 | tf_op jit(solution)/shard_map/ppermute | solution.py:353
  22.4 5.5 %collective-permute-start.8 = (bf16[2,336,128]{2,1,0:T(8,128)(2,1)S(1)}, bf16[2,336,128]{2,1,0:T(8,128)(2,1)S(1)}, u32[]{:S(2)}, u32[]{:S(2)}) collective-permute-start(bf16[2,336,128]{2,1,0:T(8,128)(2,1)S(1)} %pad_maximum_fusion.8), channel_id=1, source_target_pairs={{0,4},{2,6},{4,0},{6,2},{1,5},{3,7},{5,1},{7,3},{8,12},{10,14},{12... | collective-permute-start | bytes 516104 | tf_op jit(solution)/shard_map/ppermute | solution.py:353
  24.0 5.5 %collective-permute-start.7 = (bf16[2,336,128]{2,1,0:T(8,128)(2,1)S(1)}, bf16[2,336,128]{2,1,0:T(8,128)(2,1)S(1)}, u32[]{:S(2)}, u32[]{:S(2)}) collective-permute-start(bf16[2,336,128]{2,1,0:T(8,128)(2,1)S(1)} %pad_maximum_fusion.7), channel_id=1, source_target_pairs={{0,2},{2,0},{4,6},{6,4},{1,3},{3,1},{5,7},{7,5},{8,10},{10,8},{12,... | collective-permute-start | bytes 516104 | tf_op jit(solution)/shard_map/ppermute | solution.py:353
  25.5 5.0 %collective-permute-start.9 = (bf16[512,128]{1,0:T(8,128)(2,1)S(1)}, bf16[512,128]{1,0:T(8,128)(2,1)S(1)}, u32[]{:S(2)}, u32[]{:S(2)}) collective-permute-start(bf16[512,128]{1,0:T(8,128)(2,1)S(1)} %bitcast.54), channel_id=1, source_target_pairs={{0,8},{8,0},{16,24},{24,16},{1,9},{9,1},{17,25},{25,17},{2,10},{10... | collective-permute-start | bytes 393224 | tf_op jit(solution)/shard_map/ppermute | solution.py:353
  30.5 7.2 %collective-permute-start.12 = (bf16[4,336,128]{2,1,0:T(8,128)(2,1)S(1)}, bf16[4,336,128]{2,1,0:T(8,128)(2,1)S(1)}, u32[]{:S(2)}, u32[]{:S(2)}) collective-permute-start(bf16[4,336,128]{2,1,0:T(8,128)(2,1)S(1)} %pad_maximum_fusion.3), channel_id=1, source_target_pairs={{0,4},{2,6},{4,0},{6,2},{1,5},{3,7},{5,1},{7,3},{8,12},{10,14},{12... | collective-permute-start | bytes 1032200 | tf_op jit(solution)/shard_map/ppermute | solution.py:353
  31.0 7.2 %collective-permute-start.13 = (bf16[4,336,128]{2,1,0:T(8,128)(2,1)S(1)}, bf16[4,336,128]{2,1,0:T(8,128)(2,1)S(1)}, u32[]{:S(2)}, u32[]{:S(2)}) collective-permute-start(bf16[4,336,128]{2,1,0:T(8,128)(2,1)S(1)} %pad_maximum_fusion.4), channel_id=1, source_target_pairs={{0,2},{2,0},{4,6},{6,4},{1,3},{3,1},{5,7},{7,5},{8,10},{10,8},{12,... | collective-permute-start | bytes 1032200 | tf_op jit(solution)/shard_map/ppermute | solution.py:353
  31.6 10.0 %collective-permute-start.10 = (bf16[512,128]{1,0:T(8,128)(2,1)S(1)}, bf16[512,128]{1,0:T(8,128)(2,1)S(1)}, u32[]{:S(2)}, u32[]{:S(2)}) collective-permute-start(bf16[512,128]{1,0:T(8,128)(2,1)S(1)} %bitcast.55), channel_id=1, source_target_pairs={{0,16},{8,24},{16,0},{24,8},{1,17},{9,25},{17,1},{25,9},{2,18},{10... | collective-permute-start | bytes 393224 | tf_op jit(solution)/shard_map/ppermute | solution.py:353
  34.1 7.5 %collective-permute-start.11 = (bf16[512,128]{1,0:T(8,128)(2,1)S(1)}, bf16[512,128]{1,0:T(8,128)(2,1)S(1)}, u32[]{:S(2)}, u32[]{:S(2)}) collective-permute-start(bf16[512,128]{1,0:T(8,128)(2,1)S(1)} %bitcast.56), channel_id=1, source_target_pairs={{0,24},{8,16},{16,8},{24,0},{1,25},{9,17},{17,9},{25,1},{2,26},{10... | collective-permute-start | bytes 393224 | tf_op jit(solution)/shard_map/ppermute | solution.py:353
  38.4 13.5 %copy-start = (bf16[16,336,128]{2,1,0:T(8,128)(2,1)}, bf16[16,336,128]{2,1,0:T(8,128)(2,1)S(1)}, u32[]{:S(2)}) copy-start(bf16[16,336,128]{2,1,0:T(8,128)(2,1)S(1)} %pad_maximum_fusion.mine) | copy-start | bytes 4128772
  41.5 10.4 %collective-permute-start.16 = (bf16[16,336,128]{2,1,0:T(8,128)(2,1)S(1)}, bf16[16,336,128]{2,1,0:T(8,128)(2,1)S(1)}, u32[]{:S(2)}, u32[]{:S(2)}) collective-permute-start(bf16[16,336,128]{2,1,0:T(8,128)(2,1)S(1)} %pad_maximum_fusion.mine), channel_id=1, source_target_pairs={{0,1},{1,0},{2,3},{3,2},{4,5},{5,4},{6,7},{7,6},{8,9},{9,8},{10,11... | collective-permute-start | bytes 4128776 | tf_op jit(solution)/shard_map/ppermute | solution.py:353
  41.6 8.8 %collective-permute-start.15 = (bf16[2,512,128]{2,1,0:T(8,128)(2,1)S(1)}, bf16[2,512,128]{2,1,0:T(8,128)(2,1)S(1)}, u32[]{:S(2)}, u32[]{:S(2)}) collective-permute-start(bf16[2,512,128]{2,1,0:T(8,128)(2,1)S(1)} %pad_maximum_fusion.6), channel_id=1, source_target_pairs={{0,4},{2,6},{4,0},{6,2},{1,5},{3,7},{5,1},{7,3},{8,12},{10,14},{12... | collective-permute-start | bytes 786440 | tf_op jit(solution)/shard_map/ppermute | solution.py:353
  43.3 8.5 %collective-permute-start.14 = (bf16[2,512,128]{2,1,0:T(8,128)(2,1)S(1)}, bf16[2,512,128]{2,1,0:T(8,128)(2,1)S(1)}, u32[]{:S(2)}, u32[]{:S(2)}) collective-permute-start(bf16[2,512,128]{2,1,0:T(8,128)(2,1)S(1)} %pad_maximum_fusion.5), channel_id=1, source_target_pairs={{0,2},{2,0},{4,6},{6,4},{1,3},{3,1},{5,7},{7,5},{8,10},{10,8},{12,... | collective-permute-start | bytes 786440 | tf_op jit(solution)/shard_map/ppermute | solution.py:353
  50.4 15.5 %copy-start.1 = (bf16[4,512,128]{2,1,0:T(8,128)(2,1)}, bf16[4,512,128]{2,1,0:T(8,128)(2,1)S(1)}, u32[]{:S(2)}) copy-start(bf16[4,512,128]{2,1,0:T(8,128)(2,1)S(1)} %pad_maximum_fusion.2.rest_6_) | copy-start | bytes 1572868
  51.9 14.0 %copy-start.2 = (bf16[4,512,128]{2,1,0:T(8,128)(2,1)}, bf16[4,512,128]{2,1,0:T(8,128)(2,1)S(1)}, u32[]{:S(2)}) copy-start(bf16[4,512,128]{2,1,0:T(8,128)(2,1)S(1)} %pad_maximum_fusion.1.rest_5_) | copy-start | bytes 1572868
  51.9 1.2 copy-start.3
  53.1 13.2 %collective-permute-start.17 = (bf16[4,512,128]{2,1,0:T(8,128)(2,1)S(1)}, bf16[4,512,128]{2,1,0:T(8,128)(2,1)S(1)}, u32[]{:S(2)}, u32[]{:S(2)}) collective-permute-start(bf16[4,512,128]{2,1,0:T(8,128)(2,1)S(1)} %pad_maximum_fusion.1.rest_5_), channel_id=1, source_target_pairs={{0,4},{2,6},{4,0},{6,2},{1,5},{3,7},{5,1},{7,3},{8,12},{10,14},{12... | collective-permute-start | bytes 1572872 | tf_op jit(solution)/shard_map/ppermute | solution.py:353
  53.4 13.2 %collective-permute-start.18 = (bf16[4,512,128]{2,1,0:T(8,128)(2,1)S(1)}, bf16[4,512,128]{2,1,0:T(8,128)(2,1)S(1)}, u32[]{:S(2)}, u32[]{:S(2)}) collective-permute-start(bf16[4,512,128]{2,1,0:T(8,128)(2,1)S(1)} %pad_maximum_fusion.2.rest_6_), channel_id=1, source_target_pairs={{0,2},{2,0},{4,6},{6,4},{1,3},{3,1},{5,7},{7,5},{8,10},{10,8},{12,... | collective-permute-start | bytes 1572872 | tf_op jit(solution)/shard_map/ppermute | solution.py:353
  55.4 11.8 %collective-permute-start.19 = (bf16[4,512,128]{2,1,0:T(8,128)(2,1)S(1)}, bf16[4,512,128]{2,1,0:T(8,128)(2,1)S(1)}, u32[]{:S(2)}, u32[]{:S(2)}) collective-permute-start(bf16[4,512,128]{2,1,0:T(8,128)(2,1)S(1)} %pad_maximum_fusion.1.rest_5_), channel_id=1, source_target_pairs={{0,1},{1,0},{2,3},{3,2},{4,5},{5,4},{6,7},{7,6},{8,9},{9,8},{10,11... | collective-permute-start | bytes 1572872 | tf_op jit(solution)/shard_map/ppermute | solution.py:353
  55.4 11.8 %collective-permute-start.20 = (bf16[4,512,128]{2,1,0:T(8,128)(2,1)S(1)}, bf16[4,512,128]{2,1,0:T(8,128)(2,1)S(1)}, u32[]{:S(2)}, u32[]{:S(2)}) collective-permute-start(bf16[4,512,128]{2,1,0:T(8,128)(2,1)S(1)} %pad_maximum_fusion.2.rest_6_), channel_id=1, source_target_pairs={{0,1},{1,0},{2,3},{3,2},{4,5},{5,4},{6,7},{7,6},{8,9},{9,8},{10,11... | collective-permute-start | bytes 1572872 | tf_op jit(solution)/shard_map/ppermute | solution.py:353
  66.3 3.0 %copy-start.5 = (bf16[4,512,128]{2,1,0:T(8,128)(2,1)}, bf16[4,512,128]{2,1,0:T(8,128)(2,1)S(1)}, u32[]{:S(2)}) copy-start(bf16[4,512,128]{2,1,0:T(8,128)(2,1)S(1)} %collective-permute-done.17.rest_7_) | copy-start | bytes 1572868
  66.7 2.7 %copy-start.6 = (bf16[4,512,128]{2,1,0:T(8,128)(2,1)}, bf16[4,512,128]{2,1,0:T(8,128)(2,1)S(1)}, u32[]{:S(2)}) copy-start(bf16[4,512,128]{2,1,0:T(8,128)(2,1)S(1)} %collective-permute-done.18.rest_8_) | copy-start | bytes 1572868
  66.7 1.9 %collective-permute-start.21 = (bf16[4,512,128]{2,1,0:T(8,128)(2,1)S(1)}, bf16[4,512,128]{2,1,0:T(8,128)(2,1)S(1)}, u32[]{:S(2)}, u32[]{:S(2)}) collective-permute-start(bf16[4,512,128]{2,1,0:T(8,128)(2,1)S(1)} %collective-permute-done.17.rest_7_), channel_id=1, source_target_pairs={{0,1},{1,0},{2,3},{3,2},{4,5},{5,4},{6,7},{7,6},{8,9},{9,8},{10,11... | collective-permute-start | bytes 1572872 | tf_op jit(solution)/shard_map/ppermute | solution.py:353
  66.7 2.7 %collective-permute-start.22 = (bf16[4,512,128]{2,1,0:T(8,128)(2,1)S(1)}, bf16[4,512,128]{2,1,0:T(8,128)(2,1)S(1)}, u32[]{:S(2)}, u32[]{:S(2)}) collective-permute-start(bf16[4,512,128]{2,1,0:T(8,128)(2,1)S(1)} %collective-permute-done.18.rest_8_), channel_id=1, source_target_pairs={{0,1},{1,0},{2,3},{3,2},{4,5},{5,4},{6,7},{7,6},{8,9},{9,8},{10,11... | collective-permute-start | bytes 1572872 | tf_op jit(solution)/shard_map/ppermute | solution.py:353
  67.2 2.2 %copy-start.7 = (bf16[4,512,128]{2,1,0:T(8,128)(2,1)}, bf16[4,512,128]{2,1,0:T(8,128)(2,1)S(1)}, u32[]{:S(2)}) copy-start(bf16[4,512,128]{2,1,0:T(8,128)(2,1)S(1)} %collective-permute-done.19.rest_9_) | copy-start | bytes 1572868
  67.2 2.2 %copy-start.8 = (bf16[4,512,128]{2,1,0:T(8,128)(2,1)}, bf16[4,512,128]{2,1,0:T(8,128)(2,1)S(1)}, u32[]{:S(2)}) copy-start(bf16[4,512,128]{2,1,0:T(8,128)(2,1)S(1)} %collective-permute-done.20.rest_10_) | copy-start | bytes 1572868
  68.6 0.8 copy-start.9
  69.4 0.8 copy-start.10

commit v8 on v7

--- a/solution.py
+++ b/solution.py
@@ -68,21 +68,18 @@
 
 
 def place_of(own, n_row, n_dev):
-    here, chip, core = own[0], own[1], own[2]
+    chip, core = own[0], own[1]
 
     def at_device(r, c):
-        dr, dc, dk = here ^ r, chip ^ (c // 2), core ^ (c % 2)
+        dc, dk = chip ^ (c // 2), core ^ (c % 2)
         dx, dy = dc & 1, dc >> 1
-        order = jnp.where(dr < 2, 2 * dx, 4 + 2 * dy) + jnp.where(
-            jnp.where(dr < 2, dy, dx) > 0, n_dev // 4, 0
-        )
-        return dk * (n_dev // 2) + order + (dr & 1)
+        first, second = (dx, dy) if r < 2 else (dy, dx)
+        return dk * (n_dev // 2) + second * (n_dev // 4) + r // 2 * (n_dev // 8) + first * 2 + r % 2
 
     def device_at(d):
-        far, second = (d >> 2) & 1, (d >> 3) & 1
-        first = (d >> 1) & 1
+        far, first, second = (d >> 2) & 1, (d >> 1) & 1, (d >> 3) & 1
         dc = jnp.where(far == 0, 2 * second + first, 2 * first + second)
-        return here ^ (2 * far + (d & 1)), 2 * (chip ^ dc) + (core ^ (d >> 4))
+        return 2 * far + (d & 1), 2 * (chip ^ dc) + (core ^ (d >> 4))
 
     return at_device, device_at
 
@@ -330,7 +327,7 @@
 
     lax.fori_loop(0, ITERS, iteration, 0)
     lh, ll = split2(linv[...])
-    q = (2 * own[1] + own[2]) * n_row + own[0]
+    q = (2 * own[0] + own[1]) * n_row + own[2]
     hi, lo = ph[q, :k, :], ph[q, k:, :]
     w[0] = dot(lh, hi) + dot(ll, hi) + dot(lh, lo)
     even, odd = w[0, pl.ds(0, half, stride=2), :], w[0, pl.ds(1, half, stride=2), :]
@@ -354,11 +351,12 @@
 
 
 def along_rows(x):
-    return [x] + [swap(x, "row", s) for s in range(1, lax.axis_size("row"))]
+    sent = jnp.broadcast_to(x, (lax.axis_size("row"), *x.shape))
+    return lax.all_to_all(sent, "row", split_axis=0, concat_axis=0)
 
 
 def along_one_chip_axis(x):
-    near, far = jnp.stack(x[:2]), jnp.stack(x[2:])
+    near, far = jnp.split(x, 2)
     return [
         jnp.concatenate([near, swap(near, "chip", 1)]),
         jnp.concatenate([far, swap(far, "chip", 2)]),
@@ -370,7 +368,7 @@
     return [swap(near, "chip", 2), swap(far, "chip", 1)]
 
 
-def full_part(tile, has_full, n_chip, part, chip, core):
+def full_part(tile, has_full, n_chip, part, core):
     tile = tile.reshape(2, n_chip, part, tile.shape[1])
     none = jnp.zeros(tile.shape[1:], tile.dtype)
     kept, sent = (
@@ -378,10 +376,8 @@
         for i in (core, 1 - core)
     )
     both = kept + swap(sent, "core", 1)
-    mine = lax.dynamic_index_in_dim(both, chip, 0, False)
-    for s in range(1, n_chip):
-        mine = mine + swap(lax.dynamic_index_in_dim(both, chip ^ s, 0, False), "chip", s)
-    return mine
+    parts = lax.all_to_all(both, "chip", split_axis=0, concat_axis=0)
+    return jnp.sum(parts.astype(jnp.float32), axis=0).astype(tile.dtype)
 
 
 def whole_on_each(n_row, n_col, blocks, block_row, block_col, counts, vectors, row_mass, col_mass):
@@ -410,19 +406,17 @@
     meta = split3(mass) + split3(inv_col.reshape(own * bsize)) + meta
     meta = jnp.stack(meta + [jnp.zeros(128, bf16)] * (META - len(meta)))
     small = jnp.concatenate([off, scaled, meta], axis=0)
-    home = full_part(tile, has_full, n_col // 2, part, chip, core)
+    home = full_part(tile, has_full, n_col // 2, part, core)
     home = home.reshape(part, half, 128).transpose(1, 0, 2).reshape(half * part, 128)
 
     together = lax.optimization_barrier
     home, smalls = together((home, along_rows(small)))
-    homes, smalls = along_rows(home), along_one_chip_axis(smalls)
-    smalls, homes[1] = together((smalls, homes[1]))
+    homes, smalls = together((along_rows(home), along_one_chip_axis(smalls)))
     smalls = jnp.concatenate(smalls + along_other_chip_axis(smalls))
-    homes, smalls = together((homes, smalls))
     homes, others = together((along_one_chip_axis(homes), swap(smalls, "core", 1)))
     last = along_other_chip_axis(homes)
 
-    where = jnp.stack([row, chip, core]).astype(jnp.int32)
+    where = jnp.stack([chip, core, row]).astype(jnp.int32)
     height, width = 2 * n_col * bsize, 2 * n_row * bsize
     slots = n_dev * OFF_CAP + 2 * UNROLL
     f32, i32, vmem, smem = jnp.float32, jnp.int32, pltpu.VMEM, pltpu.SMEM

time: 135 us -> 153 us (1.13); the launches traced: 135 us -> 151 us
  waiting for transfers between devices: 24.2 us -> 45.4 us
  starting transfers between devices: 26.4 us -> 23.1 us
  Pallas kernels: 74.3 us -> 71.2 us
    all_to_all x0 -> x3, waiting for transfers between devices: none -> 23.7 us  [the longest x2 15.8 us: along_rows(): return lax.all_to_all(sent, 'row', split_axis=0, concat_axis=0)]
    ppermute x23 -> x14, starting transfers between devices: 26.4 us -> 10 us  [swap(): return lax.ppermute(x, axis, [(i, i ^ distance) for i in range(size)])]
    all_to_all x0 -> x3, starting transfers between devices: none -> 13.1 us  [the longest x2 8.35 us: along_rows(): return lax.all_to_all(sent, 'row', split_axis=0, concat_axis=0)]
    pallas_call x1, Pallas kernels: 64.4 us -> 61.5 us  [whole_on_each(): pl.pallas_call(functools.partial(iterate, n_row, n_col, n_cap, float(n_de...]
    ppermute x23 -> x14, waiting for transfers between devices: 24.2 us -> 21.7 us  [swap(): return lax.ppermute(x, axis, [(i, i ^ distance) for i in range(size)])]
    broadcast_in_dim x0 -> x2, local copies, waits for them, and re-layouts: none -> 1.64 us  [along_rows(): sent = jnp.broadcast_to(x, (lax.axis_size('row'), *x.shape))]
  transfers between devices with their start and end apart: 23 -> 17, of which waited for: 13 -> 13; matrix products, arithmetic and copies ran while one was open for 4% -> 3% of each run, Pallas kernels for 7% -> 6%
where the time goes in v8:
time: 153 us; the launch traced here: 151 us
  Pallas kernels  71.2 us (47%)
  waiting for transfers between devices  45.4 us (30%)
  starting transfers between devices  23.1 us (15%)
  local copies, waits for them, and re-layouts  6.07 us (4%)
  other arithmetic  4.26 us (3%)
    pallas_call x1, Pallas kernels, whole_on_each(): pl.pallas_call(functools.partial(iterate, n_row, n_col, n_cap, float(n_de...  61.5 us
    ppermute x14, waiting for transfers between devices, swap(): return lax.ppermute(x, axis, [(i, i ^ distance) for i in range(size)])  21.7 us
    all_to_all x2, waiting for transfers between devices, along_rows(): return lax.all_to_all(sent, 'row', split_axis=0, concat_axis=0)  15.8 us
    ppermute x14, starting transfers between devices, swap(): return lax.ppermute(x, axis, [(i, i ^ distance) for i in range(size)])  10 us
    pallas_call x1, Pallas kernels, whole_on_each(): pl.pallas_call(functools.partial(unpack, n_row, n_col), out_shape=[jax.Sh...  9.74 us
    all_to_all x2, starting transfers between devices, along_rows(): return lax.all_to_all(sent, 'row', split_axis=0, concat_axis=0)  8.35 us
    all_to_all x1, waiting for transfers between devices, full_part(): parts = lax.all_to_all(both, 'chip', split_axis=0, concat_axis=0)  7.89 us
    all_to_all x1, starting transfers between devices, full_part(): parts = lax.all_to_all(both, 'chip', split_axis=0, concat_axis=0)  4.73 us
  transfers between devices with their start and end apart: 17, of which 13 were waited for; matrix products, arithmetic and copies ran while one was open for 3% of the time, Pallas kernels for 6%

profile of v8, /device:TPU:0, one launch (start us, length us, event | category | flops | bytes accessed | tf_op | source)
XLA Modules:
  0.0 151.2 jit_solution(3577759715053630040)
XLA Ops:
  0.7 1.1 select_bitcast_fusion
  1.8 0.5 collective-permute-start
  2.4 0.7 fusion.5
  3.0 0.7 sqrt.3
  3.7 0.9 reshape.203
  4.6 0.7 fusion.6
  5.3 0.9 bitcast_add_fusion
  6.1 4.7 %all-to-all-start = ((bf16[4,16,4096]{2,1,0:T(8,128)(2,1)}), bf16[4,16,4096]{2,1,0:T(8,128)(2,1)S(1)}, u32[]{:S(2)}, u32[]{:S(2)}) async-start(bf16[4,16,4096]{2,1,0:T(8,128)(2,1)} %bitcast_add_fusion), calls=%async_computation | async-start | bytes 1048576 | tf_op jit(solution)/shard_map/all_to_all | solution.py:379
  10.9 0.1 reshape.207
  10.9 0.1 reshape.205
  11.0 0.1 copy.14
  11.1 0.1 reshape.206
  11.3 0.1 reshape.204
  11.4 0.1 bitcast_maximum_fusion
  11.5 0.1 concatenate.44
  11.6 7.9 %all-to-all-done = bf16[4,16,4096]{2,1,0:T(8,128)(2,1)S(1)} async-done(((bf16[4,16,4096]{2,1,0:T(8,128)(2,1)}), bf16[4,16,4096]{2,1,0:T(8,128)(2,1)S(1)}, u32[]{:S(2)}, u32[]{:S(2)}) %all-to-all-start) | async-done | bytes 524320 | tf_op jit(solution)/shard_map/all_to_all | solution.py:379
  19.5 0.8 broadcast_in_dim.15
  20.3 4.9 %all-to-all-start.1 = ((bf16[4,336,128]{2,1,0:T(8,128)(2,1)}), bf16[4,336,128]{2,1,0:T(8,128)(2,1)S(1)}, u32[]{:S(2)}, u32[]{:S(2)}) async-start(bf16[4,336,128]{2,1,0:T(8,128)(2,1)} %broadcast_in_dim.15), calls=%async_computation.1 | async-start | bytes 688128 | tf_op jit(solution)/shard_map/all_to_all | solution.py:355
  25.2 0.1 reduce_sum.12
  25.3 10.0 %all-to-all-done.1 = bf16[4,336,128]{2,1,0:T(8,128)(2,1)S(1)} async-done(((bf16[4,336,128]{2,1,0:T(8,128)(2,1)}), bf16[4,336,128]{2,1,0:T(8,128)(2,1)S(1)}, u32[]{:S(2)}, u32[]{:S(2)}) %all-to-all-start.1) | async-done | bytes 344096 | tf_op jit(solution)/shard_map/all_to_all | solution.py:355
  35.4 0.9 broadcast_in_dim.16
  36.2 3.5 %all-to-all-start.2 = ((bf16[4,512,128]{2,1,0:T(8,128)(2,1)}), bf16[4,512,128]{2,1,0:T(8,128)(2,1)S(1)}, u32[]{:S(2)}, u32[]{:S(2)}) async-start(bf16[4,512,128]{2,1,0:T(8,128)(2,1)} %broadcast_in_dim.16), calls=%async_computation.2 | async-start | bytes 1048576 | tf_op jit(solution)/shard_map/all_to_all | solution.py:355
  39.7 1.5 %collective-permute-start.2 = (bf16[2,336,128]{2,1,0:T(8,128)(2,1)S(1)}, bf16[2,336,128]{2,1,0:T(8,128)(2,1)S(1)}, u32[]{:S(2)}, u32[]{:S(2)}) collective-permute-start(bf16[2,336,128]{2,1,0:T(8,128)(2,1)S(1)} %get-tuple-element.43), channel_id=1, source_target_pairs={{0,4},{2,6},{4,0},{6,2},{1,5},{3,7},{5,1},{7,3},{8,12},{10,14},{12... | collective-permute-start | bytes 516104 | tf_op jit(solution)/shard_map/ppermute | solution.py:350
  41.3 0.6 collective-permute-start.1
  41.9 3.3 %collective-permute-done.2 = bf16[2,336,128]{2,1,0:T(8,128)(2,1)S(1)} collective-permute-done((bf16[2,336,128]{2,1,0:T(8,128)(2,1)S(1)}, bf16[2,336,128]{2,1,0:T(8,128)(2,1)S(1)}, u32[]{:S(2)}, u32[]{:S(2)}) %collective-permute-start.2) | collective-permute-done | bytes 172064 | tf_op jit(solution)/shard_map/ppermute | solution.py:350
  45.2 1.4 collective-permute-done.1
  46.7 5.8 %all-to-all-done.2 = bf16[4,512,128]{2,1,0:T(8,128)(2,1)S(1)} async-done(((bf16[4,512,128]{2,1,0:T(8,128)(2,1)}), bf16[4,512,128]{2,1,0:T(8,128)(2,1)S(1)}, u32[]{:S(2)}, u32[]{:S(2)}) %all-to-all-start.2) | async-done | bytes 524320 | tf_op jit(solution)/shard_map/all_to_all | solution.py:355
  52.5 1.5 collective-permute-start.5
  54.0 0.6 collective-permute-start.6
  54.7 5.1 %collective-permute-done.5 = bf16[4,336,128]{2,1,0:T(8,128)(2,1)S(1)} collective-permute-done((bf16[4,336,128]{2,1,0:T(8,128)(2,1)S(1)}, bf16[4,336,128]{2,1,0:T(8,128)(2,1)S(1)}, u32[]{:S(2)}, u32[]{:S(2)}) %collective-permute-start.5) | collective-permute-done | bytes 344096 | tf_op jit(solution)/shard_map/ppermute | solution.py:350
  59.8 1.4 collective-permute-done.6
  61.4 0.6 collective-permute-start.4
  62.0 1.4 collective-permute-start.3
  63.4 6.7 %collective-permute-done.4 = bf16[2,512,128]{2,1,0:T(8,128)(2,1)S(1)} collective-permute-done((bf16[2,512,128]{2,1,0:T(8,128)(2,1)S(1)}, bf16[2,512,128]{2,1,0:T(8,128)(2,1)S(1)}, u32[]{:S(2)}, u32[]{:S(2)}) %collective-permute-start.4) | collective-permute-done | bytes 262176 | tf_op jit(solution)/shard_map/ppermute | solution.py:350
  70.2 0.2 collective-permute-done.3
  70.5 1.1 copy-done.3
  71.7 1.5 collective-permute-start.8
  73.1 0.6 collective-permute-start.9
  73.7 0.7 pad_add_fusion.own
  74.4 0.5 collective-permute-start.11
  74.9 9.7 %unpack.1 = (s32[584]{0:T(1024)}, f32[8,128]{1,0:T(8,128)}, bf16[144,128,128]{2,1,0:T(8,128)(2,1)}, bf16[32,64,128]{2,1,0:T(8,128)(2,1)}, bf16[64,64,128]{2,1,0:...) custom-call(s32[3]{0:T(128)} %pad_add_fusion.own, bf16[16,336,128]{2,1,0:T(8,128)(2,1)} %copy-done, ...), custom_call_target="tpu_custom_call" | custom-call | bytes 11010048 | tf_op jit(solution)/shard_map/unpack/pallas_call | solution.py:428
  84.7 0.4 collective-permute-done.8.rest_7_
  85.0 1.0 collective-permute-done.9.rest_8_
  86.1 0.5 collective-permute-start.13
  86.6 1.4 collective-permute-done.12.rest_11_
  88.0 0.7 collective-permute-done.13.rest_12_
  88.8 0.7 copy-done.10
  89.5 61.5 %iterate.1 = f32[2,4096]{1,0:T(2,128)} custom-call(s32[3]{0:T(128)} %pad_add_fusion.own, s32[584]{0:T(1024)} %get-tuple-element.32.lists, f32[8,128]{1,0:T(8,128)} %get-tuple-element.33.place, bf16[144,128,128]{2,1,0:T(8,128)(2,1)} %get-tuple-element.34.rest_0_, bf16[32,64,128]{2,1,0:T(8,128)(2,1)} %get-tuple-element.35.rest_1_, ...), custom_call_target="tpu_custom_call" | custom-call | tf_op jit(solution)/shard_map/iterate/pallas_call | solution.py:449
  (51 shorter events, 0.8 us)
Async XLA Ops:
  0.0 5.3 %copy-start.4 = (bf16[1,1,128,4096]{3,2,1,0:T(8,128)(2,1)S(1)}, bf16[1,1,128,4096]{3,2,1,0:T(8,128)(2,1)}, u32[]{:S(2)}) copy-start(bf16[1,1,128,4096]{3,2,1,0:T(8,128)(2,1)} %param.7) | copy-start | bytes 3145732
  1.8 3.4 %collective-permute-start = (bf16[4,16,4096]{2,1,0:T(8,128)(2,1)S(1)}, bf16[4,16,4096]{2,1,0:T(8,128)(2,1)S(1)}, u32[]{:S(2)}, u32[]{:S(2)}) collective-permute-start(bf16[4,16,4096]{2,1,0:T(8,128)(2,1)S(1)} %select_bitcast_fusion), channel_id=1, source_target_pairs={{0,1},{1,0},{2,3},{3,2},{4,5},{5,4},{6,7},{7,6},{8,9},{9,8},{10,11... | collective-permute-start | bytes 1572872 | tf_op jit(solution)/shard_map/ppermute | solution.py:350
  5.2 5.7 %copy-start.11 = (f32[2,64]{1,0:T(2,128)S(1)}, f32[2,64]{1,0:T(2,128)}, u32[]{:S(2)}) copy-start(f32[2,64]{1,0:T(2,128)} %param.12) | copy-start | bytes 1540
  6.1 13.4 %all-to-all-start = ((bf16[4,16,4096]{2,1,0:T(8,128)(2,1)}), bf16[4,16,4096]{2,1,0:T(8,128)(2,1)S(1)}, u32[]{:S(2)}, u32[]{:S(2)}) async-start(bf16[4,16,4096]{2,1,0:T(8,128)(2,1)} %bitcast_add_fusion), calls=%async_computation | async-start | bytes 1048576 | tf_op jit(solution)/shard_map/all_to_all | solution.py:379
  20.3 15.1 %all-to-all-start.1 = ((bf16[4,336,128]{2,1,0:T(8,128)(2,1)}), bf16[4,336,128]{2,1,0:T(8,128)(2,1)S(1)}, u32[]{:S(2)}, u32[]{:S(2)}) async-start(bf16[4,336,128]{2,1,0:T(8,128)(2,1)} %broadcast_in_dim.15), calls=%async_computation.1 | async-start | bytes 688128 | tf_op jit(solution)/shard_map/all_to_all | solution.py:355
  36.2 16.3 %all-to-all-start.2 = ((bf16[4,512,128]{2,1,0:T(8,128)(2,1)}), bf16[4,512,128]{2,1,0:T(8,128)(2,1)S(1)}, u32[]{:S(2)}, u32[]{:S(2)}) async-start(bf16[4,512,128]{2,1,0:T(8,128)(2,1)} %broadcast_in_dim.16), calls=%async_computation.2 | async-start | bytes 1048576 | tf_op jit(solution)/shard_map/all_to_all | solution.py:355
  39.7 5.5 %collective-permute-start.2 = (bf16[2,336,128]{2,1,0:T(8,128)(2,1)S(1)}, bf16[2,336,128]{2,1,0:T(8,128)(2,1)S(1)}, u32[]{:S(2)}, u32[]{:S(2)}) collective-permute-start(bf16[2,336,128]{2,1,0:T(8,128)(2,1)S(1)} %get-tuple-element.43), channel_id=1, source_target_pairs={{0,4},{2,6},{4,0},{6,2},{1,5},{3,7},{5,1},{7,3},{8,12},{10,14},{12... | collective-permute-start | bytes 516104 | tf_op jit(solution)/shard_map/ppermute | solution.py:350
  41.3 5.4 %collective-permute-start.1 = (bf16[2,336,128]{2,1,0:T(8,128)(2,1)S(1)}, bf16[2,336,128]{2,1,0:T(8,128)(2,1)S(1)}, u32[]{:S(2)}, u32[]{:S(2)}) collective-permute-start(bf16[2,336,128]{2,1,0:T(8,128)(2,1)S(1)} %get-tuple-element.44), channel_id=1, source_target_pairs={{0,2},{2,0},{4,6},{6,4},{1,3},{3,1},{5,7},{7,5},{8,10},{10,8},{12,... | collective-permute-start | bytes 516104 | tf_op jit(solution)/shard_map/ppermute | solution.py:350
  52.5 7.2 %collective-permute-start.5 = (bf16[4,336,128]{2,1,0:T(8,128)(2,1)S(1)}, bf16[4,336,128]{2,1,0:T(8,128)(2,1)S(1)}, u32[]{:S(2)}, u32[]{:S(2)}) collective-permute-start(bf16[4,336,128]{2,1,0:T(8,128)(2,1)S(1)} %pad_maximum_fusion.2), channel_id=1, source_target_pairs={{0,4},{2,6},{4,0},{6,2},{1,5},{3,7},{5,1},{7,3},{8,12},{10,14},{12... | collective-permute-start | bytes 1032200 | tf_op jit(solution)/shard_map/ppermute | solution.py:350
  54.0 7.2 %collective-permute-start.6 = (bf16[4,336,128]{2,1,0:T(8,128)(2,1)S(1)}, bf16[4,336,128]{2,1,0:T(8,128)(2,1)S(1)}, u32[]{:S(2)}, u32[]{:S(2)}) collective-permute-start(bf16[4,336,128]{2,1,0:T(8,128)(2,1)S(1)} %pad_maximum_fusion.3), channel_id=1, source_target_pairs={{0,2},{2,0},{4,6},{6,4},{1,3},{3,1},{5,7},{7,5},{8,10},{10,8},{12,... | collective-permute-start | bytes 1032200 | tf_op jit(solution)/shard_map/ppermute | solution.py:350
  61.3 9.2 %copy-start = (bf16[16,336,128]{2,1,0:T(8,128)(2,1)}, bf16[16,336,128]{2,1,0:T(8,128)(2,1)S(1)}, u32[]{:S(2)}) copy-start(bf16[16,336,128]{2,1,0:T(8,128)(2,1)S(1)} %constant_dynamic-update-slice_fusion.mine) | copy-start | bytes 4128772
  61.3 9.2 %collective-permute-start.7 = (bf16[16,336,128]{2,1,0:T(8,128)(2,1)S(1)}, bf16[16,336,128]{2,1,0:T(8,128)(2,1)S(1)}, u32[]{:S(2)}, u32[]{:S(2)}) collective-permute-start(bf16[16,336,128]{2,1,0:T(8,128)(2,1)S(1)} %constant_dynamic-update-slice_fusion.mine), channel_id=1, source_target_pairs={{0,1},{1,0},{2,3},{3,2},{4,5},{5,4},{6,7},{7,6},{8,9},{9,8},{10,11... | collective-permute-start | bytes 4128776 | tf_op jit(solution)/shard_map/ppermute | solution.py:350
  61.4 8.8 %collective-permute-start.4 = (bf16[2,512,128]{2,1,0:T(8,128)(2,1)S(1)}, bf16[2,512,128]{2,1,0:T(8,128)(2,1)S(1)}, u32[]{:S(2)}, u32[]{:S(2)}) collective-permute-start(bf16[2,512,128]{2,1,0:T(8,128)(2,1)S(1)} %get-tuple-element.41), channel_id=1, source_target_pairs={{0,4},{2,6},{4,0},{6,2},{1,5},{3,7},{5,1},{7,3},{8,12},{10,14},{12... | collective-permute-start | bytes 786440 | tf_op jit(solution)/shard_map/ppermute | solution.py:350
  62.0 8.4 %collective-permute-start.3 = (bf16[2,512,128]{2,1,0:T(8,128)(2,1)S(1)}, bf16[2,512,128]{2,1,0:T(8,128)(2,1)S(1)}, u32[]{:S(2)}, u32[]{:S(2)}) collective-permute-start(bf16[2,512,128]{2,1,0:T(8,128)(2,1)S(1)} %get-tuple-element.42), channel_id=1, source_target_pairs={{0,2},{2,0},{4,6},{6,4},{1,3},{3,1},{5,7},{7,5},{8,10},{10,8},{12,... | collective-permute-start | bytes 786440 | tf_op jit(solution)/shard_map/ppermute | solution.py:350
  70.2 14.5 %copy-start.1 = (bf16[4,512,128]{2,1,0:T(8,128)(2,1)}, bf16[4,512,128]{2,1,0:T(8,128)(2,1)S(1)}, u32[]{:S(2)}) copy-start(bf16[4,512,128]{2,1,0:T(8,128)(2,1)S(1)} %pad_maximum_fusion.1.rest_6_) | copy-start | bytes 1572868
  70.5 14.2 %copy-start.2 = (bf16[4,512,128]{2,1,0:T(8,128)(2,1)}, bf16[4,512,128]{2,1,0:T(8,128)(2,1)S(1)}, u32[]{:S(2)}) copy-start(bf16[4,512,128]{2,1,0:T(8,128)(2,1)S(1)} %pad_maximum_fusion.rest_5_) | copy-start | bytes 1572868
  70.5 1.1 copy-start.3
  71.7 13.4 %collective-permute-start.8 = (bf16[4,512,128]{2,1,0:T(8,128)(2,1)S(1)}, bf16[4,512,128]{2,1,0:T(8,128)(2,1)S(1)}, u32[]{:S(2)}, u32[]{:S(2)}) collective-permute-start(bf16[4,512,128]{2,1,0:T(8,128)(2,1)S(1)} %pad_maximum_fusion.rest_5_), channel_id=1, source_target_pairs={{0,4},{2,6},{4,0},{6,2},{1,5},{3,7},{5,1},{7,3},{8,12},{10,14},{12... | collective-permute-start | bytes 1572872 | tf_op jit(solution)/shard_map/ppermute | solution.py:350
  73.1 12.9 %collective-permute-start.9 = (bf16[4,512,128]{2,1,0:T(8,128)(2,1)S(1)}, bf16[4,512,128]{2,1,0:T(8,128)(2,1)S(1)}, u32[]{:S(2)}, u32[]{:S(2)}) collective-permute-start(bf16[4,512,128]{2,1,0:T(8,128)(2,1)S(1)} %pad_maximum_fusion.1.rest_6_), channel_id=1, source_target_pairs={{0,2},{2,0},{4,6},{6,4},{1,3},{3,1},{5,7},{7,5},{8,10},{10,8},{12,... | collective-permute-start | bytes 1572872 | tf_op jit(solution)/shard_map/ppermute | solution.py:350
  74.4 12.2 %collective-permute-start.10 = (bf16[4,512,128]{2,1,0:T(8,128)(2,1)S(1)}, bf16[4,512,128]{2,1,0:T(8,128)(2,1)S(1)}, u32[]{:S(2)}, u32[]{:S(2)}) collective-permute-start(bf16[4,512,128]{2,1,0:T(8,128)(2,1)S(1)} %pad_maximum_fusion.rest_5_), channel_id=1, source_target_pairs={{0,1},{1,0},{2,3},{3,2},{4,5},{5,4},{6,7},{7,6},{8,9},{9,8},{10,11... | collective-permute-start | bytes 1572872 | tf_op jit(solution)/shard_map/ppermute | solution.py:350
  74.4 12.2 %collective-permute-start.11 = (bf16[4,512,128]{2,1,0:T(8,128)(2,1)S(1)}, bf16[4,512,128]{2,1,0:T(8,128)(2,1)S(1)}, u32[]{:S(2)}, u32[]{:S(2)}) collective-permute-start(bf16[4,512,128]{2,1,0:T(8,128)(2,1)S(1)} %pad_maximum_fusion.1.rest_6_), channel_id=1, source_target_pairs={{0,1},{1,0},{2,3},{3,2},{4,5},{5,4},{6,7},{7,6},{8,9},{9,8},{10,11... | collective-permute-start | bytes 1572872 | tf_op jit(solution)/shard_map/ppermute | solution.py:350
  85.0 3.7 %copy-start.5 = (bf16[4,512,128]{2,1,0:T(8,128)(2,1)}, bf16[4,512,128]{2,1,0:T(8,128)(2,1)S(1)}, u32[]{:S(2)}) copy-start(bf16[4,512,128]{2,1,0:T(8,128)(2,1)S(1)} %collective-permute-done.8.rest_7_) | copy-start | bytes 1572868
  86.1 2.7 %copy-start.6 = (bf16[4,512,128]{2,1,0:T(8,128)(2,1)}, bf16[4,512,128]{2,1,0:T(8,128)(2,1)S(1)}, u32[]{:S(2)}) copy-start(bf16[4,512,128]{2,1,0:T(8,128)(2,1)S(1)} %collective-permute-done.9.rest_8_) | copy-start | bytes 1572868
  86.1 1.9 %collective-permute-start.12 = (bf16[4,512,128]{2,1,0:T(8,128)(2,1)S(1)}, bf16[4,512,128]{2,1,0:T(8,128)(2,1)S(1)}, u32[]{:S(2)}, u32[]{:S(2)}) collective-permute-start(bf16[4,512,128]{2,1,0:T(8,128)(2,1)S(1)} %collective-permute-done.8.rest_7_), channel_id=1, source_target_pairs={{0,1},{1,0},{2,3},{3,2},{4,5},{5,4},{6,7},{7,6},{8,9},{9,8},{10,11... | collective-permute-start | bytes 1572872 | tf_op jit(solution)/shard_map/ppermute | solution.py:350
  86.1 2.7 %collective-permute-start.13 = (bf16[4,512,128]{2,1,0:T(8,128)(2,1)S(1)}, bf16[4,512,128]{2,1,0:T(8,128)(2,1)S(1)}, u32[]{:S(2)}, u32[]{:S(2)}) collective-permute-start(bf16[4,512,128]{2,1,0:T(8,128)(2,1)S(1)} %collective-permute-done.9.rest_8_), channel_id=1, source_target_pairs={{0,1},{1,0},{2,3},{3,2},{4,5},{5,4},{6,7},{7,6},{8,9},{9,8},{10,11... | collective-permute-start | bytes 1572872 | tf_op jit(solution)/shard_map/ppermute | solution.py:350
  86.6 2.2 %copy-start.7 = (bf16[4,512,128]{2,1,0:T(8,128)(2,1)}, bf16[4,512,128]{2,1,0:T(8,128)(2,1)S(1)}, u32[]{:S(2)}) copy-start(bf16[4,512,128]{2,1,0:T(8,128)(2,1)S(1)} %collective-permute-done.10.rest_9_) | copy-start | bytes 1572868
  86.6 2.2 %copy-start.8 = (bf16[4,512,128]{2,1,0:T(8,128)(2,1)}, bf16[4,512,128]{2,1,0:T(8,128)(2,1)S(1)}, u32[]{:S(2)}) copy-start(bf16[4,512,128]{2,1,0:T(8,128)(2,1)S(1)} %collective-permute-done.11.rest_10_) | copy-start | bytes 1572868
  88.0 0.8 copy-start.9
  88.7 0.8 copy-start.10

commit v9 on v7

--- a/solution.py
+++ b/solution.py
@@ -419,7 +419,8 @@
     smalls, homes[1] = together((smalls, homes[1]))
     smalls = jnp.concatenate(smalls + along_other_chip_axis(smalls))
     homes, smalls = together((homes, smalls))
-    homes, others = together((along_one_chip_axis(homes), swap(smalls, "core", 1)))
+    others = swap(smalls, "core", 1)
+    homes = along_one_chip_axis(homes)
     last = along_other_chip_axis(homes)
 
     where = jnp.stack([row, chip, core]).astype(jnp.int32)

time: 135 us -> 132 us (0.978); the launches traced: 135 us -> 133 us
  waiting for transfers between devices: 24.2 us -> 22.6 us
    ppermute x23, waiting for transfers between devices: 24.2 us -> 22.6 us  [swap(): return lax.ppermute(x, axis, [(i, i ^ distance) for i in range(size)])]
  transfers between devices with their start and end apart: 23 -> 23, of which waited for: 13 -> 11; matrix products, arithmetic and copies ran while one was open for 4% -> 4% of each run, Pallas kernels for 7% -> 7%
where the time goes in v9:
time: 132 us; the launch traced here: 133 us
  Pallas kernels  74.4 us (56%)
  starting transfers between devices  27.7 us (21%)
  waiting for transfers between devices  22.6 us (17%)
  local copies, waits for them, and re-layouts  3.8 us (3%)
  other arithmetic  3.67 us (3%)
    pallas_call x1, Pallas kernels, whole_on_each(): pl.pallas_call(functools.partial(iterate, n_row, n_col, n_cap, float(n_de...  64.4 us
    ppermute x23, starting transfers between devices, swap(): return lax.ppermute(x, axis, [(i, i ^ distance) for i in range(size)])  27.7 us
    ppermute x23, waiting for transfers between devices, swap(): return lax.ppermute(x, axis, [(i, i ^ distance) for i in range(size)])  22.6 us
    pallas_call x1, Pallas kernels, whole_on_each(): pl.pallas_call(functools.partial(unpack, n_row, n_col), out_shape=[jax.Sh...  9.96 us
  transfers between devices with their start and end apart: 23, of which 11 were waited for; matrix products, arithmetic and copies ran while one was open for 4% of the time, Pallas kernels for 7%

profile of v9, /device:TPU:0, one launch (start us, length us, event | category | flops | bytes accessed | tf_op | source)
XLA Modules:
  0.0 133.3 jit_solution(11587513865362680074)
XLA Ops:
  0.7 1.1 select_bitcast_fusion
  1.8 0.5 collective-permute-start
  2.4 0.7 fusion.6
  3.0 0.7 fusion.7
  3.7 0.7 sqrt.3
  4.3 0.1 reshape.207
  4.4 0.8 reshape.205
  5.2 0.1 copy.15
  5.3 0.1 reshape.206
  5.4 0.9 reshape.203
  6.3 0.1 bitcast_add_fusion
  6.4 2.6 %collective-permute-start.1 = (bf16[16,4096]{1,0:T(8,128)(2,1)S(1)}, bf16[16,4096]{1,0:T(8,128)(2,1)S(1)}, u32[]{:S(2)}, u32[]{:S(2)}) collective-permute-start(bf16[16,4096]{1,0:T(8,128)(2,1)S(1)} %get-tuple-element.51), channel_id=1, source_target_pairs={{0,2},{2,0},{4,6},{6,4},{1,3},{3,1},{5,7},{7,5},{8,10},{10,8},{12,... | collective-permute-start | bytes 393224 | tf_op jit(solution)/shard_map/ppermute | solution.py:353
  9.0 1.5 %collective-permute-start.2 = (bf16[16,4096]{1,0:T(8,128)(2,1)S(1)}, bf16[16,4096]{1,0:T(8,128)(2,1)S(1)}, u32[]{:S(2)}, u32[]{:S(2)}) collective-permute-start(bf16[16,4096]{1,0:T(8,128)(2,1)S(1)} %get-tuple-element.53), channel_id=1, source_target_pairs={{0,4},{2,6},{4,0},{6,2},{1,5},{3,7},{5,1},{7,3},{8,12},{10,14},{12... | collective-permute-start | bytes 393224 | tf_op jit(solution)/shard_map/ppermute | solution.py:353
  10.6 0.1 reshape.204
  10.7 0.1 bitcast_maximum_fusion
  10.8 0.1 concatenate.48
  10.9 2.1 %collective-permute-start.4 = (bf16[336,128]{1,0:T(8,128)(2,1)S(1)}, bf16[336,128]{1,0:T(8,128)(2,1)S(1)}, u32[]{:S(2)}, u32[]{:S(2)}) collective-permute-start(bf16[336,128]{1,0:T(8,128)(2,1)S(1)} %concatenate.48), channel_id=1, source_target_pairs={{0,8},{8,0},{16,24},{24,16},{1,9},{9,1},{17,25},{25,17},{2,10},{10... | collective-permute-start | bytes 258056 | tf_op jit(solution)/shard_map/ppermute | solution.py:353
  13.0 2.6 %collective-permute-start.5 = (bf16[336,128]{1,0:T(8,128)(2,1)S(1)}, bf16[336,128]{1,0:T(8,128)(2,1)S(1)}, u32[]{:S(2)}, u32[]{:S(2)}) collective-permute-start(bf16[336,128]{1,0:T(8,128)(2,1)S(1)} %concatenate.48), channel_id=1, source_target_pairs={{0,16},{8,24},{16,0},{24,8},{1,17},{9,25},{17,1},{25,9},{2,18},{10... | collective-permute-start | bytes 258056 | tf_op jit(solution)/shard_map/ppermute | solution.py:353
  15.6 1.8 %collective-permute-start.6 = (bf16[336,128]{1,0:T(8,128)(2,1)S(1)}, bf16[336,128]{1,0:T(8,128)(2,1)S(1)}, u32[]{:S(2)}, u32[]{:S(2)}) collective-permute-start(bf16[336,128]{1,0:T(8,128)(2,1)S(1)} %concatenate.48), channel_id=1, source_target_pairs={{0,24},{8,16},{16,8},{24,0},{1,25},{9,17},{17,9},{25,1},{2,26},{10... | collective-permute-start | bytes 258056 | tf_op jit(solution)/shard_map/ppermute | solution.py:353
  17.6 4.8 %collective-permute-done.5 = bf16[336,128]{1,0:T(8,128)(2,1)S(1)} collective-permute-done((bf16[336,128]{1,0:T(8,128)(2,1)S(1)}, bf16[336,128]{1,0:T(8,128)(2,1)S(1)}, u32[]{:S(2)}, u32[]{:S(2)}) %collective-permute-start.5) | collective-permute-done | bytes 86048 | tf_op jit(solution)/shard_map/ppermute | solution.py:353
  22.4 1.6 %collective-permute-start.8 = (bf16[2,336,128]{2,1,0:T(8,128)(2,1)S(1)}, bf16[2,336,128]{2,1,0:T(8,128)(2,1)S(1)}, u32[]{:S(2)}, u32[]{:S(2)}) collective-permute-start(bf16[2,336,128]{2,1,0:T(8,128)(2,1)S(1)} %pad_maximum_fusion.8), channel_id=1, source_target_pairs={{0,4},{2,6},{4,0},{6,2},{1,5},{3,7},{5,1},{7,3},{8,12},{10,14},{12... | collective-permute-start | bytes 516104 | tf_op jit(solution)/shard_map/ppermute | solution.py:353
  24.0 1.6 %collective-permute-start.7 = (bf16[2,336,128]{2,1,0:T(8,128)(2,1)S(1)}, bf16[2,336,128]{2,1,0:T(8,128)(2,1)S(1)}, u32[]{:S(2)}, u32[]{:S(2)}) collective-permute-start(bf16[2,336,128]{2,1,0:T(8,128)(2,1)S(1)} %pad_maximum_fusion.7), channel_id=1, source_target_pairs={{0,2},{2,0},{4,6},{6,4},{1,3},{3,1},{5,7},{7,5},{8,10},{10,8},{12,... | collective-permute-start | bytes 516104 | tf_op jit(solution)/shard_map/ppermute | solution.py:353
  25.5 1.5 %collective-permute-start.9 = (bf16[512,128]{1,0:T(8,128)(2,1)S(1)}, bf16[512,128]{1,0:T(8,128)(2,1)S(1)}, u32[]{:S(2)}, u32[]{:S(2)}) collective-permute-start(bf16[512,128]{1,0:T(8,128)(2,1)S(1)} %bitcast.54), channel_id=1, source_target_pairs={{0,8},{8,0},{16,24},{24,16},{1,9},{9,1},{17,25},{25,17},{2,10},{10... | collective-permute-start | bytes 393224 | tf_op jit(solution)/shard_map/ppermute | solution.py:353
  27.0 0.8 collective-permute-done.8
  27.9 1.6 %collective-permute-done.7 = bf16[2,336,128]{2,1,0:T(8,128)(2,1)S(1)} collective-permute-done((bf16[2,336,128]{2,1,0:T(8,128)(2,1)S(1)}, bf16[2,336,128]{2,1,0:T(8,128)(2,1)S(1)}, u32[]{:S(2)}, u32[]{:S(2)}) %collective-permute-start.7) | collective-permute-done | bytes 172064 | tf_op jit(solution)/shard_map/ppermute | solution.py:353
  29.5 1.0 collective-permute-done.9
  30.5 0.5 collective-permute-start.12
  31.0 0.6 collective-permute-start.13
  31.6 2.5 %collective-permute-start.10 = (bf16[512,128]{1,0:T(8,128)(2,1)S(1)}, bf16[512,128]{1,0:T(8,128)(2,1)S(1)}, u32[]{:S(2)}, u32[]{:S(2)}) collective-permute-start(bf16[512,128]{1,0:T(8,128)(2,1)S(1)} %bitcast.55), channel_id=1, source_target_pairs={{0,16},{8,24},{16,0},{24,8},{1,17},{9,25},{17,1},{25,9},{2,18},{10... | collective-permute-start | bytes 393224 | tf_op jit(solution)/shard_map/ppermute | solution.py:353
  34.1 1.3 %collective-permute-start.11 = (bf16[512,128]{1,0:T(8,128)(2,1)S(1)}, bf16[512,128]{1,0:T(8,128)(2,1)S(1)}, u32[]{:S(2)}, u32[]{:S(2)}) collective-permute-start(bf16[512,128]{1,0:T(8,128)(2,1)S(1)} %bitcast.56), channel_id=1, source_target_pairs={{0,24},{8,16},{16,8},{24,0},{1,25},{9,17},{17,9},{25,1},{2,26},{10... | collective-permute-start | bytes 393224 | tf_op jit(solution)/shard_map/ppermute | solution.py:353
  35.4 2.3 %collective-permute-done.12 = bf16[4,336,128]{2,1,0:T(8,128)(2,1)S(1)} collective-permute-done((bf16[4,336,128]{2,1,0:T(8,128)(2,1)S(1)}, bf16[4,336,128]{2,1,0:T(8,128)(2,1)S(1)}, u32[]{:S(2)}, u32[]{:S(2)}) %collective-permute-start.12) | collective-permute-done | bytes 344096 | tf_op jit(solution)/shard_map/ppermute | solution.py:353
  37.7 0.5 collective-permute-done.13
  38.3 0.2 pad_maximum_fusion.mine
  38.4 3.1 %collective-permute-done.10 = bf16[512,128]{1,0:T(8,128)(2,1)S(1)} collective-permute-done((bf16[512,128]{1,0:T(8,128)(2,1)S(1)}, bf16[512,128]{1,0:T(8,128)(2,1)S(1)}, u32[]{:S(2)}, u32[]{:S(2)}) %collective-permute-start.10) | collective-permute-done | bytes 131104 | tf_op jit(solution)/shard_map/ppermute | solution.py:353
  41.6 1.7 %collective-permute-start.16 = (bf16[2,512,128]{2,1,0:T(8,128)(2,1)S(1)}, bf16[2,512,128]{2,1,0:T(8,128)(2,1)S(1)}, u32[]{:S(2)}, u32[]{:S(2)}) collective-permute-start(bf16[2,512,128]{2,1,0:T(8,128)(2,1)S(1)} %pad_maximum_fusion.6), channel_id=1, source_target_pairs={{0,4},{2,6},{4,0},{6,2},{1,5},{3,7},{5,1},{7,3},{8,12},{10,14},{12... | collective-permute-start | bytes 786440 | tf_op jit(solution)/shard_map/ppermute | solution.py:353
  43.3 1.3 collective-permute-start.14
  44.6 5.7 %collective-permute-done.16 = bf16[2,512,128]{2,1,0:T(8,128)(2,1)S(1)} collective-permute-done((bf16[2,512,128]{2,1,0:T(8,128)(2,1)S(1)}, bf16[2,512,128]{2,1,0:T(8,128)(2,1)S(1)}, u32[]{:S(2)}, u32[]{:S(2)}) %collective-permute-start.16) | collective-permute-done | bytes 262176 | tf_op jit(solution)/shard_map/ppermute | solution.py:353
  50.4 1.5 %collective-permute-start.17 = (bf16[4,512,128]{2,1,0:T(8,128)(2,1)S(1)}, bf16[4,512,128]{2,1,0:T(8,128)(2,1)S(1)}, u32[]{:S(2)}, u32[]{:S(2)}) collective-permute-start(bf16[4,512,128]{2,1,0:T(8,128)(2,1)S(1)} %pad_maximum_fusion.2.rest_6_), channel_id=1, source_target_pairs={{0,2},{2,0},{4,6},{6,4},{1,3},{3,1},{5,7},{7,5},{8,10},{10,8},{12,... | collective-permute-start | bytes 1572872 | tf_op jit(solution)/shard_map/ppermute | solution.py:353
  51.9 1.6 %collective-permute-start.15 = (bf16[4,512,128]{2,1,0:T(8,128)(2,1)S(1)}, bf16[4,512,128]{2,1,0:T(8,128)(2,1)S(1)}, u32[]{:S(2)}, u32[]{:S(2)}) collective-permute-start(bf16[4,512,128]{2,1,0:T(8,128)(2,1)S(1)} %pad_maximum_fusion.1.rest_5_), channel_id=1, source_target_pairs={{0,4},{2,6},{4,0},{6,2},{1,5},{3,7},{5,1},{7,3},{8,12},{10,14},{12... | collective-permute-start | bytes 1572872 | tf_op jit(solution)/shard_map/ppermute | solution.py:353
  53.5 0.7 pad_add_fusion.own
  54.2 0.5 collective-permute-start.19
  54.7 10.0 %unpack.1 = (s32[584]{0:T(1024)}, f32[8,128]{1,0:T(8,128)}, bf16[144,128,128]{2,1,0:T(8,128)(2,1)}, bf16[32,64,128]{2,1,0:T(8,128)(2,1)}, bf16[64,64,128]{2,1,0:...) custom-call(s32[3]{0:T(128)} %pad_add_fusion.own, bf16[16,336,128]{2,1,0:T(8,128)(2,1)} %copy-done, ...), custom_call_target="tpu_custom_call" | custom-call | bytes 11010048 | tf_op jit(solution)/shard_map/unpack/pallas_call | solution.py:435
  64.7 0.6 collective-permute-done.15.rest_7_
  65.3 0.5 collective-permute-start.22
  65.8 1.4 %collective-permute-done.21.rest_11_ = bf16[4,512,128]{2,1,0:T(8,128)(2,1)S(1)} collective-permute-done((bf16[4,512,128]{2,1,0:T(8,128)(2,1)S(1)}, bf16[4,512,128]{2,1,0:T(8,128)(2,1)S(1)}, u32[]{:S(2)}, u32[]{:S(2)}) %collective-permute-start.21) | collective-permute-done | bytes 524320 | tf_op jit(solution)/shard_map/ppermute | solution.py:353
  67.2 0.7 collective-permute-done.22.rest_12_
  68.0 0.7 copy-done.9
  68.8 64.4 %iterate.1 = f32[2,4096]{1,0:T(2,128)} custom-call(s32[3]{0:T(128)} %pad_add_fusion.own, s32[584]{0:T(1024)} %get-tuple-element.42.lists, f32[8,128]{1,0:T(8,128)} %get-tuple-element.43.place, bf16[144,128,128]{2,1,0:T(8,128)(2,1)} %get-tuple-element.44.rest_0_, bf16[32,64,128]{2,1,0:T(8,128)(2,1)} %get-tuple-element.45.rest_1_, ...), custom_call_target="tpu_custom_call" | custom-call | tf_op jit(solution)/shard_map/iterate/pallas_call | solution.py:456
  (57 shorter events, 0.7 us)
Async XLA Ops:
  0.0 6.3 %copy-start.3 = (bf16[1,1,128,4096]{3,2,1,0:T(8,128)(2,1)S(1)}, bf16[1,1,128,4096]{3,2,1,0:T(8,128)(2,1)}, u32[]{:S(2)}) copy-start(bf16[1,1,128,4096]{3,2,1,0:T(8,128)(2,1)} %param.7) | copy-start | bytes 3145732
  1.8 4.5 %collective-permute-start = (bf16[4,16,4096]{2,1,0:T(8,128)(2,1)S(1)}, bf16[4,16,4096]{2,1,0:T(8,128)(2,1)S(1)}, u32[]{:S(2)}, u32[]{:S(2)}) collective-permute-start(bf16[4,16,4096]{2,1,0:T(8,128)(2,1)S(1)} %select_bitcast_fusion), channel_id=1, source_target_pairs={{0,1},{1,0},{2,3},{3,2},{4,5},{5,4},{6,7},{7,6},{8,9},{9,8},{10,11... | collective-permute-start | bytes 1572872 | tf_op jit(solution)/shard_map/ppermute | solution.py:353
  6.4 9.2 %collective-permute-start.1 = (bf16[16,4096]{1,0:T(8,128)(2,1)S(1)}, bf16[16,4096]{1,0:T(8,128)(2,1)S(1)}, u32[]{:S(2)}, u32[]{:S(2)}) collective-permute-start(bf16[16,4096]{1,0:T(8,128)(2,1)S(1)} %get-tuple-element.51), channel_id=1, source_target_pairs={{0,2},{2,0},{4,6},{6,4},{1,3},{3,1},{5,7},{7,5},{8,10},{10,8},{12,... | collective-permute-start | bytes 393224 | tf_op jit(solution)/shard_map/ppermute | solution.py:353
  9.0 8.4 %collective-permute-start.2 = (bf16[16,4096]{1,0:T(8,128)(2,1)S(1)}, bf16[16,4096]{1,0:T(8,128)(2,1)S(1)}, u32[]{:S(2)}, u32[]{:S(2)}) collective-permute-start(bf16[16,4096]{1,0:T(8,128)(2,1)S(1)} %get-tuple-element.53), channel_id=1, source_target_pairs={{0,4},{2,6},{4,0},{6,2},{1,5},{3,7},{5,1},{7,3},{8,12},{10,14},{12... | collective-permute-start | bytes 393224 | tf_op jit(solution)/shard_map/ppermute | solution.py:353
  10.5 6.9 %collective-permute-start.3 = (bf16[16,4096]{1,0:T(8,128)(2,1)S(1)}, bf16[16,4096]{1,0:T(8,128)(2,1)S(1)}, u32[]{:S(2)}, u32[]{:S(2)}) collective-permute-start(bf16[16,4096]{1,0:T(8,128)(2,1)S(1)} %get-tuple-element.52), channel_id=1, source_target_pairs={{0,6},{2,4},{4,2},{6,0},{1,7},{3,5},{5,3},{7,1},{8,14},{10,12},{12... | collective-permute-start | bytes 393224 | tf_op jit(solution)/shard_map/ppermute | solution.py:353
  10.9 6.6 %collective-permute-start.4 = (bf16[336,128]{1,0:T(8,128)(2,1)S(1)}, bf16[336,128]{1,0:T(8,128)(2,1)S(1)}, u32[]{:S(2)}, u32[]{:S(2)}) collective-permute-start(bf16[336,128]{1,0:T(8,128)(2,1)S(1)} %concatenate.48), channel_id=1, source_target_pairs={{0,8},{8,0},{16,24},{24,16},{1,9},{9,1},{17,25},{25,17},{2,10},{10... | collective-permute-start | bytes 258056 | tf_op jit(solution)/shard_map/ppermute | solution.py:353
  13.0 9.3 %collective-permute-start.5 = (bf16[336,128]{1,0:T(8,128)(2,1)S(1)}, bf16[336,128]{1,0:T(8,128)(2,1)S(1)}, u32[]{:S(2)}, u32[]{:S(2)}) collective-permute-start(bf16[336,128]{1,0:T(8,128)(2,1)S(1)} %concatenate.48), channel_id=1, source_target_pairs={{0,16},{8,24},{16,0},{24,8},{1,17},{9,25},{17,1},{25,9},{2,18},{10... | collective-permute-start | bytes 258056 | tf_op jit(solution)/shard_map/ppermute | solution.py:353
  15.6 6.7 %collective-permute-start.6 = (bf16[336,128]{1,0:T(8,128)(2,1)S(1)}, bf16[336,128]{1,0:T(8,128)(2,1)S(1)}, u32[]{:S(2)}, u32[]{:S(2)}) collective-permute-start(bf16[336,128]{1,0:T(8,128)(2,1)S(1)} %concatenate.48), channel_id=1, source_target_pairs={{0,24},{8,16},{16,8},{24,0},{1,25},{9,17},{17,9},{25,1},{2,26},{10... | collective-permute-start | bytes 258056 | tf_op jit(solution)/shard_map/ppermute | solution.py:353
  22.4 5.5 %collective-permute-start.8 = (bf16[2,336,128]{2,1,0:T(8,128)(2,1)S(1)}, bf16[2,336,128]{2,1,0:T(8,128)(2,1)S(1)}, u32[]{:S(2)}, u32[]{:S(2)}) collective-permute-start(bf16[2,336,128]{2,1,0:T(8,128)(2,1)S(1)} %pad_maximum_fusion.8), channel_id=1, source_target_pairs={{0,4},{2,6},{4,0},{6,2},{1,5},{3,7},{5,1},{7,3},{8,12},{10,14},{12... | collective-permute-start | bytes 516104 | tf_op jit(solution)/shard_map/ppermute | solution.py:353
  24.0 5.5 %collective-permute-start.7 = (bf16[2,336,128]{2,1,0:T(8,128)(2,1)S(1)}, bf16[2,336,128]{2,1,0:T(8,128)(2,1)S(1)}, u32[]{:S(2)}, u32[]{:S(2)}) collective-permute-start(bf16[2,336,128]{2,1,0:T(8,128)(2,1)S(1)} %pad_maximum_fusion.7), channel_id=1, source_target_pairs={{0,2},{2,0},{4,6},{6,4},{1,3},{3,1},{5,7},{7,5},{8,10},{10,8},{12,... | collective-permute-start | bytes 516104 | tf_op jit(solution)/shard_map/ppermute | solution.py:353
  25.5 5.0 %collective-permute-start.9 = (bf16[512,128]{1,0:T(8,128)(2,1)S(1)}, bf16[512,128]{1,0:T(8,128)(2,1)S(1)}, u32[]{:S(2)}, u32[]{:S(2)}) collective-permute-start(bf16[512,128]{1,0:T(8,128)(2,1)S(1)} %bitcast.54), channel_id=1, source_target_pairs={{0,8},{8,0},{16,24},{24,16},{1,9},{9,1},{17,25},{25,17},{2,10},{10... | collective-permute-start | bytes 393224 | tf_op jit(solution)/shard_map/ppermute | solution.py:353
  30.5 7.2 %collective-permute-start.12 = (bf16[4,336,128]{2,1,0:T(8,128)(2,1)S(1)}, bf16[4,336,128]{2,1,0:T(8,128)(2,1)S(1)}, u32[]{:S(2)}, u32[]{:S(2)}) collective-permute-start(bf16[4,336,128]{2,1,0:T(8,128)(2,1)S(1)} %pad_maximum_fusion.3), channel_id=1, source_target_pairs={{0,4},{2,6},{4,0},{6,2},{1,5},{3,7},{5,1},{7,3},{8,12},{10,14},{12... | collective-permute-start | bytes 1032200 | tf_op jit(solution)/shard_map/ppermute | solution.py:353
  31.0 7.2 %collective-permute-start.13 = (bf16[4,336,128]{2,1,0:T(8,128)(2,1)S(1)}, bf16[4,336,128]{2,1,0:T(8,128)(2,1)S(1)}, u32[]{:S(2)}, u32[]{:S(2)}) collective-permute-start(bf16[4,336,128]{2,1,0:T(8,128)(2,1)S(1)} %pad_maximum_fusion.4), channel_id=1, source_target_pairs={{0,2},{2,0},{4,6},{6,4},{1,3},{3,1},{5,7},{7,5},{8,10},{10,8},{12,... | collective-permute-start | bytes 1032200 | tf_op jit(solution)/shard_map/ppermute | solution.py:353
  31.6 10.0 %collective-permute-start.10 = (bf16[512,128]{1,0:T(8,128)(2,1)S(1)}, bf16[512,128]{1,0:T(8,128)(2,1)S(1)}, u32[]{:S(2)}, u32[]{:S(2)}) collective-permute-start(bf16[512,128]{1,0:T(8,128)(2,1)S(1)} %bitcast.55), channel_id=1, source_target_pairs={{0,16},{8,24},{16,0},{24,8},{1,17},{9,25},{17,1},{25,9},{2,18},{10... | collective-permute-start | bytes 393224 | tf_op jit(solution)/shard_map/ppermute | solution.py:353
  34.1 7.5 %collective-permute-start.11 = (bf16[512,128]{1,0:T(8,128)(2,1)S(1)}, bf16[512,128]{1,0:T(8,128)(2,1)S(1)}, u32[]{:S(2)}, u32[]{:S(2)}) collective-permute-start(bf16[512,128]{1,0:T(8,128)(2,1)S(1)} %bitcast.56), channel_id=1, source_target_pairs={{0,24},{8,16},{16,8},{24,0},{1,25},{9,17},{17,9},{25,1},{2,26},{10... | collective-permute-start | bytes 393224 | tf_op jit(solution)/shard_map/ppermute | solution.py:353
  38.4 13.5 %copy-start = (bf16[16,336,128]{2,1,0:T(8,128)(2,1)}, bf16[16,336,128]{2,1,0:T(8,128)(2,1)S(1)}, u32[]{:S(2)}) copy-start(bf16[16,336,128]{2,1,0:T(8,128)(2,1)S(1)} %pad_maximum_fusion.mine) | copy-start | bytes 4128772
  41.5 13.2 %collective-permute-start.18 = (bf16[16,336,128]{2,1,0:T(8,128)(2,1)S(1)}, bf16[16,336,128]{2,1,0:T(8,128)(2,1)}, u32[]{:S(2)}, u32[]{:S(2)}) collective-permute-start(bf16[16,336,128]{2,1,0:T(8,128)(2,1)S(1)} %pad_maximum_fusion.mine), channel_id=1, source_target_pairs={{0,1},{1,0},{2,3},{3,2},{4,5},{5,4},{6,7},{7,6},{8,9},{9,8},{10,11... | collective-permute-start | bytes 4128776 | tf_op jit(solution)/shard_map/ppermute | solution.py:353
  41.6 8.8 %collective-permute-start.16 = (bf16[2,512,128]{2,1,0:T(8,128)(2,1)S(1)}, bf16[2,512,128]{2,1,0:T(8,128)(2,1)S(1)}, u32[]{:S(2)}, u32[]{:S(2)}) collective-permute-start(bf16[2,512,128]{2,1,0:T(8,128)(2,1)S(1)} %pad_maximum_fusion.6), channel_id=1, source_target_pairs={{0,4},{2,6},{4,0},{6,2},{1,5},{3,7},{5,1},{7,3},{8,12},{10,14},{12... | collective-permute-start | bytes 786440 | tf_op jit(solution)/shard_map/ppermute | solution.py:353
  43.3 8.5 %collective-permute-start.14 = (bf16[2,512,128]{2,1,0:T(8,128)(2,1)S(1)}, bf16[2,512,128]{2,1,0:T(8,128)(2,1)S(1)}, u32[]{:S(2)}, u32[]{:S(2)}) collective-permute-start(bf16[2,512,128]{2,1,0:T(8,128)(2,1)S(1)} %pad_maximum_fusion.5), channel_id=1, source_target_pairs={{0,2},{2,0},{4,6},{6,4},{1,3},{3,1},{5,7},{7,5},{8,10},{10,8},{12,... | collective-permute-start | bytes 786440 | tf_op jit(solution)/shard_map/ppermute | solution.py:353
  50.4 14.3 %copy-start.1 = (bf16[4,512,128]{2,1,0:T(8,128)(2,1)}, bf16[4,512,128]{2,1,0:T(8,128)(2,1)S(1)}, u32[]{:S(2)}) copy-start(bf16[4,512,128]{2,1,0:T(8,128)(2,1)S(1)} %pad_maximum_fusion.2.rest_6_) | copy-start | bytes 1572868
  50.4 14.3 %collective-permute-start.17 = (bf16[4,512,128]{2,1,0:T(8,128)(2,1)S(1)}, bf16[4,512,128]{2,1,0:T(8,128)(2,1)S(1)}, u32[]{:S(2)}, u32[]{:S(2)}) collective-permute-start(bf16[4,512,128]{2,1,0:T(8,128)(2,1)S(1)} %pad_maximum_fusion.2.rest_6_), channel_id=1, source_target_pairs={{0,2},{2,0},{4,6},{6,4},{1,3},{3,1},{5,7},{7,5},{8,10},{10,8},{12,... | collective-permute-start | bytes 1572872 | tf_op jit(solution)/shard_map/ppermute | solution.py:353
  51.9 12.7 %copy-start.2 = (bf16[4,512,128]{2,1,0:T(8,128)(2,1)}, bf16[4,512,128]{2,1,0:T(8,128)(2,1)S(1)}, u32[]{:S(2)}) copy-start(bf16[4,512,128]{2,1,0:T(8,128)(2,1)S(1)} %pad_maximum_fusion.1.rest_5_) | copy-start | bytes 1572868
  51.9 13.3 %collective-permute-start.15 = (bf16[4,512,128]{2,1,0:T(8,128)(2,1)S(1)}, bf16[4,512,128]{2,1,0:T(8,128)(2,1)S(1)}, u32[]{:S(2)}, u32[]{:S(2)}) collective-permute-start(bf16[4,512,128]{2,1,0:T(8,128)(2,1)S(1)} %pad_maximum_fusion.1.rest_5_), channel_id=1, source_target_pairs={{0,4},{2,6},{4,0},{6,2},{1,5},{3,7},{5,1},{7,3},{8,12},{10,14},{12... | collective-permute-start | bytes 1572872 | tf_op jit(solution)/shard_map/ppermute | solution.py:353
  54.2 11.6 %collective-permute-start.20 = (bf16[4,512,128]{2,1,0:T(8,128)(2,1)S(1)}, bf16[4,512,128]{2,1,0:T(8,128)(2,1)S(1)}, u32[]{:S(2)}, u32[]{:S(2)}) collective-permute-start(bf16[4,512,128]{2,1,0:T(8,128)(2,1)S(1)} %pad_maximum_fusion.2.rest_6_), channel_id=1, source_target_pairs={{0,1},{1,0},{2,3},{3,2},{4,5},{5,4},{6,7},{7,6},{8,9},{9,8},{10,11... | collective-permute-start | bytes 1572872 | tf_op jit(solution)/shard_map/ppermute | solution.py:353
  54.2 11.6 %collective-permute-start.19 = (bf16[4,512,128]{2,1,0:T(8,128)(2,1)S(1)}, bf16[4,512,128]{2,1,0:T(8,128)(2,1)S(1)}, u32[]{:S(2)}, u32[]{:S(2)}) collective-permute-start(bf16[4,512,128]{2,1,0:T(8,128)(2,1)S(1)} %pad_maximum_fusion.1.rest_5_), channel_id=1, source_target_pairs={{0,1},{1,0},{2,3},{3,2},{4,5},{5,4},{6,7},{7,6},{8,9},{9,8},{10,11... | collective-permute-start | bytes 1572872 | tf_op jit(solution)/shard_map/ppermute | solution.py:353
  64.7 3.3 %copy-start.4 = (bf16[4,512,128]{2,1,0:T(8,128)(2,1)}, bf16[4,512,128]{2,1,0:T(8,128)(2,1)S(1)}, u32[]{:S(2)}) copy-start(bf16[4,512,128]{2,1,0:T(8,128)(2,1)S(1)} %collective-permute-done.17.rest_8_) | copy-start | bytes 1572868
  65.3 2.7 %copy-start.5 = (bf16[4,512,128]{2,1,0:T(8,128)(2,1)}, bf16[4,512,128]{2,1,0:T(8,128)(2,1)S(1)}, u32[]{:S(2)}) copy-start(bf16[4,512,128]{2,1,0:T(8,128)(2,1)S(1)} %collective-permute-done.15.rest_7_) | copy-start | bytes 1572868
  65.3 1.9 %collective-permute-start.21 = (bf16[4,512,128]{2,1,0:T(8,128)(2,1)S(1)}, bf16[4,512,128]{2,1,0:T(8,128)(2,1)S(1)}, u32[]{:S(2)}, u32[]{:S(2)}) collective-permute-start(bf16[4,512,128]{2,1,0:T(8,128)(2,1)S(1)} %collective-permute-done.15.rest_7_), channel_id=1, source_target_pairs={{0,1},{1,0},{2,3},{3,2},{4,5},{5,4},{6,7},{7,6},{8,9},{9,8},{10,11... | collective-permute-start | bytes 1572872 | tf_op jit(solution)/shard_map/ppermute | solution.py:353
  65.3 2.7 %collective-permute-start.22 = (bf16[4,512,128]{2,1,0:T(8,128)(2,1)S(1)}, bf16[4,512,128]{2,1,0:T(8,128)(2,1)S(1)}, u32[]{:S(2)}, u32[]{:S(2)}) collective-permute-start(bf16[4,512,128]{2,1,0:T(8,128)(2,1)S(1)} %collective-permute-done.17.rest_8_), channel_id=1, source_target_pairs={{0,1},{1,0},{2,3},{3,2},{4,5},{5,4},{6,7},{7,6},{8,9},{9,8},{10,11... | collective-permute-start | bytes 1572872 | tf_op jit(solution)/shard_map/ppermute | solution.py:353
  65.8 2.2 %copy-start.6 = (bf16[4,512,128]{2,1,0:T(8,128)(2,1)}, bf16[4,512,128]{2,1,0:T(8,128)(2,1)S(1)}, u32[]{:S(2)}) copy-start(bf16[4,512,128]{2,1,0:T(8,128)(2,1)S(1)} %collective-permute-done.20.rest_10_) | copy-start | bytes 1572868
  65.8 2.2 %copy-start.7 = (bf16[4,512,128]{2,1,0:T(8,128)(2,1)}, bf16[4,512,128]{2,1,0:T(8,128)(2,1)S(1)}, u32[]{:S(2)}) copy-start(bf16[4,512,128]{2,1,0:T(8,128)(2,1)S(1)} %collective-permute-done.19.rest_9_) | copy-start | bytes 1572868
  67.2 0.8 copy-start.8
  68.0 0.8 copy-start.9

commit v10 on v9

--- a/solution.py
+++ b/solution.py
@@ -12,7 +12,7 @@
 META = 16
 UNROLL = 16
 BATCH = 4
-VMEM_LIMIT = 56 * 1024 * 1024
+VMEM_LIMIT = 40 * 1024 * 1024
 
 NT = (((1,), (1,)), ((), ()))
 NN = (((1,), (0,)), ((), ()))
@@ -414,7 +414,8 @@
     home = home.reshape(part, half, 128).transpose(1, 0, 2).reshape(half * part, 128)
 
     together = lax.optimization_barrier
-    home, smalls = together((home, along_rows(small)))
+    where = jnp.stack([row, chip, core]).astype(jnp.int32)
+    home, smalls, where = together((home, along_rows(small), where))
     homes, smalls = along_rows(home), along_one_chip_axis(smalls)
     smalls, homes[1] = together((smalls, homes[1]))
     smalls = jnp.concatenate(smalls + along_other_chip_axis(smalls))
@@ -423,7 +424,6 @@
     homes = along_one_chip_axis(homes)
     last = along_other_chip_axis(homes)
 
-    where = jnp.stack([row, chip, core]).astype(jnp.int32)
     height, width = 2 * n_col * bsize, 2 * n_row * bsize
     slots = n_dev * OFF_CAP + 2 * UNROLL
     f32, i32, vmem, smem = jnp.float32, jnp.int32, pltpu.VMEM, pltpu.SMEM

time: 132 us -> 131 us (level)
  Pallas kernels: 74.4 us -> 69.7 us
  waiting for transfers between devices: 22.6 us -> 26.7 us
    ppermute x23, waiting for transfers between devices: 22.6 us -> 26.7 us  [swap(): return lax.ppermute(x, axis, [(i, i ^ distance) for i in range(size)])]
    pallas_call x1, Pallas kernels: 9.96 us -> 6.6 us  [whole_on_each(): pl.pallas_call(functools.partial(unpack, n_row, n_col), out_shape=[jax.Sh...]
  transfers between devices with their start and end apart: 23 -> 23, of which waited for: 11 -> 12; matrix products, arithmetic and copies ran while one was open for 4% -> 4% of each run, Pallas kernels for 7% -> 5%
where the time goes in v10:
time: 131 us
  Pallas kernels  69.7 us (53%)
  starting transfers between devices  27.6 us (21%)
  waiting for transfers between devices  26.7 us (20%)
  other arithmetic  3.1 us (2%)
  local copies, waits for them, and re-layouts  2.99 us (2%)
    pallas_call x1, Pallas kernels, whole_on_each(): pl.pallas_call(functools.partial(iterate, n_row, n_col, n_cap, float(n_de...  63.1 us
    ppermute x23, starting transfers between devices, swap(): return lax.ppermute(x, axis, [(i, i ^ distance) for i in range(size)])  27.6 us
    ppermute x23, waiting for transfers between devices, swap(): return lax.ppermute(x, axis, [(i, i ^ distance) for i in range(size)])  26.7 us
    pallas_call x1, Pallas kernels, whole_on_each(): pl.pallas_call(functools.partial(unpack, n_row, n_col), out_shape=[jax.Sh...  6.6 us
  transfers between devices with their start and end apart: 23, of which 12 were waited for; matrix products, arithmetic and copies ran while one was open for 4% of the time, Pallas kernels for 5%

profile of v10, /device:TPU:0, one launch (start us, length us, event | category | flops | bytes accessed | tf_op | source)
XLA Modules:
  0.0 131.2 jit_solution(13732046232425002875)
XLA Ops:
  0.7 1.1 select_bitcast_fusion
  1.8 0.5 collective-permute-start
  2.4 0.7 fusion.6
  3.0 0.7 fusion.7
  3.7 0.7 sqrt.3
  4.4 0.1 reshape.207
  4.4 0.8 reshape.205
  5.2 0.1 copy.15
  5.3 0.1 reshape.206
  5.4 0.9 reshape.203
  6.3 0.1 bitcast_add_fusion
  6.4 2.6 %collective-permute-start.1 = (bf16[16,4096]{1,0:T(8,128)(2,1)S(1)}, bf16[16,4096]{1,0:T(8,128)(2,1)S(1)}, u32[]{:S(2)}, u32[]{:S(2)}) collective-permute-start(bf16[16,4096]{1,0:T(8,128)(2,1)S(1)} %get-tuple-element.53), channel_id=1, source_target_pairs={{0,2},{2,0},{4,6},{6,4},{1,3},{3,1},{5,7},{7,5},{8,10},{10,8},{12,... | collective-permute-start | bytes 393224 | tf_op jit(solution)/shard_map/ppermute | solution.py:353
  9.0 1.5 %collective-permute-start.2 = (bf16[16,4096]{1,0:T(8,128)(2,1)S(1)}, bf16[16,4096]{1,0:T(8,128)(2,1)S(1)}, u32[]{:S(2)}, u32[]{:S(2)}) collective-permute-start(bf16[16,4096]{1,0:T(8,128)(2,1)S(1)} %get-tuple-element.55), channel_id=1, source_target_pairs={{0,4},{2,6},{4,0},{6,2},{1,5},{3,7},{5,1},{7,3},{8,12},{10,14},{12... | collective-permute-start | bytes 393224 | tf_op jit(solution)/shard_map/ppermute | solution.py:353
  10.5 0.1 bitcast_maximum_fusion
  10.7 0.1 reshape.204
  10.8 0.1 concatenate.48
  10.9 2.1 %collective-permute-start.4 = (bf16[336,128]{1,0:T(8,128)(2,1)S(1)}, bf16[336,128]{1,0:T(8,128)(2,1)S(1)}, u32[]{:S(2)}, u32[]{:S(2)}) collective-permute-start(bf16[336,128]{1,0:T(8,128)(2,1)S(1)} %concatenate.48), channel_id=1, source_target_pairs={{0,8},{8,0},{16,24},{24,16},{1,9},{9,1},{17,25},{25,17},{2,10},{10... | collective-permute-start | bytes 258056 | tf_op jit(solution)/shard_map/ppermute | solution.py:353
  13.0 2.6 %collective-permute-start.5 = (bf16[336,128]{1,0:T(8,128)(2,1)S(1)}, bf16[336,128]{1,0:T(8,128)(2,1)S(1)}, u32[]{:S(2)}, u32[]{:S(2)}) collective-permute-start(bf16[336,128]{1,0:T(8,128)(2,1)S(1)} %concatenate.48), channel_id=1, source_target_pairs={{0,16},{8,24},{16,0},{24,8},{1,17},{9,25},{17,1},{25,9},{2,18},{10... | collective-permute-start | bytes 258056 | tf_op jit(solution)/shard_map/ppermute | solution.py:353
  15.6 0.1 pad_add_fusion.own
  15.7 1.7 %collective-permute-start.6 = (bf16[336,128]{1,0:T(8,128)(2,1)S(1)}, bf16[336,128]{1,0:T(8,128)(2,1)S(1)}, u32[]{:S(2)}, u32[]{:S(2)}) collective-permute-start(bf16[336,128]{1,0:T(8,128)(2,1)S(1)} %concatenate.48), channel_id=1, source_target_pairs={{0,24},{8,16},{16,8},{24,0},{1,25},{9,17},{17,9},{25,1},{2,26},{10... | collective-permute-start | bytes 258056 | tf_op jit(solution)/shard_map/ppermute | solution.py:353
  17.6 4.8 %collective-permute-done.5 = bf16[336,128]{1,0:T(8,128)(2,1)S(1)} collective-permute-done((bf16[336,128]{1,0:T(8,128)(2,1)S(1)}, bf16[336,128]{1,0:T(8,128)(2,1)S(1)}, u32[]{:S(2)}, u32[]{:S(2)}) %collective-permute-start.5) | collective-permute-done | bytes 86048 | tf_op jit(solution)/shard_map/ppermute | solution.py:353
  22.4 1.6 %collective-permute-start.8 = (bf16[2,336,128]{2,1,0:T(8,128)(2,1)S(1)}, bf16[2,336,128]{2,1,0:T(8,128)(2,1)S(1)}, u32[]{:S(2)}, u32[]{:S(2)}) collective-permute-start(bf16[2,336,128]{2,1,0:T(8,128)(2,1)S(1)} %pad_maximum_fusion.8), channel_id=1, source_target_pairs={{0,4},{2,6},{4,0},{6,2},{1,5},{3,7},{5,1},{7,3},{8,12},{10,14},{12... | collective-permute-start | bytes 516104 | tf_op jit(solution)/shard_map/ppermute | solution.py:353
  24.0 1.6 %collective-permute-start.7 = (bf16[2,336,128]{2,1,0:T(8,128)(2,1)S(1)}, bf16[2,336,128]{2,1,0:T(8,128)(2,1)S(1)}, u32[]{:S(2)}, u32[]{:S(2)}) collective-permute-start(bf16[2,336,128]{2,1,0:T(8,128)(2,1)S(1)} %pad_maximum_fusion.7), channel_id=1, source_target_pairs={{0,2},{2,0},{4,6},{6,4},{1,3},{3,1},{5,7},{7,5},{8,10},{10,8},{12,... | collective-permute-start | bytes 516104 | tf_op jit(solution)/shard_map/ppermute | solution.py:353
  25.5 1.5 %collective-permute-start.9 = (bf16[512,128]{1,0:T(8,128)(2,1)S(1)}, bf16[512,128]{1,0:T(8,128)(2,1)S(1)}, u32[]{:S(2)}, u32[]{:S(2)}) collective-permute-start(bf16[512,128]{1,0:T(8,128)(2,1)S(1)} %bitcast.54), channel_id=1, source_target_pairs={{0,8},{8,0},{16,24},{24,16},{1,9},{9,1},{17,25},{25,17},{2,10},{10... | collective-permute-start | bytes 393224 | tf_op jit(solution)/shard_map/ppermute | solution.py:353
  27.0 0.8 collective-permute-done.8
  27.9 1.6 %collective-permute-done.7 = bf16[2,336,128]{2,1,0:T(8,128)(2,1)S(1)} collective-permute-done((bf16[2,336,128]{2,1,0:T(8,128)(2,1)S(1)}, bf16[2,336,128]{2,1,0:T(8,128)(2,1)S(1)}, u32[]{:S(2)}, u32[]{:S(2)}) %collective-permute-start.7) | collective-permute-done | bytes 172064 | tf_op jit(solution)/shard_map/ppermute | solution.py:353
  29.5 1.0 collective-permute-done.9
  30.5 0.5 collective-permute-start.12
  31.0 0.6 collective-permute-start.13
  31.6 2.5 %collective-permute-start.10 = (bf16[512,128]{1,0:T(8,128)(2,1)S(1)}, bf16[512,128]{1,0:T(8,128)(2,1)S(1)}, u32[]{:S(2)}, u32[]{:S(2)}) collective-permute-start(bf16[512,128]{1,0:T(8,128)(2,1)S(1)} %bitcast.55), channel_id=1, source_target_pairs={{0,16},{8,24},{16,0},{24,8},{1,17},{9,25},{17,1},{25,9},{2,18},{10... | collective-permute-start | bytes 393224 | tf_op jit(solution)/shard_map/ppermute | solution.py:353
  34.1 1.3 %collective-permute-start.11 = (bf16[512,128]{1,0:T(8,128)(2,1)S(1)}, bf16[512,128]{1,0:T(8,128)(2,1)S(1)}, u32[]{:S(2)}, u32[]{:S(2)}) collective-permute-start(bf16[512,128]{1,0:T(8,128)(2,1)S(1)} %bitcast.56), channel_id=1, source_target_pairs={{0,24},{8,16},{16,8},{24,0},{1,25},{9,17},{17,9},{25,1},{2,26},{10... | collective-permute-start | bytes 393224 | tf_op jit(solution)/shard_map/ppermute | solution.py:353
  35.4 2.3 %collective-permute-done.12 = bf16[4,336,128]{2,1,0:T(8,128)(2,1)S(1)} collective-permute-done((bf16[4,336,128]{2,1,0:T(8,128)(2,1)S(1)}, bf16[4,336,128]{2,1,0:T(8,128)(2,1)S(1)}, u32[]{:S(2)}, u32[]{:S(2)}) %collective-permute-start.12) | collective-permute-done | bytes 344096 | tf_op jit(solution)/shard_map/ppermute | solution.py:353
  37.8 0.5 collective-permute-done.13
  38.3 0.2 pad_maximum_fusion.mine
  38.4 3.1 %collective-permute-done.10 = bf16[512,128]{1,0:T(8,128)(2,1)S(1)} collective-permute-done((bf16[512,128]{1,0:T(8,128)(2,1)S(1)}, bf16[512,128]{1,0:T(8,128)(2,1)S(1)}, u32[]{:S(2)}, u32[]{:S(2)}) %collective-permute-start.10) | collective-permute-done | bytes 131104 | tf_op jit(solution)/shard_map/ppermute | solution.py:353
  41.6 1.7 %collective-permute-start.16 = (bf16[2,512,128]{2,1,0:T(8,128)(2,1)S(1)}, bf16[2,512,128]{2,1,0:T(8,128)(2,1)S(1)}, u32[]{:S(2)}, u32[]{:S(2)}) collective-permute-start(bf16[2,512,128]{2,1,0:T(8,128)(2,1)S(1)} %pad_maximum_fusion.6), channel_id=1, source_target_pairs={{0,4},{2,6},{4,0},{6,2},{1,5},{3,7},{5,1},{7,3},{8,12},{10,14},{12... | collective-permute-start | bytes 786440 | tf_op jit(solution)/shard_map/ppermute | solution.py:353
  43.3 1.3 collective-permute-start.14
  44.6 5.7 %collective-permute-done.16 = bf16[2,512,128]{2,1,0:T(8,128)(2,1)S(1)} collective-permute-done((bf16[2,512,128]{2,1,0:T(8,128)(2,1)S(1)}, bf16[2,512,128]{2,1,0:T(8,128)(2,1)S(1)}, u32[]{:S(2)}, u32[]{:S(2)}) %collective-permute-start.16) | collective-permute-done | bytes 262176 | tf_op jit(solution)/shard_map/ppermute | solution.py:353
  50.4 1.5 %collective-permute-start.17 = (bf16[4,512,128]{2,1,0:T(8,128)(2,1)S(1)}, bf16[4,512,128]{2,1,0:T(8,128)(2,1)S(1)}, u32[]{:S(2)}, u32[]{:S(2)}) collective-permute-start(bf16[4,512,128]{2,1,0:T(8,128)(2,1)S(1)} %pad_maximum_fusion.2.rest_6_), channel_id=1, source_target_pairs={{0,2},{2,0},{4,6},{6,4},{1,3},{3,1},{5,7},{7,5},{8,10},{10,8},{12,... | collective-permute-start | bytes 1572872 | tf_op jit(solution)/shard_map/ppermute | solution.py:353
  51.9 1.6 %collective-permute-start.15 = (bf16[4,512,128]{2,1,0:T(8,128)(2,1)S(1)}, bf16[4,512,128]{2,1,0:T(8,128)(2,1)S(1)}, u32[]{:S(2)}, u32[]{:S(2)}) collective-permute-start(bf16[4,512,128]{2,1,0:T(8,128)(2,1)S(1)} %pad_maximum_fusion.1.rest_5_), channel_id=1, source_target_pairs={{0,4},{2,6},{4,0},{6,2},{1,5},{3,7},{5,1},{7,3},{8,12},{10,14},{12... | collective-permute-start | bytes 1572872 | tf_op jit(solution)/shard_map/ppermute | solution.py:353
  53.5 0.5 collective-permute-start.19
  54.0 6.6 %unpack.1 = (s32[584]{0:T(1024)S(1)}, f32[8,128]{1,0:T(8,128)S(1)}, bf16[144,128,128]{2,1,0:T(8,128)(2,1)S(1)}, bf16[32,64,128]{2,1,0:T(8,128)(2,1)S(1)}, bf16[6...) custom-call(s32[3]{0:T(128)S(1)} %pad_add_fusion.own, ...), custom_call_target="tpu_custom_call" | custom-call | bytes 11010048 | tf_op jit(solution)/shard_map/unpack/pallas_call | solution.py:435
  60.6 3.4 %collective-permute-done.17.rest_8_ = bf16[4,512,128]{2,1,0:T(8,128)(2,1)S(1)} collective-permute-done((bf16[4,512,128]{2,1,0:T(8,128)(2,1)S(1)}, bf16[4,512,128]{2,1,0:T(8,128)(2,1)S(1)}, u32[]{:S(2)}, u32[]{:S(2)}) %collective-permute-start.17) | collective-permute-done | bytes 524320 | tf_op jit(solution)/shard_map/ppermute | solution.py:353
  64.0 1.2 collective-permute-done.15.rest_7_
  65.3 0.5 collective-permute-start.22
  65.8 1.4 %collective-permute-done.21.rest_11_ = bf16[4,512,128]{2,1,0:T(8,128)(2,1)S(1)} collective-permute-done((bf16[4,512,128]{2,1,0:T(8,128)(2,1)S(1)}, bf16[4,512,128]{2,1,0:T(8,128)(2,1)S(1)}, u32[]{:S(2)}, u32[]{:S(2)}) %collective-permute-start.21) | collective-permute-done | bytes 524320 | tf_op jit(solution)/shard_map/ppermute | solution.py:353
  67.2 0.7 collective-permute-done.22.rest_12_
  67.9 63.1 %iterate.1 = f32[2,4096]{1,0:T(2,128)} custom-call(s32[3]{0:T(128)S(1)} %pad_add_fusion.own, s32[584]{0:T(1024)S(1)} %get-tuple-element.44.lists, f32[8,128]{1,0:T(8,128)S(1)} %get-tuple-element.45.place, bf16[144,128,128]{2,1,0:T(8,128)(2,1)S(1)} %get-tuple-element.46.rest_0_, bf16[32,64,128]{2,1,0:T(8,128)(2,1)S(1)} %get-tuple-element.47.rest_1_, ...), custom_call_target="tpu_custom_call" | custom-call | tf_op jit(solution)/shard_map/iterate/pallas_call | solution.py:456
  (39 shorter events, 0.6 us)
Async XLA Ops:
  0.0 6.3 %copy-start = (bf16[1,1,128,4096]{3,2,1,0:T(8,128)(2,1)S(1)}, bf16[1,1,128,4096]{3,2,1,0:T(8,128)(2,1)}, u32[]{:S(2)}) copy-start(bf16[1,1,128,4096]{3,2,1,0:T(8,128)(2,1)} %param.7) | copy-start | bytes 3145732
  1.8 4.5 %collective-permute-start = (bf16[4,16,4096]{2,1,0:T(8,128)(2,1)S(1)}, bf16[4,16,4096]{2,1,0:T(8,128)(2,1)S(1)}, u32[]{:S(2)}, u32[]{:S(2)}) collective-permute-start(bf16[4,16,4096]{2,1,0:T(8,128)(2,1)S(1)} %select_bitcast_fusion), channel_id=1, source_target_pairs={{0,1},{1,0},{2,3},{3,2},{4,5},{5,4},{6,7},{7,6},{8,9},{9,8},{10,11... | collective-permute-start | bytes 1572872 | tf_op jit(solution)/shard_map/ppermute | solution.py:353
  6.4 9.3 %collective-permute-start.1 = (bf16[16,4096]{1,0:T(8,128)(2,1)S(1)}, bf16[16,4096]{1,0:T(8,128)(2,1)S(1)}, u32[]{:S(2)}, u32[]{:S(2)}) collective-permute-start(bf16[16,4096]{1,0:T(8,128)(2,1)S(1)} %get-tuple-element.53), channel_id=1, source_target_pairs={{0,2},{2,0},{4,6},{6,4},{1,3},{3,1},{5,7},{7,5},{8,10},{10,8},{12,... | collective-permute-start | bytes 393224 | tf_op jit(solution)/shard_map/ppermute | solution.py:353
  9.0 8.4 %collective-permute-start.2 = (bf16[16,4096]{1,0:T(8,128)(2,1)S(1)}, bf16[16,4096]{1,0:T(8,128)(2,1)S(1)}, u32[]{:S(2)}, u32[]{:S(2)}) collective-permute-start(bf16[16,4096]{1,0:T(8,128)(2,1)S(1)} %get-tuple-element.55), channel_id=1, source_target_pairs={{0,4},{2,6},{4,0},{6,2},{1,5},{3,7},{5,1},{7,3},{8,12},{10,14},{12... | collective-permute-start | bytes 393224 | tf_op jit(solution)/shard_map/ppermute | solution.py:353
  10.5 6.9 %collective-permute-start.3 = (bf16[16,4096]{1,0:T(8,128)(2,1)S(1)}, bf16[16,4096]{1,0:T(8,128)(2,1)S(1)}, u32[]{:S(2)}, u32[]{:S(2)}) collective-permute-start(bf16[16,4096]{1,0:T(8,128)(2,1)S(1)} %get-tuple-element.54), channel_id=1, source_target_pairs={{0,6},{2,4},{4,2},{6,0},{1,7},{3,5},{5,3},{7,1},{8,14},{10,12},{12... | collective-permute-start | bytes 393224 | tf_op jit(solution)/shard_map/ppermute | solution.py:353
  10.9 6.6 %collective-permute-start.4 = (bf16[336,128]{1,0:T(8,128)(2,1)S(1)}, bf16[336,128]{1,0:T(8,128)(2,1)S(1)}, u32[]{:S(2)}, u32[]{:S(2)}) collective-permute-start(bf16[336,128]{1,0:T(8,128)(2,1)S(1)} %concatenate.48), channel_id=1, source_target_pairs={{0,8},{8,0},{16,24},{24,16},{1,9},{9,1},{17,25},{25,17},{2,10},{10... | collective-permute-start | bytes 258056 | tf_op jit(solution)/shard_map/ppermute | solution.py:353
  13.0 9.3 %collective-permute-start.5 = (bf16[336,128]{1,0:T(8,128)(2,1)S(1)}, bf16[336,128]{1,0:T(8,128)(2,1)S(1)}, u32[]{:S(2)}, u32[]{:S(2)}) collective-permute-start(bf16[336,128]{1,0:T(8,128)(2,1)S(1)} %concatenate.48), channel_id=1, source_target_pairs={{0,16},{8,24},{16,0},{24,8},{1,17},{9,25},{17,1},{25,9},{2,18},{10... | collective-permute-start | bytes 258056 | tf_op jit(solution)/shard_map/ppermute | solution.py:353
  15.7 6.7 %collective-permute-start.6 = (bf16[336,128]{1,0:T(8,128)(2,1)S(1)}, bf16[336,128]{1,0:T(8,128)(2,1)S(1)}, u32[]{:S(2)}, u32[]{:S(2)}) collective-permute-start(bf16[336,128]{1,0:T(8,128)(2,1)S(1)} %concatenate.48), channel_id=1, source_target_pairs={{0,24},{8,16},{16,8},{24,0},{1,25},{9,17},{17,9},{25,1},{2,26},{10... | collective-permute-start | bytes 258056 | tf_op jit(solution)/shard_map/ppermute | solution.py:353
  22.4 5.5 %collective-permute-start.8 = (bf16[2,336,128]{2,1,0:T(8,128)(2,1)S(1)}, bf16[2,336,128]{2,1,0:T(8,128)(2,1)S(1)}, u32[]{:S(2)}, u32[]{:S(2)}) collective-permute-start(bf16[2,336,128]{2,1,0:T(8,128)(2,1)S(1)} %pad_maximum_fusion.8), channel_id=1, source_target_pairs={{0,4},{2,6},{4,0},{6,2},{1,5},{3,7},{5,1},{7,3},{8,12},{10,14},{12... | collective-permute-start | bytes 516104 | tf_op jit(solution)/shard_map/ppermute | solution.py:353
  24.0 5.5 %collective-permute-start.7 = (bf16[2,336,128]{2,1,0:T(8,128)(2,1)S(1)}, bf16[2,336,128]{2,1,0:T(8,128)(2,1)S(1)}, u32[]{:S(2)}, u32[]{:S(2)}) collective-permute-start(bf16[2,336,128]{2,1,0:T(8,128)(2,1)S(1)} %pad_maximum_fusion.7), channel_id=1, source_target_pairs={{0,2},{2,0},{4,6},{6,4},{1,3},{3,1},{5,7},{7,5},{8,10},{10,8},{12,... | collective-permute-start | bytes 516104 | tf_op jit(solution)/shard_map/ppermute | solution.py:353
  25.5 5.0 %collective-permute-start.9 = (bf16[512,128]{1,0:T(8,128)(2,1)S(1)}, bf16[512,128]{1,0:T(8,128)(2,1)S(1)}, u32[]{:S(2)}, u32[]{:S(2)}) collective-permute-start(bf16[512,128]{1,0:T(8,128)(2,1)S(1)} %bitcast.54), channel_id=1, source_target_pairs={{0,8},{8,0},{16,24},{24,16},{1,9},{9,1},{17,25},{25,17},{2,10},{10... | collective-permute-start | bytes 393224 | tf_op jit(solution)/shard_map/ppermute | solution.py:353
  30.5 7.2 %collective-permute-start.12 = (bf16[4,336,128]{2,1,0:T(8,128)(2,1)S(1)}, bf16[4,336,128]{2,1,0:T(8,128)(2,1)S(1)}, u32[]{:S(2)}, u32[]{:S(2)}) collective-permute-start(bf16[4,336,128]{2,1,0:T(8,128)(2,1)S(1)} %pad_maximum_fusion.3), channel_id=1, source_target_pairs={{0,4},{2,6},{4,0},{6,2},{1,5},{3,7},{5,1},{7,3},{8,12},{10,14},{12... | collective-permute-start | bytes 1032200 | tf_op jit(solution)/shard_map/ppermute | solution.py:353
  31.0 7.2 %collective-permute-start.13 = (bf16[4,336,128]{2,1,0:T(8,128)(2,1)S(1)}, bf16[4,336,128]{2,1,0:T(8,128)(2,1)S(1)}, u32[]{:S(2)}, u32[]{:S(2)}) collective-permute-start(bf16[4,336,128]{2,1,0:T(8,128)(2,1)S(1)} %pad_maximum_fusion.4), channel_id=1, source_target_pairs={{0,2},{2,0},{4,6},{6,4},{1,3},{3,1},{5,7},{7,5},{8,10},{10,8},{12,... | collective-permute-start | bytes 1032200 | tf_op jit(solution)/shard_map/ppermute | solution.py:353
  31.6 10.0 %collective-permute-start.10 = (bf16[512,128]{1,0:T(8,128)(2,1)S(1)}, bf16[512,128]{1,0:T(8,128)(2,1)S(1)}, u32[]{:S(2)}, u32[]{:S(2)}) collective-permute-start(bf16[512,128]{1,0:T(8,128)(2,1)S(1)} %bitcast.55), channel_id=1, source_target_pairs={{0,16},{8,24},{16,0},{24,8},{1,17},{9,25},{17,1},{25,9},{2,18},{10... | collective-permute-start | bytes 393224 | tf_op jit(solution)/shard_map/ppermute | solution.py:353
  34.1 7.5 %collective-permute-start.11 = (bf16[512,128]{1,0:T(8,128)(2,1)S(1)}, bf16[512,128]{1,0:T(8,128)(2,1)S(1)}, u32[]{:S(2)}, u32[]{:S(2)}) collective-permute-start(bf16[512,128]{1,0:T(8,128)(2,1)S(1)} %bitcast.56), channel_id=1, source_target_pairs={{0,24},{8,16},{16,8},{24,0},{1,25},{9,17},{17,9},{25,1},{2,26},{10... | collective-permute-start | bytes 393224 | tf_op jit(solution)/shard_map/ppermute | solution.py:353
  41.5 12.5 %collective-permute-start.18 = (bf16[16,336,128]{2,1,0:T(8,128)(2,1)S(1)}, bf16[16,336,128]{2,1,0:T(8,128)(2,1)S(1)}, u32[]{:S(2)}, u32[]{:S(2)}) collective-permute-start(bf16[16,336,128]{2,1,0:T(8,128)(2,1)S(1)} %pad_maximum_fusion.mine), channel_id=1, source_target_pairs={{0,1},{1,0},{2,3},{3,2},{4,5},{5,4},{6,7},{7,6},{8,9},{9,8},{10,11... | collective-permute-start | bytes 4128776 | tf_op jit(solution)/shard_map/ppermute | solution.py:353
  41.6 8.8 %collective-permute-start.16 = (bf16[2,512,128]{2,1,0:T(8,128)(2,1)S(1)}, bf16[2,512,128]{2,1,0:T(8,128)(2,1)S(1)}, u32[]{:S(2)}, u32[]{:S(2)}) collective-permute-start(bf16[2,512,128]{2,1,0:T(8,128)(2,1)S(1)} %pad_maximum_fusion.6), channel_id=1, source_target_pairs={{0,4},{2,6},{4,0},{6,2},{1,5},{3,7},{5,1},{7,3},{8,12},{10,14},{12... | collective-permute-start | bytes 786440 | tf_op jit(solution)/shard_map/ppermute | solution.py:353
  43.3 8.5 %collective-permute-start.14 = (bf16[2,512,128]{2,1,0:T(8,128)(2,1)S(1)}, bf16[2,512,128]{2,1,0:T(8,128)(2,1)S(1)}, u32[]{:S(2)}, u32[]{:S(2)}) collective-permute-start(bf16[2,512,128]{2,1,0:T(8,128)(2,1)S(1)} %pad_maximum_fusion.5), channel_id=1, source_target_pairs={{0,2},{2,0},{4,6},{6,4},{1,3},{3,1},{5,7},{7,5},{8,10},{10,8},{12,... | collective-permute-start | bytes 786440 | tf_op jit(solution)/shard_map/ppermute | solution.py:353
  50.4 13.6 %collective-permute-start.17 = (bf16[4,512,128]{2,1,0:T(8,128)(2,1)S(1)}, bf16[4,512,128]{2,1,0:T(8,128)(2,1)S(1)}, u32[]{:S(2)}, u32[]{:S(2)}) collective-permute-start(bf16[4,512,128]{2,1,0:T(8,128)(2,1)S(1)} %pad_maximum_fusion.2.rest_6_), channel_id=1, source_target_pairs={{0,2},{2,0},{4,6},{6,4},{1,3},{3,1},{5,7},{7,5},{8,10},{10,8},{12,... | collective-permute-start | bytes 1572872 | tf_op jit(solution)/shard_map/ppermute | solution.py:353
  51.9 13.3 %collective-permute-start.15 = (bf16[4,512,128]{2,1,0:T(8,128)(2,1)S(1)}, bf16[4,512,128]{2,1,0:T(8,128)(2,1)S(1)}, u32[]{:S(2)}, u32[]{:S(2)}) collective-permute-start(bf16[4,512,128]{2,1,0:T(8,128)(2,1)S(1)} %pad_maximum_fusion.1.rest_5_), channel_id=1, source_target_pairs={{0,4},{2,6},{4,0},{6,2},{1,5},{3,7},{5,1},{7,3},{8,12},{10,14},{12... | collective-permute-start | bytes 1572872 | tf_op jit(solution)/shard_map/ppermute | solution.py:353
  53.5 12.3 %collective-permute-start.20 = (bf16[4,512,128]{2,1,0:T(8,128)(2,1)S(1)}, bf16[4,512,128]{2,1,0:T(8,128)(2,1)S(1)}, u32[]{:S(2)}, u32[]{:S(2)}) collective-permute-start(bf16[4,512,128]{2,1,0:T(8,128)(2,1)S(1)} %pad_maximum_fusion.2.rest_6_), channel_id=1, source_target_pairs={{0,1},{1,0},{2,3},{3,2},{4,5},{5,4},{6,7},{7,6},{8,9},{9,8},{10,11... | collective-permute-start | bytes 1572872 | tf_op jit(solution)/shard_map/ppermute | solution.py:353
  53.5 12.3 %collective-permute-start.19 = (bf16[4,512,128]{2,1,0:T(8,128)(2,1)S(1)}, bf16[4,512,128]{2,1,0:T(8,128)(2,1)S(1)}, u32[]{:S(2)}, u32[]{:S(2)}) collective-permute-start(bf16[4,512,128]{2,1,0:T(8,128)(2,1)S(1)} %pad_maximum_fusion.1.rest_5_), channel_id=1, source_target_pairs={{0,1},{1,0},{2,3},{3,2},{4,5},{5,4},{6,7},{7,6},{8,9},{9,8},{10,11... | collective-permute-start | bytes 1572872 | tf_op jit(solution)/shard_map/ppermute | solution.py:353
  65.3 1.9 %collective-permute-start.21 = (bf16[4,512,128]{2,1,0:T(8,128)(2,1)S(1)}, bf16[4,512,128]{2,1,0:T(8,128)(2,1)S(1)}, u32[]{:S(2)}, u32[]{:S(2)}) collective-permute-start(bf16[4,512,128]{2,1,0:T(8,128)(2,1)S(1)} %collective-permute-done.15.rest_7_), channel_id=1, source_target_pairs={{0,1},{1,0},{2,3},{3,2},{4,5},{5,4},{6,7},{7,6},{8,9},{9,8},{10,11... | collective-permute-start | bytes 1572872 | tf_op jit(solution)/shard_map/ppermute | solution.py:353
  65.3 2.7 %collective-permute-start.22 = (bf16[4,512,128]{2,1,0:T(8,128)(2,1)S(1)}, bf16[4,512,128]{2,1,0:T(8,128)(2,1)S(1)}, u32[]{:S(2)}, u32[]{:S(2)}) collective-permute-start(bf16[4,512,128]{2,1,0:T(8,128)(2,1)S(1)} %collective-permute-done.17.rest_8_), channel_id=1, source_target_pairs={{0,1},{1,0},{2,3},{3,2},{4,5},{5,4},{6,7},{7,6},{8,9},{9,8},{10,11... | collective-permute-start | bytes 1572872 | tf_op jit(solution)/shard_map/ppermute | solution.py:353

commit v11 on v10

--- a/solution.py
+++ b/solution.py
@@ -114,21 +114,32 @@
 def add_products(n_group, blk, dims, lists, from_at, source, to_at, first, second):
     left = left_half(source.shape[1:])
 
+    def multiply(pairs):
+        return [
+            dot(
+                jnp.where(left, source[lists[from_at + 2 * p]], source[lists[from_at + 2 * p + 1]]),
+                blk[p],
+                dims,
+            )
+            for p in pairs
+        ]
+
+    def add(pairs, prods):
+        for p, prod in zip(pairs, prods):
+            a, b = lists[to_at + 2 * p], lists[to_at + 2 * p + 1]
+            first[a] = first[a] + prod
+            second[b] = second[b] + prod
+
     def group(i, carry):
-        for at in range(0, UNROLL, BATCH):
-            pairs = [i * UNROLL + at + u for u in range(BATCH)]
-            prods = [
-                dot(
-                    jnp.where(left, source[lists[from_at + 2 * p]], source[lists[from_at + 2 * p + 1]]),
-                    blk[p],
-                    dims,
-                )
-                for p in pairs
-            ]
-            for p, prod in zip(pairs, prods):
-                a, b = lists[to_at + 2 * p], lists[to_at + 2 * p + 1]
-                first[a] = first[a] + prod
-                second[b] = second[b] + prod
+        batches = [
+            [i * UNROLL + at + u for u in range(BATCH)] for at in range(0, UNROLL, BATCH)
+        ]
+        prods = multiply(batches[0])
+        for now, later in zip(batches, batches[1:]):
+            ahead = multiply(later)
+            add(now, prods)
+            prods = ahead
+        add(batches[-1], prods)
         return carry
 
     lax.fori_loop(0, n_group, group, 0)
@@ -236,22 +247,24 @@
 
         parts = [at_device(r, 2 * i + j) for j in range(2) for i in range(n_col // 2)]
 
-        def build(m, carry, parts=parts, select=select):
-            at = pl.multiple_of(m * part, part)
-            slots = jnp.concatenate(
-                [full[d, pl.ds(at, part), :] for d in parts], axis=0
-            )
-            dense = dot(select, slots)
-            for u in range(cpairs):
-                a = dense[2 * u * rblk : (2 * u + 1) * rblk]
-                b = dense[(2 * u + 1) * rblk : (2 * u + 2) * rblk]
-                even = jnp.where(left, a, pltpu.roll(b, 64, 1))
-                odd = jnp.where(left, pltpu.roll(a, 64, 1), b)
-                tmp[u, pl.ds(m, rblk, stride=k), :] = even
-                tmp[u, pl.ds(m + half, rblk, stride=k), :] = odd
+        def build(i, carry, parts=parts, select=select):
+            ms = [4 * i + d for d in range(4)]
+            denses = []
+            for m in ms:
+                at = pl.multiple_of(m * part, part)
+                slots = jnp.concatenate([full[d, pl.ds(at, part), :] for d in parts], axis=0)
+                denses.append(dot(select, slots))
+            for m, dense in zip(ms, denses):
+                for u in range(cpairs):
+                    a = dense[2 * u * rblk : (2 * u + 1) * rblk]
+                    b = dense[(2 * u + 1) * rblk : (2 * u + 2) * rblk]
+                    even = jnp.where(left, a, pltpu.roll(b, 64, 1))
+                    odd = jnp.where(left, pltpu.roll(a, 64, 1), b)
+                    tmp[u, pl.ds(m, rblk, stride=k), :] = even
+                    tmp[u, pl.ds(m + half, rblk, stride=k), :] = odd
             return carry
 
-        lax.fori_loop(0, half, build, 0, unroll=8)
+        lax.fori_loop(0, half // 4, build, 0, unroll=2)
 
         def cut(i, carry, r=r):
             at = pl.multiple_of(i * k, k)
@@ -298,15 +311,20 @@
             x = w[p] + gather_pair(p, w1, w2)
             store_twice(wt, wd, p, x * rm[p, 0:1, :])
 
-        for r in range(n_row):
-            base = homes[r] * cpairs
+        def back(r, u):
             vec = jnp.concatenate([wt[r * rpairs + p] for p in range(rpairs)], axis=1)
-            for u in range(0, cpairs, 2):
-                cols = slice(u * 128, (u + 2) * 128)
-                tail = slice(width + u * 128, width + (u + 2) * 128)
-                prod = dot(vec, home[r, :, cols]) + dot(vec, home[r, :, tail])
-                y[base + u] = y[base + u] + prod[:, :128]
-                y[base + u + 1] = y[base + u + 1] + prod[:, 128:]
+            cols = slice(u * 128, (u + 2) * 128)
+            tail = slice(width + u * 128, width + (u + 2) * 128)
+            return dot(vec, home[r, :, cols]) + dot(vec, home[r, :, tail])
+
+        steps = [(r, u) for r in range(n_row) for u in range(0, cpairs, 2)]
+        prod = back(*steps[0])
+        for i, (r, u) in enumerate(steps):
+            ahead = back(*steps[i + 1]) if i + 1 < len(steps) else None
+            q = homes[r] * cpairs + u
+            y[q] = y[q] + prod[:, :128]
+            y[q + 1] = y[q + 1] + prod[:, 128:]
+            prod = ahead
 
         add_products(n_group, blk, NN, lists, slots, wd, 0, y1, y2)
 

time: 131 us -> 133 us (1.015); the launches traced: 131 us -> 131 us
  no operation moved by 1% of the time
where the time goes in v11:
time: 133 us; the launch traced here: 131 us
  Pallas kernels  69.6 us (52%)
  starting transfers between devices  27.6 us (21%)
  waiting for transfers between devices  26.7 us (20%)
  other arithmetic  3.1 us (2%)
  local copies, waits for them, and re-layouts  2.99 us (2%)
    pallas_call x1, Pallas kernels, whole_on_each(): pl.pallas_call(functools.partial(iterate, n_row, n_col, n_cap, float(n_de...  63 us
    ppermute x23, starting transfers between devices, swap(): return lax.ppermute(x, axis, [(i, i ^ distance) for i in range(size)])  27.6 us
    ppermute x23, waiting for transfers between devices, swap(): return lax.ppermute(x, axis, [(i, i ^ distance) for i in range(size)])  26.7 us
    pallas_call x1, Pallas kernels, whole_on_each(): pl.pallas_call(functools.partial(unpack, n_row, n_col), out_shape=[jax.Sh...  6.6 us
  transfers between devices with their start and end apart: 23, of which 12 were waited for; matrix products, arithmetic and copies ran while one was open for 4% of the time, Pallas kernels for 5%

profile of v11, /device:TPU:0, one launch (start us, length us, event | category | flops | bytes accessed | tf_op | source)
XLA Modules:
  0.0 131.1 jit_solution(432769706815102738)
XLA Ops:
  0.7 1.1 select_bitcast_fusion
  1.8 0.5 collective-permute-start
  2.4 0.7 fusion.6
  3.0 0.7 fusion.7
  3.7 0.7 sqrt.3
  4.4 0.1 reshape.207
  4.4 0.8 reshape.205
  5.2 0.1 copy.15
  5.3 0.1 reshape.206
  5.4 0.9 reshape.203
  6.3 0.1 bitcast_add_fusion
  6.4 2.6 %collective-permute-start.1 = (bf16[16,4096]{1,0:T(8,128)(2,1)S(1)}, bf16[16,4096]{1,0:T(8,128)(2,1)S(1)}, u32[]{:S(2)}, u32[]{:S(2)}) collective-permute-start(bf16[16,4096]{1,0:T(8,128)(2,1)S(1)} %get-tuple-element.53), channel_id=1, source_target_pairs={{0,2},{2,0},{4,6},{6,4},{1,3},{3,1},{5,7},{7,5},{8,10},{10,8},{12,... | collective-permute-start | bytes 393224 | tf_op jit(solution)/shard_map/ppermute | solution.py:371
  9.0 1.5 %collective-permute-start.2 = (bf16[16,4096]{1,0:T(8,128)(2,1)S(1)}, bf16[16,4096]{1,0:T(8,128)(2,1)S(1)}, u32[]{:S(2)}, u32[]{:S(2)}) collective-permute-start(bf16[16,4096]{1,0:T(8,128)(2,1)S(1)} %get-tuple-element.55), channel_id=1, source_target_pairs={{0,4},{2,6},{4,0},{6,2},{1,5},{3,7},{5,1},{7,3},{8,12},{10,14},{12... | collective-permute-start | bytes 393224 | tf_op jit(solution)/shard_map/ppermute | solution.py:371
  10.5 0.1 bitcast_maximum_fusion
  10.7 0.1 reshape.204
  10.8 0.1 concatenate.48
  10.9 2.1 %collective-permute-start.4 = (bf16[336,128]{1,0:T(8,128)(2,1)S(1)}, bf16[336,128]{1,0:T(8,128)(2,1)S(1)}, u32[]{:S(2)}, u32[]{:S(2)}) collective-permute-start(bf16[336,128]{1,0:T(8,128)(2,1)S(1)} %concatenate.48), channel_id=1, source_target_pairs={{0,8},{8,0},{16,24},{24,16},{1,9},{9,1},{17,25},{25,17},{2,10},{10... | collective-permute-start | bytes 258056 | tf_op jit(solution)/shard_map/ppermute | solution.py:371
  13.0 2.6 %collective-permute-start.5 = (bf16[336,128]{1,0:T(8,128)(2,1)S(1)}, bf16[336,128]{1,0:T(8,128)(2,1)S(1)}, u32[]{:S(2)}, u32[]{:S(2)}) collective-permute-start(bf16[336,128]{1,0:T(8,128)(2,1)S(1)} %concatenate.48), channel_id=1, source_target_pairs={{0,16},{8,24},{16,0},{24,8},{1,17},{9,25},{17,1},{25,9},{2,18},{10... | collective-permute-start | bytes 258056 | tf_op jit(solution)/shard_map/ppermute | solution.py:371
  15.6 0.1 pad_add_fusion.own
  15.7 1.7 %collective-permute-start.6 = (bf16[336,128]{1,0:T(8,128)(2,1)S(1)}, bf16[336,128]{1,0:T(8,128)(2,1)S(1)}, u32[]{:S(2)}, u32[]{:S(2)}) collective-permute-start(bf16[336,128]{1,0:T(8,128)(2,1)S(1)} %concatenate.48), channel_id=1, source_target_pairs={{0,24},{8,16},{16,8},{24,0},{1,25},{9,17},{17,9},{25,1},{2,26},{10... | collective-permute-start | bytes 258056 | tf_op jit(solution)/shard_map/ppermute | solution.py:371
  17.6 4.8 %collective-permute-done.5 = bf16[336,128]{1,0:T(8,128)(2,1)S(1)} collective-permute-done((bf16[336,128]{1,0:T(8,128)(2,1)S(1)}, bf16[336,128]{1,0:T(8,128)(2,1)S(1)}, u32[]{:S(2)}, u32[]{:S(2)}) %collective-permute-start.5) | collective-permute-done | bytes 86048 | tf_op jit(solution)/shard_map/ppermute | solution.py:371
  22.4 1.6 %collective-permute-start.8 = (bf16[2,336,128]{2,1,0:T(8,128)(2,1)S(1)}, bf16[2,336,128]{2,1,0:T(8,128)(2,1)S(1)}, u32[]{:S(2)}, u32[]{:S(2)}) collective-permute-start(bf16[2,336,128]{2,1,0:T(8,128)(2,1)S(1)} %pad_maximum_fusion.8), channel_id=1, source_target_pairs={{0,4},{2,6},{4,0},{6,2},{1,5},{3,7},{5,1},{7,3},{8,12},{10,14},{12... | collective-permute-start | bytes 516104 | tf_op jit(solution)/shard_map/ppermute | solution.py:371
  24.0 1.6 %collective-permute-start.7 = (bf16[2,336,128]{2,1,0:T(8,128)(2,1)S(1)}, bf16[2,336,128]{2,1,0:T(8,128)(2,1)S(1)}, u32[]{:S(2)}, u32[]{:S(2)}) collective-permute-start(bf16[2,336,128]{2,1,0:T(8,128)(2,1)S(1)} %pad_maximum_fusion.7), channel_id=1, source_target_pairs={{0,2},{2,0},{4,6},{6,4},{1,3},{3,1},{5,7},{7,5},{8,10},{10,8},{12,... | collective-permute-start | bytes 516104 | tf_op jit(solution)/shard_map/ppermute | solution.py:371
  25.5 1.5 %collective-permute-start.9 = (bf16[512,128]{1,0:T(8,128)(2,1)S(1)}, bf16[512,128]{1,0:T(8,128)(2,1)S(1)}, u32[]{:S(2)}, u32[]{:S(2)}) collective-permute-start(bf16[512,128]{1,0:T(8,128)(2,1)S(1)} %bitcast.54), channel_id=1, source_target_pairs={{0,8},{8,0},{16,24},{24,16},{1,9},{9,1},{17,25},{25,17},{2,10},{10... | collective-permute-start | bytes 393224 | tf_op jit(solution)/shard_map/ppermute | solution.py:371
  27.0 0.8 collective-permute-done.8
  27.9 1.6 %collective-permute-done.7 = bf16[2,336,128]{2,1,0:T(8,128)(2,1)S(1)} collective-permute-done((bf16[2,336,128]{2,1,0:T(8,128)(2,1)S(1)}, bf16[2,336,128]{2,1,0:T(8,128)(2,1)S(1)}, u32[]{:S(2)}, u32[]{:S(2)}) %collective-permute-start.7) | collective-permute-done | bytes 172064 | tf_op jit(solution)/shard_map/ppermute | solution.py:371
  29.5 1.0 collective-permute-done.9
  30.5 0.5 collective-permute-start.12
  31.0 0.6 collective-permute-start.13
  31.6 2.5 %collective-permute-start.10 = (bf16[512,128]{1,0:T(8,128)(2,1)S(1)}, bf16[512,128]{1,0:T(8,128)(2,1)S(1)}, u32[]{:S(2)}, u32[]{:S(2)}) collective-permute-start(bf16[512,128]{1,0:T(8,128)(2,1)S(1)} %bitcast.55), channel_id=1, source_target_pairs={{0,16},{8,24},{16,0},{24,8},{1,17},{9,25},{17,1},{25,9},{2,18},{10... | collective-permute-start | bytes 393224 | tf_op jit(solution)/shard_map/ppermute | solution.py:371
  34.1 1.3 %collective-permute-start.11 = (bf16[512,128]{1,0:T(8,128)(2,1)S(1)}, bf16[512,128]{1,0:T(8,128)(2,1)S(1)}, u32[]{:S(2)}, u32[]{:S(2)}) collective-permute-start(bf16[512,128]{1,0:T(8,128)(2,1)S(1)} %bitcast.56), channel_id=1, source_target_pairs={{0,24},{8,16},{16,8},{24,0},{1,25},{9,17},{17,9},{25,1},{2,26},{10... | collective-permute-start | bytes 393224 | tf_op jit(solution)/shard_map/ppermute | solution.py:371
  35.4 2.3 %collective-permute-done.12 = bf16[4,336,128]{2,1,0:T(8,128)(2,1)S(1)} collective-permute-done((bf16[4,336,128]{2,1,0:T(8,128)(2,1)S(1)}, bf16[4,336,128]{2,1,0:T(8,128)(2,1)S(1)}, u32[]{:S(2)}, u32[]{:S(2)}) %collective-permute-start.12) | collective-permute-done | bytes 344096 | tf_op jit(solution)/shard_map/ppermute | solution.py:371
  37.8 0.5 collective-permute-done.13
  38.3 0.2 pad_maximum_fusion.mine
  38.4 3.1 %collective-permute-done.10 = bf16[512,128]{1,0:T(8,128)(2,1)S(1)} collective-permute-done((bf16[512,128]{1,0:T(8,128)(2,1)S(1)}, bf16[512,128]{1,0:T(8,128)(2,1)S(1)}, u32[]{:S(2)}, u32[]{:S(2)}) %collective-permute-start.10) | collective-permute-done | bytes 131104 | tf_op jit(solution)/shard_map/ppermute | solution.py:371
  41.6 1.7 %collective-permute-start.16 = (bf16[2,512,128]{2,1,0:T(8,128)(2,1)S(1)}, bf16[2,512,128]{2,1,0:T(8,128)(2,1)S(1)}, u32[]{:S(2)}, u32[]{:S(2)}) collective-permute-start(bf16[2,512,128]{2,1,0:T(8,128)(2,1)S(1)} %pad_maximum_fusion.6), channel_id=1, source_target_pairs={{0,4},{2,6},{4,0},{6,2},{1,5},{3,7},{5,1},{7,3},{8,12},{10,14},{12... | collective-permute-start | bytes 786440 | tf_op jit(solution)/shard_map/ppermute | solution.py:371
  43.3 1.3 collective-permute-start.14
  44.6 5.7 %collective-permute-done.16 = bf16[2,512,128]{2,1,0:T(8,128)(2,1)S(1)} collective-permute-done((bf16[2,512,128]{2,1,0:T(8,128)(2,1)S(1)}, bf16[2,512,128]{2,1,0:T(8,128)(2,1)S(1)}, u32[]{:S(2)}, u32[]{:S(2)}) %collective-permute-start.16) | collective-permute-done | bytes 262176 | tf_op jit(solution)/shard_map/ppermute | solution.py:371
  50.4 1.5 %collective-permute-start.17 = (bf16[4,512,128]{2,1,0:T(8,128)(2,1)S(1)}, bf16[4,512,128]{2,1,0:T(8,128)(2,1)S(1)}, u32[]{:S(2)}, u32[]{:S(2)}) collective-permute-start(bf16[4,512,128]{2,1,0:T(8,128)(2,1)S(1)} %pad_maximum_fusion.2.rest_6_), channel_id=1, source_target_pairs={{0,2},{2,0},{4,6},{6,4},{1,3},{3,1},{5,7},{7,5},{8,10},{10,8},{12,... | collective-permute-start | bytes 1572872 | tf_op jit(solution)/shard_map/ppermute | solution.py:371
  51.9 1.6 %collective-permute-start.15 = (bf16[4,512,128]{2,1,0:T(8,128)(2,1)S(1)}, bf16[4,512,128]{2,1,0:T(8,128)(2,1)S(1)}, u32[]{:S(2)}, u32[]{:S(2)}) collective-permute-start(bf16[4,512,128]{2,1,0:T(8,128)(2,1)S(1)} %pad_maximum_fusion.1.rest_5_), channel_id=1, source_target_pairs={{0,4},{2,6},{4,0},{6,2},{1,5},{3,7},{5,1},{7,3},{8,12},{10,14},{12... | collective-permute-start | bytes 1572872 | tf_op jit(solution)/shard_map/ppermute | solution.py:371
  53.5 0.5 collective-permute-start.19
  54.0 6.6 %unpack.1 = (s32[584]{0:T(1024)S(1)}, f32[8,128]{1,0:T(8,128)S(1)}, bf16[144,128,128]{2,1,0:T(8,128)(2,1)S(1)}, bf16[32,64,128]{2,1,0:T(8,128)(2,1)S(1)}, bf16[6...) custom-call(s32[3]{0:T(128)S(1)} %pad_add_fusion.own, ...), custom_call_target="tpu_custom_call" | custom-call | bytes 11010048 | tf_op jit(solution)/shard_map/unpack/pallas_call | solution.py:453
  60.6 3.4 %collective-permute-done.17.rest_8_ = bf16[4,512,128]{2,1,0:T(8,128)(2,1)S(1)} collective-permute-done((bf16[4,512,128]{2,1,0:T(8,128)(2,1)S(1)}, bf16[4,512,128]{2,1,0:T(8,128)(2,1)S(1)}, u32[]{:S(2)}, u32[]{:S(2)}) %collective-permute-start.17) | collective-permute-done | bytes 524320 | tf_op jit(solution)/shard_map/ppermute | solution.py:371
  64.0 1.2 collective-permute-done.15.rest_7_
  65.3 0.5 collective-permute-start.22
  65.8 1.4 %collective-permute-done.21.rest_11_ = bf16[4,512,128]{2,1,0:T(8,128)(2,1)S(1)} collective-permute-done((bf16[4,512,128]{2,1,0:T(8,128)(2,1)S(1)}, bf16[4,512,128]{2,1,0:T(8,128)(2,1)S(1)}, u32[]{:S(2)}, u32[]{:S(2)}) %collective-permute-start.21) | collective-permute-done | bytes 524320 | tf_op jit(solution)/shard_map/ppermute | solution.py:371
  67.2 0.7 collective-permute-done.22.rest_12_
  67.9 63.0 %iterate.1 = f32[2,4096]{1,0:T(2,128)} custom-call(s32[3]{0:T(128)S(1)} %pad_add_fusion.own, s32[584]{0:T(1024)S(1)} %get-tuple-element.44.lists, f32[8,128]{1,0:T(8,128)S(1)} %get-tuple-element.45.place, bf16[144,128,128]{2,1,0:T(8,128)(2,1)S(1)} %get-tuple-element.46.rest_0_, bf16[32,64,128]{2,1,0:T(8,128)(2,1)S(1)} %get-tuple-element.47.rest_1_, ...), custom_call_target="tpu_custom_call" | custom-call | tf_op jit(solution)/shard_map/iterate/pallas_call | solution.py:474
  (39 shorter events, 0.6 us)
Async XLA Ops:
  0.0 6.3 %copy-start = (bf16[1,1,128,4096]{3,2,1,0:T(8,128)(2,1)S(1)}, bf16[1,1,128,4096]{3,2,1,0:T(8,128)(2,1)}, u32[]{:S(2)}) copy-start(bf16[1,1,128,4096]{3,2,1,0:T(8,128)(2,1)} %param.7) | copy-start | bytes 3145732
  1.8 4.5 %collective-permute-start = (bf16[4,16,4096]{2,1,0:T(8,128)(2,1)S(1)}, bf16[4,16,4096]{2,1,0:T(8,128)(2,1)S(1)}, u32[]{:S(2)}, u32[]{:S(2)}) collective-permute-start(bf16[4,16,4096]{2,1,0:T(8,128)(2,1)S(1)} %select_bitcast_fusion), channel_id=1, source_target_pairs={{0,1},{1,0},{2,3},{3,2},{4,5},{5,4},{6,7},{7,6},{8,9},{9,8},{10,11... | collective-permute-start | bytes 1572872 | tf_op jit(solution)/shard_map/ppermute | solution.py:371
  6.4 9.3 %collective-permute-start.1 = (bf16[16,4096]{1,0:T(8,128)(2,1)S(1)}, bf16[16,4096]{1,0:T(8,128)(2,1)S(1)}, u32[]{:S(2)}, u32[]{:S(2)}) collective-permute-start(bf16[16,4096]{1,0:T(8,128)(2,1)S(1)} %get-tuple-element.53), channel_id=1, source_target_pairs={{0,2},{2,0},{4,6},{6,4},{1,3},{3,1},{5,7},{7,5},{8,10},{10,8},{12,... | collective-permute-start | bytes 393224 | tf_op jit(solution)/shard_map/ppermute | solution.py:371
  9.0 8.4 %collective-permute-start.2 = (bf16[16,4096]{1,0:T(8,128)(2,1)S(1)}, bf16[16,4096]{1,0:T(8,128)(2,1)S(1)}, u32[]{:S(2)}, u32[]{:S(2)}) collective-permute-start(bf16[16,4096]{1,0:T(8,128)(2,1)S(1)} %get-tuple-element.55), channel_id=1, source_target_pairs={{0,4},{2,6},{4,0},{6,2},{1,5},{3,7},{5,1},{7,3},{8,12},{10,14},{12... | collective-permute-start | bytes 393224 | tf_op jit(solution)/shard_map/ppermute | solution.py:371
  10.5 6.9 %collective-permute-start.3 = (bf16[16,4096]{1,0:T(8,128)(2,1)S(1)}, bf16[16,4096]{1,0:T(8,128)(2,1)S(1)}, u32[]{:S(2)}, u32[]{:S(2)}) collective-permute-start(bf16[16,4096]{1,0:T(8,128)(2,1)S(1)} %get-tuple-element.54), channel_id=1, source_target_pairs={{0,6},{2,4},{4,2},{6,0},{1,7},{3,5},{5,3},{7,1},{8,14},{10,12},{12... | collective-permute-start | bytes 393224 | tf_op jit(solution)/shard_map/ppermute | solution.py:371
  10.9 6.6 %collective-permute-start.4 = (bf16[336,128]{1,0:T(8,128)(2,1)S(1)}, bf16[336,128]{1,0:T(8,128)(2,1)S(1)}, u32[]{:S(2)}, u32[]{:S(2)}) collective-permute-start(bf16[336,128]{1,0:T(8,128)(2,1)S(1)} %concatenate.48), channel_id=1, source_target_pairs={{0,8},{8,0},{16,24},{24,16},{1,9},{9,1},{17,25},{25,17},{2,10},{10... | collective-permute-start | bytes 258056 | tf_op jit(solution)/shard_map/ppermute | solution.py:371
  13.0 9.3 %collective-permute-start.5 = (bf16[336,128]{1,0:T(8,128)(2,1)S(1)}, bf16[336,128]{1,0:T(8,128)(2,1)S(1)}, u32[]{:S(2)}, u32[]{:S(2)}) collective-permute-start(bf16[336,128]{1,0:T(8,128)(2,1)S(1)} %concatenate.48), channel_id=1, source_target_pairs={{0,16},{8,24},{16,0},{24,8},{1,17},{9,25},{17,1},{25,9},{2,18},{10... | collective-permute-start | bytes 258056 | tf_op jit(solution)/shard_map/ppermute | solution.py:371
  15.7 6.7 %collective-permute-start.6 = (bf16[336,128]{1,0:T(8,128)(2,1)S(1)}, bf16[336,128]{1,0:T(8,128)(2,1)S(1)}, u32[]{:S(2)}, u32[]{:S(2)}) collective-permute-start(bf16[336,128]{1,0:T(8,128)(2,1)S(1)} %concatenate.48), channel_id=1, source_target_pairs={{0,24},{8,16},{16,8},{24,0},{1,25},{9,17},{17,9},{25,1},{2,26},{10... | collective-permute-start | bytes 258056 | tf_op jit(solution)/shard_map/ppermute | solution.py:371
  22.4 5.5 %collective-permute-start.8 = (bf16[2,336,128]{2,1,0:T(8,128)(2,1)S(1)}, bf16[2,336,128]{2,1,0:T(8,128)(2,1)S(1)}, u32[]{:S(2)}, u32[]{:S(2)}) collective-permute-start(bf16[2,336,128]{2,1,0:T(8,128)(2,1)S(1)} %pad_maximum_fusion.8), channel_id=1, source_target_pairs={{0,4},{2,6},{4,0},{6,2},{1,5},{3,7},{5,1},{7,3},{8,12},{10,14},{12... | collective-permute-start | bytes 516104 | tf_op jit(solution)/shard_map/ppermute | solution.py:371
  24.0 5.5 %collective-permute-start.7 = (bf16[2,336,128]{2,1,0:T(8,128)(2,1)S(1)}, bf16[2,336,128]{2,1,0:T(8,128)(2,1)S(1)}, u32[]{:S(2)}, u32[]{:S(2)}) collective-permute-start(bf16[2,336,128]{2,1,0:T(8,128)(2,1)S(1)} %pad_maximum_fusion.7), channel_id=1, source_target_pairs={{0,2},{2,0},{4,6},{6,4},{1,3},{3,1},{5,7},{7,5},{8,10},{10,8},{12,... | collective-permute-start | bytes 516104 | tf_op jit(solution)/shard_map/ppermute | solution.py:371
  25.5 5.0 %collective-permute-start.9 = (bf16[512,128]{1,0:T(8,128)(2,1)S(1)}, bf16[512,128]{1,0:T(8,128)(2,1)S(1)}, u32[]{:S(2)}, u32[]{:S(2)}) collective-permute-start(bf16[512,128]{1,0:T(8,128)(2,1)S(1)} %bitcast.54), channel_id=1, source_target_pairs={{0,8},{8,0},{16,24},{24,16},{1,9},{9,1},{17,25},{25,17},{2,10},{10... | collective-permute-start | bytes 393224 | tf_op jit(solution)/shard_map/ppermute | solution.py:371
  30.5 7.2 %collective-permute-start.12 = (bf16[4,336,128]{2,1,0:T(8,128)(2,1)S(1)}, bf16[4,336,128]{2,1,0:T(8,128)(2,1)S(1)}, u32[]{:S(2)}, u32[]{:S(2)}) collective-permute-start(bf16[4,336,128]{2,1,0:T(8,128)(2,1)S(1)} %pad_maximum_fusion.3), channel_id=1, source_target_pairs={{0,4},{2,6},{4,0},{6,2},{1,5},{3,7},{5,1},{7,3},{8,12},{10,14},{12... | collective-permute-start | bytes 1032200 | tf_op jit(solution)/shard_map/ppermute | solution.py:371
  31.0 7.2 %collective-permute-start.13 = (bf16[4,336,128]{2,1,0:T(8,128)(2,1)S(1)}, bf16[4,336,128]{2,1,0:T(8,128)(2,1)S(1)}, u32[]{:S(2)}, u32[]{:S(2)}) collective-permute-start(bf16[4,336,128]{2,1,0:T(8,128)(2,1)S(1)} %pad_maximum_fusion.4), channel_id=1, source_target_pairs={{0,2},{2,0},{4,6},{6,4},{1,3},{3,1},{5,7},{7,5},{8,10},{10,8},{12,... | collective-permute-start | bytes 1032200 | tf_op jit(solution)/shard_map/ppermute | solution.py:371
  31.6 10.0 %collective-permute-start.10 = (bf16[512,128]{1,0:T(8,128)(2,1)S(1)}, bf16[512,128]{1,0:T(8,128)(2,1)S(1)}, u32[]{:S(2)}, u32[]{:S(2)}) collective-permute-start(bf16[512,128]{1,0:T(8,128)(2,1)S(1)} %bitcast.55), channel_id=1, source_target_pairs={{0,16},{8,24},{16,0},{24,8},{1,17},{9,25},{17,1},{25,9},{2,18},{10... | collective-permute-start | bytes 393224 | tf_op jit(solution)/shard_map/ppermute | solution.py:371
  34.1 7.5 %collective-permute-start.11 = (bf16[512,128]{1,0:T(8,128)(2,1)S(1)}, bf16[512,128]{1,0:T(8,128)(2,1)S(1)}, u32[]{:S(2)}, u32[]{:S(2)}) collective-permute-start(bf16[512,128]{1,0:T(8,128)(2,1)S(1)} %bitcast.56), channel_id=1, source_target_pairs={{0,24},{8,16},{16,8},{24,0},{1,25},{9,17},{17,9},{25,1},{2,26},{10... | collective-permute-start | bytes 393224 | tf_op jit(solution)/shard_map/ppermute | solution.py:371
  41.5 12.5 %collective-permute-start.18 = (bf16[16,336,128]{2,1,0:T(8,128)(2,1)S(1)}, bf16[16,336,128]{2,1,0:T(8,128)(2,1)S(1)}, u32[]{:S(2)}, u32[]{:S(2)}) collective-permute-start(bf16[16,336,128]{2,1,0:T(8,128)(2,1)S(1)} %pad_maximum_fusion.mine), channel_id=1, source_target_pairs={{0,1},{1,0},{2,3},{3,2},{4,5},{5,4},{6,7},{7,6},{8,9},{9,8},{10,11... | collective-permute-start | bytes 4128776 | tf_op jit(solution)/shard_map/ppermute | solution.py:371
  41.6 8.8 %collective-permute-start.16 = (bf16[2,512,128]{2,1,0:T(8,128)(2,1)S(1)}, bf16[2,512,128]{2,1,0:T(8,128)(2,1)S(1)}, u32[]{:S(2)}, u32[]{:S(2)}) collective-permute-start(bf16[2,512,128]{2,1,0:T(8,128)(2,1)S(1)} %pad_maximum_fusion.6), channel_id=1, source_target_pairs={{0,4},{2,6},{4,0},{6,2},{1,5},{3,7},{5,1},{7,3},{8,12},{10,14},{12... | collective-permute-start | bytes 786440 | tf_op jit(solution)/shard_map/ppermute | solution.py:371
  43.3 8.5 %collective-permute-start.14 = (bf16[2,512,128]{2,1,0:T(8,128)(2,1)S(1)}, bf16[2,512,128]{2,1,0:T(8,128)(2,1)S(1)}, u32[]{:S(2)}, u32[]{:S(2)}) collective-permute-start(bf16[2,512,128]{2,1,0:T(8,128)(2,1)S(1)} %pad_maximum_fusion.5), channel_id=1, source_target_pairs={{0,2},{2,0},{4,6},{6,4},{1,3},{3,1},{5,7},{7,5},{8,10},{10,8},{12,... | collective-permute-start | bytes 786440 | tf_op jit(solution)/shard_map/ppermute | solution.py:371
  50.4 13.6 %collective-permute-start.17 = (bf16[4,512,128]{2,1,0:T(8,128)(2,1)S(1)}, bf16[4,512,128]{2,1,0:T(8,128)(2,1)S(1)}, u32[]{:S(2)}, u32[]{:S(2)}) collective-permute-start(bf16[4,512,128]{2,1,0:T(8,128)(2,1)S(1)} %pad_maximum_fusion.2.rest_6_), channel_id=1, source_target_pairs={{0,2},{2,0},{4,6},{6,4},{1,3},{3,1},{5,7},{7,5},{8,10},{10,8},{12,... | collective-permute-start | bytes 1572872 | tf_op jit(solution)/shard_map/ppermute | solution.py:371
  51.9 13.3 %collective-permute-start.15 = (bf16[4,512,128]{2,1,0:T(8,128)(2,1)S(1)}, bf16[4,512,128]{2,1,0:T(8,128)(2,1)S(1)}, u32[]{:S(2)}, u32[]{:S(2)}) collective-permute-start(bf16[4,512,128]{2,1,0:T(8,128)(2,1)S(1)} %pad_maximum_fusion.1.rest_5_), channel_id=1, source_target_pairs={{0,4},{2,6},{4,0},{6,2},{1,5},{3,7},{5,1},{7,3},{8,12},{10,14},{12... | collective-permute-start | bytes 1572872 | tf_op jit(solution)/shard_map/ppermute | solution.py:371
  53.5 12.3 %collective-permute-start.20 = (bf16[4,512,128]{2,1,0:T(8,128)(2,1)S(1)}, bf16[4,512,128]{2,1,0:T(8,128)(2,1)S(1)}, u32[]{:S(2)}, u32[]{:S(2)}) collective-permute-start(bf16[4,512,128]{2,1,0:T(8,128)(2,1)S(1)} %pad_maximum_fusion.2.rest_6_), channel_id=1, source_target_pairs={{0,1},{1,0},{2,3},{3,2},{4,5},{5,4},{6,7},{7,6},{8,9},{9,8},{10,11... | collective-permute-start | bytes 1572872 | tf_op jit(solution)/shard_map/ppermute | solution.py:371
  53.5 12.3 %collective-permute-start.19 = (bf16[4,512,128]{2,1,0:T(8,128)(2,1)S(1)}, bf16[4,512,128]{2,1,0:T(8,128)(2,1)S(1)}, u32[]{:S(2)}, u32[]{:S(2)}) collective-permute-start(bf16[4,512,128]{2,1,0:T(8,128)(2,1)S(1)} %pad_maximum_fusion.1.rest_5_), channel_id=1, source_target_pairs={{0,1},{1,0},{2,3},{3,2},{4,5},{5,4},{6,7},{7,6},{8,9},{9,8},{10,11... | collective-permute-start | bytes 1572872 | tf_op jit(solution)/shard_map/ppermute | solution.py:371
  65.3 1.9 %collective-permute-start.21 = (bf16[4,512,128]{2,1,0:T(8,128)(2,1)S(1)}, bf16[4,512,128]{2,1,0:T(8,128)(2,1)S(1)}, u32[]{:S(2)}, u32[]{:S(2)}) collective-permute-start(bf16[4,512,128]{2,1,0:T(8,128)(2,1)S(1)} %collective-permute-done.15.rest_7_), channel_id=1, source_target_pairs={{0,1},{1,0},{2,3},{3,2},{4,5},{5,4},{6,7},{7,6},{8,9},{9,8},{10,11... | collective-permute-start | bytes 1572872 | tf_op jit(solution)/shard_map/ppermute | solution.py:371
  65.3 2.7 %collective-permute-start.22 = (bf16[4,512,128]{2,1,0:T(8,128)(2,1)S(1)}, bf16[4,512,128]{2,1,0:T(8,128)(2,1)S(1)}, u32[]{:S(2)}, u32[]{:S(2)}) collective-permute-start(bf16[4,512,128]{2,1,0:T(8,128)(2,1)S(1)} %collective-permute-done.17.rest_8_), channel_id=1, source_target_pairs={{0,1},{1,0},{2,3},{3,2},{4,5},{5,4},{6,7},{7,6},{8,9},{9,8},{10,11... | collective-permute-start | bytes 1572872 | tf_op jit(solution)/shard_map/ppermute | solution.py:371

commit v12 on v11

--- a/solution.py
+++ b/solution.py
@@ -94,6 +94,12 @@
     return copies
 
 
+def clear(refs):
+    for ref in refs:
+        for q in range(ref.shape[0]):
+            ref[q] = jnp.zeros_like(ref[q])
+
+
 def left_half(shape):
     return lax.broadcasted_iota(jnp.int32, shape, len(shape) - 1) < 64
 
@@ -146,7 +152,8 @@
 
 
 def unpack(
-    n_row, n_col, own, mine, other, lists, place, blk, vs, vd, rm, ic, ints, meta, sems, small
+    n_row, n_col, own, mine, other,
+    lists, place, blk, vs, vd, rm, ic, w1, w2, ints, meta, sems, small,
 ):
     n_dev = n_row * n_col
     k = vs.shape[1]
@@ -211,11 +218,14 @@
         index = small[at_device(r, h), meta_at : meta_at + META, :].astype(jnp.float32)
         place[r : r + 1, :] = index[7:8] * float(rblk) + index[6:7]
 
+    clear([w1, w2])
+    add_products(lists[2 * slots], blk, NT, lists, 0, vd, slots, w1, w2)
+
 
 def iterate(n_row, n_col, n_cap, total, own, lists, place, *rest):
-    sources, fulls, out = rest[:5], rest[5:13], rest[13]
-    sems, full, tmp, home, blk, vs, vd, rm, ic = rest[14:23]
-    w, w1, w2, wt, wd, y, y1, y2, ph, linv = rest[23:]
+    sources, fulls, out = rest[:7], rest[7:15], rest[15]
+    sems, full, tmp, home, blk, vs, vd, rm, ic, w1, w2 = rest[16:27]
+    w, wt, wd, y, y1, y2, ph, linv = rest[27:]
     slots = 2 * blk.shape[0]
     n_dev = n_row * n_col
     k = vs.shape[1]
@@ -233,7 +243,7 @@
             at += ref.shape[0]
         return pairs
 
-    copies = copy_in(laid_out(fulls, full) + list(zip(sources, (blk, vs, vd, rm, ic))), sems)
+    copies = copy_in(laid_out(fulls, full) + list(zip(sources, (blk, vs, vd, rm, ic, w1, w2))), sems)
     for copy in copies[: len(fulls)]:
         copy.wait()
     n_group = lists[2 * slots]
@@ -276,12 +286,7 @@
 
         lax.fori_loop(0, rblk, cut, 0, unroll=8)
 
-    def clear(refs):
-        for ref in refs:
-            for q in range(ref.shape[0]):
-                ref[q] = jnp.zeros_like(ref[q])
-
-    clear([y, y1, y2, w1, w2])
+    clear([y, y1, y2])
     for copy in copies[len(fulls) :]:
         copy.wait()
 
@@ -306,7 +311,10 @@
                 w[r * rpairs + p] = prod[:, :128]
                 w[r * rpairs + p + 1] = prod[:, 128:]
 
-        add_products(n_group, blk, NT, lists, 0, vd, slots, w1, w2)
+        @pl.when(it > 0)
+        def _():
+            add_products(n_group, blk, NT, lists, 0, vd, slots, w1, w2)
+
         for p in range(n_dev):
             x = w[p] + gather_pair(p, w1, w2)
             store_twice(wt, wd, p, x * rm[p, 0:1, :])
@@ -449,6 +457,7 @@
     smem_spec, vmem_spec, any_spec = (pl.BlockSpec(memory_space=m) for m in (smem, vmem, pl.ANY))
     arrays = [
         ((8, 128), f32), ((slots // 2, 128, 128), bf16), (pair, bf16), (twice, bf16), (mass, f32), (mass, f32),
+        (twice, f32), (twice, f32),
     ]
     lists, *unpacked = pl.pallas_call(
         functools.partial(unpack, n_row, n_col),
@@ -474,15 +483,15 @@
     return pl.pallas_call(
         functools.partial(iterate, n_row, n_col, n_cap, float(n_dev * own * bsize)),
         out_shape=jax.ShapeDtypeStruct((own, k * bsize), f32),
-        in_specs=[smem_spec] * 2 + [vmem_spec] + [any_spec] * (5 + len(fulls)),
+        in_specs=[smem_spec] * 2 + [vmem_spec] + [any_spec] * (len(arrays) - 1 + len(fulls)),
         out_specs=vmem_spec,
         scratch_shapes=[
-            pltpu.SemaphoreType.DMA((5 + len(fulls),)),
+            pltpu.SemaphoreType.DMA((len(arrays) - 1 + len(fulls),)),
             vmem((n_dev,) + home.shape, bf16),
             vmem((n_row, height, 128), f32),
             vmem((n_row, height, 2 * width), bf16),
             *[vmem(*v) for v in arrays[1:]],
-            vmem(pair, f32), vmem(twice, f32), vmem(twice, f32), vmem(pair, bf16), vmem(twice, bf16),
+            vmem(pair, f32), vmem(pair, bf16), vmem(twice, bf16),
             vmem(pair, f32), vmem(twice, f32), vmem(twice, f32),
             vmem((n_dev, 2 * k, 128), bf16),
             vmem((k, k), f32),

time: 133 us -> 131 us (0.985)
  waiting for transfers between devices: 26.7 us -> 22.4 us
  local copies, waits for them, and re-layouts: 2.99 us -> 5.14 us
    ppermute x23, waiting for transfers between devices: 26.7 us -> 22.4 us  [swap(): return lax.ppermute(x, axis, [(i, i ^ distance) for i in range(size)])]
    pallas_call x1, Pallas kernels: 63 us -> 60.9 us  [whole_on_each(): pl.pallas_call(functools.partial(iterate, n_row, n_col, n_cap, float(n_de...]
    unnamed x3 -> x5, local copies, waits for them, and re-layouts: 0.02 us -> 2.18 us
    pallas_call x1, Pallas kernels: 6.6 us -> 8.73 us  [whole_on_each(): pl.pallas_call(functools.partial(unpack, n_row, n_col), out_shape=[jax.Sh...]
  transfers between devices with their start and end apart: 23 -> 23, of which waited for: 12 -> 11; matrix products, arithmetic and copies ran while one was open for 4% -> 4% of each run, Pallas kernels for 5% -> 7%
where the time goes in v12:
time: 131 us; the launch traced here: 129 us
  Pallas kernels  69.6 us (53%)
  starting transfers between devices  27.6 us (21%)
  waiting for transfers between devices  22.4 us (17%)
  local copies, waits for them, and re-layouts  5.14 us (4%)
  other arithmetic  3.1 us (2%)
    pallas_call x1, Pallas kernels, whole_on_each(): pl.pallas_call(functools.partial(iterate, n_row, n_col, n_cap, float(n_de...  60.9 us
    ppermute x23, starting transfers between devices, swap(): return lax.ppermute(x, axis, [(i, i ^ distance) for i in range(size)])  27.6 us
    ppermute x23, waiting for transfers between devices, swap(): return lax.ppermute(x, axis, [(i, i ^ distance) for i in range(size)])  22.4 us
    pallas_call x1, Pallas kernels, whole_on_each(): pl.pallas_call(functools.partial(unpack, n_row, n_col), out_shape=[jax.Sh...  8.73 us
  transfers between devices with their start and end apart: 23, of which 11 were waited for; matrix products, arithmetic and copies ran while one was open for 4% of the time, Pallas kernels for 7%

profile of v12, /device:TPU:0, one launch (start us, length us, event | category | flops | bytes accessed | tf_op | source)
XLA Modules:
  0.0 129.0 jit_solution(14691129531572832799)
XLA Ops:
  0.7 1.1 select_bitcast_fusion
  1.8 0.5 collective-permute-start
  2.4 0.7 fusion.6
  3.0 0.7 fusion.7
  3.7 0.7 sqrt.3
  4.4 0.1 reshape.207
  4.4 0.8 reshape.205
  5.2 0.1 copy.15
  5.3 0.1 reshape.206
  5.4 0.9 reshape.203
  6.3 0.1 bitcast_add_fusion
  6.4 2.6 %collective-permute-start.1 = (bf16[16,4096]{1,0:T(8,128)(2,1)S(1)}, bf16[16,4096]{1,0:T(8,128)(2,1)S(1)}, u32[]{:S(2)}, u32[]{:S(2)}) collective-permute-start(bf16[16,4096]{1,0:T(8,128)(2,1)S(1)} %get-tuple-element.57), channel_id=1, source_target_pairs={{0,2},{2,0},{4,6},{6,4},{1,3},{3,1},{5,7},{7,5},{8,10},{10,8},{12,... | collective-permute-start | bytes 393224 | tf_op jit(solution)/shard_map/ppermute | solution.py:379
  9.0 1.5 %collective-permute-start.2 = (bf16[16,4096]{1,0:T(8,128)(2,1)S(1)}, bf16[16,4096]{1,0:T(8,128)(2,1)S(1)}, u32[]{:S(2)}, u32[]{:S(2)}) collective-permute-start(bf16[16,4096]{1,0:T(8,128)(2,1)S(1)} %get-tuple-element.59), channel_id=1, source_target_pairs={{0,4},{2,6},{4,0},{6,2},{1,5},{3,7},{5,1},{7,3},{8,12},{10,14},{12... | collective-permute-start | bytes 393224 | tf_op jit(solution)/shard_map/ppermute | solution.py:379
  10.5 0.1 bitcast_maximum_fusion
  10.7 0.1 reshape.204
  10.8 0.1 concatenate.48
  10.9 2.1 %collective-permute-start.4 = (bf16[336,128]{1,0:T(8,128)(2,1)S(1)}, bf16[336,128]{1,0:T(8,128)(2,1)S(1)}, u32[]{:S(2)}, u32[]{:S(2)}) collective-permute-start(bf16[336,128]{1,0:T(8,128)(2,1)S(1)} %concatenate.48), channel_id=1, source_target_pairs={{0,8},{8,0},{16,24},{24,16},{1,9},{9,1},{17,25},{25,17},{2,10},{10... | collective-permute-start | bytes 258056 | tf_op jit(solution)/shard_map/ppermute | solution.py:379
  13.0 2.6 %collective-permute-start.5 = (bf16[336,128]{1,0:T(8,128)(2,1)S(1)}, bf16[336,128]{1,0:T(8,128)(2,1)S(1)}, u32[]{:S(2)}, u32[]{:S(2)}) collective-permute-start(bf16[336,128]{1,0:T(8,128)(2,1)S(1)} %concatenate.48), channel_id=1, source_target_pairs={{0,16},{8,24},{16,0},{24,8},{1,17},{9,25},{17,1},{25,9},{2,18},{10... | collective-permute-start | bytes 258056 | tf_op jit(solution)/shard_map/ppermute | solution.py:379
  15.6 0.1 pad_add_fusion.own
  15.7 1.7 %collective-permute-start.6 = (bf16[336,128]{1,0:T(8,128)(2,1)S(1)}, bf16[336,128]{1,0:T(8,128)(2,1)S(1)}, u32[]{:S(2)}, u32[]{:S(2)}) collective-permute-start(bf16[336,128]{1,0:T(8,128)(2,1)S(1)} %concatenate.48), channel_id=1, source_target_pairs={{0,24},{8,16},{16,8},{24,0},{1,25},{9,17},{17,9},{25,1},{2,26},{10... | collective-permute-start | bytes 258056 | tf_op jit(solution)/shard_map/ppermute | solution.py:379
  17.6 4.8 %collective-permute-done.5 = bf16[336,128]{1,0:T(8,128)(2,1)S(1)} collective-permute-done((bf16[336,128]{1,0:T(8,128)(2,1)S(1)}, bf16[336,128]{1,0:T(8,128)(2,1)S(1)}, u32[]{:S(2)}, u32[]{:S(2)}) %collective-permute-start.5) | collective-permute-done | bytes 86048 | tf_op jit(solution)/shard_map/ppermute | solution.py:379
  22.4 1.6 %collective-permute-start.8 = (bf16[2,336,128]{2,1,0:T(8,128)(2,1)S(1)}, bf16[2,336,128]{2,1,0:T(8,128)(2,1)S(1)}, u32[]{:S(2)}, u32[]{:S(2)}) collective-permute-start(bf16[2,336,128]{2,1,0:T(8,128)(2,1)S(1)} %pad_maximum_fusion.8), channel_id=1, source_target_pairs={{0,4},{2,6},{4,0},{6,2},{1,5},{3,7},{5,1},{7,3},{8,12},{10,14},{12... | collective-permute-start | bytes 516104 | tf_op jit(solution)/shard_map/ppermute | solution.py:379
  24.0 1.6 %collective-permute-start.7 = (bf16[2,336,128]{2,1,0:T(8,128)(2,1)S(1)}, bf16[2,336,128]{2,1,0:T(8,128)(2,1)S(1)}, u32[]{:S(2)}, u32[]{:S(2)}) collective-permute-start(bf16[2,336,128]{2,1,0:T(8,128)(2,1)S(1)} %pad_maximum_fusion.7), channel_id=1, source_target_pairs={{0,2},{2,0},{4,6},{6,4},{1,3},{3,1},{5,7},{7,5},{8,10},{10,8},{12,... | collective-permute-start | bytes 516104 | tf_op jit(solution)/shard_map/ppermute | solution.py:379
  25.5 1.5 %collective-permute-start.9 = (bf16[512,128]{1,0:T(8,128)(2,1)S(1)}, bf16[512,128]{1,0:T(8,128)(2,1)S(1)}, u32[]{:S(2)}, u32[]{:S(2)}) collective-permute-start(bf16[512,128]{1,0:T(8,128)(2,1)S(1)} %bitcast.54), channel_id=1, source_target_pairs={{0,8},{8,0},{16,24},{24,16},{1,9},{9,1},{17,25},{25,17},{2,10},{10... | collective-permute-start | bytes 393224 | tf_op jit(solution)/shard_map/ppermute | solution.py:379
  27.0 0.8 collective-permute-done.8
  27.9 1.6 %collective-permute-done.7 = bf16[2,336,128]{2,1,0:T(8,128)(2,1)S(1)} collective-permute-done((bf16[2,336,128]{2,1,0:T(8,128)(2,1)S(1)}, bf16[2,336,128]{2,1,0:T(8,128)(2,1)S(1)}, u32[]{:S(2)}, u32[]{:S(2)}) %collective-permute-start.7) | collective-permute-done | bytes 172064 | tf_op jit(solution)/shard_map/ppermute | solution.py:379
  29.5 1.0 collective-permute-done.9
  30.5 0.5 collective-permute-start.12
  31.0 0.6 collective-permute-start.13
  31.6 2.5 %collective-permute-start.10 = (bf16[512,128]{1,0:T(8,128)(2,1)S(1)}, bf16[512,128]{1,0:T(8,128)(2,1)S(1)}, u32[]{:S(2)}, u32[]{:S(2)}) collective-permute-start(bf16[512,128]{1,0:T(8,128)(2,1)S(1)} %bitcast.55), channel_id=1, source_target_pairs={{0,16},{8,24},{16,0},{24,8},{1,17},{9,25},{17,1},{25,9},{2,18},{10... | collective-permute-start | bytes 393224 | tf_op jit(solution)/shard_map/ppermute | solution.py:379
  34.1 1.3 %collective-permute-start.11 = (bf16[512,128]{1,0:T(8,128)(2,1)S(1)}, bf16[512,128]{1,0:T(8,128)(2,1)S(1)}, u32[]{:S(2)}, u32[]{:S(2)}) collective-permute-start(bf16[512,128]{1,0:T(8,128)(2,1)S(1)} %bitcast.56), channel_id=1, source_target_pairs={{0,24},{8,16},{16,8},{24,0},{1,25},{9,17},{17,9},{25,1},{2,26},{10... | collective-permute-start | bytes 393224 | tf_op jit(solution)/shard_map/ppermute | solution.py:379
  35.4 2.3 %collective-permute-done.12 = bf16[4,336,128]{2,1,0:T(8,128)(2,1)S(1)} collective-permute-done((bf16[4,336,128]{2,1,0:T(8,128)(2,1)S(1)}, bf16[4,336,128]{2,1,0:T(8,128)(2,1)S(1)}, u32[]{:S(2)}, u32[]{:S(2)}) %collective-permute-start.12) | collective-permute-done | bytes 344096 | tf_op jit(solution)/shard_map/ppermute | solution.py:379
  37.8 0.5 collective-permute-done.13
  38.3 0.2 pad_maximum_fusion.mine
  38.4 3.1 %collective-permute-done.10 = bf16[512,128]{1,0:T(8,128)(2,1)S(1)} collective-permute-done((bf16[512,128]{1,0:T(8,128)(2,1)S(1)}, bf16[512,128]{1,0:T(8,128)(2,1)S(1)}, u32[]{:S(2)}, u32[]{:S(2)}) %collective-permute-start.10) | collective-permute-done | bytes 131104 | tf_op jit(solution)/shard_map/ppermute | solution.py:379
  41.6 1.7 %collective-permute-start.16 = (bf16[2,512,128]{2,1,0:T(8,128)(2,1)S(1)}, bf16[2,512,128]{2,1,0:T(8,128)(2,1)S(1)}, u32[]{:S(2)}, u32[]{:S(2)}) collective-permute-start(bf16[2,512,128]{2,1,0:T(8,128)(2,1)S(1)} %pad_maximum_fusion.6), channel_id=1, source_target_pairs={{0,4},{2,6},{4,0},{6,2},{1,5},{3,7},{5,1},{7,3},{8,12},{10,14},{12... | collective-permute-start | bytes 786440 | tf_op jit(solution)/shard_map/ppermute | solution.py:379
  43.3 1.3 %collective-permute-start.14 = (bf16[2,512,128]{2,1,0:T(8,128)(2,1)S(1)}, bf16[2,512,128]{2,1,0:T(8,128)(2,1)S(1)}, u32[]{:S(2)}, u32[]{:S(2)}) collective-permute-start(bf16[2,512,128]{2,1,0:T(8,128)(2,1)S(1)} %pad_maximum_fusion.5), channel_id=1, source_target_pairs={{0,2},{2,0},{4,6},{6,4},{1,3},{3,1},{5,7},{7,5},{8,10},{10,8},{12,... | collective-permute-start | bytes 786440 | tf_op jit(solution)/shard_map/ppermute | solution.py:379
  44.6 5.7 %collective-permute-done.16 = bf16[2,512,128]{2,1,0:T(8,128)(2,1)S(1)} collective-permute-done((bf16[2,512,128]{2,1,0:T(8,128)(2,1)S(1)}, bf16[2,512,128]{2,1,0:T(8,128)(2,1)S(1)}, u32[]{:S(2)}, u32[]{:S(2)}) %collective-permute-start.16) | collective-permute-done | bytes 262176 | tf_op jit(solution)/shard_map/ppermute | solution.py:379
  50.4 1.5 %collective-permute-start.17 = (bf16[4,512,128]{2,1,0:T(8,128)(2,1)S(1)}, bf16[4,512,128]{2,1,0:T(8,128)(2,1)S(1)}, u32[]{:S(2)}, u32[]{:S(2)}) collective-permute-start(bf16[4,512,128]{2,1,0:T(8,128)(2,1)S(1)} %pad_maximum_fusion.2.rest_8_), channel_id=1, source_target_pairs={{0,2},{2,0},{4,6},{6,4},{1,3},{3,1},{5,7},{7,5},{8,10},{10,8},{12,... | collective-permute-start | bytes 1572872 | tf_op jit(solution)/shard_map/ppermute | solution.py:379
  51.9 1.6 %collective-permute-start.15 = (bf16[4,512,128]{2,1,0:T(8,128)(2,1)S(1)}, bf16[4,512,128]{2,1,0:T(8,128)(2,1)S(1)}, u32[]{:S(2)}, u32[]{:S(2)}) collective-permute-start(bf16[4,512,128]{2,1,0:T(8,128)(2,1)S(1)} %pad_maximum_fusion.1.rest_7_), channel_id=1, source_target_pairs={{0,4},{2,6},{4,0},{6,2},{1,5},{3,7},{5,1},{7,3},{8,12},{10,14},{12... | collective-permute-start | bytes 1572872 | tf_op jit(solution)/shard_map/ppermute | solution.py:379
  53.5 0.5 collective-permute-start.19
  54.0 8.7 %unpack.1 = (s32[584]{0:T(1024)S(1)}, f32[8,128]{1,0:T(8,128)S(1)}, bf16[144,128,128]{2,1,0:T(8,128)(2,1)S(1)}, bf16[32,64,128]{2,1,0:T(8,128)(2,1)S(1)}, bf16[6...) custom-call(s32[3]{0:T(128)S(1)} %pad_add_fusion.own, ...), custom_call_target="tpu_custom_call" | custom-call | bytes 11010048 | tf_op jit(solution)/shard_map/unpack/pallas_call | solution.py:462
  62.8 2.2 %copy-done = bf16[144,128,128]{2,1,0:T(8,128)(2,1)} copy-done((bf16[144,128,128]{2,1,0:T(8,128)(2,1)}, bf16[144,128,128]{2,1,0:T(8,128)(2,1)S(1)}, u32[]{:S(2)}) %copy-start) | copy-done | bytes 4718616
  64.9 0.3 collective-permute-done.15.rest_9_
  65.3 0.5 collective-permute-start.22
  65.8 1.4 %collective-permute-done.21.rest_13_ = bf16[4,512,128]{2,1,0:T(8,128)(2,1)S(1)} collective-permute-done((bf16[4,512,128]{2,1,0:T(8,128)(2,1)S(1)}, bf16[4,512,128]{2,1,0:T(8,128)(2,1)S(1)}, u32[]{:S(2)}, u32[]{:S(2)}) %collective-permute-start.21) | collective-permute-done | bytes 524320 | tf_op jit(solution)/shard_map/ppermute | solution.py:379
  67.2 0.7 collective-permute-done.22.rest_14_
  67.9 60.9 %iterate.1 = f32[2,4096]{1,0:T(2,128)} custom-call(s32[3]{0:T(128)S(1)} %pad_add_fusion.own, s32[584]{0:T(1024)S(1)} %get-tuple-element.46.lists, f32[8,128]{1,0:T(8,128)S(1)} %get-tuple-element.47.place, bf16[144,128,128]{2,1,0:T(8,128)(2,1)} %copy-done, bf16[32,64,128]{2,1,0:T(8,128)(2,1)S(1)} %get-tuple-element.49.rest_1_, ...), custom_call_target="tpu_custom_call" | custom-call | tf_op jit(solution)/shard_map/iterate/pallas_call | solution.py:483
  (41 shorter events, 0.6 us)
Async XLA Ops:
  0.0 6.3 %copy-start.1 = (bf16[1,1,128,4096]{3,2,1,0:T(8,128)(2,1)S(1)}, bf16[1,1,128,4096]{3,2,1,0:T(8,128)(2,1)}, u32[]{:S(2)}) copy-start(bf16[1,1,128,4096]{3,2,1,0:T(8,128)(2,1)} %param.7) | copy-start | bytes 3145732
  1.8 4.5 %collective-permute-start = (bf16[4,16,4096]{2,1,0:T(8,128)(2,1)S(1)}, bf16[4,16,4096]{2,1,0:T(8,128)(2,1)S(1)}, u32[]{:S(2)}, u32[]{:S(2)}) collective-permute-start(bf16[4,16,4096]{2,1,0:T(8,128)(2,1)S(1)} %select_bitcast_fusion), channel_id=1, source_target_pairs={{0,1},{1,0},{2,3},{3,2},{4,5},{5,4},{6,7},{7,6},{8,9},{9,8},{10,11... | collective-permute-start | bytes 1572872 | tf_op jit(solution)/shard_map/ppermute | solution.py:379
  6.4 9.3 %collective-permute-start.1 = (bf16[16,4096]{1,0:T(8,128)(2,1)S(1)}, bf16[16,4096]{1,0:T(8,128)(2,1)S(1)}, u32[]{:S(2)}, u32[]{:S(2)}) collective-permute-start(bf16[16,4096]{1,0:T(8,128)(2,1)S(1)} %get-tuple-element.57), channel_id=1, source_target_pairs={{0,2},{2,0},{4,6},{6,4},{1,3},{3,1},{5,7},{7,5},{8,10},{10,8},{12,... | collective-permute-start | bytes 393224 | tf_op jit(solution)/shard_map/ppermute | solution.py:379
  9.0 8.4 %collective-permute-start.2 = (bf16[16,4096]{1,0:T(8,128)(2,1)S(1)}, bf16[16,4096]{1,0:T(8,128)(2,1)S(1)}, u32[]{:S(2)}, u32[]{:S(2)}) collective-permute-start(bf16[16,4096]{1,0:T(8,128)(2,1)S(1)} %get-tuple-element.59), channel_id=1, source_target_pairs={{0,4},{2,6},{4,0},{6,2},{1,5},{3,7},{5,1},{7,3},{8,12},{10,14},{12... | collective-permute-start | bytes 393224 | tf_op jit(solution)/shard_map/ppermute | solution.py:379
  10.5 6.9 %collective-permute-start.3 = (bf16[16,4096]{1,0:T(8,128)(2,1)S(1)}, bf16[16,4096]{1,0:T(8,128)(2,1)S(1)}, u32[]{:S(2)}, u32[]{:S(2)}) collective-permute-start(bf16[16,4096]{1,0:T(8,128)(2,1)S(1)} %get-tuple-element.58), channel_id=1, source_target_pairs={{0,6},{2,4},{4,2},{6,0},{1,7},{3,5},{5,3},{7,1},{8,14},{10,12},{12... | collective-permute-start | bytes 393224 | tf_op jit(solution)/shard_map/ppermute | solution.py:379
  10.9 6.6 %collective-permute-start.4 = (bf16[336,128]{1,0:T(8,128)(2,1)S(1)}, bf16[336,128]{1,0:T(8,128)(2,1)S(1)}, u32[]{:S(2)}, u32[]{:S(2)}) collective-permute-start(bf16[336,128]{1,0:T(8,128)(2,1)S(1)} %concatenate.48), channel_id=1, source_target_pairs={{0,8},{8,0},{16,24},{24,16},{1,9},{9,1},{17,25},{25,17},{2,10},{10... | collective-permute-start | bytes 258056 | tf_op jit(solution)/shard_map/ppermute | solution.py:379
  13.0 9.3 %collective-permute-start.5 = (bf16[336,128]{1,0:T(8,128)(2,1)S(1)}, bf16[336,128]{1,0:T(8,128)(2,1)S(1)}, u32[]{:S(2)}, u32[]{:S(2)}) collective-permute-start(bf16[336,128]{1,0:T(8,128)(2,1)S(1)} %concatenate.48), channel_id=1, source_target_pairs={{0,16},{8,24},{16,0},{24,8},{1,17},{9,25},{17,1},{25,9},{2,18},{10... | collective-permute-start | bytes 258056 | tf_op jit(solution)/shard_map/ppermute | solution.py:379
  15.7 6.7 %collective-permute-start.6 = (bf16[336,128]{1,0:T(8,128)(2,1)S(1)}, bf16[336,128]{1,0:T(8,128)(2,1)S(1)}, u32[]{:S(2)}, u32[]{:S(2)}) collective-permute-start(bf16[336,128]{1,0:T(8,128)(2,1)S(1)} %concatenate.48), channel_id=1, source_target_pairs={{0,24},{8,16},{16,8},{24,0},{1,25},{9,17},{17,9},{25,1},{2,26},{10... | collective-permute-start | bytes 258056 | tf_op jit(solution)/shard_map/ppermute | solution.py:379
  22.4 5.5 %collective-permute-start.8 = (bf16[2,336,128]{2,1,0:T(8,128)(2,1)S(1)}, bf16[2,336,128]{2,1,0:T(8,128)(2,1)S(1)}, u32[]{:S(2)}, u32[]{:S(2)}) collective-permute-start(bf16[2,336,128]{2,1,0:T(8,128)(2,1)S(1)} %pad_maximum_fusion.8), channel_id=1, source_target_pairs={{0,4},{2,6},{4,0},{6,2},{1,5},{3,7},{5,1},{7,3},{8,12},{10,14},{12... | collective-permute-start | bytes 516104 | tf_op jit(solution)/shard_map/ppermute | solution.py:379
  24.0 5.5 %collective-permute-start.7 = (bf16[2,336,128]{2,1,0:T(8,128)(2,1)S(1)}, bf16[2,336,128]{2,1,0:T(8,128)(2,1)S(1)}, u32[]{:S(2)}, u32[]{:S(2)}) collective-permute-start(bf16[2,336,128]{2,1,0:T(8,128)(2,1)S(1)} %pad_maximum_fusion.7), channel_id=1, source_target_pairs={{0,2},{2,0},{4,6},{6,4},{1,3},{3,1},{5,7},{7,5},{8,10},{10,8},{12,... | collective-permute-start | bytes 516104 | tf_op jit(solution)/shard_map/ppermute | solution.py:379
  25.5 5.0 %collective-permute-start.9 = (bf16[512,128]{1,0:T(8,128)(2,1)S(1)}, bf16[512,128]{1,0:T(8,128)(2,1)S(1)}, u32[]{:S(2)}, u32[]{:S(2)}) collective-permute-start(bf16[512,128]{1,0:T(8,128)(2,1)S(1)} %bitcast.54), channel_id=1, source_target_pairs={{0,8},{8,0},{16,24},{24,16},{1,9},{9,1},{17,25},{25,17},{2,10},{10... | collective-permute-start | bytes 393224 | tf_op jit(solution)/shard_map/ppermute | solution.py:379
  30.5 7.2 %collective-permute-start.12 = (bf16[4,336,128]{2,1,0:T(8,128)(2,1)S(1)}, bf16[4,336,128]{2,1,0:T(8,128)(2,1)S(1)}, u32[]{:S(2)}, u32[]{:S(2)}) collective-permute-start(bf16[4,336,128]{2,1,0:T(8,128)(2,1)S(1)} %pad_maximum_fusion.3), channel_id=1, source_target_pairs={{0,4},{2,6},{4,0},{6,2},{1,5},{3,7},{5,1},{7,3},{8,12},{10,14},{12... | collective-permute-start | bytes 1032200 | tf_op jit(solution)/shard_map/ppermute | solution.py:379
  31.0 7.2 %collective-permute-start.13 = (bf16[4,336,128]{2,1,0:T(8,128)(2,1)S(1)}, bf16[4,336,128]{2,1,0:T(8,128)(2,1)S(1)}, u32[]{:S(2)}, u32[]{:S(2)}) collective-permute-start(bf16[4,336,128]{2,1,0:T(8,128)(2,1)S(1)} %pad_maximum_fusion.4), channel_id=1, source_target_pairs={{0,2},{2,0},{4,6},{6,4},{1,3},{3,1},{5,7},{7,5},{8,10},{10,8},{12,... | collective-permute-start | bytes 1032200 | tf_op jit(solution)/shard_map/ppermute | solution.py:379
  31.6 10.0 %collective-permute-start.10 = (bf16[512,128]{1,0:T(8,128)(2,1)S(1)}, bf16[512,128]{1,0:T(8,128)(2,1)S(1)}, u32[]{:S(2)}, u32[]{:S(2)}) collective-permute-start(bf16[512,128]{1,0:T(8,128)(2,1)S(1)} %bitcast.55), channel_id=1, source_target_pairs={{0,16},{8,24},{16,0},{24,8},{1,17},{9,25},{17,1},{25,9},{2,18},{10... | collective-permute-start | bytes 393224 | tf_op jit(solution)/shard_map/ppermute | solution.py:379
  34.1 7.5 %collective-permute-start.11 = (bf16[512,128]{1,0:T(8,128)(2,1)S(1)}, bf16[512,128]{1,0:T(8,128)(2,1)S(1)}, u32[]{:S(2)}, u32[]{:S(2)}) collective-permute-start(bf16[512,128]{1,0:T(8,128)(2,1)S(1)} %bitcast.56), channel_id=1, source_target_pairs={{0,24},{8,16},{16,8},{24,0},{1,25},{9,17},{17,9},{25,1},{2,26},{10... | collective-permute-start | bytes 393224 | tf_op jit(solution)/shard_map/ppermute | solution.py:379
  41.5 12.5 %collective-permute-start.18 = (bf16[16,336,128]{2,1,0:T(8,128)(2,1)S(1)}, bf16[16,336,128]{2,1,0:T(8,128)(2,1)S(1)}, u32[]{:S(2)}, u32[]{:S(2)}) collective-permute-start(bf16[16,336,128]{2,1,0:T(8,128)(2,1)S(1)} %pad_maximum_fusion.mine), channel_id=1, source_target_pairs={{0,1},{1,0},{2,3},{3,2},{4,5},{5,4},{6,7},{7,6},{8,9},{9,8},{10,11... | collective-permute-start | bytes 4128776 | tf_op jit(solution)/shard_map/ppermute | solution.py:379
  41.6 8.8 %collective-permute-start.16 = (bf16[2,512,128]{2,1,0:T(8,128)(2,1)S(1)}, bf16[2,512,128]{2,1,0:T(8,128)(2,1)S(1)}, u32[]{:S(2)}, u32[]{:S(2)}) collective-permute-start(bf16[2,512,128]{2,1,0:T(8,128)(2,1)S(1)} %pad_maximum_fusion.6), channel_id=1, source_target_pairs={{0,4},{2,6},{4,0},{6,2},{1,5},{3,7},{5,1},{7,3},{8,12},{10,14},{12... | collective-permute-start | bytes 786440 | tf_op jit(solution)/shard_map/ppermute | solution.py:379
  43.3 8.5 %collective-permute-start.14 = (bf16[2,512,128]{2,1,0:T(8,128)(2,1)S(1)}, bf16[2,512,128]{2,1,0:T(8,128)(2,1)S(1)}, u32[]{:S(2)}, u32[]{:S(2)}) collective-permute-start(bf16[2,512,128]{2,1,0:T(8,128)(2,1)S(1)} %pad_maximum_fusion.5), channel_id=1, source_target_pairs={{0,2},{2,0},{4,6},{6,4},{1,3},{3,1},{5,7},{7,5},{8,10},{10,8},{12,... | collective-permute-start | bytes 786440 | tf_op jit(solution)/shard_map/ppermute | solution.py:379
  50.4 14.5 %collective-permute-start.17 = (bf16[4,512,128]{2,1,0:T(8,128)(2,1)S(1)}, bf16[4,512,128]{2,1,0:T(8,128)(2,1)S(1)}, u32[]{:S(2)}, u32[]{:S(2)}) collective-permute-start(bf16[4,512,128]{2,1,0:T(8,128)(2,1)S(1)} %pad_maximum_fusion.2.rest_8_), channel_id=1, source_target_pairs={{0,2},{2,0},{4,6},{6,4},{1,3},{3,1},{5,7},{7,5},{8,10},{10,8},{12,... | collective-permute-start | bytes 1572872 | tf_op jit(solution)/shard_map/ppermute | solution.py:379
  51.9 13.3 %collective-permute-start.15 = (bf16[4,512,128]{2,1,0:T(8,128)(2,1)S(1)}, bf16[4,512,128]{2,1,0:T(8,128)(2,1)S(1)}, u32[]{:S(2)}, u32[]{:S(2)}) collective-permute-start(bf16[4,512,128]{2,1,0:T(8,128)(2,1)S(1)} %pad_maximum_fusion.1.rest_7_), channel_id=1, source_target_pairs={{0,4},{2,6},{4,0},{6,2},{1,5},{3,7},{5,1},{7,3},{8,12},{10,14},{12... | collective-permute-start | bytes 1572872 | tf_op jit(solution)/shard_map/ppermute | solution.py:379
  53.5 12.3 %collective-permute-start.20 = (bf16[4,512,128]{2,1,0:T(8,128)(2,1)S(1)}, bf16[4,512,128]{2,1,0:T(8,128)(2,1)S(1)}, u32[]{:S(2)}, u32[]{:S(2)}) collective-permute-start(bf16[4,512,128]{2,1,0:T(8,128)(2,1)S(1)} %pad_maximum_fusion.2.rest_8_), channel_id=1, source_target_pairs={{0,1},{1,0},{2,3},{3,2},{4,5},{5,4},{6,7},{7,6},{8,9},{9,8},{10,11... | collective-permute-start | bytes 1572872 | tf_op jit(solution)/shard_map/ppermute | solution.py:379
  53.5 12.3 %collective-permute-start.19 = (bf16[4,512,128]{2,1,0:T(8,128)(2,1)S(1)}, bf16[4,512,128]{2,1,0:T(8,128)(2,1)S(1)}, u32[]{:S(2)}, u32[]{:S(2)}) collective-permute-start(bf16[4,512,128]{2,1,0:T(8,128)(2,1)S(1)} %pad_maximum_fusion.1.rest_7_), channel_id=1, source_target_pairs={{0,1},{1,0},{2,3},{3,2},{4,5},{5,4},{6,7},{7,6},{8,9},{9,8},{10,11... | collective-permute-start | bytes 1572872 | tf_op jit(solution)/shard_map/ppermute | solution.py:379
  62.8 2.2 %copy-start = (bf16[144,128,128]{2,1,0:T(8,128)(2,1)}, bf16[144,128,128]{2,1,0:T(8,128)(2,1)S(1)}, u32[]{:S(2)}) copy-start(bf16[144,128,128]{2,1,0:T(8,128)(2,1)S(1)} %get-tuple-element.48.rest_0_) | copy-start | bytes 14155780
  65.3 1.9 %collective-permute-start.21 = (bf16[4,512,128]{2,1,0:T(8,128)(2,1)S(1)}, bf16[4,512,128]{2,1,0:T(8,128)(2,1)S(1)}, u32[]{:S(2)}, u32[]{:S(2)}) collective-permute-start(bf16[4,512,128]{2,1,0:T(8,128)(2,1)S(1)} %collective-permute-done.15.rest_9_), channel_id=1, source_target_pairs={{0,1},{1,0},{2,3},{3,2},{4,5},{5,4},{6,7},{7,6},{8,9},{9,8},{10,11... | collective-permute-start | bytes 1572872 | tf_op jit(solution)/shard_map/ppermute | solution.py:379
  65.3 2.7 %collective-permute-start.22 = (bf16[4,512,128]{2,1,0:T(8,128)(2,1)S(1)}, bf16[4,512,128]{2,1,0:T(8,128)(2,1)S(1)}, u32[]{:S(2)}, u32[]{:S(2)}) collective-permute-start(bf16[4,512,128]{2,1,0:T(8,128)(2,1)S(1)} %collective-permute-done.17.rest_10_), channel_id=1, source_target_pairs={{0,1},{1,0},{2,3},{3,2},{4,5},{5,4},{6,7},{7,6},{8,9},{9,8},{10,11... | collective-permute-start | bytes 1572872 | tf_op jit(solution)/shard_map/ppermute | solution.py:379

commit v13 on v12

--- a/solution.py
+++ b/solution.py
@@ -12,7 +12,7 @@
 META = 16
 UNROLL = 16
 BATCH = 4
-VMEM_LIMIT = 40 * 1024 * 1024
+VMEM_LIMIT = 36 * 1024 * 1024
 
 NT = (((1,), (1,)), ((), ()))
 NN = (((1,), (0,)), ((), ()))
@@ -153,7 +153,7 @@
 
 def unpack(
     n_row, n_col, own, mine, other,
-    lists, place, blk, vs, vd, rm, ic, w1, w2, ints, meta, sems, small,
+    lists, place, blk, rm, ic, vs, vd, w1, w2, ints, meta, sems, small,
 ):
     n_dev = n_row * n_col
     k = vs.shape[1]
@@ -223,9 +223,10 @@
 
 
 def iterate(n_row, n_col, n_cap, total, own, lists, place, *rest):
-    sources, fulls, out = rest[:7], rest[7:15], rest[15]
-    sems, full, tmp, home, blk, vs, vd, rm, ic, w1, w2 = rest[16:27]
-    w, wt, wd, y, y1, y2, ph, linv = rest[27:]
+    blk, rm, ic, *starts = rest[:7]
+    fulls, out = rest[7:15], rest[15]
+    sems, full, tmp, home, vs, vd, w1, w2 = rest[16:24]
+    w, wt, wd, y, y1, y2, ph, linv = rest[24:]
     slots = 2 * blk.shape[0]
     n_dev = n_row * n_col
     k = vs.shape[1]
@@ -243,8 +244,12 @@
             at += ref.shape[0]
         return pairs
 
-    copies = copy_in(laid_out(fulls, full) + list(zip(sources, (blk, vs, vd, rm, ic, w1, w2))), sems)
-    for copy in copies[: len(fulls)]:
+    copies = copy_in(laid_out(fulls, full), sems)
+    for start, ref in zip(starts, (vs, vd, w1, w2)):
+        for q in range(ref.shape[0]):
+            ref[q] = start[q]
+    clear([y, y1, y2])
+    for copy in copies:
         copy.wait()
     n_group = lists[2 * slots]
 
@@ -286,9 +291,6 @@
 
         lax.fori_loop(0, rblk, cut, 0, unroll=8)
 
-    clear([y, y1, y2])
-    for copy in copies[len(fulls) :]:
-        copy.wait()
 
     def iteration(it, carry):
         @pl.when(it > 0)
@@ -456,13 +458,13 @@
     pair, twice, mass = (n_dev, k, 128), (2 * n_dev, k, 128), (n_dev, 8, 128)
     smem_spec, vmem_spec, any_spec = (pl.BlockSpec(memory_space=m) for m in (smem, vmem, pl.ANY))
     arrays = [
-        ((8, 128), f32), ((slots // 2, 128, 128), bf16), (pair, bf16), (twice, bf16), (mass, f32), (mass, f32),
-        (twice, f32), (twice, f32),
+        ((8, 128), f32), ((slots // 2, 128, 128), bf16), (mass, f32), (mass, f32),
+        (pair, bf16), (twice, bf16), (twice, f32), (twice, f32),
     ]
     lists, *unpacked = pl.pallas_call(
         functools.partial(unpack, n_row, n_col),
         out_shape=[jax.ShapeDtypeStruct((2 * slots + 8,), i32)]
-        + [jax.ShapeDtypeStruct(*v) for v in arrays],
+        + [vmem(*v) for v in arrays],
         in_specs=[smem_spec, any_spec, any_spec],
         out_specs=[smem_spec] + [vmem_spec] * len(arrays),
         scratch_shapes=[
@@ -471,7 +473,7 @@
             pltpu.SemaphoreType.DMA((3,)),
             vmem((n_dev,) + small.shape, bf16),
         ],
-        compiler_params=pltpu.CompilerParams(vmem_limit_bytes=VMEM_LIMIT),
+        compiler_params=pltpu.CompilerParams(vmem_limit_bytes=VMEM_LIMIT // 2),
         cost_estimate=pl.CostEstimate(
             flops=0, bytes_accessed=4 * n_dev * small.size * 2, transcendentals=0
         ),
@@ -483,14 +485,14 @@
     return pl.pallas_call(
         functools.partial(iterate, n_row, n_col, n_cap, float(n_dev * own * bsize)),
         out_shape=jax.ShapeDtypeStruct((own, k * bsize), f32),
-        in_specs=[smem_spec] * 2 + [vmem_spec] + [any_spec] * (len(arrays) - 1 + len(fulls)),
+        in_specs=[smem_spec] * 2 + [vmem_spec] * len(arrays) + [any_spec] * len(fulls),
         out_specs=vmem_spec,
         scratch_shapes=[
-            pltpu.SemaphoreType.DMA((len(arrays) - 1 + len(fulls),)),
+            pltpu.SemaphoreType.DMA((len(fulls),)),
             vmem((n_dev,) + home.shape, bf16),
             vmem((n_row, height, 128), f32),
             vmem((n_row, height, 2 * width), bf16),
-            *[vmem(*v) for v in arrays[1:]],
+            *[vmem(*v) for v in arrays[4:]],
             vmem(pair, f32), vmem(pair, bf16), vmem(twice, bf16),
             vmem(pair, f32), vmem(twice, f32), vmem(twice, f32),
             vmem((n_dev, 2 * k, 128), bf16),
@@ -498,7 +500,7 @@
         ],
         compiler_params=pltpu.CompilerParams(vmem_limit_bytes=VMEM_LIMIT),
         name="iterate",
-    )(where, lists, *unpacked, *fulls)
+    )(where, lists, *(pltpu.with_memory_space_constraint(v, vmem) for v in unpacked), *fulls)
 
 
 def rotate(projected, gram):

time: 131 us -> 130 us (level); the launches traced: 129 us -> 131 us
  Pallas kernels: 69.6 us -> 72.5 us
  local copies, waits for them, and re-layouts: 5.14 us -> 2.99 us
  waiting for transfers between devices: 22.4 us -> 24.1 us
    pallas_call x1, Pallas kernels: 60.9 us -> 63.3 us  [whole_on_each(): pl.pallas_call(functools.partial(iterate, n_row, n_col, n_cap, float(n_de...]
    unnamed x5 -> x3, local copies, waits for them, and re-layouts: 2.18 us -> 0.02 us
    ppermute x23, waiting for transfers between devices: 22.4 us -> 24.1 us  [swap(): return lax.ppermute(x, axis, [(i, i ^ distance) for i in range(size)])]
  transfers between devices with their start and end apart: 23 -> 23, of which waited for: 11 -> 12; matrix products, arithmetic and copies ran while one was open for 4% -> 4% of each run, Pallas kernels for 7% -> 7%
where the time goes in v13:
time: 130 us; the launch traced here: 131 us
  Pallas kernels  72.5 us (56%)
  starting transfers between devices  27.6 us (21%)
  waiting for transfers between devices  24.1 us (19%)
  other arithmetic  3.1 us (2%)
  local copies, waits for them, and re-layouts  2.99 us (2%)
    pallas_call x1, Pallas kernels, whole_on_each(): pl.pallas_call(functools.partial(iterate, n_row, n_col, n_cap, float(n_de...  63.3 us
    ppermute x23, starting transfers between devices, swap(): return lax.ppermute(x, axis, [(i, i ^ distance) for i in range(size)])  27.6 us
    ppermute x23, waiting for transfers between devices, swap(): return lax.ppermute(x, axis, [(i, i ^ distance) for i in range(size)])  24.1 us
    pallas_call x1, Pallas kernels, whole_on_each(): pl.pallas_call(functools.partial(unpack, n_row, n_col), out_shape=[jax.Sh...  9.2 us
  transfers between devices with their start and end apart: 23, of which 12 were waited for; matrix products, arithmetic and copies ran while one was open for 4% of the time, Pallas kernels for 7%

profile of v13, /device:TPU:0, one launch (start us, length us, event | category | flops | bytes accessed | tf_op | source)
XLA Modules:
  0.0 131.4 jit_solution(16942118622239953604)
XLA Ops:
  0.7 1.1 select_bitcast_fusion
  1.8 0.5 collective-permute-start
  2.4 0.7 fusion.6
  3.0 0.7 fusion.7
  3.7 0.7 sqrt.3
  4.4 0.1 reshape.207
  4.4 0.8 reshape.205
  5.2 0.1 copy.15
  5.3 0.1 reshape.206
  5.4 0.9 reshape.203
  6.3 0.1 bitcast_add_fusion
  6.4 2.6 %collective-permute-start.1 = (bf16[16,4096]{1,0:T(8,128)(2,1)S(1)}, bf16[16,4096]{1,0:T(8,128)(2,1)S(1)}, u32[]{:S(2)}, u32[]{:S(2)}) collective-permute-start(bf16[16,4096]{1,0:T(8,128)(2,1)S(1)} %get-tuple-element.57), channel_id=1, source_target_pairs={{0,2},{2,0},{4,6},{6,4},{1,3},{3,1},{5,7},{7,5},{8,10},{10,8},{12,... | collective-permute-start | bytes 393224 | tf_op jit(solution)/shard_map/ppermute | solution.py:381
  9.0 1.5 %collective-permute-start.2 = (bf16[16,4096]{1,0:T(8,128)(2,1)S(1)}, bf16[16,4096]{1,0:T(8,128)(2,1)S(1)}, u32[]{:S(2)}, u32[]{:S(2)}) collective-permute-start(bf16[16,4096]{1,0:T(8,128)(2,1)S(1)} %get-tuple-element.59), channel_id=1, source_target_pairs={{0,4},{2,6},{4,0},{6,2},{1,5},{3,7},{5,1},{7,3},{8,12},{10,14},{12... | collective-permute-start | bytes 393224 | tf_op jit(solution)/shard_map/ppermute | solution.py:381
  10.5 0.1 bitcast_maximum_fusion
  10.7 0.1 reshape.204
  10.8 0.1 concatenate.48
  10.9 2.1 %collective-permute-start.4 = (bf16[336,128]{1,0:T(8,128)(2,1)S(1)}, bf16[336,128]{1,0:T(8,128)(2,1)S(1)}, u32[]{:S(2)}, u32[]{:S(2)}) collective-permute-start(bf16[336,128]{1,0:T(8,128)(2,1)S(1)} %concatenate.48), channel_id=1, source_target_pairs={{0,8},{8,0},{16,24},{24,16},{1,9},{9,1},{17,25},{25,17},{2,10},{10... | collective-permute-start | bytes 258056 | tf_op jit(solution)/shard_map/ppermute | solution.py:381
  13.0 2.6 %collective-permute-start.5 = (bf16[336,128]{1,0:T(8,128)(2,1)S(1)}, bf16[336,128]{1,0:T(8,128)(2,1)S(1)}, u32[]{:S(2)}, u32[]{:S(2)}) collective-permute-start(bf16[336,128]{1,0:T(8,128)(2,1)S(1)} %concatenate.48), channel_id=1, source_target_pairs={{0,16},{8,24},{16,0},{24,8},{1,17},{9,25},{17,1},{25,9},{2,18},{10... | collective-permute-start | bytes 258056 | tf_op jit(solution)/shard_map/ppermute | solution.py:381
  15.6 0.1 pad_add_fusion.own
  15.7 1.7 %collective-permute-start.6 = (bf16[336,128]{1,0:T(8,128)(2,1)S(1)}, bf16[336,128]{1,0:T(8,128)(2,1)S(1)}, u32[]{:S(2)}, u32[]{:S(2)}) collective-permute-start(bf16[336,128]{1,0:T(8,128)(2,1)S(1)} %concatenate.48), channel_id=1, source_target_pairs={{0,24},{8,16},{16,8},{24,0},{1,25},{9,17},{17,9},{25,1},{2,26},{10... | collective-permute-start | bytes 258056 | tf_op jit(solution)/shard_map/ppermute | solution.py:381
  17.6 4.8 %collective-permute-done.5 = bf16[336,128]{1,0:T(8,128)(2,1)S(1)} collective-permute-done((bf16[336,128]{1,0:T(8,128)(2,1)S(1)}, bf16[336,128]{1,0:T(8,128)(2,1)S(1)}, u32[]{:S(2)}, u32[]{:S(2)}) %collective-permute-start.5) | collective-permute-done | bytes 86048 | tf_op jit(solution)/shard_map/ppermute | solution.py:381
  22.4 1.6 %collective-permute-start.8 = (bf16[2,336,128]{2,1,0:T(8,128)(2,1)S(1)}, bf16[2,336,128]{2,1,0:T(8,128)(2,1)S(1)}, u32[]{:S(2)}, u32[]{:S(2)}) collective-permute-start(bf16[2,336,128]{2,1,0:T(8,128)(2,1)S(1)} %pad_maximum_fusion.8), channel_id=1, source_target_pairs={{0,4},{2,6},{4,0},{6,2},{1,5},{3,7},{5,1},{7,3},{8,12},{10,14},{12... | collective-permute-start | bytes 516104 | tf_op jit(solution)/shard_map/ppermute | solution.py:381
  24.0 1.6 %collective-permute-start.7 = (bf16[2,336,128]{2,1,0:T(8,128)(2,1)S(1)}, bf16[2,336,128]{2,1,0:T(8,128)(2,1)S(1)}, u32[]{:S(2)}, u32[]{:S(2)}) collective-permute-start(bf16[2,336,128]{2,1,0:T(8,128)(2,1)S(1)} %pad_maximum_fusion.7), channel_id=1, source_target_pairs={{0,2},{2,0},{4,6},{6,4},{1,3},{3,1},{5,7},{7,5},{8,10},{10,8},{12,... | collective-permute-start | bytes 516104 | tf_op jit(solution)/shard_map/ppermute | solution.py:381
  25.5 1.5 %collective-permute-start.9 = (bf16[512,128]{1,0:T(8,128)(2,1)S(1)}, bf16[512,128]{1,0:T(8,128)(2,1)S(1)}, u32[]{:S(2)}, u32[]{:S(2)}) collective-permute-start(bf16[512,128]{1,0:T(8,128)(2,1)S(1)} %bitcast.54), channel_id=1, source_target_pairs={{0,8},{8,0},{16,24},{24,16},{1,9},{9,1},{17,25},{25,17},{2,10},{10... | collective-permute-start | bytes 393224 | tf_op jit(solution)/shard_map/ppermute | solution.py:381
  27.0 0.8 collective-permute-done.8
  27.9 1.6 %collective-permute-done.7 = bf16[2,336,128]{2,1,0:T(8,128)(2,1)S(1)} collective-permute-done((bf16[2,336,128]{2,1,0:T(8,128)(2,1)S(1)}, bf16[2,336,128]{2,1,0:T(8,128)(2,1)S(1)}, u32[]{:S(2)}, u32[]{:S(2)}) %collective-permute-start.7) | collective-permute-done | bytes 172064 | tf_op jit(solution)/shard_map/ppermute | solution.py:381
  29.5 1.0 collective-permute-done.9
  30.5 0.5 collective-permute-start.12
  31.0 0.6 collective-permute-start.13
  31.6 2.5 %collective-permute-start.10 = (bf16[512,128]{1,0:T(8,128)(2,1)S(1)}, bf16[512,128]{1,0:T(8,128)(2,1)S(1)}, u32[]{:S(2)}, u32[]{:S(2)}) collective-permute-start(bf16[512,128]{1,0:T(8,128)(2,1)S(1)} %bitcast.55), channel_id=1, source_target_pairs={{0,16},{8,24},{16,0},{24,8},{1,17},{9,25},{17,1},{25,9},{2,18},{10... | collective-permute-start | bytes 393224 | tf_op jit(solution)/shard_map/ppermute | solution.py:381
  34.1 1.3 %collective-permute-start.11 = (bf16[512,128]{1,0:T(8,128)(2,1)S(1)}, bf16[512,128]{1,0:T(8,128)(2,1)S(1)}, u32[]{:S(2)}, u32[]{:S(2)}) collective-permute-start(bf16[512,128]{1,0:T(8,128)(2,1)S(1)} %bitcast.56), channel_id=1, source_target_pairs={{0,24},{8,16},{16,8},{24,0},{1,25},{9,17},{17,9},{25,1},{2,26},{10... | collective-permute-start | bytes 393224 | tf_op jit(solution)/shard_map/ppermute | solution.py:381
  35.4 2.3 %collective-permute-done.12 = bf16[4,336,128]{2,1,0:T(8,128)(2,1)S(1)} collective-permute-done((bf16[4,336,128]{2,1,0:T(8,128)(2,1)S(1)}, bf16[4,336,128]{2,1,0:T(8,128)(2,1)S(1)}, u32[]{:S(2)}, u32[]{:S(2)}) %collective-permute-start.12) | collective-permute-done | bytes 344096 | tf_op jit(solution)/shard_map/ppermute | solution.py:381
  37.8 0.5 collective-permute-done.13
  38.3 0.2 pad_maximum_fusion.mine
  38.4 3.1 %collective-permute-done.10 = bf16[512,128]{1,0:T(8,128)(2,1)S(1)} collective-permute-done((bf16[512,128]{1,0:T(8,128)(2,1)S(1)}, bf16[512,128]{1,0:T(8,128)(2,1)S(1)}, u32[]{:S(2)}, u32[]{:S(2)}) %collective-permute-start.10) | collective-permute-done | bytes 131104 | tf_op jit(solution)/shard_map/ppermute | solution.py:381
  41.6 1.7 %collective-permute-start.16 = (bf16[2,512,128]{2,1,0:T(8,128)(2,1)S(1)}, bf16[2,512,128]{2,1,0:T(8,128)(2,1)S(1)}, u32[]{:S(2)}, u32[]{:S(2)}) collective-permute-start(bf16[2,512,128]{2,1,0:T(8,128)(2,1)S(1)} %pad_maximum_fusion.6), channel_id=1, source_target_pairs={{0,4},{2,6},{4,0},{6,2},{1,5},{3,7},{5,1},{7,3},{8,12},{10,14},{12... | collective-permute-start | bytes 786440 | tf_op jit(solution)/shard_map/ppermute | solution.py:381
  43.3 1.3 collective-permute-start.14
  44.6 5.7 %collective-permute-done.16 = bf16[2,512,128]{2,1,0:T(8,128)(2,1)S(1)} collective-permute-done((bf16[2,512,128]{2,1,0:T(8,128)(2,1)S(1)}, bf16[2,512,128]{2,1,0:T(8,128)(2,1)S(1)}, u32[]{:S(2)}, u32[]{:S(2)}) %collective-permute-start.16) | collective-permute-done | bytes 262176 | tf_op jit(solution)/shard_map/ppermute | solution.py:381
  50.4 1.5 %collective-permute-start.17 = (bf16[4,512,128]{2,1,0:T(8,128)(2,1)S(1)}, bf16[4,512,128]{2,1,0:T(8,128)(2,1)S(1)}, u32[]{:S(2)}, u32[]{:S(2)}) collective-permute-start(bf16[4,512,128]{2,1,0:T(8,128)(2,1)S(1)} %pad_maximum_fusion.2.rest_8_), channel_id=1, source_target_pairs={{0,2},{2,0},{4,6},{6,4},{1,3},{3,1},{5,7},{7,5},{8,10},{10,8},{12,... | collective-permute-start | bytes 1572872 | tf_op jit(solution)/shard_map/ppermute | solution.py:381
  51.9 1.6 %collective-permute-start.15 = (bf16[4,512,128]{2,1,0:T(8,128)(2,1)S(1)}, bf16[4,512,128]{2,1,0:T(8,128)(2,1)S(1)}, u32[]{:S(2)}, u32[]{:S(2)}) collective-permute-start(bf16[4,512,128]{2,1,0:T(8,128)(2,1)S(1)} %pad_maximum_fusion.1.rest_7_), channel_id=1, source_target_pairs={{0,4},{2,6},{4,0},{6,2},{1,5},{3,7},{5,1},{7,3},{8,12},{10,14},{12... | collective-permute-start | bytes 1572872 | tf_op jit(solution)/shard_map/ppermute | solution.py:381
  53.5 0.5 collective-permute-start.19
  54.0 9.2 %unpack.1 = (s32[584]{0:T(1024)S(1)}, f32[8,128]{1,0:T(8,128)S(1)}, bf16[144,128,128]{2,1,0:T(8,128)(2,1)S(1)}, f32[32,8,128]{2,1,0:T(8,128)S(1)}, f32[32,8,128]...) custom-call(s32[3]{0:T(128)S(1)} %pad_add_fusion.own, ...), custom_call_target="tpu_custom_call" | custom-call | bytes 11010048 | tf_op jit(solution)/shard_map/unpack/pallas_call | solution.py:464
  63.2 0.8 collective-permute-done.17.rest_10_
  64.0 1.2 collective-permute-done.15.rest_9_
  65.3 0.5 collective-permute-start.22
  65.8 1.4 %collective-permute-done.21.rest_13_ = bf16[4,512,128]{2,1,0:T(8,128)(2,1)S(1)} collective-permute-done((bf16[4,512,128]{2,1,0:T(8,128)(2,1)S(1)}, bf16[4,512,128]{2,1,0:T(8,128)(2,1)S(1)}, u32[]{:S(2)}, u32[]{:S(2)}) %collective-permute-start.21) | collective-permute-done | bytes 524320 | tf_op jit(solution)/shard_map/ppermute | solution.py:381
  67.2 0.7 collective-permute-done.22.rest_14_
  67.9 63.3 %iterate.1 = f32[2,4096]{1,0:T(2,128)} custom-call(s32[3]{0:T(128)S(1)} %pad_add_fusion.own, s32[584]{0:T(1024)S(1)} %get-tuple-element.46.lists, f32[8,128]{1,0:T(8,128)S(1)} %get-tuple-element.47.place, bf16[144,128,128]{2,1,0:T(8,128)(2,1)S(1)} %get-tuple-element.48.rest_0_, f32[32,8,128]{2,1,0:T(8,128)S(1)} %get-tuple-element.49.rest_1_, ...), custom_call_target="tpu_custom_call" | custom-call | tf_op jit(solution)/shard_map/iterate/pallas_call | solution.py:485
  (39 shorter events, 0.6 us)
Async XLA Ops:
  0.0 6.3 %copy-start = (bf16[1,1,128,4096]{3,2,1,0:T(8,128)(2,1)S(1)}, bf16[1,1,128,4096]{3,2,1,0:T(8,128)(2,1)}, u32[]{:S(2)}) copy-start(bf16[1,1,128,4096]{3,2,1,0:T(8,128)(2,1)} %param.7) | copy-start | bytes 3145732
  1.8 4.5 %collective-permute-start = (bf16[4,16,4096]{2,1,0:T(8,128)(2,1)S(1)}, bf16[4,16,4096]{2,1,0:T(8,128)(2,1)S(1)}, u32[]{:S(2)}, u32[]{:S(2)}) collective-permute-start(bf16[4,16,4096]{2,1,0:T(8,128)(2,1)S(1)} %select_bitcast_fusion), channel_id=1, source_target_pairs={{0,1},{1,0},{2,3},{3,2},{4,5},{5,4},{6,7},{7,6},{8,9},{9,8},{10,11... | collective-permute-start | bytes 1572872 | tf_op jit(solution)/shard_map/ppermute | solution.py:381
  6.4 9.3 %collective-permute-start.1 = (bf16[16,4096]{1,0:T(8,128)(2,1)S(1)}, bf16[16,4096]{1,0:T(8,128)(2,1)S(1)}, u32[]{:S(2)}, u32[]{:S(2)}) collective-permute-start(bf16[16,4096]{1,0:T(8,128)(2,1)S(1)} %get-tuple-element.57), channel_id=1, source_target_pairs={{0,2},{2,0},{4,6},{6,4},{1,3},{3,1},{5,7},{7,5},{8,10},{10,8},{12,... | collective-permute-start | bytes 393224 | tf_op jit(solution)/shard_map/ppermute | solution.py:381
  9.0 8.4 %collective-permute-start.2 = (bf16[16,4096]{1,0:T(8,128)(2,1)S(1)}, bf16[16,4096]{1,0:T(8,128)(2,1)S(1)}, u32[]{:S(2)}, u32[]{:S(2)}) collective-permute-start(bf16[16,4096]{1,0:T(8,128)(2,1)S(1)} %get-tuple-element.59), channel_id=1, source_target_pairs={{0,4},{2,6},{4,0},{6,2},{1,5},{3,7},{5,1},{7,3},{8,12},{10,14},{12... | collective-permute-start | bytes 393224 | tf_op jit(solution)/shard_map/ppermute | solution.py:381
  10.5 6.9 %collective-permute-start.3 = (bf16[16,4096]{1,0:T(8,128)(2,1)S(1)}, bf16[16,4096]{1,0:T(8,128)(2,1)S(1)}, u32[]{:S(2)}, u32[]{:S(2)}) collective-permute-start(bf16[16,4096]{1,0:T(8,128)(2,1)S(1)} %get-tuple-element.58), channel_id=1, source_target_pairs={{0,6},{2,4},{4,2},{6,0},{1,7},{3,5},{5,3},{7,1},{8,14},{10,12},{12... | collective-permute-start | bytes 393224 | tf_op jit(solution)/shard_map/ppermute | solution.py:381
  10.9 6.6 %collective-permute-start.4 = (bf16[336,128]{1,0:T(8,128)(2,1)S(1)}, bf16[336,128]{1,0:T(8,128)(2,1)S(1)}, u32[]{:S(2)}, u32[]{:S(2)}) collective-permute-start(bf16[336,128]{1,0:T(8,128)(2,1)S(1)} %concatenate.48), channel_id=1, source_target_pairs={{0,8},{8,0},{16,24},{24,16},{1,9},{9,1},{17,25},{25,17},{2,10},{10... | collective-permute-start | bytes 258056 | tf_op jit(solution)/shard_map/ppermute | solution.py:381
  13.0 9.3 %collective-permute-start.5 = (bf16[336,128]{1,0:T(8,128)(2,1)S(1)}, bf16[336,128]{1,0:T(8,128)(2,1)S(1)}, u32[]{:S(2)}, u32[]{:S(2)}) collective-permute-start(bf16[336,128]{1,0:T(8,128)(2,1)S(1)} %concatenate.48), channel_id=1, source_target_pairs={{0,16},{8,24},{16,0},{24,8},{1,17},{9,25},{17,1},{25,9},{2,18},{10... | collective-permute-start | bytes 258056 | tf_op jit(solution)/shard_map/ppermute | solution.py:381
  15.7 6.7 %collective-permute-start.6 = (bf16[336,128]{1,0:T(8,128)(2,1)S(1)}, bf16[336,128]{1,0:T(8,128)(2,1)S(1)}, u32[]{:S(2)}, u32[]{:S(2)}) collective-permute-start(bf16[336,128]{1,0:T(8,128)(2,1)S(1)} %concatenate.48), channel_id=1, source_target_pairs={{0,24},{8,16},{16,8},{24,0},{1,25},{9,17},{17,9},{25,1},{2,26},{10... | collective-permute-start | bytes 258056 | tf_op jit(solution)/shard_map/ppermute | solution.py:381
  22.4 5.5 %collective-permute-start.8 = (bf16[2,336,128]{2,1,0:T(8,128)(2,1)S(1)}, bf16[2,336,128]{2,1,0:T(8,128)(2,1)S(1)}, u32[]{:S(2)}, u32[]{:S(2)}) collective-permute-start(bf16[2,336,128]{2,1,0:T(8,128)(2,1)S(1)} %pad_maximum_fusion.8), channel_id=1, source_target_pairs={{0,4},{2,6},{4,0},{6,2},{1,5},{3,7},{5,1},{7,3},{8,12},{10,14},{12... | collective-permute-start | bytes 516104 | tf_op jit(solution)/shard_map/ppermute | solution.py:381
  24.0 5.5 %collective-permute-start.7 = (bf16[2,336,128]{2,1,0:T(8,128)(2,1)S(1)}, bf16[2,336,128]{2,1,0:T(8,128)(2,1)S(1)}, u32[]{:S(2)}, u32[]{:S(2)}) collective-permute-start(bf16[2,336,128]{2,1,0:T(8,128)(2,1)S(1)} %pad_maximum_fusion.7), channel_id=1, source_target_pairs={{0,2},{2,0},{4,6},{6,4},{1,3},{3,1},{5,7},{7,5},{8,10},{10,8},{12,... | collective-permute-start | bytes 516104 | tf_op jit(solution)/shard_map/ppermute | solution.py:381
  25.5 5.0 %collective-permute-start.9 = (bf16[512,128]{1,0:T(8,128)(2,1)S(1)}, bf16[512,128]{1,0:T(8,128)(2,1)S(1)}, u32[]{:S(2)}, u32[]{:S(2)}) collective-permute-start(bf16[512,128]{1,0:T(8,128)(2,1)S(1)} %bitcast.54), channel_id=1, source_target_pairs={{0,8},{8,0},{16,24},{24,16},{1,9},{9,1},{17,25},{25,17},{2,10},{10... | collective-permute-start | bytes 393224 | tf_op jit(solution)/shard_map/ppermute | solution.py:381
  30.5 7.2 %collective-permute-start.12 = (bf16[4,336,128]{2,1,0:T(8,128)(2,1)S(1)}, bf16[4,336,128]{2,1,0:T(8,128)(2,1)S(1)}, u32[]{:S(2)}, u32[]{:S(2)}) collective-permute-start(bf16[4,336,128]{2,1,0:T(8,128)(2,1)S(1)} %pad_maximum_fusion.3), channel_id=1, source_target_pairs={{0,4},{2,6},{4,0},{6,2},{1,5},{3,7},{5,1},{7,3},{8,12},{10,14},{12... | collective-permute-start | bytes 1032200 | tf_op jit(solution)/shard_map/ppermute | solution.py:381
  31.0 7.2 %collective-permute-start.13 = (bf16[4,336,128]{2,1,0:T(8,128)(2,1)S(1)}, bf16[4,336,128]{2,1,0:T(8,128)(2,1)S(1)}, u32[]{:S(2)}, u32[]{:S(2)}) collective-permute-start(bf16[4,336,128]{2,1,0:T(8,128)(2,1)S(1)} %pad_maximum_fusion.4), channel_id=1, source_target_pairs={{0,2},{2,0},{4,6},{6,4},{1,3},{3,1},{5,7},{7,5},{8,10},{10,8},{12,... | collective-permute-start | bytes 1032200 | tf_op jit(solution)/shard_map/ppermute | solution.py:381
  31.6 10.0 %collective-permute-start.10 = (bf16[512,128]{1,0:T(8,128)(2,1)S(1)}, bf16[512,128]{1,0:T(8,128)(2,1)S(1)}, u32[]{:S(2)}, u32[]{:S(2)}) collective-permute-start(bf16[512,128]{1,0:T(8,128)(2,1)S(1)} %bitcast.55), channel_id=1, source_target_pairs={{0,16},{8,24},{16,0},{24,8},{1,17},{9,25},{17,1},{25,9},{2,18},{10... | collective-permute-start | bytes 393224 | tf_op jit(solution)/shard_map/ppermute | solution.py:381
  34.1 7.5 %collective-permute-start.11 = (bf16[512,128]{1,0:T(8,128)(2,1)S(1)}, bf16[512,128]{1,0:T(8,128)(2,1)S(1)}, u32[]{:S(2)}, u32[]{:S(2)}) collective-permute-start(bf16[512,128]{1,0:T(8,128)(2,1)S(1)} %bitcast.56), channel_id=1, source_target_pairs={{0,24},{8,16},{16,8},{24,0},{1,25},{9,17},{17,9},{25,1},{2,26},{10... | collective-permute-start | bytes 393224 | tf_op jit(solution)/shard_map/ppermute | solution.py:381
  41.5 12.5 %collective-permute-start.18 = (bf16[16,336,128]{2,1,0:T(8,128)(2,1)S(1)}, bf16[16,336,128]{2,1,0:T(8,128)(2,1)S(1)}, u32[]{:S(2)}, u32[]{:S(2)}) collective-permute-start(bf16[16,336,128]{2,1,0:T(8,128)(2,1)S(1)} %pad_maximum_fusion.mine), channel_id=1, source_target_pairs={{0,1},{1,0},{2,3},{3,2},{4,5},{5,4},{6,7},{7,6},{8,9},{9,8},{10,11... | collective-permute-start | bytes 4128776 | tf_op jit(solution)/shard_map/ppermute | solution.py:381
  41.6 8.8 %collective-permute-start.16 = (bf16[2,512,128]{2,1,0:T(8,128)(2,1)S(1)}, bf16[2,512,128]{2,1,0:T(8,128)(2,1)S(1)}, u32[]{:S(2)}, u32[]{:S(2)}) collective-permute-start(bf16[2,512,128]{2,1,0:T(8,128)(2,1)S(1)} %pad_maximum_fusion.6), channel_id=1, source_target_pairs={{0,4},{2,6},{4,0},{6,2},{1,5},{3,7},{5,1},{7,3},{8,12},{10,14},{12... | collective-permute-start | bytes 786440 | tf_op jit(solution)/shard_map/ppermute | solution.py:381
  43.3 8.5 %collective-permute-start.14 = (bf16[2,512,128]{2,1,0:T(8,128)(2,1)S(1)}, bf16[2,512,128]{2,1,0:T(8,128)(2,1)S(1)}, u32[]{:S(2)}, u32[]{:S(2)}) collective-permute-start(bf16[2,512,128]{2,1,0:T(8,128)(2,1)S(1)} %pad_maximum_fusion.5), channel_id=1, source_target_pairs={{0,2},{2,0},{4,6},{6,4},{1,3},{3,1},{5,7},{7,5},{8,10},{10,8},{12,... | collective-permute-start | bytes 786440 | tf_op jit(solution)/shard_map/ppermute | solution.py:381
  50.4 13.6 %collective-permute-start.17 = (bf16[4,512,128]{2,1,0:T(8,128)(2,1)S(1)}, bf16[4,512,128]{2,1,0:T(8,128)(2,1)S(1)}, u32[]{:S(2)}, u32[]{:S(2)}) collective-permute-start(bf16[4,512,128]{2,1,0:T(8,128)(2,1)S(1)} %pad_maximum_fusion.2.rest_8_), channel_id=1, source_target_pairs={{0,2},{2,0},{4,6},{6,4},{1,3},{3,1},{5,7},{7,5},{8,10},{10,8},{12,... | collective-permute-start | bytes 1572872 | tf_op jit(solution)/shard_map/ppermute | solution.py:381
  51.9 13.3 %collective-permute-start.15 = (bf16[4,512,128]{2,1,0:T(8,128)(2,1)S(1)}, bf16[4,512,128]{2,1,0:T(8,128)(2,1)S(1)}, u32[]{:S(2)}, u32[]{:S(2)}) collective-permute-start(bf16[4,512,128]{2,1,0:T(8,128)(2,1)S(1)} %pad_maximum_fusion.1.rest_7_), channel_id=1, source_target_pairs={{0,4},{2,6},{4,0},{6,2},{1,5},{3,7},{5,1},{7,3},{8,12},{10,14},{12... | collective-permute-start | bytes 1572872 | tf_op jit(solution)/shard_map/ppermute | solution.py:381
  53.5 12.3 %collective-permute-start.20 = (bf16[4,512,128]{2,1,0:T(8,128)(2,1)S(1)}, bf16[4,512,128]{2,1,0:T(8,128)(2,1)S(1)}, u32[]{:S(2)}, u32[]{:S(2)}) collective-permute-start(bf16[4,512,128]{2,1,0:T(8,128)(2,1)S(1)} %pad_maximum_fusion.2.rest_8_), channel_id=1, source_target_pairs={{0,1},{1,0},{2,3},{3,2},{4,5},{5,4},{6,7},{7,6},{8,9},{9,8},{10,11... | collective-permute-start | bytes 1572872 | tf_op jit(solution)/shard_map/ppermute | solution.py:381
  53.5 12.3 %collective-permute-start.19 = (bf16[4,512,128]{2,1,0:T(8,128)(2,1)S(1)}, bf16[4,512,128]{2,1,0:T(8,128)(2,1)S(1)}, u32[]{:S(2)}, u32[]{:S(2)}) collective-permute-start(bf16[4,512,128]{2,1,0:T(8,128)(2,1)S(1)} %pad_maximum_fusion.1.rest_7_), channel_id=1, source_target_pairs={{0,1},{1,0},{2,3},{3,2},{4,5},{5,4},{6,7},{7,6},{8,9},{9,8},{10,11... | collective-permute-start | bytes 1572872 | tf_op jit(solution)/shard_map/ppermute | solution.py:381
  65.3 1.9 %collective-permute-start.21 = (bf16[4,512,128]{2,1,0:T(8,128)(2,1)S(1)}, bf16[4,512,128]{2,1,0:T(8,128)(2,1)S(1)}, u32[]{:S(2)}, u32[]{:S(2)}) collective-permute-start(bf16[4,512,128]{2,1,0:T(8,128)(2,1)S(1)} %collective-permute-done.15.rest_9_), channel_id=1, source_target_pairs={{0,1},{1,0},{2,3},{3,2},{4,5},{5,4},{6,7},{7,6},{8,9},{9,8},{10,11... | collective-permute-start | bytes 1572872 | tf_op jit(solution)/shard_map/ppermute | solution.py:381
  65.3 2.7 %collective-permute-start.22 = (bf16[4,512,128]{2,1,0:T(8,128)(2,1)S(1)}, bf16[4,512,128]{2,1,0:T(8,128)(2,1)S(1)}, u32[]{:S(2)}, u32[]{:S(2)}) collective-permute-start(bf16[4,512,128]{2,1,0:T(8,128)(2,1)S(1)} %collective-permute-done.17.rest_10_), channel_id=1, source_target_pairs={{0,1},{1,0},{2,3},{3,2},{4,5},{5,4},{6,7},{7,6},{8,9},{9,8},{10,11... | collective-permute-start | bytes 1572872 | tf_op jit(solution)/shard_map/ppermute | solution.py:381

commit v14 on v13

--- a/solution.py
+++ b/solution.py
@@ -371,9 +371,50 @@
 
 
 def split3(x):
-    a = lax.reduce_precision(x, 8, 7)
-    b = lax.reduce_precision(x - a, 8, 7)
-    return [v.astype(jnp.bfloat16) for v in (a, b, x - a - b)]
+    parts = []
+    for _ in range(3):
+        parts.append(x.astype(jnp.bfloat16).astype(jnp.float32))
+        x = x - parts[-1]
+    return parts
+
+
+def prepare(count, *rest):
+    sources, out, sems, first, second, both = rest[:5], *rest[5:10]
+    for copy in copy_in(list(zip(sources, rest[10:])), sems):
+        copy.wait()
+    rows, cols, vectors, row_mass, col_mass = rest[10:]
+    f32, bf16 = jnp.float32, jnp.bfloat16
+    half = first.shape[0]
+    for i in range(half):
+        first[i : i + 1, :] = vectors[0:1, i * 128 : (i + 1) * 128]
+        second[i : i + 1, :] = vectors[1:2, i * 128 : (i + 1) * 128]
+    x, z = first[...], second[...]
+    left = left_half(x.shape)
+    both[pl.ds(0, half, stride=2), :] = jnp.where(left, x, pltpu.roll(z, 64, 1))
+    both[pl.ds(1, half, stride=2), :] = jnp.where(left, pltpu.roll(x, 64, 1), z)
+    inv = 1.0 / jnp.sqrt(jnp.concatenate([col_mass[0:1, :], col_mass[1:2, :]], axis=1))
+    out[: 2 * half, :] = (both[...] * inv).astype(bf16)
+
+    sub = lax.broadcasted_iota(jnp.int32, (META, 128), 0)
+
+    def stacked(at, values):
+        result = jnp.zeros((META, 128), f32)
+        for i, value in enumerate(values):
+            result = jnp.where(sub == at + i, value, result)
+        return result
+
+    mass = jnp.concatenate([row_mass[0:1, :], row_mass[1:2, :]], axis=1)
+    source = lax.broadcasted_iota(jnp.int32, (128, 128), 0)
+    lane = lax.broadcasted_iota(jnp.int32, (128, 128), 1)
+    chosen = source == (lane // 64) * 64 + 2 * (lane % half) + (lane % 64) // half
+    masses = dot(stacked(0, split3(mass)).astype(bf16), jnp.where(chosen, 1.0, 0.0).astype(bf16))
+    r, c = rows[...].astype(f32), cols[...].astype(f32)
+    lane = lane[:8]
+    moved = pltpu.roll(jnp.broadcast_to(c, (8, 128)), OFF_CAP, 1)
+    short = jnp.where(lane == 2 * OFF_CAP, count[0, 0].astype(f32), 0.0)
+    short = jnp.where(lane < OFF_CAP, r, jnp.where(lane < 2 * OFF_CAP, moved, short))
+    packed = masses + stacked(3, split3(inv) + [r, c, short[0:1]])
+    out[2 * half :, :] = packed.astype(bf16)
 
 
 def swap(x, axis, distance):
@@ -426,18 +467,20 @@
     row, chip, core = (lax.axis_index(name) for name in ("row", "chip", "core"))
 
     off = tile[:OFF_CAP].reshape(OFF_CAP * half, 128)
-    inv_col = 1.0 / jnp.sqrt(col_mass)
-    scaled = (vectors.reshape(own, k, bsize) * inv_col[:, None, :]).astype(bf16)
-    scaled = scaled.transpose(1, 0, 2).reshape(k, own * bsize)
-    mass = row_mass.reshape(own, half, 2).transpose(0, 2, 1).reshape(own * bsize)
-    rows, cols = block_row[0, 0], block_col[0, 0]
-    short = jnp.concatenate(
-        [rows[:OFF_CAP], cols[:OFF_CAP], count[None], jnp.zeros(128 - 2 * OFF_CAP - 1, jnp.int32)]
-    )
-    meta = [v.astype(bf16) for v in (rows, cols, short)]
-    meta = split3(mass) + split3(inv_col.reshape(own * bsize)) + meta
-    meta = jnp.stack(meta + [jnp.zeros(128, bf16)] * (META - len(meta)))
-    small = jnp.concatenate([off, scaled, meta], axis=0)
+    sources = (block_row[0], block_col[0], vectors, row_mass, col_mass)
+    laid_out = pl.pallas_call(
+        prepare,
+        out_shape=jax.ShapeDtypeStruct((k + META, own * bsize), bf16),
+        in_specs=[pl.BlockSpec(memory_space=pltpu.SMEM)]
+        + [pl.BlockSpec(memory_space=pltpu.HBM)] * len(sources),
+        out_specs=pl.BlockSpec(memory_space=pltpu.VMEM),
+        scratch_shapes=[pltpu.SemaphoreType.DMA((len(sources),))]
+        + [pltpu.VMEM((rows, own * bsize), jnp.float32) for rows in (half, half, k)]
+        + [pltpu.VMEM(v.shape, v.dtype) for v in sources],
+        name="prepare",
+    )(counts, *(pltpu.with_memory_space_constraint(v, pltpu.HBM) for v in sources))
+    small = jnp.concatenate([off, laid_out], axis=0)
+
     home = full_part(tile, has_full, n_col // 2, part, chip, core)
     home = home.reshape(part, half, 128).transpose(1, 0, 2).reshape(half * part, 128)
 

time: 130 us -> 128 us (0.985); the launches traced: 131 us -> 127 us
  local copies, waits for them, and re-layouts: 2.99 us -> 1 us
  Pallas kernels: 72.5 us -> 71 us
  other arithmetic: 3.1 us -> 1.69 us
    pallas_call x1, Pallas kernels: 63.3 us -> 60.7 us  [whole_on_each(): pl.pallas_call(functools.partial(iterate, n_row, n_col, n_cap, float(n_de...]
    reshape x5 -> x0, local copies, waits for them, and re-layouts: 1.91 us -> none  [the longest x1 0.87 us: whole_on_each(): scaled = (vectors.reshape(own, k, bsize) * inv_col[:, None, :]).astype(bf16)]
    pallas_call x0 -> x1, Pallas kernels: none -> 1.64 us  [whole_on_each(): pl.pallas_call(prepare, out_shape=jax.ShapeDtypeStruct((k + META, own * b...]
    convert_element_type x3 -> x0, other arithmetic: 1.32 us -> none  [the longest x2 1.32 us: whole_on_each(): meta = [v.astype(bf16) for v in (rows, cols, short)]]
  transfers between devices with their start and end apart: 23 -> 23, of which waited for: 12 -> 13; matrix products, arithmetic and copies ran while one was open for 4% -> 1% of each run, Pallas kernels for 7% -> 8%
where the time goes in v14:
time: 128 us; the launch traced here: 127 us
  Pallas kernels  71 us (55%)
  starting transfers between devices  27.6 us (22%)
  waiting for transfers between devices  24.9 us (19%)
  other arithmetic  1.69 us (1%)
    pallas_call x1, Pallas kernels, whole_on_each(): pl.pallas_call(functools.partial(iterate, n_row, n_col, n_cap, float(n_de...  60.7 us
    ppermute x23, starting transfers between devices, swap(): return lax.ppermute(x, axis, [(i, i ^ distance) for i in range(size)])  27.6 us
    ppermute x23, waiting for transfers between devices, swap(): return lax.ppermute(x, axis, [(i, i ^ distance) for i in range(size)])  24.9 us
    pallas_call x1, Pallas kernels, whole_on_each(): pl.pallas_call(functools.partial(unpack, n_row, n_col), out_shape=[jax.Sh...  8.73 us
  transfers between devices with their start and end apart: 23, of which 13 were waited for; matrix products, arithmetic and copies ran while one was open for 1% of the time, Pallas kernels for 8%

profile of v14, /device:TPU:0, one launch (start us, length us, event | category | flops | bytes accessed | tf_op | source)
XLA Modules:
  0.0 127.3 jit_solution(4940933723771620691)
XLA Ops:
  0.7 1.1 select_bitcast_fusion
  1.8 0.5 collective-permute-start
  2.3 0.8 slice.4
  3.2 1.6 %prepare.1 = bf16[80,128]{1,0:T(8,128)(2,1)} custom-call(s32[1,1]{1,0:T(1,128)S(6)} %copy.10.count, s32[1,128]{1,0:T(1,128)} %bitcast.63, s32[1,128]{1,0:T(1,128)} %bitcast.64, f32[2,4096]{1,0:T(2,128)} %rest_2_.1, f32[2,64]{1,0:T(2,128)} %rest_3_.1, f32[2,64]{1,0:T(2,128)} %rest_4_.1), custom_call_target="tpu_custom_call" | custom-call | tf_op jit(solution)/shard_map/prepare/pallas_call | solution.py:471
  4.9 0.0 copy-start.1
  4.9 0.1 bitcast_add_fusion
  5.0 2.6 %collective-permute-start.1 = (bf16[16,4096]{1,0:T(8,128)(2,1)S(1)}, bf16[16,4096]{1,0:T(8,128)(2,1)S(1)}, u32[]{:S(2)}, u32[]{:S(2)}) collective-permute-start(bf16[16,4096]{1,0:T(8,128)(2,1)S(1)} %get-tuple-element.57), channel_id=1, source_target_pairs={{0,2},{2,0},{4,6},{6,4},{1,3},{3,1},{5,7},{7,5},{8,10},{10,8},{12,... | collective-permute-start | bytes 393224 | tf_op jit(solution)/shard_map/ppermute | solution.py:422
  7.6 1.5 %collective-permute-start.2 = (bf16[16,4096]{1,0:T(8,128)(2,1)S(1)}, bf16[16,4096]{1,0:T(8,128)(2,1)S(1)}, u32[]{:S(2)}, u32[]{:S(2)}) collective-permute-start(bf16[16,4096]{1,0:T(8,128)(2,1)S(1)} %get-tuple-element.59), channel_id=1, source_target_pairs={{0,4},{2,6},{4,0},{6,2},{1,5},{3,7},{5,1},{7,3},{8,12},{10,14},{12... | collective-permute-start | bytes 393224 | tf_op jit(solution)/shard_map/ppermute | solution.py:422
  9.2 0.0 collective-permute-start.3
  9.2 2.1 %collective-permute-start.4 = (bf16[336,128]{1,0:T(8,128)(2,1)S(1)}, bf16[336,128]{1,0:T(8,128)(2,1)S(1)}, u32[]{:S(2)}, u32[]{:S(2)}) collective-permute-start(bf16[336,128]{1,0:T(8,128)(2,1)S(1)} %pad_maximum_fusion.9), channel_id=1, source_target_pairs={{0,8},{8,0},{16,24},{24,16},{1,9},{9,1},{17,25},{25,17},{2,10},{10... | collective-permute-start | bytes 258056 | tf_op jit(solution)/shard_map/ppermute | solution.py:422
  11.3 2.6 %collective-permute-start.5 = (bf16[336,128]{1,0:T(8,128)(2,1)S(1)}, bf16[336,128]{1,0:T(8,128)(2,1)S(1)}, u32[]{:S(2)}, u32[]{:S(2)}) collective-permute-start(bf16[336,128]{1,0:T(8,128)(2,1)S(1)} %pad_maximum_fusion.9), channel_id=1, source_target_pairs={{0,16},{8,24},{16,0},{24,8},{1,17},{9,25},{17,1},{25,9},{2,18},{10... | collective-permute-start | bytes 258056 | tf_op jit(solution)/shard_map/ppermute | solution.py:422
  13.9 0.1 pad_add_fusion.own
  14.0 2.0 %collective-permute-start.6 = (bf16[336,128]{1,0:T(8,128)(2,1)S(1)}, bf16[336,128]{1,0:T(8,128)(2,1)S(1)}, u32[]{:S(2)}, u32[]{:S(2)}) collective-permute-start(bf16[336,128]{1,0:T(8,128)(2,1)S(1)} %pad_maximum_fusion.9), channel_id=1, source_target_pairs={{0,24},{8,16},{16,8},{24,0},{1,25},{9,17},{17,9},{25,1},{2,26},{10... | collective-permute-start | bytes 258056 | tf_op jit(solution)/shard_map/ppermute | solution.py:422
  16.0 0.1 collective-permute-done.2
  16.1 0.1 copy.8
  16.2 4.4 %collective-permute-done.5 = bf16[336,128]{1,0:T(8,128)(2,1)S(1)} collective-permute-done((bf16[336,128]{1,0:T(8,128)(2,1)S(1)}, bf16[336,128]{1,0:T(8,128)(2,1)S(1)}, u32[]{:S(2)}, u32[]{:S(2)}) %collective-permute-start.5) | collective-permute-done | bytes 86048 | tf_op jit(solution)/shard_map/ppermute | solution.py:422
  20.6 1.6 %collective-permute-start.8 = (bf16[2,336,128]{2,1,0:T(8,128)(2,1)S(1)}, bf16[2,336,128]{2,1,0:T(8,128)(2,1)S(1)}, u32[]{:S(2)}, u32[]{:S(2)}) collective-permute-start(bf16[2,336,128]{2,1,0:T(8,128)(2,1)S(1)} %pad_maximum_fusion.8), channel_id=1, source_target_pairs={{0,4},{2,6},{4,0},{6,2},{1,5},{3,7},{5,1},{7,3},{8,12},{10,14},{12... | collective-permute-start | bytes 516104 | tf_op jit(solution)/shard_map/ppermute | solution.py:422
  22.2 1.6 %collective-permute-start.7 = (bf16[2,336,128]{2,1,0:T(8,128)(2,1)S(1)}, bf16[2,336,128]{2,1,0:T(8,128)(2,1)S(1)}, u32[]{:S(2)}, u32[]{:S(2)}) collective-permute-start(bf16[2,336,128]{2,1,0:T(8,128)(2,1)S(1)} %pad_maximum_fusion.7), channel_id=1, source_target_pairs={{0,2},{2,0},{4,6},{6,4},{1,3},{3,1},{5,7},{7,5},{8,10},{10,8},{12,... | collective-permute-start | bytes 516104 | tf_op jit(solution)/shard_map/ppermute | solution.py:422
  23.8 1.5 %collective-permute-start.9 = (bf16[512,128]{1,0:T(8,128)(2,1)S(1)}, bf16[512,128]{1,0:T(8,128)(2,1)S(1)}, u32[]{:S(2)}, u32[]{:S(2)}) collective-permute-start(bf16[512,128]{1,0:T(8,128)(2,1)S(1)} %bitcast.43), channel_id=1, source_target_pairs={{0,8},{8,0},{16,24},{24,16},{1,9},{9,1},{17,25},{25,17},{2,10},{10... | collective-permute-start | bytes 393224 | tf_op jit(solution)/shard_map/ppermute | solution.py:422
  25.3 0.8 collective-permute-done.8
  26.1 1.6 %collective-permute-done.7 = bf16[2,336,128]{2,1,0:T(8,128)(2,1)S(1)} collective-permute-done((bf16[2,336,128]{2,1,0:T(8,128)(2,1)S(1)}, bf16[2,336,128]{2,1,0:T(8,128)(2,1)S(1)}, u32[]{:S(2)}, u32[]{:S(2)}) %collective-permute-start.7) | collective-permute-done | bytes 172064 | tf_op jit(solution)/shard_map/ppermute | solution.py:422
  27.7 1.0 collective-permute-done.9
  28.7 0.5 collective-permute-start.12
  29.2 0.6 collective-permute-start.13
  29.8 2.6 %collective-permute-start.10 = (bf16[512,128]{1,0:T(8,128)(2,1)S(1)}, bf16[512,128]{1,0:T(8,128)(2,1)S(1)}, u32[]{:S(2)}, u32[]{:S(2)}) collective-permute-start(bf16[512,128]{1,0:T(8,128)(2,1)S(1)} %bitcast.44), channel_id=1, source_target_pairs={{0,16},{8,24},{16,0},{24,8},{1,17},{9,25},{17,1},{25,9},{2,18},{10... | collective-permute-start | bytes 393224 | tf_op jit(solution)/shard_map/ppermute | solution.py:422
  32.4 1.3 collective-permute-start.11
  33.6 2.3 %collective-permute-done.12 = bf16[4,336,128]{2,1,0:T(8,128)(2,1)S(1)} collective-permute-done((bf16[4,336,128]{2,1,0:T(8,128)(2,1)S(1)}, bf16[4,336,128]{2,1,0:T(8,128)(2,1)S(1)}, u32[]{:S(2)}, u32[]{:S(2)}) %collective-permute-start.12) | collective-permute-done | bytes 344096 | tf_op jit(solution)/shard_map/ppermute | solution.py:422
  36.0 0.5 collective-permute-done.13
  36.5 0.2 pad_maximum_fusion.mine
  36.7 3.6 %collective-permute-done.10 = bf16[512,128]{1,0:T(8,128)(2,1)S(1)} collective-permute-done((bf16[512,128]{1,0:T(8,128)(2,1)S(1)}, bf16[512,128]{1,0:T(8,128)(2,1)S(1)}, u32[]{:S(2)}, u32[]{:S(2)}) %collective-permute-start.10) | collective-permute-done | bytes 131104 | tf_op jit(solution)/shard_map/ppermute | solution.py:422
  40.2 0.0 collective-permute-done.11
  40.2 0.0 collective-permute-start.18
  40.3 1.6 %collective-permute-start.16 = (bf16[2,512,128]{2,1,0:T(8,128)(2,1)S(1)}, bf16[2,512,128]{2,1,0:T(8,128)(2,1)S(1)}, u32[]{:S(2)}, u32[]{:S(2)}) collective-permute-start(bf16[2,512,128]{2,1,0:T(8,128)(2,1)S(1)} %pad_maximum_fusion.6), channel_id=1, source_target_pairs={{0,4},{2,6},{4,0},{6,2},{1,5},{3,7},{5,1},{7,3},{8,12},{10,14},{12... | collective-permute-start | bytes 786440 | tf_op jit(solution)/shard_map/ppermute | solution.py:422
  41.9 1.3 collective-permute-start.14
  43.1 5.9 %collective-permute-done.16 = bf16[2,512,128]{2,1,0:T(8,128)(2,1)S(1)} collective-permute-done((bf16[2,512,128]{2,1,0:T(8,128)(2,1)S(1)}, bf16[2,512,128]{2,1,0:T(8,128)(2,1)S(1)}, u32[]{:S(2)}, u32[]{:S(2)}) %collective-permute-start.16) | collective-permute-done | bytes 262176 | tf_op jit(solution)/shard_map/ppermute | solution.py:422
  49.1 0.1 pad_maximum_fusion.2.rest_8_
  49.1 1.3 collective-permute-start.17
  50.4 0.0 collective-permute-done.14
  50.4 0.1 pad_maximum_fusion.1.rest_7_
  50.4 1.6 %collective-permute-start.15 = (bf16[4,512,128]{2,1,0:T(8,128)(2,1)S(1)}, bf16[4,512,128]{2,1,0:T(8,128)(2,1)S(1)}, u32[]{:S(2)}, u32[]{:S(2)}) collective-permute-start(bf16[4,512,128]{2,1,0:T(8,128)(2,1)S(1)} %pad_maximum_fusion.1.rest_7_), channel_id=1, source_target_pairs={{0,4},{2,6},{4,0},{6,2},{1,5},{3,7},{5,1},{7,3},{8,12},{10,14},{12... | collective-permute-start | bytes 1572872 | tf_op jit(solution)/shard_map/ppermute | solution.py:422
  52.0 0.5 collective-permute-start.19
  52.5 8.7 %unpack.1 = (s32[584]{0:T(1024)S(1)}, f32[8,128]{1,0:T(8,128)S(1)}, bf16[144,128,128]{2,1,0:T(8,128)(2,1)S(1)}, f32[32,8,128]{2,1,0:T(8,128)S(1)}, f32[32,8,128]...) custom-call(s32[3]{0:T(128)S(1)} %pad_add_fusion.own, ...), custom_call_target="tpu_custom_call" | custom-call | bytes 11010048 | tf_op jit(solution)/shard_map/unpack/pallas_call | solution.py:507
  61.3 1.5 %collective-permute-done.17.rest_10_ = bf16[4,512,128]{2,1,0:T(8,128)(2,1)S(1)} collective-permute-done((bf16[4,512,128]{2,1,0:T(8,128)(2,1)S(1)}, bf16[4,512,128]{2,1,0:T(8,128)(2,1)S(1)}, u32[]{:S(2)}, u32[]{:S(2)}) %collective-permute-start.17) | collective-permute-done | bytes 524320 | tf_op jit(solution)/shard_map/ppermute | solution.py:422
  62.7 1.0 collective-permute-done.15.rest_9_
  63.8 0.5 collective-permute-start.22
  64.3 1.4 %collective-permute-done.21.rest_13_ = bf16[4,512,128]{2,1,0:T(8,128)(2,1)S(1)} collective-permute-done((bf16[4,512,128]{2,1,0:T(8,128)(2,1)S(1)}, bf16[4,512,128]{2,1,0:T(8,128)(2,1)S(1)}, u32[]{:S(2)}, u32[]{:S(2)}) %collective-permute-start.21) | collective-permute-done | bytes 524320 | tf_op jit(solution)/shard_map/ppermute | solution.py:422
  65.7 0.7 collective-permute-done.22.rest_14_
  66.4 60.7 %iterate.1 = f32[2,4096]{1,0:T(2,128)} custom-call(s32[3]{0:T(128)S(1)} %pad_add_fusion.own, s32[584]{0:T(1024)S(1)} %get-tuple-element.46.lists, f32[8,128]{1,0:T(8,128)S(1)} %get-tuple-element.47.place, bf16[144,128,128]{2,1,0:T(8,128)(2,1)S(1)} %get-tuple-element.48.rest_0_, f32[32,8,128]{2,1,0:T(8,128)S(1)} %get-tuple-element.49.rest_1_, ...), custom_call_target="tpu_custom_call" | custom-call | tf_op jit(solution)/shard_map/iterate/pallas_call | solution.py:528
  (24 shorter events, 0.3 us)
Async XLA Ops:
  0.0 4.9 %copy-start = (bf16[1,1,128,4096]{3,2,1,0:T(8,128)(2,1)S(1)}, bf16[1,1,128,4096]{3,2,1,0:T(8,128)(2,1)}, u32[]{:S(2)}) copy-start(bf16[1,1,128,4096]{3,2,1,0:T(8,128)(2,1)} %param.7) | copy-start | bytes 3145732
  1.8 3.1 %collective-permute-start = (bf16[4,16,4096]{2,1,0:T(8,128)(2,1)S(1)}, bf16[4,16,4096]{2,1,0:T(8,128)(2,1)S(1)}, u32[]{:S(2)}, u32[]{:S(2)}) collective-permute-start(bf16[4,16,4096]{2,1,0:T(8,128)(2,1)S(1)} %select_bitcast_fusion), channel_id=1, source_target_pairs={{0,1},{1,0},{2,3},{3,2},{4,5},{5,4},{6,7},{7,6},{8,9},{9,8},{10,11... | collective-permute-start | bytes 1572872 | tf_op jit(solution)/shard_map/ppermute | solution.py:422
  4.9 4.3 %copy-start.1 = (bf16[80,128]{1,0:T(8,128)(2,1)S(1)}, bf16[80,128]{1,0:T(8,128)(2,1)}, u32[]{:S(2)}) copy-start(bf16[80,128]{1,0:T(8,128)(2,1)} %prepare.1) | copy-start | bytes 61444
  5.0 8.9 %collective-permute-start.1 = (bf16[16,4096]{1,0:T(8,128)(2,1)S(1)}, bf16[16,4096]{1,0:T(8,128)(2,1)S(1)}, u32[]{:S(2)}, u32[]{:S(2)}) collective-permute-start(bf16[16,4096]{1,0:T(8,128)(2,1)S(1)} %get-tuple-element.57), channel_id=1, source_target_pairs={{0,2},{2,0},{4,6},{6,4},{1,3},{3,1},{5,7},{7,5},{8,10},{10,8},{12,... | collective-permute-start | bytes 393224 | tf_op jit(solution)/shard_map/ppermute | solution.py:422
  7.6 8.4 %collective-permute-start.2 = (bf16[16,4096]{1,0:T(8,128)(2,1)S(1)}, bf16[16,4096]{1,0:T(8,128)(2,1)S(1)}, u32[]{:S(2)}, u32[]{:S(2)}) collective-permute-start(bf16[16,4096]{1,0:T(8,128)(2,1)S(1)} %get-tuple-element.59), channel_id=1, source_target_pairs={{0,4},{2,6},{4,0},{6,2},{1,5},{3,7},{5,1},{7,3},{8,12},{10,14},{12... | collective-permute-start | bytes 393224 | tf_op jit(solution)/shard_map/ppermute | solution.py:422
  9.2 6.9 %collective-permute-start.3 = (bf16[16,4096]{1,0:T(8,128)(2,1)S(1)}, bf16[16,4096]{1,0:T(8,128)(2,1)S(1)}, u32[]{:S(2)}, u32[]{:S(2)}) collective-permute-start(bf16[16,4096]{1,0:T(8,128)(2,1)S(1)} %get-tuple-element.58), channel_id=1, source_target_pairs={{0,6},{2,4},{4,2},{6,0},{1,7},{3,5},{5,3},{7,1},{8,14},{10,12},{12... | collective-permute-start | bytes 393224 | tf_op jit(solution)/shard_map/ppermute | solution.py:422
  9.2 7.0 %collective-permute-start.4 = (bf16[336,128]{1,0:T(8,128)(2,1)S(1)}, bf16[336,128]{1,0:T(8,128)(2,1)S(1)}, u32[]{:S(2)}, u32[]{:S(2)}) collective-permute-start(bf16[336,128]{1,0:T(8,128)(2,1)S(1)} %pad_maximum_fusion.9), channel_id=1, source_target_pairs={{0,8},{8,0},{16,24},{24,16},{1,9},{9,1},{17,25},{25,17},{2,10},{10... | collective-permute-start | bytes 258056 | tf_op jit(solution)/shard_map/ppermute | solution.py:422
  11.3 9.3 %collective-permute-start.5 = (bf16[336,128]{1,0:T(8,128)(2,1)S(1)}, bf16[336,128]{1,0:T(8,128)(2,1)S(1)}, u32[]{:S(2)}, u32[]{:S(2)}) collective-permute-start(bf16[336,128]{1,0:T(8,128)(2,1)S(1)} %pad_maximum_fusion.9), channel_id=1, source_target_pairs={{0,16},{8,24},{16,0},{24,8},{1,17},{9,25},{17,1},{25,9},{2,18},{10... | collective-permute-start | bytes 258056 | tf_op jit(solution)/shard_map/ppermute | solution.py:422
  14.0 6.6 %collective-permute-start.6 = (bf16[336,128]{1,0:T(8,128)(2,1)S(1)}, bf16[336,128]{1,0:T(8,128)(2,1)S(1)}, u32[]{:S(2)}, u32[]{:S(2)}) collective-permute-start(bf16[336,128]{1,0:T(8,128)(2,1)S(1)} %pad_maximum_fusion.9), channel_id=1, source_target_pairs={{0,24},{8,16},{16,8},{24,0},{1,25},{9,17},{17,9},{25,1},{2,26},{10... | collective-permute-start | bytes 258056 | tf_op jit(solution)/shard_map/ppermute | solution.py:422
  20.6 5.5 %collective-permute-start.8 = (bf16[2,336,128]{2,1,0:T(8,128)(2,1)S(1)}, bf16[2,336,128]{2,1,0:T(8,128)(2,1)S(1)}, u32[]{:S(2)}, u32[]{:S(2)}) collective-permute-start(bf16[2,336,128]{2,1,0:T(8,128)(2,1)S(1)} %pad_maximum_fusion.8), channel_id=1, source_target_pairs={{0,4},{2,6},{4,0},{6,2},{1,5},{3,7},{5,1},{7,3},{8,12},{10,14},{12... | collective-permute-start | bytes 516104 | tf_op jit(solution)/shard_map/ppermute | solution.py:422
  22.2 5.5 %collective-permute-start.7 = (bf16[2,336,128]{2,1,0:T(8,128)(2,1)S(1)}, bf16[2,336,128]{2,1,0:T(8,128)(2,1)S(1)}, u32[]{:S(2)}, u32[]{:S(2)}) collective-permute-start(bf16[2,336,128]{2,1,0:T(8,128)(2,1)S(1)} %pad_maximum_fusion.7), channel_id=1, source_target_pairs={{0,2},{2,0},{4,6},{6,4},{1,3},{3,1},{5,7},{7,5},{8,10},{10,8},{12,... | collective-permute-start | bytes 516104 | tf_op jit(solution)/shard_map/ppermute | solution.py:422
  23.8 5.0 %collective-permute-start.9 = (bf16[512,128]{1,0:T(8,128)(2,1)S(1)}, bf16[512,128]{1,0:T(8,128)(2,1)S(1)}, u32[]{:S(2)}, u32[]{:S(2)}) collective-permute-start(bf16[512,128]{1,0:T(8,128)(2,1)S(1)} %bitcast.43), channel_id=1, source_target_pairs={{0,8},{8,0},{16,24},{24,16},{1,9},{9,1},{17,25},{25,17},{2,10},{10... | collective-permute-start | bytes 393224 | tf_op jit(solution)/shard_map/ppermute | solution.py:422
  28.7 7.2 %collective-permute-start.12 = (bf16[4,336,128]{2,1,0:T(8,128)(2,1)S(1)}, bf16[4,336,128]{2,1,0:T(8,128)(2,1)S(1)}, u32[]{:S(2)}, u32[]{:S(2)}) collective-permute-start(bf16[4,336,128]{2,1,0:T(8,128)(2,1)S(1)} %pad_maximum_fusion.3), channel_id=1, source_target_pairs={{0,4},{2,6},{4,0},{6,2},{1,5},{3,7},{5,1},{7,3},{8,12},{10,14},{12... | collective-permute-start | bytes 1032200 | tf_op jit(solution)/shard_map/ppermute | solution.py:422
  29.2 7.2 %collective-permute-start.13 = (bf16[4,336,128]{2,1,0:T(8,128)(2,1)S(1)}, bf16[4,336,128]{2,1,0:T(8,128)(2,1)S(1)}, u32[]{:S(2)}, u32[]{:S(2)}) collective-permute-start(bf16[4,336,128]{2,1,0:T(8,128)(2,1)S(1)} %pad_maximum_fusion.4), channel_id=1, source_target_pairs={{0,2},{2,0},{4,6},{6,4},{1,3},{3,1},{5,7},{7,5},{8,10},{10,8},{12,... | collective-permute-start | bytes 1032200 | tf_op jit(solution)/shard_map/ppermute | solution.py:422
  29.8 10.4 %collective-permute-start.10 = (bf16[512,128]{1,0:T(8,128)(2,1)S(1)}, bf16[512,128]{1,0:T(8,128)(2,1)S(1)}, u32[]{:S(2)}, u32[]{:S(2)}) collective-permute-start(bf16[512,128]{1,0:T(8,128)(2,1)S(1)} %bitcast.44), channel_id=1, source_target_pairs={{0,16},{8,24},{16,0},{24,8},{1,17},{9,25},{17,1},{25,9},{2,18},{10... | collective-permute-start | bytes 393224 | tf_op jit(solution)/shard_map/ppermute | solution.py:422
  32.4 7.8 %collective-permute-start.11 = (bf16[512,128]{1,0:T(8,128)(2,1)S(1)}, bf16[512,128]{1,0:T(8,128)(2,1)S(1)}, u32[]{:S(2)}, u32[]{:S(2)}) collective-permute-start(bf16[512,128]{1,0:T(8,128)(2,1)S(1)} %bitcast.45), channel_id=1, source_target_pairs={{0,24},{8,16},{16,8},{24,0},{1,25},{9,17},{17,9},{25,1},{2,26},{10... | collective-permute-start | bytes 393224 | tf_op jit(solution)/shard_map/ppermute | solution.py:422
  40.2 12.3 %collective-permute-start.18 = (bf16[16,336,128]{2,1,0:T(8,128)(2,1)S(1)}, bf16[16,336,128]{2,1,0:T(8,128)(2,1)S(1)}, u32[]{:S(2)}, u32[]{:S(2)}) collective-permute-start(bf16[16,336,128]{2,1,0:T(8,128)(2,1)S(1)} %pad_maximum_fusion.mine), channel_id=1, source_target_pairs={{0,1},{1,0},{2,3},{3,2},{4,5},{5,4},{6,7},{7,6},{8,9},{9,8},{10,11... | collective-permute-start | bytes 4128776 | tf_op jit(solution)/shard_map/ppermute | solution.py:422
  40.3 8.8 %collective-permute-start.16 = (bf16[2,512,128]{2,1,0:T(8,128)(2,1)S(1)}, bf16[2,512,128]{2,1,0:T(8,128)(2,1)S(1)}, u32[]{:S(2)}, u32[]{:S(2)}) collective-permute-start(bf16[2,512,128]{2,1,0:T(8,128)(2,1)S(1)} %pad_maximum_fusion.6), channel_id=1, source_target_pairs={{0,4},{2,6},{4,0},{6,2},{1,5},{3,7},{5,1},{7,3},{8,12},{10,14},{12... | collective-permute-start | bytes 786440 | tf_op jit(solution)/shard_map/ppermute | solution.py:422
  41.9 8.5 %collective-permute-start.14 = (bf16[2,512,128]{2,1,0:T(8,128)(2,1)S(1)}, bf16[2,512,128]{2,1,0:T(8,128)(2,1)S(1)}, u32[]{:S(2)}, u32[]{:S(2)}) collective-permute-start(bf16[2,512,128]{2,1,0:T(8,128)(2,1)S(1)} %pad_maximum_fusion.5), channel_id=1, source_target_pairs={{0,2},{2,0},{4,6},{6,4},{1,3},{3,1},{5,7},{7,5},{8,10},{10,8},{12,... | collective-permute-start | bytes 786440 | tf_op jit(solution)/shard_map/ppermute | solution.py:422
  49.1 13.6 %collective-permute-start.17 = (bf16[4,512,128]{2,1,0:T(8,128)(2,1)S(1)}, bf16[4,512,128]{2,1,0:T(8,128)(2,1)S(1)}, u32[]{:S(2)}, u32[]{:S(2)}) collective-permute-start(bf16[4,512,128]{2,1,0:T(8,128)(2,1)S(1)} %pad_maximum_fusion.2.rest_8_), channel_id=1, source_target_pairs={{0,2},{2,0},{4,6},{6,4},{1,3},{3,1},{5,7},{7,5},{8,10},{10,8},{12,... | collective-permute-start | bytes 1572872 | tf_op jit(solution)/shard_map/ppermute | solution.py:422
  50.4 13.3 %collective-permute-start.15 = (bf16[4,512,128]{2,1,0:T(8,128)(2,1)S(1)}, bf16[4,512,128]{2,1,0:T(8,128)(2,1)S(1)}, u32[]{:S(2)}, u32[]{:S(2)}) collective-permute-start(bf16[4,512,128]{2,1,0:T(8,128)(2,1)S(1)} %pad_maximum_fusion.1.rest_7_), channel_id=1, source_target_pairs={{0,4},{2,6},{4,0},{6,2},{1,5},{3,7},{5,1},{7,3},{8,12},{10,14},{12... | collective-permute-start | bytes 1572872 | tf_op jit(solution)/shard_map/ppermute | solution.py:422
  52.0 12.3 %collective-permute-start.20 = (bf16[4,512,128]{2,1,0:T(8,128)(2,1)S(1)}, bf16[4,512,128]{2,1,0:T(8,128)(2,1)S(1)}, u32[]{:S(2)}, u32[]{:S(2)}) collective-permute-start(bf16[4,512,128]{2,1,0:T(8,128)(2,1)S(1)} %pad_maximum_fusion.2.rest_8_), channel_id=1, source_target_pairs={{0,1},{1,0},{2,3},{3,2},{4,5},{5,4},{6,7},{7,6},{8,9},{9,8},{10,11... | collective-permute-start | bytes 1572872 | tf_op jit(solution)/shard_map/ppermute | solution.py:422
  52.0 12.3 %collective-permute-start.19 = (bf16[4,512,128]{2,1,0:T(8,128)(2,1)S(1)}, bf16[4,512,128]{2,1,0:T(8,128)(2,1)S(1)}, u32[]{:S(2)}, u32[]{:S(2)}) collective-permute-start(bf16[4,512,128]{2,1,0:T(8,128)(2,1)S(1)} %pad_maximum_fusion.1.rest_7_), channel_id=1, source_target_pairs={{0,1},{1,0},{2,3},{3,2},{4,5},{5,4},{6,7},{7,6},{8,9},{9,8},{10,11... | collective-permute-start | bytes 1572872 | tf_op jit(solution)/shard_map/ppermute | solution.py:422
  63.8 1.9 %collective-permute-start.21 = (bf16[4,512,128]{2,1,0:T(8,128)(2,1)S(1)}, bf16[4,512,128]{2,1,0:T(8,128)(2,1)S(1)}, u32[]{:S(2)}, u32[]{:S(2)}) collective-permute-start(bf16[4,512,128]{2,1,0:T(8,128)(2,1)S(1)} %collective-permute-done.15.rest_9_), channel_id=1, source_target_pairs={{0,1},{1,0},{2,3},{3,2},{4,5},{5,4},{6,7},{7,6},{8,9},{9,8},{10,11... | collective-permute-start | bytes 1572872 | tf_op jit(solution)/shard_map/ppermute | solution.py:422
  63.8 2.7 %collective-permute-start.22 = (bf16[4,512,128]{2,1,0:T(8,128)(2,1)S(1)}, bf16[4,512,128]{2,1,0:T(8,128)(2,1)S(1)}, u32[]{:S(2)}, u32[]{:S(2)}) collective-permute-start(bf16[4,512,128]{2,1,0:T(8,128)(2,1)S(1)} %collective-permute-done.17.rest_10_), channel_id=1, source_target_pairs={{0,1},{1,0},{2,3},{3,2},{4,5},{5,4},{6,7},{7,6},{8,9},{9,8},{10,11... | collective-permute-start | bytes 1572872 | tf_op jit(solution)/shard_map/ppermute | solution.py:422

commit v15 on v14

--- a/solution.py
+++ b/solution.py
@@ -379,13 +379,17 @@
 
 
 def prepare(count, *rest):
-    sources, out, sems, first, second, both = rest[:5], *rest[5:10]
-    for copy in copy_in(list(zip(sources, rest[10:])), sems):
+    sources, out, sems, spread, first, second, both = rest[:6], *rest[6:12]
+    sources = (sources[0].at[pl.ds(0, 16)], *sources[1:])
+    for copy in copy_in(list(zip(sources, rest[12:])), sems):
         copy.wait()
-    rows, cols, vectors, row_mass, col_mass = rest[10:]
+    tile, rows, cols, vectors, row_mass, col_mass = rest[12:]
     f32, bf16 = jnp.float32, jnp.bfloat16
     half = first.shape[0]
+    vec_at = OFF_CAP * half
+    slots = tile[...].astype(f32)[:OFF_CAP]
     for i in range(half):
+        spread[pl.ds(i, OFF_CAP, stride=half), :] = slots[:, i * 128 : (i + 1) * 128]
         first[i : i + 1, :] = vectors[0:1, i * 128 : (i + 1) * 128]
         second[i : i + 1, :] = vectors[1:2, i * 128 : (i + 1) * 128]
     x, z = first[...], second[...]
@@ -393,7 +397,8 @@
     both[pl.ds(0, half, stride=2), :] = jnp.where(left, x, pltpu.roll(z, 64, 1))
     both[pl.ds(1, half, stride=2), :] = jnp.where(left, pltpu.roll(x, 64, 1), z)
     inv = 1.0 / jnp.sqrt(jnp.concatenate([col_mass[0:1, :], col_mass[1:2, :]], axis=1))
-    out[: 2 * half, :] = (both[...] * inv).astype(bf16)
+    out[:vec_at, :] = spread[...].astype(bf16)
+    out[vec_at : vec_at + 2 * half, :] = (both[...] * inv).astype(bf16)
 
     sub = lax.broadcasted_iota(jnp.int32, (META, 128), 0)
 
@@ -414,7 +419,7 @@
     short = jnp.where(lane == 2 * OFF_CAP, count[0, 0].astype(f32), 0.0)
     short = jnp.where(lane < OFF_CAP, r, jnp.where(lane < 2 * OFF_CAP, moved, short))
     packed = masses + stacked(3, split3(inv) + [r, c, short[0:1]])
-    out[2 * half :, :] = packed.astype(bf16)
+    out[vec_at + 2 * half :, :] = packed.astype(bf16)
 
 
 def swap(x, axis, distance):
@@ -466,20 +471,19 @@
     bf16 = jnp.bfloat16
     row, chip, core = (lax.axis_index(name) for name in ("row", "chip", "core"))
 
-    off = tile[:OFF_CAP].reshape(OFF_CAP * half, 128)
-    sources = (block_row[0], block_col[0], vectors, row_mass, col_mass)
-    laid_out = pl.pallas_call(
+    sources = (tile, block_row[0], block_col[0], vectors, row_mass, col_mass)
+    small = pl.pallas_call(
         prepare,
-        out_shape=jax.ShapeDtypeStruct((k + META, own * bsize), bf16),
+        out_shape=jax.ShapeDtypeStruct((OFF_CAP * half + k + META, own * bsize), bf16),
         in_specs=[pl.BlockSpec(memory_space=pltpu.SMEM)]
         + [pl.BlockSpec(memory_space=pltpu.HBM)] * len(sources),
         out_specs=pl.BlockSpec(memory_space=pltpu.VMEM),
         scratch_shapes=[pltpu.SemaphoreType.DMA((len(sources),))]
-        + [pltpu.VMEM((rows, own * bsize), jnp.float32) for rows in (half, half, k)]
-        + [pltpu.VMEM(v.shape, v.dtype) for v in sources],
+        + [pltpu.VMEM((rows, own * bsize), jnp.float32) for rows in (OFF_CAP * half, half, half, k)]
+        + [pltpu.VMEM((16, bsize * bsize), bf16)]
+        + [pltpu.VMEM(v.shape, v.dtype) for v in sources[1:]],
         name="prepare",
     )(counts, *(pltpu.with_memory_space_constraint(v, pltpu.HBM) for v in sources))
-    small = jnp.concatenate([off, laid_out], axis=0)
 
     home = full_part(tile, has_full, n_col // 2, part, chip, core)
     home = home.reshape(part, half, 128).transpose(1, 0, 2).reshape(half * part, 128)

time: 128 us -> 126 us (0.984)
  Pallas kernels: 71 us -> 68 us
  waiting for transfers between devices: 24.9 us -> 27.9 us
  starting transfers between devices: 27.6 us -> 26.2 us
    ppermute x23, waiting for transfers between devices: 24.9 us -> 27.9 us  [swap(): return lax.ppermute(x, axis, [(i, i ^ distance) for i in range(size)])]
    pallas_call x1, Pallas kernels: 60.7 us -> 58 us  [whole_on_each(): pl.pallas_call(functools.partial(iterate, n_row, n_col, n_cap, float(n_de...]
    ppermute x23, starting transfers between devices: 27.6 us -> 26.2 us  [swap(): return lax.ppermute(x, axis, [(i, i ^ distance) for i in range(size)])]
  transfers between devices with their start and end apart: 23 -> 23, of which waited for: 13 -> 14; matrix products, arithmetic and copies ran while one was open for 1% -> 0% of each run, Pallas kernels for 8% -> 8%
where the time goes in v15:
time: 126 us; the launch traced here: 125 us
  Pallas kernels  68 us (54%)
  waiting for transfers between devices  27.9 us (22%)
  starting transfers between devices  26.2 us (21%)
  other arithmetic  1.68 us (1%)
    pallas_call x1, Pallas kernels, whole_on_each(): pl.pallas_call(functools.partial(iterate, n_row, n_col, n_cap, float(n_de...  58 us
    ppermute x23, waiting for transfers between devices, swap(): return lax.ppermute(x, axis, [(i, i ^ distance) for i in range(size)])  27.9 us
    ppermute x23, starting transfers between devices, swap(): return lax.ppermute(x, axis, [(i, i ^ distance) for i in range(size)])  26.2 us
    pallas_call x1, Pallas kernels, whole_on_each(): pl.pallas_call(functools.partial(unpack, n_row, n_col), out_shape=[jax.Sh...  8.27 us
  transfers between devices with their start and end apart: 23, of which 14 were waited for; matrix products, arithmetic and copies ran while one was open for 0% of the time, Pallas kernels for 8%

profile of v15, /device:TPU:0, one launch (start us, length us, event | category | flops | bytes accessed | tf_op | source)
XLA Modules:
  0.0 125.0 jit_solution(3906678662239179562)
XLA Ops:
  0.7 1.1 select_bitcast_fusion
  1.8 0.5 collective-permute-start
  2.3 1.5 %collective-permute-done = bf16[4,16,4096]{2,1,0:T(8,128)(2,1)S(1)} collective-permute-done((bf16[4,16,4096]{2,1,0:T(8,128)(2,1)S(1)}, bf16[4,16,4096]{2,1,0:T(8,128)(2,1)S(1)}, u32[]{:S(2)}, u32[]{:S(2)}) %collective-permute-start) | collective-permute-done | bytes 524320 | tf_op jit(solution)/shard_map/ppermute | solution.py:427
  3.9 0.1 bitcast_add_fusion
  4.0 2.9 %collective-permute-start.1 = (bf16[16,4096]{1,0:T(8,128)(2,1)S(1)}, bf16[16,4096]{1,0:T(8,128)(2,1)S(1)}, u32[]{:S(2)}, u32[]{:S(2)}) collective-permute-start(bf16[16,4096]{1,0:T(8,128)(2,1)S(1)} %get-tuple-element.57), channel_id=1, source_target_pairs={{0,2},{2,0},{4,6},{6,4},{1,3},{3,1},{5,7},{7,5},{8,10},{10,8},{12,... | collective-permute-start | bytes 393224 | tf_op jit(solution)/shard_map/ppermute | solution.py:427
  6.9 1.5 %collective-permute-start.2 = (bf16[16,4096]{1,0:T(8,128)(2,1)S(1)}, bf16[16,4096]{1,0:T(8,128)(2,1)S(1)}, u32[]{:S(2)}, u32[]{:S(2)}) collective-permute-start(bf16[16,4096]{1,0:T(8,128)(2,1)S(1)} %get-tuple-element.59), channel_id=1, source_target_pairs={{0,4},{2,6},{4,0},{6,2},{1,5},{3,7},{5,1},{7,3},{8,12},{10,14},{12... | collective-permute-start | bytes 393224 | tf_op jit(solution)/shard_map/ppermute | solution.py:427
  8.4 0.0 collective-permute-start.3
  8.5 1.8 %prepare.1 = bf16[336,128]{1,0:T(8,128)(2,1)} custom-call(s32[1,1]{1,0:T(1,128)S(6)} %copy.10.count, bf16[128,4096]{1,0:T(8,128)(2,1)} %bitcast.41, s32[1,128]{1,0:T(1,128)} %bitcast.63, s32[1,128]{1,0:T(1,128)} %bitcast.64, f32[2,4096]{1,0:T(2,128)} %rest_3_.1, f32[2,64]{1,0:T(2,128)} %rest_4_.1, f32[2,64]{1,0:T(2,128)} %rest_5_.1), custom_call_target="tpu_custom_call" | custom-call | tf_op jit(solution)/shard_map/prepare/pallas_call | solution.py:475
  10.3 2.1 %collective-permute-start.4 = (bf16[336,128]{1,0:T(8,128)(2,1)}, bf16[336,128]{1,0:T(8,128)(2,1)S(1)}, u32[]{:S(2)}, u32[]{:S(2)}) collective-permute-start(bf16[336,128]{1,0:T(8,128)(2,1)} %prepare.1), channel_id=1, source_target_pairs={{0,8},{8,0},{16,24},{24,16},{1,9},{9,1},{17,25},{25,17},{2,10},{10... | collective-permute-start | bytes 258056 | tf_op jit(solution)/shard_map/ppermute | solution.py:427
  12.4 2.6 %collective-permute-start.5 = (bf16[336,128]{1,0:T(8,128)(2,1)}, bf16[336,128]{1,0:T(8,128)(2,1)S(1)}, u32[]{:S(2)}, u32[]{:S(2)}) collective-permute-start(bf16[336,128]{1,0:T(8,128)(2,1)} %prepare.1), channel_id=1, source_target_pairs={{0,16},{8,24},{16,0},{24,8},{1,17},{9,25},{17,1},{25,9},{2,18},{10... | collective-permute-start | bytes 258056 | tf_op jit(solution)/shard_map/ppermute | solution.py:427
  15.0 0.1 pad_add_fusion.own
  15.0 0.0 collective-permute-done.1
  15.0 0.0 collective-permute-start.6
  15.1 0.0 collective-permute-done.2
  15.1 0.1 copy.8
  15.2 5.4 %collective-permute-done.5 = bf16[336,128]{1,0:T(8,128)(2,1)S(1)} collective-permute-done((bf16[336,128]{1,0:T(8,128)(2,1)}, bf16[336,128]{1,0:T(8,128)(2,1)S(1)}, u32[]{:S(2)}, u32[]{:S(2)}) %collective-permute-start.5) | collective-permute-done | bytes 86048 | tf_op jit(solution)/shard_map/ppermute | solution.py:427
  20.6 1.0 collective-permute-done.6
  21.7 1.6 %collective-permute-start.8 = (bf16[2,336,128]{2,1,0:T(8,128)(2,1)S(1)}, bf16[2,336,128]{2,1,0:T(8,128)(2,1)S(1)}, u32[]{:S(2)}, u32[]{:S(2)}) collective-permute-start(bf16[2,336,128]{2,1,0:T(8,128)(2,1)S(1)} %pad_maximum_fusion.8), channel_id=1, source_target_pairs={{0,4},{2,6},{4,0},{6,2},{1,5},{3,7},{5,1},{7,3},{8,12},{10,14},{12... | collective-permute-start | bytes 516104 | tf_op jit(solution)/shard_map/ppermute | solution.py:427
  23.3 1.6 %collective-permute-start.7 = (bf16[2,336,128]{2,1,0:T(8,128)(2,1)S(1)}, bf16[2,336,128]{2,1,0:T(8,128)(2,1)S(1)}, u32[]{:S(2)}, u32[]{:S(2)}) collective-permute-start(bf16[2,336,128]{2,1,0:T(8,128)(2,1)S(1)} %pad_maximum_fusion.7), channel_id=1, source_target_pairs={{0,2},{2,0},{4,6},{6,4},{1,3},{3,1},{5,7},{7,5},{8,10},{10,8},{12,... | collective-permute-start | bytes 516104 | tf_op jit(solution)/shard_map/ppermute | solution.py:427
  24.8 1.4 %collective-permute-start.9 = (bf16[512,128]{1,0:T(8,128)(2,1)S(1)}, bf16[512,128]{1,0:T(8,128)(2,1)S(1)}, u32[]{:S(2)}, u32[]{:S(2)}) collective-permute-start(bf16[512,128]{1,0:T(8,128)(2,1)S(1)} %bitcast.43), channel_id=1, source_target_pairs={{0,8},{8,0},{16,24},{24,16},{1,9},{9,1},{17,25},{25,17},{2,10},{10... | collective-permute-start | bytes 393224 | tf_op jit(solution)/shard_map/ppermute | solution.py:427
  26.2 0.9 collective-permute-done.8
  27.2 1.6 %collective-permute-done.7 = bf16[2,336,128]{2,1,0:T(8,128)(2,1)S(1)} collective-permute-done((bf16[2,336,128]{2,1,0:T(8,128)(2,1)S(1)}, bf16[2,336,128]{2,1,0:T(8,128)(2,1)S(1)}, u32[]{:S(2)}, u32[]{:S(2)}) %collective-permute-start.7) | collective-permute-done | bytes 172064 | tf_op jit(solution)/shard_map/ppermute | solution.py:427
  28.8 1.0 collective-permute-done.9
  29.8 0.5 collective-permute-start.12
  30.3 0.6 collective-permute-start.13
  30.9 2.3 %collective-permute-start.10 = (bf16[512,128]{1,0:T(8,128)(2,1)S(1)}, bf16[512,128]{1,0:T(8,128)(2,1)S(1)}, u32[]{:S(2)}, u32[]{:S(2)}) collective-permute-start(bf16[512,128]{1,0:T(8,128)(2,1)S(1)} %bitcast.44), channel_id=1, source_target_pairs={{0,16},{8,24},{16,0},{24,8},{1,17},{9,25},{17,1},{25,9},{2,18},{10... | collective-permute-start | bytes 393224 | tf_op jit(solution)/shard_map/ppermute | solution.py:427
  33.3 1.4 %collective-permute-start.11 = (bf16[512,128]{1,0:T(8,128)(2,1)S(1)}, bf16[512,128]{1,0:T(8,128)(2,1)S(1)}, u32[]{:S(2)}, u32[]{:S(2)}) collective-permute-start(bf16[512,128]{1,0:T(8,128)(2,1)S(1)} %bitcast.45), channel_id=1, source_target_pairs={{0,24},{8,16},{16,8},{24,0},{1,25},{9,17},{17,9},{25,1},{2,26},{10... | collective-permute-start | bytes 393224 | tf_op jit(solution)/shard_map/ppermute | solution.py:427
  34.6 2.4 %collective-permute-done.12 = bf16[4,336,128]{2,1,0:T(8,128)(2,1)S(1)} collective-permute-done((bf16[4,336,128]{2,1,0:T(8,128)(2,1)S(1)}, bf16[4,336,128]{2,1,0:T(8,128)(2,1)S(1)}, u32[]{:S(2)}, u32[]{:S(2)}) %collective-permute-start.12) | collective-permute-done | bytes 344096 | tf_op jit(solution)/shard_map/ppermute | solution.py:427
  37.0 0.5 collective-permute-done.13
  37.6 0.2 pad_maximum_fusion.mine
  37.7 2.8 %collective-permute-done.10 = bf16[512,128]{1,0:T(8,128)(2,1)S(1)} collective-permute-done((bf16[512,128]{1,0:T(8,128)(2,1)S(1)}, bf16[512,128]{1,0:T(8,128)(2,1)S(1)}, u32[]{:S(2)}, u32[]{:S(2)}) %collective-permute-start.10) | collective-permute-done | bytes 131104 | tf_op jit(solution)/shard_map/ppermute | solution.py:427
  40.5 0.0 collective-permute-done.11
  40.6 1.7 %collective-permute-start.16 = (bf16[2,512,128]{2,1,0:T(8,128)(2,1)S(1)}, bf16[2,512,128]{2,1,0:T(8,128)(2,1)S(1)}, u32[]{:S(2)}, u32[]{:S(2)}) collective-permute-start(bf16[2,512,128]{2,1,0:T(8,128)(2,1)S(1)} %pad_maximum_fusion.6), channel_id=1, source_target_pairs={{0,4},{2,6},{4,0},{6,2},{1,5},{3,7},{5,1},{7,3},{8,12},{10,14},{12... | collective-permute-start | bytes 786440 | tf_op jit(solution)/shard_map/ppermute | solution.py:427
  42.3 1.4 %collective-permute-start.14 = (bf16[2,512,128]{2,1,0:T(8,128)(2,1)S(1)}, bf16[2,512,128]{2,1,0:T(8,128)(2,1)S(1)}, u32[]{:S(2)}, u32[]{:S(2)}) collective-permute-start(bf16[2,512,128]{2,1,0:T(8,128)(2,1)S(1)} %pad_maximum_fusion.5), channel_id=1, source_target_pairs={{0,2},{2,0},{4,6},{6,4},{1,3},{3,1},{5,7},{7,5},{8,10},{10,8},{12,... | collective-permute-start | bytes 786440 | tf_op jit(solution)/shard_map/ppermute | solution.py:427
  43.7 5.7 %collective-permute-done.16 = bf16[2,512,128]{2,1,0:T(8,128)(2,1)S(1)} collective-permute-done((bf16[2,512,128]{2,1,0:T(8,128)(2,1)S(1)}, bf16[2,512,128]{2,1,0:T(8,128)(2,1)S(1)}, u32[]{:S(2)}, u32[]{:S(2)}) %collective-permute-start.16) | collective-permute-done | bytes 262176 | tf_op jit(solution)/shard_map/ppermute | solution.py:427
  49.3 0.1 pad_maximum_fusion.2.rest_8_
  49.4 1.4 %collective-permute-start.17 = (bf16[4,512,128]{2,1,0:T(8,128)(2,1)S(1)}, bf16[4,512,128]{2,1,0:T(8,128)(2,1)S(1)}, u32[]{:S(2)}, u32[]{:S(2)}) collective-permute-start(bf16[4,512,128]{2,1,0:T(8,128)(2,1)S(1)} %pad_maximum_fusion.2.rest_8_), channel_id=1, source_target_pairs={{0,2},{2,0},{4,6},{6,4},{1,3},{3,1},{5,7},{7,5},{8,10},{10,8},{12,... | collective-permute-start | bytes 1572872 | tf_op jit(solution)/shard_map/ppermute | solution.py:427
  50.8 0.0 collective-permute-done.14
  50.8 0.1 pad_maximum_fusion.1.rest_7_
  50.9 1.7 %collective-permute-start.15 = (bf16[4,512,128]{2,1,0:T(8,128)(2,1)S(1)}, bf16[4,512,128]{2,1,0:T(8,128)(2,1)S(1)}, u32[]{:S(2)}, u32[]{:S(2)}) collective-permute-start(bf16[4,512,128]{2,1,0:T(8,128)(2,1)S(1)} %pad_maximum_fusion.1.rest_7_), channel_id=1, source_target_pairs={{0,4},{2,6},{4,0},{6,2},{1,5},{3,7},{5,1},{7,3},{8,12},{10,14},{12... | collective-permute-start | bytes 1572872 | tf_op jit(solution)/shard_map/ppermute | solution.py:427
  52.6 0.5 collective-permute-start.19
  53.1 8.3 %unpack.1 = (s32[584]{0:T(1024)S(1)}, f32[8,128]{1,0:T(8,128)S(1)}, bf16[144,128,128]{2,1,0:T(8,128)(2,1)S(1)}, f32[32,8,128]{2,1,0:T(8,128)S(1)}, f32[32,8,128]...) custom-call(s32[3]{0:T(128)S(1)} %pad_add_fusion.own, ...), custom_call_target="tpu_custom_call" | custom-call | bytes 11010048 | tf_op jit(solution)/shard_map/unpack/pallas_call | solution.py:511
  61.3 1.7 %collective-permute-done.17.rest_10_ = bf16[4,512,128]{2,1,0:T(8,128)(2,1)S(1)} collective-permute-done((bf16[4,512,128]{2,1,0:T(8,128)(2,1)S(1)}, bf16[4,512,128]{2,1,0:T(8,128)(2,1)S(1)}, u32[]{:S(2)}, u32[]{:S(2)}) %collective-permute-start.17) | collective-permute-done | bytes 524320 | tf_op jit(solution)/shard_map/ppermute | solution.py:427
  63.0 1.2 collective-permute-done.15.rest_9_
  64.2 0.5 collective-permute-start.22
  64.7 1.4 %collective-permute-done.21.rest_13_ = bf16[4,512,128]{2,1,0:T(8,128)(2,1)S(1)} collective-permute-done((bf16[4,512,128]{2,1,0:T(8,128)(2,1)S(1)}, bf16[4,512,128]{2,1,0:T(8,128)(2,1)S(1)}, u32[]{:S(2)}, u32[]{:S(2)}) %collective-permute-start.21) | collective-permute-done | bytes 524320 | tf_op jit(solution)/shard_map/ppermute | solution.py:427
  66.1 0.7 collective-permute-done.22.rest_14_
  66.9 58.0 %iterate.1 = f32[2,4096]{1,0:T(2,128)} custom-call(s32[3]{0:T(128)S(1)} %pad_add_fusion.own, s32[584]{0:T(1024)S(1)} %get-tuple-element.46.lists, f32[8,128]{1,0:T(8,128)S(1)} %get-tuple-element.47.place, bf16[144,128,128]{2,1,0:T(8,128)(2,1)S(1)} %get-tuple-element.48.rest_0_, f32[32,8,128]{2,1,0:T(8,128)S(1)} %get-tuple-element.49.rest_1_, ...), custom_call_target="tpu_custom_call" | custom-call | tf_op jit(solution)/shard_map/iterate/pallas_call | solution.py:532
  (21 shorter events, 0.3 us)
Async XLA Ops:
  0.0 3.9 %copy-start = (bf16[1,1,128,4096]{3,2,1,0:T(8,128)(2,1)S(1)}, bf16[1,1,128,4096]{3,2,1,0:T(8,128)(2,1)}, u32[]{:S(2)}) copy-start(bf16[1,1,128,4096]{3,2,1,0:T(8,128)(2,1)} %param.7) | copy-start | bytes 3145732
  1.8 2.1 %collective-permute-start = (bf16[4,16,4096]{2,1,0:T(8,128)(2,1)S(1)}, bf16[4,16,4096]{2,1,0:T(8,128)(2,1)S(1)}, u32[]{:S(2)}, u32[]{:S(2)}) collective-permute-start(bf16[4,16,4096]{2,1,0:T(8,128)(2,1)S(1)} %select_bitcast_fusion), channel_id=1, source_target_pairs={{0,1},{1,0},{2,3},{3,2},{4,5},{5,4},{6,7},{7,6},{8,9},{9,8},{10,11... | collective-permute-start | bytes 1572872 | tf_op jit(solution)/shard_map/ppermute | solution.py:427
  4.0 11.0 %collective-permute-start.1 = (bf16[16,4096]{1,0:T(8,128)(2,1)S(1)}, bf16[16,4096]{1,0:T(8,128)(2,1)S(1)}, u32[]{:S(2)}, u32[]{:S(2)}) collective-permute-start(bf16[16,4096]{1,0:T(8,128)(2,1)S(1)} %get-tuple-element.57), channel_id=1, source_target_pairs={{0,2},{2,0},{4,6},{6,4},{1,3},{3,1},{5,7},{7,5},{8,10},{10,8},{12,... | collective-permute-start | bytes 393224 | tf_op jit(solution)/shard_map/ppermute | solution.py:427
  6.9 8.1 %collective-permute-start.2 = (bf16[16,4096]{1,0:T(8,128)(2,1)S(1)}, bf16[16,4096]{1,0:T(8,128)(2,1)S(1)}, u32[]{:S(2)}, u32[]{:S(2)}) collective-permute-start(bf16[16,4096]{1,0:T(8,128)(2,1)S(1)} %get-tuple-element.59), channel_id=1, source_target_pairs={{0,4},{2,6},{4,0},{6,2},{1,5},{3,7},{5,1},{7,3},{8,12},{10,14},{12... | collective-permute-start | bytes 393224 | tf_op jit(solution)/shard_map/ppermute | solution.py:427
  8.4 6.6 %collective-permute-start.3 = (bf16[16,4096]{1,0:T(8,128)(2,1)S(1)}, bf16[16,4096]{1,0:T(8,128)(2,1)S(1)}, u32[]{:S(2)}, u32[]{:S(2)}) collective-permute-start(bf16[16,4096]{1,0:T(8,128)(2,1)S(1)} %get-tuple-element.58), channel_id=1, source_target_pairs={{0,6},{2,4},{4,2},{6,0},{1,7},{3,5},{5,3},{7,1},{8,14},{10,12},{12... | collective-permute-start | bytes 393224 | tf_op jit(solution)/shard_map/ppermute | solution.py:427
  10.3 13.0 %copy-start.1 = (bf16[336,128]{1,0:T(8,128)(2,1)S(1)}, bf16[336,128]{1,0:T(8,128)(2,1)}, u32[]{:S(2)}) copy-start(bf16[336,128]{1,0:T(8,128)(2,1)} %prepare.1) | copy-start | bytes 258052
  10.3 4.9 %collective-permute-start.4 = (bf16[336,128]{1,0:T(8,128)(2,1)}, bf16[336,128]{1,0:T(8,128)(2,1)S(1)}, u32[]{:S(2)}, u32[]{:S(2)}) collective-permute-start(bf16[336,128]{1,0:T(8,128)(2,1)} %prepare.1), channel_id=1, source_target_pairs={{0,8},{8,0},{16,24},{24,16},{1,9},{9,1},{17,25},{25,17},{2,10},{10... | collective-permute-start | bytes 258056 | tf_op jit(solution)/shard_map/ppermute | solution.py:427
  12.4 8.3 %collective-permute-start.5 = (bf16[336,128]{1,0:T(8,128)(2,1)}, bf16[336,128]{1,0:T(8,128)(2,1)S(1)}, u32[]{:S(2)}, u32[]{:S(2)}) collective-permute-start(bf16[336,128]{1,0:T(8,128)(2,1)} %prepare.1), channel_id=1, source_target_pairs={{0,16},{8,24},{16,0},{24,8},{1,17},{9,25},{17,1},{25,9},{2,18},{10... | collective-permute-start | bytes 258056 | tf_op jit(solution)/shard_map/ppermute | solution.py:427
  15.0 6.6 %collective-permute-start.6 = (bf16[336,128]{1,0:T(8,128)(2,1)}, bf16[336,128]{1,0:T(8,128)(2,1)S(1)}, u32[]{:S(2)}, u32[]{:S(2)}) collective-permute-start(bf16[336,128]{1,0:T(8,128)(2,1)} %prepare.1), channel_id=1, source_target_pairs={{0,24},{8,16},{16,8},{24,0},{1,25},{9,17},{17,9},{25,1},{2,26},{10... | collective-permute-start | bytes 258056 | tf_op jit(solution)/shard_map/ppermute | solution.py:427
  21.7 5.5 %collective-permute-start.8 = (bf16[2,336,128]{2,1,0:T(8,128)(2,1)S(1)}, bf16[2,336,128]{2,1,0:T(8,128)(2,1)S(1)}, u32[]{:S(2)}, u32[]{:S(2)}) collective-permute-start(bf16[2,336,128]{2,1,0:T(8,128)(2,1)S(1)} %pad_maximum_fusion.8), channel_id=1, source_target_pairs={{0,4},{2,6},{4,0},{6,2},{1,5},{3,7},{5,1},{7,3},{8,12},{10,14},{12... | collective-permute-start | bytes 516104 | tf_op jit(solution)/shard_map/ppermute | solution.py:427
  23.3 5.5 %collective-permute-start.7 = (bf16[2,336,128]{2,1,0:T(8,128)(2,1)S(1)}, bf16[2,336,128]{2,1,0:T(8,128)(2,1)S(1)}, u32[]{:S(2)}, u32[]{:S(2)}) collective-permute-start(bf16[2,336,128]{2,1,0:T(8,128)(2,1)S(1)} %pad_maximum_fusion.7), channel_id=1, source_target_pairs={{0,2},{2,0},{4,6},{6,4},{1,3},{3,1},{5,7},{7,5},{8,10},{10,8},{12,... | collective-permute-start | bytes 516104 | tf_op jit(solution)/shard_map/ppermute | solution.py:427
  24.8 5.0 %collective-permute-start.9 = (bf16[512,128]{1,0:T(8,128)(2,1)S(1)}, bf16[512,128]{1,0:T(8,128)(2,1)S(1)}, u32[]{:S(2)}, u32[]{:S(2)}) collective-permute-start(bf16[512,128]{1,0:T(8,128)(2,1)S(1)} %bitcast.43), channel_id=1, source_target_pairs={{0,8},{8,0},{16,24},{24,16},{1,9},{9,1},{17,25},{25,17},{2,10},{10... | collective-permute-start | bytes 393224 | tf_op jit(solution)/shard_map/ppermute | solution.py:427
  29.8 7.2 %collective-permute-start.12 = (bf16[4,336,128]{2,1,0:T(8,128)(2,1)S(1)}, bf16[4,336,128]{2,1,0:T(8,128)(2,1)S(1)}, u32[]{:S(2)}, u32[]{:S(2)}) collective-permute-start(bf16[4,336,128]{2,1,0:T(8,128)(2,1)S(1)} %pad_maximum_fusion.3), channel_id=1, source_target_pairs={{0,4},{2,6},{4,0},{6,2},{1,5},{3,7},{5,1},{7,3},{8,12},{10,14},{12... | collective-permute-start | bytes 1032200 | tf_op jit(solution)/shard_map/ppermute | solution.py:427
  30.3 7.2 %collective-permute-start.13 = (bf16[4,336,128]{2,1,0:T(8,128)(2,1)S(1)}, bf16[4,336,128]{2,1,0:T(8,128)(2,1)S(1)}, u32[]{:S(2)}, u32[]{:S(2)}) collective-permute-start(bf16[4,336,128]{2,1,0:T(8,128)(2,1)S(1)} %pad_maximum_fusion.4), channel_id=1, source_target_pairs={{0,2},{2,0},{4,6},{6,4},{1,3},{3,1},{5,7},{7,5},{8,10},{10,8},{12,... | collective-permute-start | bytes 1032200 | tf_op jit(solution)/shard_map/ppermute | solution.py:427
  30.9 9.6 %collective-permute-start.10 = (bf16[512,128]{1,0:T(8,128)(2,1)S(1)}, bf16[512,128]{1,0:T(8,128)(2,1)S(1)}, u32[]{:S(2)}, u32[]{:S(2)}) collective-permute-start(bf16[512,128]{1,0:T(8,128)(2,1)S(1)} %bitcast.44), channel_id=1, source_target_pairs={{0,16},{8,24},{16,0},{24,8},{1,17},{9,25},{17,1},{25,9},{2,18},{10... | collective-permute-start | bytes 393224 | tf_op jit(solution)/shard_map/ppermute | solution.py:427
  33.3 7.3 %collective-permute-start.11 = (bf16[512,128]{1,0:T(8,128)(2,1)S(1)}, bf16[512,128]{1,0:T(8,128)(2,1)S(1)}, u32[]{:S(2)}, u32[]{:S(2)}) collective-permute-start(bf16[512,128]{1,0:T(8,128)(2,1)S(1)} %bitcast.45), channel_id=1, source_target_pairs={{0,24},{8,16},{16,8},{24,0},{1,25},{9,17},{17,9},{25,1},{2,26},{10... | collective-permute-start | bytes 393224 | tf_op jit(solution)/shard_map/ppermute | solution.py:427
  40.5 12.5 %collective-permute-start.18 = (bf16[16,336,128]{2,1,0:T(8,128)(2,1)S(1)}, bf16[16,336,128]{2,1,0:T(8,128)(2,1)S(1)}, u32[]{:S(2)}, u32[]{:S(2)}) collective-permute-start(bf16[16,336,128]{2,1,0:T(8,128)(2,1)S(1)} %pad_maximum_fusion.mine), channel_id=1, source_target_pairs={{0,1},{1,0},{2,3},{3,2},{4,5},{5,4},{6,7},{7,6},{8,9},{9,8},{10,11... | collective-permute-start | bytes 4128776 | tf_op jit(solution)/shard_map/ppermute | solution.py:427
  40.6 8.8 %collective-permute-start.16 = (bf16[2,512,128]{2,1,0:T(8,128)(2,1)S(1)}, bf16[2,512,128]{2,1,0:T(8,128)(2,1)S(1)}, u32[]{:S(2)}, u32[]{:S(2)}) collective-permute-start(bf16[2,512,128]{2,1,0:T(8,128)(2,1)S(1)} %pad_maximum_fusion.6), channel_id=1, source_target_pairs={{0,4},{2,6},{4,0},{6,2},{1,5},{3,7},{5,1},{7,3},{8,12},{10,14},{12... | collective-permute-start | bytes 786440 | tf_op jit(solution)/shard_map/ppermute | solution.py:427
  42.3 8.5 %collective-permute-start.14 = (bf16[2,512,128]{2,1,0:T(8,128)(2,1)S(1)}, bf16[2,512,128]{2,1,0:T(8,128)(2,1)S(1)}, u32[]{:S(2)}, u32[]{:S(2)}) collective-permute-start(bf16[2,512,128]{2,1,0:T(8,128)(2,1)S(1)} %pad_maximum_fusion.5), channel_id=1, source_target_pairs={{0,2},{2,0},{4,6},{6,4},{1,3},{3,1},{5,7},{7,5},{8,10},{10,8},{12,... | collective-permute-start | bytes 786440 | tf_op jit(solution)/shard_map/ppermute | solution.py:427
  49.4 13.6 %collective-permute-start.17 = (bf16[4,512,128]{2,1,0:T(8,128)(2,1)S(1)}, bf16[4,512,128]{2,1,0:T(8,128)(2,1)S(1)}, u32[]{:S(2)}, u32[]{:S(2)}) collective-permute-start(bf16[4,512,128]{2,1,0:T(8,128)(2,1)S(1)} %pad_maximum_fusion.2.rest_8_), channel_id=1, source_target_pairs={{0,2},{2,0},{4,6},{6,4},{1,3},{3,1},{5,7},{7,5},{8,10},{10,8},{12,... | collective-permute-start | bytes 1572872 | tf_op jit(solution)/shard_map/ppermute | solution.py:427
  50.9 13.3 %collective-permute-start.15 = (bf16[4,512,128]{2,1,0:T(8,128)(2,1)S(1)}, bf16[4,512,128]{2,1,0:T(8,128)(2,1)S(1)}, u32[]{:S(2)}, u32[]{:S(2)}) collective-permute-start(bf16[4,512,128]{2,1,0:T(8,128)(2,1)S(1)} %pad_maximum_fusion.1.rest_7_), channel_id=1, source_target_pairs={{0,4},{2,6},{4,0},{6,2},{1,5},{3,7},{5,1},{7,3},{8,12},{10,14},{12... | collective-permute-start | bytes 1572872 | tf_op jit(solution)/shard_map/ppermute | solution.py:427
  52.6 12.2 %collective-permute-start.20 = (bf16[4,512,128]{2,1,0:T(8,128)(2,1)S(1)}, bf16[4,512,128]{2,1,0:T(8,128)(2,1)S(1)}, u32[]{:S(2)}, u32[]{:S(2)}) collective-permute-start(bf16[4,512,128]{2,1,0:T(8,128)(2,1)S(1)} %pad_maximum_fusion.2.rest_8_), channel_id=1, source_target_pairs={{0,1},{1,0},{2,3},{3,2},{4,5},{5,4},{6,7},{7,6},{8,9},{9,8},{10,11... | collective-permute-start | bytes 1572872 | tf_op jit(solution)/shard_map/ppermute | solution.py:427
  52.6 12.2 %collective-permute-start.19 = (bf16[4,512,128]{2,1,0:T(8,128)(2,1)S(1)}, bf16[4,512,128]{2,1,0:T(8,128)(2,1)S(1)}, u32[]{:S(2)}, u32[]{:S(2)}) collective-permute-start(bf16[4,512,128]{2,1,0:T(8,128)(2,1)S(1)} %pad_maximum_fusion.1.rest_7_), channel_id=1, source_target_pairs={{0,1},{1,0},{2,3},{3,2},{4,5},{5,4},{6,7},{7,6},{8,9},{9,8},{10,11... | collective-permute-start | bytes 1572872 | tf_op jit(solution)/shard_map/ppermute | solution.py:427
  64.2 1.9 %collective-permute-start.21 = (bf16[4,512,128]{2,1,0:T(8,128)(2,1)S(1)}, bf16[4,512,128]{2,1,0:T(8,128)(2,1)S(1)}, u32[]{:S(2)}, u32[]{:S(2)}) collective-permute-start(bf16[4,512,128]{2,1,0:T(8,128)(2,1)S(1)} %collective-permute-done.15.rest_9_), channel_id=1, source_target_pairs={{0,1},{1,0},{2,3},{3,2},{4,5},{5,4},{6,7},{7,6},{8,9},{9,8},{10,11... | collective-permute-start | bytes 1572872 | tf_op jit(solution)/shard_map/ppermute | solution.py:427
  64.2 2.7 %collective-permute-start.22 = (bf16[4,512,128]{2,1,0:T(8,128)(2,1)S(1)}, bf16[4,512,128]{2,1,0:T(8,128)(2,1)S(1)}, u32[]{:S(2)}, u32[]{:S(2)}) collective-permute-start(bf16[4,512,128]{2,1,0:T(8,128)(2,1)S(1)} %collective-permute-done.17.rest_10_), channel_id=1, source_target_pairs={{0,1},{1,0},{2,3},{3,2},{4,5},{5,4},{6,7},{7,6},{8,9},{9,8},{10,11... | collective-permute-start | bytes 1572872 | tf_op jit(solution)/shard_map/ppermute | solution.py:427

commit v16 on v15

--- a/solution.py
+++ b/solution.py
@@ -490,9 +490,9 @@
 
     together = lax.optimization_barrier
     where = jnp.stack([row, chip, core]).astype(jnp.int32)
-    home, smalls, where = together((home, along_rows(small), where))
+    smalls = along_rows(small)
     homes, smalls = along_rows(home), along_one_chip_axis(smalls)
-    smalls, homes[1] = together((smalls, homes[1]))
+    smalls, homes[1], where = together((smalls, homes[1], where))
     smalls = jnp.concatenate(smalls + along_other_chip_axis(smalls))
     homes, smalls = together((homes, smalls))
     others = swap(smalls, "core", 1)

time: 126 us -> 127 us (level)
  Pallas kernels: 68 us -> 71.2 us
  starting transfers between devices: 26.2 us -> 24.7 us
    pallas_call x1, Pallas kernels: 58 us -> 60.7 us  [whole_on_each(): pl.pallas_call(functools.partial(iterate, n_row, n_col, n_cap, float(n_de...]
    ppermute x23, starting transfers between devices: 26.2 us -> 24.7 us  [swap(): return lax.ppermute(x, axis, [(i, i ^ distance) for i in range(size)])]
  transfers between devices with their start and end apart: 23 -> 23, of which waited for: 14 -> 12; matrix products, arithmetic and copies ran while one was open for 0% -> 1% of each run, Pallas kernels for 8% -> 8%
where the time goes in v16:
time: 127 us
  Pallas kernels  71.2 us (56%)
  waiting for transfers between devices  28.1 us (22%)
  starting transfers between devices  24.7 us (19%)
  other arithmetic  1.71 us (1%)
    pallas_call x1, Pallas kernels, whole_on_each(): pl.pallas_call(functools.partial(iterate, n_row, n_col, n_cap, float(n_de...  60.7 us
    ppermute x23, waiting for transfers between devices, swap(): return lax.ppermute(x, axis, [(i, i ^ distance) for i in range(size)])  28.1 us
    ppermute x23, starting transfers between devices, swap(): return lax.ppermute(x, axis, [(i, i ^ distance) for i in range(size)])  24.7 us
    pallas_call x1, Pallas kernels, whole_on_each(): pl.pallas_call(functools.partial(unpack, n_row, n_col), out_shape=[jax.Sh...  8.73 us
  transfers between devices with their start and end apart: 23, of which 12 were waited for; matrix products, arithmetic and copies ran while one was open for 1% of the time, Pallas kernels for 8%

profile of v16, /device:TPU:0, one launch (start us, length us, event | category | flops | bytes accessed | tf_op | source)
XLA Modules:
  0.0 126.9 jit_solution(8145466229282096209)
XLA Ops:
  0.7 1.1 select_bitcast_fusion
  1.8 0.5 collective-permute-start.5
  2.3 1.8 %prepare.1 = bf16[336,128]{1,0:T(8,128)(2,1)} custom-call(s32[1,1]{1,0:T(1,128)S(6)} %copy.10.count, bf16[128,4096]{1,0:T(8,128)(2,1)} %bitcast.41, s32[1,128]{1,0:T(1,128)} %bitcast.63, s32[1,128]{1,0:T(1,128)} %bitcast.64, f32[2,4096]{1,0:T(2,128)} %rest_3_.1, f32[2,64]{1,0:T(2,128)} %rest_4_.1, f32[2,64]{1,0:T(2,128)} %rest_5_.1), custom_call_target="tpu_custom_call" | custom-call | tf_op jit(solution)/shard_map/prepare/pallas_call | solution.py:475
  4.1 3.7 %collective-permute-start.2 = (bf16[336,128]{1,0:T(8,128)(2,1)}, bf16[336,128]{1,0:T(8,128)(2,1)S(1)}, u32[]{:S(2)}, u32[]{:S(2)}) collective-permute-start(bf16[336,128]{1,0:T(8,128)(2,1)} %prepare.1), channel_id=1, source_target_pairs={{0,16},{8,24},{16,0},{24,8},{1,17},{9,25},{17,1},{25,9},{2,18},{10... | collective-permute-start | bytes 258056 | tf_op jit(solution)/shard_map/ppermute | solution.py:427
  7.8 1.3 %collective-permute-start.3 = (bf16[336,128]{1,0:T(8,128)(2,1)}, bf16[336,128]{1,0:T(8,128)(2,1)S(1)}, u32[]{:S(2)}, u32[]{:S(2)}) collective-permute-start(bf16[336,128]{1,0:T(8,128)(2,1)} %prepare.1), channel_id=1, source_target_pairs={{0,24},{8,16},{16,8},{24,0},{1,25},{9,17},{17,9},{25,1},{2,26},{10... | collective-permute-start | bytes 258056 | tf_op jit(solution)/shard_map/ppermute | solution.py:427
  9.2 0.2 collective-permute-start
  9.4 0.1 pad_add_fusion.own
  9.5 0.0 collective-permute-done.5
  9.5 0.1 bitcast_add_fusion
  9.6 1.6 %collective-permute-start.6 = (bf16[16,4096]{1,0:T(8,128)(2,1)S(1)}, bf16[16,4096]{1,0:T(8,128)(2,1)S(1)}, u32[]{:S(2)}, u32[]{:S(2)}) collective-permute-start(bf16[16,4096]{1,0:T(8,128)(2,1)S(1)} %get-tuple-element.47), channel_id=1, source_target_pairs={{0,2},{2,0},{4,6},{6,4},{1,3},{3,1},{5,7},{7,5},{8,10},{10,8},{12,... | collective-permute-start | bytes 393224 | tf_op jit(solution)/shard_map/ppermute | solution.py:427
  11.2 1.5 %collective-permute-start.7 = (bf16[16,4096]{1,0:T(8,128)(2,1)S(1)}, bf16[16,4096]{1,0:T(8,128)(2,1)S(1)}, u32[]{:S(2)}, u32[]{:S(2)}) collective-permute-start(bf16[16,4096]{1,0:T(8,128)(2,1)S(1)} %get-tuple-element.49), channel_id=1, source_target_pairs={{0,4},{2,6},{4,0},{6,2},{1,5},{3,7},{5,1},{7,3},{8,12},{10,14},{12... | collective-permute-start | bytes 393224 | tf_op jit(solution)/shard_map/ppermute | solution.py:427
  12.7 2.4 %collective-permute-done.2 = bf16[336,128]{1,0:T(8,128)(2,1)S(1)} collective-permute-done((bf16[336,128]{1,0:T(8,128)(2,1)}, bf16[336,128]{1,0:T(8,128)(2,1)S(1)}, u32[]{:S(2)}, u32[]{:S(2)}) %collective-permute-start.2) | collective-permute-done | bytes 86048 | tf_op jit(solution)/shard_map/ppermute | solution.py:427
  15.1 2.8 %collective-permute-start.8 = (bf16[16,4096]{1,0:T(8,128)(2,1)S(1)}, bf16[16,4096]{1,0:T(8,128)(2,1)S(1)}, u32[]{:S(2)}, u32[]{:S(2)}) collective-permute-start(bf16[16,4096]{1,0:T(8,128)(2,1)S(1)} %get-tuple-element.48), channel_id=1, source_target_pairs={{0,6},{2,4},{4,2},{6,0},{1,7},{3,5},{5,3},{7,1},{8,14},{10,12},{12... | collective-permute-start | bytes 393224 | tf_op jit(solution)/shard_map/ppermute | solution.py:427
  17.9 0.6 collective-permute-start.4
  18.5 0.3 collective-permute-start.1
  18.8 3.0 %collective-permute-done.8 = bf16[16,4096]{1,0:T(8,128)(2,1)S(1)} collective-permute-done((bf16[16,4096]{1,0:T(8,128)(2,1)S(1)}, bf16[16,4096]{1,0:T(8,128)(2,1)S(1)}, u32[]{:S(2)}, u32[]{:S(2)}) %collective-permute-start.8) | collective-permute-done | bytes 131104 | tf_op jit(solution)/shard_map/ppermute | solution.py:427
  21.8 0.1 copy.8
  21.8 0.6 collective-permute-start.9
  22.4 1.9 %collective-permute-done.4 = bf16[2,336,128]{2,1,0:T(8,128)(2,1)S(1)} collective-permute-done((bf16[2,336,128]{2,1,0:T(8,128)(2,1)S(1)}, bf16[2,336,128]{2,1,0:T(8,128)(2,1)S(1)}, u32[]{:S(2)}, u32[]{:S(2)}) %collective-permute-start.4) | collective-permute-done | bytes 172064 | tf_op jit(solution)/shard_map/ppermute | solution.py:427
  24.4 0.0 collective-permute-done.1
  24.5 2.4 %collective-permute-done.9 = bf16[512,128]{1,0:T(8,128)(2,1)S(1)} collective-permute-done((bf16[512,128]{1,0:T(8,128)(2,1)S(1)}, bf16[512,128]{1,0:T(8,128)(2,1)S(1)}, u32[]{:S(2)}, u32[]{:S(2)}) %collective-permute-start.9) | collective-permute-done | bytes 131104 | tf_op jit(solution)/shard_map/ppermute | solution.py:427
  26.9 2.3 %collective-permute-start.12 = (bf16[4,336,128]{2,1,0:T(8,128)(2,1)S(1)}, bf16[4,336,128]{2,1,0:T(8,128)(2,1)S(1)}, u32[]{:S(2)}, u32[]{:S(2)}) collective-permute-start(bf16[4,336,128]{2,1,0:T(8,128)(2,1)S(1)} %pad_maximum_fusion.3), channel_id=1, source_target_pairs={{0,4},{2,6},{4,0},{6,2},{1,5},{3,7},{5,1},{7,3},{8,12},{10,14},{12... | collective-permute-start | bytes 1032200 | tf_op jit(solution)/shard_map/ppermute | solution.py:427
  29.2 1.4 %collective-permute-start.13 = (bf16[4,336,128]{2,1,0:T(8,128)(2,1)S(1)}, bf16[4,336,128]{2,1,0:T(8,128)(2,1)S(1)}, u32[]{:S(2)}, u32[]{:S(2)}) collective-permute-start(bf16[4,336,128]{2,1,0:T(8,128)(2,1)S(1)} %pad_maximum_fusion.4), channel_id=1, source_target_pairs={{0,2},{2,0},{4,6},{6,4},{1,3},{3,1},{5,7},{7,5},{8,10},{10,8},{12,... | collective-permute-start | bytes 1032200 | tf_op jit(solution)/shard_map/ppermute | solution.py:427
  30.6 2.0 %collective-permute-start.10 = (bf16[512,128]{1,0:T(8,128)(2,1)S(1)}, bf16[512,128]{1,0:T(8,128)(2,1)S(1)}, u32[]{:S(2)}, u32[]{:S(2)}) collective-permute-start(bf16[512,128]{1,0:T(8,128)(2,1)S(1)} %bitcast.44), channel_id=1, source_target_pairs={{0,16},{8,24},{16,0},{24,8},{1,17},{9,25},{17,1},{25,9},{2,18},{10... | collective-permute-start | bytes 393224 | tf_op jit(solution)/shard_map/ppermute | solution.py:427
  32.6 1.5 %collective-permute-start.11 = (bf16[512,128]{1,0:T(8,128)(2,1)S(1)}, bf16[512,128]{1,0:T(8,128)(2,1)S(1)}, u32[]{:S(2)}, u32[]{:S(2)}) collective-permute-start(bf16[512,128]{1,0:T(8,128)(2,1)S(1)} %bitcast.45), channel_id=1, source_target_pairs={{0,24},{8,16},{16,8},{24,0},{1,25},{9,17},{17,9},{25,1},{2,26},{10... | collective-permute-start | bytes 393224 | tf_op jit(solution)/shard_map/ppermute | solution.py:427
  34.0 0.4 collective-permute-done.12
  34.4 2.0 %collective-permute-done.13 = bf16[4,336,128]{2,1,0:T(8,128)(2,1)S(1)} collective-permute-done((bf16[4,336,128]{2,1,0:T(8,128)(2,1)S(1)}, bf16[4,336,128]{2,1,0:T(8,128)(2,1)S(1)}, u32[]{:S(2)}, u32[]{:S(2)}) %collective-permute-start.13) | collective-permute-done | bytes 344096 | tf_op jit(solution)/shard_map/ppermute | solution.py:427
  36.4 0.2 pad_maximum_fusion.mine
  36.6 3.4 %collective-permute-done.10 = bf16[512,128]{1,0:T(8,128)(2,1)S(1)} collective-permute-done((bf16[512,128]{1,0:T(8,128)(2,1)S(1)}, bf16[512,128]{1,0:T(8,128)(2,1)S(1)}, u32[]{:S(2)}, u32[]{:S(2)}) %collective-permute-start.10) | collective-permute-done | bytes 131104 | tf_op jit(solution)/shard_map/ppermute | solution.py:427
  40.0 0.0 collective-permute-done.11
  40.1 1.1 collective-permute-start.16
  41.2 0.6 collective-permute-start.14
  41.8 7.1 %collective-permute-done.16 = bf16[2,512,128]{2,1,0:T(8,128)(2,1)S(1)} collective-permute-done((bf16[2,512,128]{2,1,0:T(8,128)(2,1)S(1)}, bf16[2,512,128]{2,1,0:T(8,128)(2,1)S(1)}, u32[]{:S(2)}, u32[]{:S(2)}) %collective-permute-start.16) | collective-permute-done | bytes 262176 | tf_op jit(solution)/shard_map/ppermute | solution.py:427
  48.9 0.1 pad_maximum_fusion.2.rest_8_
  48.9 1.0 collective-permute-start.17
  49.9 0.0 collective-permute-done.14
  49.9 0.1 pad_maximum_fusion.1.rest_7_
  50.0 0.8 collective-permute-start.15
  50.8 0.5 collective-permute-start.19
  51.3 0.0 collective-permute-done.18.other
  51.3 8.7 %unpack.1 = (s32[584]{0:T(1024)S(1)}, f32[8,128]{1,0:T(8,128)S(1)}, bf16[144,128,128]{2,1,0:T(8,128)(2,1)S(1)}, f32[32,8,128]{2,1,0:T(8,128)S(1)}, f32[32,8,128]...) custom-call(s32[3]{0:T(128)S(1)} %pad_add_fusion.own, ...), custom_call_target="tpu_custom_call" | custom-call | bytes 11010048 | tf_op jit(solution)/shard_map/unpack/pallas_call | solution.py:511
  60.1 2.5 %collective-permute-done.17.rest_10_ = bf16[4,512,128]{2,1,0:T(8,128)(2,1)S(1)} collective-permute-done((bf16[4,512,128]{2,1,0:T(8,128)(2,1)S(1)}, bf16[4,512,128]{2,1,0:T(8,128)(2,1)S(1)}, u32[]{:S(2)}, u32[]{:S(2)}) %collective-permute-start.17) | collective-permute-done | bytes 524320 | tf_op jit(solution)/shard_map/ppermute | solution.py:427
  62.5 0.8 collective-permute-done.15.rest_9_
  63.3 0.0 collective-permute-start.21
  63.3 0.5 collective-permute-start.22
  63.9 1.4 %collective-permute-done.21.rest_13_ = bf16[4,512,128]{2,1,0:T(8,128)(2,1)S(1)} collective-permute-done((bf16[4,512,128]{2,1,0:T(8,128)(2,1)S(1)}, bf16[4,512,128]{2,1,0:T(8,128)(2,1)S(1)}, u32[]{:S(2)}, u32[]{:S(2)}) %collective-permute-start.21) | collective-permute-done | bytes 524320 | tf_op jit(solution)/shard_map/ppermute | solution.py:427
  65.2 0.7 collective-permute-done.22.rest_14_
  66.0 60.7 %iterate.1 = f32[2,4096]{1,0:T(2,128)} custom-call(s32[3]{0:T(128)S(1)} %pad_add_fusion.own, s32[584]{0:T(1024)S(1)} %get-tuple-element.36.lists, f32[8,128]{1,0:T(8,128)S(1)} %get-tuple-element.37.place, bf16[144,128,128]{2,1,0:T(8,128)(2,1)S(1)} %get-tuple-element.38.rest_0_, f32[32,8,128]{2,1,0:T(8,128)S(1)} %get-tuple-element.39.rest_1_, ...), custom_call_target="tpu_custom_call" | custom-call | tf_op jit(solution)/shard_map/iterate/pallas_call | solution.py:532
  (21 shorter events, 0.3 us)
Async XLA Ops:
  0.0 9.5 %copy-start = (bf16[1,1,128,4096]{3,2,1,0:T(8,128)(2,1)S(1)}, bf16[1,1,128,4096]{3,2,1,0:T(8,128)(2,1)}, u32[]{:S(2)}) copy-start(bf16[1,1,128,4096]{3,2,1,0:T(8,128)(2,1)} %param.7) | copy-start | bytes 3145732
  1.8 7.6 %collective-permute-start.5 = (bf16[4,16,4096]{2,1,0:T(8,128)(2,1)S(1)}, bf16[4,16,4096]{2,1,0:T(8,128)(2,1)S(1)}, u32[]{:S(2)}, u32[]{:S(2)}) collective-permute-start(bf16[4,16,4096]{2,1,0:T(8,128)(2,1)S(1)} %select_bitcast_fusion), channel_id=1, source_target_pairs={{0,1},{1,0},{2,3},{3,2},{4,5},{5,4},{6,7},{7,6},{8,9},{9,8},{10,11... | collective-permute-start | bytes 1572872 | tf_op jit(solution)/shard_map/ppermute | solution.py:427
  4.1 10.9 %collective-permute-start.2 = (bf16[336,128]{1,0:T(8,128)(2,1)}, bf16[336,128]{1,0:T(8,128)(2,1)S(1)}, u32[]{:S(2)}, u32[]{:S(2)}) collective-permute-start(bf16[336,128]{1,0:T(8,128)(2,1)} %prepare.1), channel_id=1, source_target_pairs={{0,16},{8,24},{16,0},{24,8},{1,17},{9,25},{17,1},{25,9},{2,18},{10... | collective-permute-start | bytes 258056 | tf_op jit(solution)/shard_map/ppermute | solution.py:427
  7.8 10.0 %collective-permute-start.3 = (bf16[336,128]{1,0:T(8,128)(2,1)}, bf16[336,128]{1,0:T(8,128)(2,1)S(1)}, u32[]{:S(2)}, u32[]{:S(2)}) collective-permute-start(bf16[336,128]{1,0:T(8,128)(2,1)} %prepare.1), channel_id=1, source_target_pairs={{0,24},{8,16},{16,8},{24,0},{1,25},{9,17},{17,9},{25,1},{2,26},{10... | collective-permute-start | bytes 258056 | tf_op jit(solution)/shard_map/ppermute | solution.py:427
  9.2 9.3 %collective-permute-start = (bf16[336,128]{1,0:T(8,128)(2,1)}, bf16[336,128]{1,0:T(8,128)(2,1)S(1)}, u32[]{:S(2)}, u32[]{:S(2)}) collective-permute-start(bf16[336,128]{1,0:T(8,128)(2,1)} %prepare.1), channel_id=1, source_target_pairs={{0,8},{8,0},{16,24},{24,16},{1,9},{9,1},{17,25},{25,17},{2,10},{10... | collective-permute-start | bytes 258056 | tf_op jit(solution)/shard_map/ppermute | solution.py:427
  9.4 9.1 %copy-start.1 = (bf16[336,128]{1,0:T(8,128)(2,1)S(1)}, bf16[336,128]{1,0:T(8,128)(2,1)}, u32[]{:S(2)}) copy-start(bf16[336,128]{1,0:T(8,128)(2,1)} %prepare.1) | copy-start | bytes 258052
  9.6 9.2 %collective-permute-start.6 = (bf16[16,4096]{1,0:T(8,128)(2,1)S(1)}, bf16[16,4096]{1,0:T(8,128)(2,1)S(1)}, u32[]{:S(2)}, u32[]{:S(2)}) collective-permute-start(bf16[16,4096]{1,0:T(8,128)(2,1)S(1)} %get-tuple-element.47), channel_id=1, source_target_pairs={{0,2},{2,0},{4,6},{6,4},{1,3},{3,1},{5,7},{7,5},{8,10},{10,8},{12,... | collective-permute-start | bytes 393224 | tf_op jit(solution)/shard_map/ppermute | solution.py:427
  11.2 7.6 %collective-permute-start.7 = (bf16[16,4096]{1,0:T(8,128)(2,1)S(1)}, bf16[16,4096]{1,0:T(8,128)(2,1)S(1)}, u32[]{:S(2)}, u32[]{:S(2)}) collective-permute-start(bf16[16,4096]{1,0:T(8,128)(2,1)S(1)} %get-tuple-element.49), channel_id=1, source_target_pairs={{0,4},{2,6},{4,0},{6,2},{1,5},{3,7},{5,1},{7,3},{8,12},{10,14},{12... | collective-permute-start | bytes 393224 | tf_op jit(solution)/shard_map/ppermute | solution.py:427
  15.1 6.6 %collective-permute-start.8 = (bf16[16,4096]{1,0:T(8,128)(2,1)S(1)}, bf16[16,4096]{1,0:T(8,128)(2,1)S(1)}, u32[]{:S(2)}, u32[]{:S(2)}) collective-permute-start(bf16[16,4096]{1,0:T(8,128)(2,1)S(1)} %get-tuple-element.48), channel_id=1, source_target_pairs={{0,6},{2,4},{4,2},{6,0},{1,7},{3,5},{5,3},{7,1},{8,14},{10,12},{12... | collective-permute-start | bytes 393224 | tf_op jit(solution)/shard_map/ppermute | solution.py:427
  17.9 6.5 %collective-permute-start.4 = (bf16[2,336,128]{2,1,0:T(8,128)(2,1)S(1)}, bf16[2,336,128]{2,1,0:T(8,128)(2,1)S(1)}, u32[]{:S(2)}, u32[]{:S(2)}) collective-permute-start(bf16[2,336,128]{2,1,0:T(8,128)(2,1)S(1)} %pad_maximum_fusion.8), channel_id=1, source_target_pairs={{0,4},{2,6},{4,0},{6,2},{1,5},{3,7},{5,1},{7,3},{8,12},{10,14},{12... | collective-permute-start | bytes 516104 | tf_op jit(solution)/shard_map/ppermute | solution.py:427
  18.5 6.0 %collective-permute-start.1 = (bf16[2,336,128]{2,1,0:T(8,128)(2,1)S(1)}, bf16[2,336,128]{2,1,0:T(8,128)(2,1)S(1)}, u32[]{:S(2)}, u32[]{:S(2)}) collective-permute-start(bf16[2,336,128]{2,1,0:T(8,128)(2,1)S(1)} %pad_maximum_fusion.7), channel_id=1, source_target_pairs={{0,2},{2,0},{4,6},{6,4},{1,3},{3,1},{5,7},{7,5},{8,10},{10,8},{12,... | collective-permute-start | bytes 516104 | tf_op jit(solution)/shard_map/ppermute | solution.py:427
  21.8 5.0 %collective-permute-start.9 = (bf16[512,128]{1,0:T(8,128)(2,1)S(1)}, bf16[512,128]{1,0:T(8,128)(2,1)S(1)}, u32[]{:S(2)}, u32[]{:S(2)}) collective-permute-start(bf16[512,128]{1,0:T(8,128)(2,1)S(1)} %bitcast.43), channel_id=1, source_target_pairs={{0,8},{8,0},{16,24},{24,16},{1,9},{9,1},{17,25},{25,17},{2,10},{10... | collective-permute-start | bytes 393224 | tf_op jit(solution)/shard_map/ppermute | solution.py:427
  26.9 7.5 %collective-permute-start.12 = (bf16[4,336,128]{2,1,0:T(8,128)(2,1)S(1)}, bf16[4,336,128]{2,1,0:T(8,128)(2,1)S(1)}, u32[]{:S(2)}, u32[]{:S(2)}) collective-permute-start(bf16[4,336,128]{2,1,0:T(8,128)(2,1)S(1)} %pad_maximum_fusion.3), channel_id=1, source_target_pairs={{0,4},{2,6},{4,0},{6,2},{1,5},{3,7},{5,1},{7,3},{8,12},{10,14},{12... | collective-permute-start | bytes 1032200 | tf_op jit(solution)/shard_map/ppermute | solution.py:427
  29.2 7.2 %collective-permute-start.13 = (bf16[4,336,128]{2,1,0:T(8,128)(2,1)S(1)}, bf16[4,336,128]{2,1,0:T(8,128)(2,1)S(1)}, u32[]{:S(2)}, u32[]{:S(2)}) collective-permute-start(bf16[4,336,128]{2,1,0:T(8,128)(2,1)S(1)} %pad_maximum_fusion.4), channel_id=1, source_target_pairs={{0,2},{2,0},{4,6},{6,4},{1,3},{3,1},{5,7},{7,5},{8,10},{10,8},{12,... | collective-permute-start | bytes 1032200 | tf_op jit(solution)/shard_map/ppermute | solution.py:427
  30.6 9.5 %collective-permute-start.10 = (bf16[512,128]{1,0:T(8,128)(2,1)S(1)}, bf16[512,128]{1,0:T(8,128)(2,1)S(1)}, u32[]{:S(2)}, u32[]{:S(2)}) collective-permute-start(bf16[512,128]{1,0:T(8,128)(2,1)S(1)} %bitcast.44), channel_id=1, source_target_pairs={{0,16},{8,24},{16,0},{24,8},{1,17},{9,25},{17,1},{25,9},{2,18},{10... | collective-permute-start | bytes 393224 | tf_op jit(solution)/shard_map/ppermute | solution.py:427
  32.6 7.5 %collective-permute-start.11 = (bf16[512,128]{1,0:T(8,128)(2,1)S(1)}, bf16[512,128]{1,0:T(8,128)(2,1)S(1)}, u32[]{:S(2)}, u32[]{:S(2)}) collective-permute-start(bf16[512,128]{1,0:T(8,128)(2,1)S(1)} %bitcast.45), channel_id=1, source_target_pairs={{0,24},{8,16},{16,8},{24,0},{1,25},{9,17},{17,9},{25,1},{2,26},{10... | collective-permute-start | bytes 393224 | tf_op jit(solution)/shard_map/ppermute | solution.py:427
  40.0 11.3 %collective-permute-start.18 = (bf16[16,336,128]{2,1,0:T(8,128)(2,1)S(1)}, bf16[16,336,128]{2,1,0:T(8,128)(2,1)S(1)}, u32[]{:S(2)}, u32[]{:S(2)}) collective-permute-start(bf16[16,336,128]{2,1,0:T(8,128)(2,1)S(1)} %pad_maximum_fusion.mine), channel_id=1, source_target_pairs={{0,1},{1,0},{2,3},{3,2},{4,5},{5,4},{6,7},{7,6},{8,9},{9,8},{10,11... | collective-permute-start | bytes 4128776 | tf_op jit(solution)/shard_map/ppermute | solution.py:427
  40.1 8.8 %collective-permute-start.16 = (bf16[2,512,128]{2,1,0:T(8,128)(2,1)S(1)}, bf16[2,512,128]{2,1,0:T(8,128)(2,1)S(1)}, u32[]{:S(2)}, u32[]{:S(2)}) collective-permute-start(bf16[2,512,128]{2,1,0:T(8,128)(2,1)S(1)} %pad_maximum_fusion.6), channel_id=1, source_target_pairs={{0,4},{2,6},{4,0},{6,2},{1,5},{3,7},{5,1},{7,3},{8,12},{10,14},{12... | collective-permute-start | bytes 786440 | tf_op jit(solution)/shard_map/ppermute | solution.py:427
  41.2 8.8 %collective-permute-start.14 = (bf16[2,512,128]{2,1,0:T(8,128)(2,1)S(1)}, bf16[2,512,128]{2,1,0:T(8,128)(2,1)S(1)}, u32[]{:S(2)}, u32[]{:S(2)}) collective-permute-start(bf16[2,512,128]{2,1,0:T(8,128)(2,1)S(1)} %pad_maximum_fusion.5), channel_id=1, source_target_pairs={{0,2},{2,0},{4,6},{6,4},{1,3},{3,1},{5,7},{7,5},{8,10},{10,8},{12,... | collective-permute-start | bytes 786440 | tf_op jit(solution)/shard_map/ppermute | solution.py:427
  48.9 13.6 %collective-permute-start.17 = (bf16[4,512,128]{2,1,0:T(8,128)(2,1)S(1)}, bf16[4,512,128]{2,1,0:T(8,128)(2,1)S(1)}, u32[]{:S(2)}, u32[]{:S(2)}) collective-permute-start(bf16[4,512,128]{2,1,0:T(8,128)(2,1)S(1)} %pad_maximum_fusion.2.rest_8_), channel_id=1, source_target_pairs={{0,2},{2,0},{4,6},{6,4},{1,3},{3,1},{5,7},{7,5},{8,10},{10,8},{12,... | collective-permute-start | bytes 1572872 | tf_op jit(solution)/shard_map/ppermute | solution.py:427
  50.0 13.3 %collective-permute-start.15 = (bf16[4,512,128]{2,1,0:T(8,128)(2,1)S(1)}, bf16[4,512,128]{2,1,0:T(8,128)(2,1)S(1)}, u32[]{:S(2)}, u32[]{:S(2)}) collective-permute-start(bf16[4,512,128]{2,1,0:T(8,128)(2,1)S(1)} %pad_maximum_fusion.1.rest_7_), channel_id=1, source_target_pairs={{0,4},{2,6},{4,0},{6,2},{1,5},{3,7},{5,1},{7,3},{8,12},{10,14},{12... | collective-permute-start | bytes 1572872 | tf_op jit(solution)/shard_map/ppermute | solution.py:427
  50.8 13.0 %collective-permute-start.20 = (bf16[4,512,128]{2,1,0:T(8,128)(2,1)S(1)}, bf16[4,512,128]{2,1,0:T(8,128)(2,1)S(1)}, u32[]{:S(2)}, u32[]{:S(2)}) collective-permute-start(bf16[4,512,128]{2,1,0:T(8,128)(2,1)S(1)} %pad_maximum_fusion.2.rest_8_), channel_id=1, source_target_pairs={{0,1},{1,0},{2,3},{3,2},{4,5},{5,4},{6,7},{7,6},{8,9},{9,8},{10,11... | collective-permute-start | bytes 1572872 | tf_op jit(solution)/shard_map/ppermute | solution.py:427
  50.8 13.0 %collective-permute-start.19 = (bf16[4,512,128]{2,1,0:T(8,128)(2,1)S(1)}, bf16[4,512,128]{2,1,0:T(8,128)(2,1)S(1)}, u32[]{:S(2)}, u32[]{:S(2)}) collective-permute-start(bf16[4,512,128]{2,1,0:T(8,128)(2,1)S(1)} %pad_maximum_fusion.1.rest_7_), channel_id=1, source_target_pairs={{0,1},{1,0},{2,3},{3,2},{4,5},{5,4},{6,7},{7,6},{8,9},{9,8},{10,11... | collective-permute-start | bytes 1572872 | tf_op jit(solution)/shard_map/ppermute | solution.py:427
  63.3 1.9 %collective-permute-start.21 = (bf16[4,512,128]{2,1,0:T(8,128)(2,1)S(1)}, bf16[4,512,128]{2,1,0:T(8,128)(2,1)S(1)}, u32[]{:S(2)}, u32[]{:S(2)}) collective-permute-start(bf16[4,512,128]{2,1,0:T(8,128)(2,1)S(1)} %collective-permute-done.15.rest_9_), channel_id=1, source_target_pairs={{0,1},{1,0},{2,3},{3,2},{4,5},{5,4},{6,7},{7,6},{8,9},{9,8},{10,11... | collective-permute-start | bytes 1572872 | tf_op jit(solution)/shard_map/ppermute | solution.py:427
  63.3 2.7 %collective-permute-start.22 = (bf16[4,512,128]{2,1,0:T(8,128)(2,1)S(1)}, bf16[4,512,128]{2,1,0:T(8,128)(2,1)S(1)}, u32[]{:S(2)}, u32[]{:S(2)}) collective-permute-start(bf16[4,512,128]{2,1,0:T(8,128)(2,1)S(1)} %collective-permute-done.17.rest_10_), channel_id=1, source_target_pairs={{0,1},{1,0},{2,3},{3,2},{4,5},{5,4},{6,7},{7,6},{8,9},{9,8},{10,11... | collective-permute-start | bytes 1572872 | tf_op jit(solution)/shard_map/ppermute | solution.py:427

commit v17 on v15

--- a/solution.py
+++ b/solution.py
@@ -244,21 +244,23 @@
             at += ref.shape[0]
         return pairs
 
-    copies = copy_in(laid_out(fulls, full), sems)
+    pairs = laid_out(fulls, full)
+    copies = copy_in(pairs[0::2] + pairs[1::2], sems)
     for start, ref in zip(starts, (vs, vd, w1, w2)):
         for q in range(ref.shape[0]):
             ref[q] = start[q]
     clear([y, y1, y2])
-    for copy in copies:
-        copy.wait()
     n_group = lists[2 * slots]
 
     left = lax.broadcasted_iota(jnp.int32, (rblk, 128), 1) < 64
-    homes = []
-    for r in range(n_row):
-        homes.append(lists[2 * slots + 1 + r])
+    homes = [lists[2 * slots + 1 + r] for r in range(n_row)]
+    for distance in range(n_row):
+        if distance % 2 == 0:
+            for copy in copies[2 * distance : 2 * distance + 4]:
+                copy.wait()
+        r = own[0] ^ distance
         want = lax.broadcasted_iota(jnp.int32, (cblk * rblk, n_cap), 0).astype(jnp.float32)
-        select = jnp.where(want == place[r : r + 1, :], 1.0, 0.0).astype(jnp.bfloat16)
+        select = jnp.where(want == place[pl.ds(r, 1), :], 1.0, 0.0).astype(jnp.bfloat16)
 
         parts = [at_device(r, 2 * i + j) for j in range(2) for i in range(n_col // 2)]
 

time: 126 us -> 128 us (1.016)
  Pallas kernels: 68 us -> 71.1 us
    pallas_call x1, Pallas kernels: 58 us -> 60.5 us  [whole_on_each(): pl.pallas_call(functools.partial(iterate, n_row, n_col, n_cap, float(n_de...]
where the time goes in v17:
time: 128 us
  Pallas kernels  71.1 us (56%)
  waiting for transfers between devices  27.4 us (21%)
  starting transfers between devices  26.2 us (20%)
  other arithmetic  1.68 us (1%)
    pallas_call x1, Pallas kernels, whole_on_each(): pl.pallas_call(functools.partial(iterate, n_row, n_col, n_cap, float(n_de...  60.5 us
    ppermute x23, waiting for transfers between devices, swap(): return lax.ppermute(x, axis, [(i, i ^ distance) for i in range(size)])  27.4 us
    ppermute x23, starting transfers between devices, swap(): return lax.ppermute(x, axis, [(i, i ^ distance) for i in range(size)])  26.2 us
    pallas_call x1, Pallas kernels, whole_on_each(): pl.pallas_call(functools.partial(unpack, n_row, n_col), out_shape=[jax.Sh...  8.74 us
  transfers between devices with their start and end apart: 23, of which 14 were waited for; matrix products, arithmetic and copies ran while one was open for 0% of the time, Pallas kernels for 8%

profile of v17, /device:TPU:0, one launch (start us, length us, event | category | flops | bytes accessed | tf_op | source)
XLA Modules:
  0.0 127.6 jit_solution(6144002936887177887)
XLA Ops:
  0.7 1.1 select_bitcast_fusion
  1.8 0.5 collective-permute-start
  2.3 1.5 %collective-permute-done = bf16[4,16,4096]{2,1,0:T(8,128)(2,1)S(1)} collective-permute-done((bf16[4,16,4096]{2,1,0:T(8,128)(2,1)S(1)}, bf16[4,16,4096]{2,1,0:T(8,128)(2,1)S(1)}, u32[]{:S(2)}, u32[]{:S(2)}) %collective-permute-start) | collective-permute-done | bytes 524320 | tf_op jit(solution)/shard_map/ppermute | solution.py:429
  3.9 0.1 bitcast_add_fusion
  4.0 2.9 %collective-permute-start.1 = (bf16[16,4096]{1,0:T(8,128)(2,1)S(1)}, bf16[16,4096]{1,0:T(8,128)(2,1)S(1)}, u32[]{:S(2)}, u32[]{:S(2)}) collective-permute-start(bf16[16,4096]{1,0:T(8,128)(2,1)S(1)} %get-tuple-element.57), channel_id=1, source_target_pairs={{0,2},{2,0},{4,6},{6,4},{1,3},{3,1},{5,7},{7,5},{8,10},{10,8},{12,... | collective-permute-start | bytes 393224 | tf_op jit(solution)/shard_map/ppermute | solution.py:429
  6.9 1.5 %collective-permute-start.2 = (bf16[16,4096]{1,0:T(8,128)(2,1)S(1)}, bf16[16,4096]{1,0:T(8,128)(2,1)S(1)}, u32[]{:S(2)}, u32[]{:S(2)}) collective-permute-start(bf16[16,4096]{1,0:T(8,128)(2,1)S(1)} %get-tuple-element.59), channel_id=1, source_target_pairs={{0,4},{2,6},{4,0},{6,2},{1,5},{3,7},{5,1},{7,3},{8,12},{10,14},{12... | collective-permute-start | bytes 393224 | tf_op jit(solution)/shard_map/ppermute | solution.py:429
  8.4 0.0 collective-permute-start.3
  8.5 1.8 %prepare.1 = bf16[336,128]{1,0:T(8,128)(2,1)} custom-call(s32[1,1]{1,0:T(1,128)S(6)} %copy.10.count, bf16[128,4096]{1,0:T(8,128)(2,1)} %bitcast.41, s32[1,128]{1,0:T(1,128)} %bitcast.63, s32[1,128]{1,0:T(1,128)} %bitcast.64, f32[2,4096]{1,0:T(2,128)} %rest_3_.1, f32[2,64]{1,0:T(2,128)} %rest_4_.1, f32[2,64]{1,0:T(2,128)} %rest_5_.1), custom_call_target="tpu_custom_call" | custom-call | tf_op jit(solution)/shard_map/prepare/pallas_call | solution.py:477
  10.3 2.1 %collective-permute-start.4 = (bf16[336,128]{1,0:T(8,128)(2,1)}, bf16[336,128]{1,0:T(8,128)(2,1)S(1)}, u32[]{:S(2)}, u32[]{:S(2)}) collective-permute-start(bf16[336,128]{1,0:T(8,128)(2,1)} %prepare.1), channel_id=1, source_target_pairs={{0,8},{8,0},{16,24},{24,16},{1,9},{9,1},{17,25},{25,17},{2,10},{10... | collective-permute-start | bytes 258056 | tf_op jit(solution)/shard_map/ppermute | solution.py:429
  12.4 2.6 %collective-permute-start.5 = (bf16[336,128]{1,0:T(8,128)(2,1)}, bf16[336,128]{1,0:T(8,128)(2,1)S(1)}, u32[]{:S(2)}, u32[]{:S(2)}) collective-permute-start(bf16[336,128]{1,0:T(8,128)(2,1)} %prepare.1), channel_id=1, source_target_pairs={{0,16},{8,24},{16,0},{24,8},{1,17},{9,25},{17,1},{25,9},{2,18},{10... | collective-permute-start | bytes 258056 | tf_op jit(solution)/shard_map/ppermute | solution.py:429
  15.0 0.1 pad_add_fusion.own
  15.0 0.0 collective-permute-done.1
  15.0 0.0 collective-permute-start.6
  15.1 0.0 collective-permute-done.2
  15.1 0.1 copy.8
  15.2 5.4 %collective-permute-done.5 = bf16[336,128]{1,0:T(8,128)(2,1)S(1)} collective-permute-done((bf16[336,128]{1,0:T(8,128)(2,1)}, bf16[336,128]{1,0:T(8,128)(2,1)S(1)}, u32[]{:S(2)}, u32[]{:S(2)}) %collective-permute-start.5) | collective-permute-done | bytes 86048 | tf_op jit(solution)/shard_map/ppermute | solution.py:429
  20.6 1.0 collective-permute-done.6
  21.7 1.6 %collective-permute-start.8 = (bf16[2,336,128]{2,1,0:T(8,128)(2,1)S(1)}, bf16[2,336,128]{2,1,0:T(8,128)(2,1)S(1)}, u32[]{:S(2)}, u32[]{:S(2)}) collective-permute-start(bf16[2,336,128]{2,1,0:T(8,128)(2,1)S(1)} %pad_maximum_fusion.8), channel_id=1, source_target_pairs={{0,4},{2,6},{4,0},{6,2},{1,5},{3,7},{5,1},{7,3},{8,12},{10,14},{12... | collective-permute-start | bytes 516104 | tf_op jit(solution)/shard_map/ppermute | solution.py:429
  23.3 1.6 %collective-permute-start.7 = (bf16[2,336,128]{2,1,0:T(8,128)(2,1)S(1)}, bf16[2,336,128]{2,1,0:T(8,128)(2,1)S(1)}, u32[]{:S(2)}, u32[]{:S(2)}) collective-permute-start(bf16[2,336,128]{2,1,0:T(8,128)(2,1)S(1)} %pad_maximum_fusion.7), channel_id=1, source_target_pairs={{0,2},{2,0},{4,6},{6,4},{1,3},{3,1},{5,7},{7,5},{8,10},{10,8},{12,... | collective-permute-start | bytes 516104 | tf_op jit(solution)/shard_map/ppermute | solution.py:429
  24.8 1.4 %collective-permute-start.9 = (bf16[512,128]{1,0:T(8,128)(2,1)S(1)}, bf16[512,128]{1,0:T(8,128)(2,1)S(1)}, u32[]{:S(2)}, u32[]{:S(2)}) collective-permute-start(bf16[512,128]{1,0:T(8,128)(2,1)S(1)} %bitcast.43), channel_id=1, source_target_pairs={{0,8},{8,0},{16,24},{24,16},{1,9},{9,1},{17,25},{25,17},{2,10},{10... | collective-permute-start | bytes 393224 | tf_op jit(solution)/shard_map/ppermute | solution.py:429
  26.2 0.9 collective-permute-done.8
  27.2 1.6 %collective-permute-done.7 = bf16[2,336,128]{2,1,0:T(8,128)(2,1)S(1)} collective-permute-done((bf16[2,336,128]{2,1,0:T(8,128)(2,1)S(1)}, bf16[2,336,128]{2,1,0:T(8,128)(2,1)S(1)}, u32[]{:S(2)}, u32[]{:S(2)}) %collective-permute-start.7) | collective-permute-done | bytes 172064 | tf_op jit(solution)/shard_map/ppermute | solution.py:429
  28.8 1.0 collective-permute-done.9
  29.8 0.5 collective-permute-start.12
  30.3 0.6 collective-permute-start.13
  30.9 2.3 %collective-permute-start.10 = (bf16[512,128]{1,0:T(8,128)(2,1)S(1)}, bf16[512,128]{1,0:T(8,128)(2,1)S(1)}, u32[]{:S(2)}, u32[]{:S(2)}) collective-permute-start(bf16[512,128]{1,0:T(8,128)(2,1)S(1)} %bitcast.44), channel_id=1, source_target_pairs={{0,16},{8,24},{16,0},{24,8},{1,17},{9,25},{17,1},{25,9},{2,18},{10... | collective-permute-start | bytes 393224 | tf_op jit(solution)/shard_map/ppermute | solution.py:429
  33.3 1.4 %collective-permute-start.11 = (bf16[512,128]{1,0:T(8,128)(2,1)S(1)}, bf16[512,128]{1,0:T(8,128)(2,1)S(1)}, u32[]{:S(2)}, u32[]{:S(2)}) collective-permute-start(bf16[512,128]{1,0:T(8,128)(2,1)S(1)} %bitcast.45), channel_id=1, source_target_pairs={{0,24},{8,16},{16,8},{24,0},{1,25},{9,17},{17,9},{25,1},{2,26},{10... | collective-permute-start | bytes 393224 | tf_op jit(solution)/shard_map/ppermute | solution.py:429
  34.6 2.4 %collective-permute-done.12 = bf16[4,336,128]{2,1,0:T(8,128)(2,1)S(1)} collective-permute-done((bf16[4,336,128]{2,1,0:T(8,128)(2,1)S(1)}, bf16[4,336,128]{2,1,0:T(8,128)(2,1)S(1)}, u32[]{:S(2)}, u32[]{:S(2)}) %collective-permute-start.12) | collective-permute-done | bytes 344096 | tf_op jit(solution)/shard_map/ppermute | solution.py:429
  37.0 0.5 collective-permute-done.13
  37.6 0.2 pad_maximum_fusion.mine
  37.7 2.8 %collective-permute-done.10 = bf16[512,128]{1,0:T(8,128)(2,1)S(1)} collective-permute-done((bf16[512,128]{1,0:T(8,128)(2,1)S(1)}, bf16[512,128]{1,0:T(8,128)(2,1)S(1)}, u32[]{:S(2)}, u32[]{:S(2)}) %collective-permute-start.10) | collective-permute-done | bytes 131104 | tf_op jit(solution)/shard_map/ppermute | solution.py:429
  40.5 0.0 collective-permute-done.11
  40.6 1.7 %collective-permute-start.16 = (bf16[2,512,128]{2,1,0:T(8,128)(2,1)S(1)}, bf16[2,512,128]{2,1,0:T(8,128)(2,1)S(1)}, u32[]{:S(2)}, u32[]{:S(2)}) collective-permute-start(bf16[2,512,128]{2,1,0:T(8,128)(2,1)S(1)} %pad_maximum_fusion.6), channel_id=1, source_target_pairs={{0,4},{2,6},{4,0},{6,2},{1,5},{3,7},{5,1},{7,3},{8,12},{10,14},{12... | collective-permute-start | bytes 786440 | tf_op jit(solution)/shard_map/ppermute | solution.py:429
  42.3 1.4 %collective-permute-start.14 = (bf16[2,512,128]{2,1,0:T(8,128)(2,1)S(1)}, bf16[2,512,128]{2,1,0:T(8,128)(2,1)S(1)}, u32[]{:S(2)}, u32[]{:S(2)}) collective-permute-start(bf16[2,512,128]{2,1,0:T(8,128)(2,1)S(1)} %pad_maximum_fusion.5), channel_id=1, source_target_pairs={{0,2},{2,0},{4,6},{6,4},{1,3},{3,1},{5,7},{7,5},{8,10},{10,8},{12,... | collective-permute-start | bytes 786440 | tf_op jit(solution)/shard_map/ppermute | solution.py:429
  43.7 5.7 %collective-permute-done.16 = bf16[2,512,128]{2,1,0:T(8,128)(2,1)S(1)} collective-permute-done((bf16[2,512,128]{2,1,0:T(8,128)(2,1)S(1)}, bf16[2,512,128]{2,1,0:T(8,128)(2,1)S(1)}, u32[]{:S(2)}, u32[]{:S(2)}) %collective-permute-start.16) | collective-permute-done | bytes 262176 | tf_op jit(solution)/shard_map/ppermute | solution.py:429
  49.3 0.1 pad_maximum_fusion.2.rest_8_
  49.4 1.4 %collective-permute-start.17 = (bf16[4,512,128]{2,1,0:T(8,128)(2,1)S(1)}, bf16[4,512,128]{2,1,0:T(8,128)(2,1)S(1)}, u32[]{:S(2)}, u32[]{:S(2)}) collective-permute-start(bf16[4,512,128]{2,1,0:T(8,128)(2,1)S(1)} %pad_maximum_fusion.2.rest_8_), channel_id=1, source_target_pairs={{0,2},{2,0},{4,6},{6,4},{1,3},{3,1},{5,7},{7,5},{8,10},{10,8},{12,... | collective-permute-start | bytes 1572872 | tf_op jit(solution)/shard_map/ppermute | solution.py:429
  50.8 0.0 collective-permute-done.14
  50.8 0.1 pad_maximum_fusion.1.rest_7_
  50.9 1.7 %collective-permute-start.15 = (bf16[4,512,128]{2,1,0:T(8,128)(2,1)S(1)}, bf16[4,512,128]{2,1,0:T(8,128)(2,1)S(1)}, u32[]{:S(2)}, u32[]{:S(2)}) collective-permute-start(bf16[4,512,128]{2,1,0:T(8,128)(2,1)S(1)} %pad_maximum_fusion.1.rest_7_), channel_id=1, source_target_pairs={{0,4},{2,6},{4,0},{6,2},{1,5},{3,7},{5,1},{7,3},{8,12},{10,14},{12... | collective-permute-start | bytes 1572872 | tf_op jit(solution)/shard_map/ppermute | solution.py:429
  52.6 0.5 collective-permute-start.19
  53.1 8.7 %unpack.1 = (s32[584]{0:T(1024)S(1)}, f32[8,128]{1,0:T(8,128)S(1)}, bf16[144,128,128]{2,1,0:T(8,128)(2,1)S(1)}, f32[32,8,128]{2,1,0:T(8,128)S(1)}, f32[32,8,128]...) custom-call(s32[3]{0:T(128)S(1)} %pad_add_fusion.own, ...), custom_call_target="tpu_custom_call" | custom-call | bytes 11010048 | tf_op jit(solution)/shard_map/unpack/pallas_call | solution.py:513
  61.8 1.2 collective-permute-done.17.rest_10_
  63.0 1.2 collective-permute-done.15.rest_9_
  64.2 0.5 collective-permute-start.22
  64.7 1.4 %collective-permute-done.21.rest_13_ = bf16[4,512,128]{2,1,0:T(8,128)(2,1)S(1)} collective-permute-done((bf16[4,512,128]{2,1,0:T(8,128)(2,1)S(1)}, bf16[4,512,128]{2,1,0:T(8,128)(2,1)S(1)}, u32[]{:S(2)}, u32[]{:S(2)}) %collective-permute-start.21) | collective-permute-done | bytes 524320 | tf_op jit(solution)/shard_map/ppermute | solution.py:429
  66.1 0.7 collective-permute-done.22.rest_14_
  66.9 60.5 %iterate.1 = f32[2,4096]{1,0:T(2,128)} custom-call(s32[3]{0:T(128)S(1)} %pad_add_fusion.own, s32[584]{0:T(1024)S(1)} %get-tuple-element.46.lists, f32[8,128]{1,0:T(8,128)S(1)} %get-tuple-element.47.place, bf16[144,128,128]{2,1,0:T(8,128)(2,1)S(1)} %get-tuple-element.48.rest_0_, f32[32,8,128]{2,1,0:T(8,128)S(1)} %get-tuple-element.49.rest_1_, ...), custom_call_target="tpu_custom_call" | custom-call | tf_op jit(solution)/shard_map/iterate/pallas_call | solution.py:534
  (21 shorter events, 0.3 us)
Async XLA Ops:
  0.0 3.9 %copy-start = (bf16[1,1,128,4096]{3,2,1,0:T(8,128)(2,1)S(1)}, bf16[1,1,128,4096]{3,2,1,0:T(8,128)(2,1)}, u32[]{:S(2)}) copy-start(bf16[1,1,128,4096]{3,2,1,0:T(8,128)(2,1)} %param.7) | copy-start | bytes 3145732
  1.8 2.1 %collective-permute-start = (bf16[4,16,4096]{2,1,0:T(8,128)(2,1)S(1)}, bf16[4,16,4096]{2,1,0:T(8,128)(2,1)S(1)}, u32[]{:S(2)}, u32[]{:S(2)}) collective-permute-start(bf16[4,16,4096]{2,1,0:T(8,128)(2,1)S(1)} %select_bitcast_fusion), channel_id=1, source_target_pairs={{0,1},{1,0},{2,3},{3,2},{4,5},{5,4},{6,7},{7,6},{8,9},{9,8},{10,11... | collective-permute-start | bytes 1572872 | tf_op jit(solution)/shard_map/ppermute | solution.py:429
  4.0 11.0 %collective-permute-start.1 = (bf16[16,4096]{1,0:T(8,128)(2,1)S(1)}, bf16[16,4096]{1,0:T(8,128)(2,1)S(1)}, u32[]{:S(2)}, u32[]{:S(2)}) collective-permute-start(bf16[16,4096]{1,0:T(8,128)(2,1)S(1)} %get-tuple-element.57), channel_id=1, source_target_pairs={{0,2},{2,0},{4,6},{6,4},{1,3},{3,1},{5,7},{7,5},{8,10},{10,8},{12,... | collective-permute-start | bytes 393224 | tf_op jit(solution)/shard_map/ppermute | solution.py:429
  6.9 8.1 %collective-permute-start.2 = (bf16[16,4096]{1,0:T(8,128)(2,1)S(1)}, bf16[16,4096]{1,0:T(8,128)(2,1)S(1)}, u32[]{:S(2)}, u32[]{:S(2)}) collective-permute-start(bf16[16,4096]{1,0:T(8,128)(2,1)S(1)} %get-tuple-element.59), channel_id=1, source_target_pairs={{0,4},{2,6},{4,0},{6,2},{1,5},{3,7},{5,1},{7,3},{8,12},{10,14},{12... | collective-permute-start | bytes 393224 | tf_op jit(solution)/shard_map/ppermute | solution.py:429
  8.4 6.6 %collective-permute-start.3 = (bf16[16,4096]{1,0:T(8,128)(2,1)S(1)}, bf16[16,4096]{1,0:T(8,128)(2,1)S(1)}, u32[]{:S(2)}, u32[]{:S(2)}) collective-permute-start(bf16[16,4096]{1,0:T(8,128)(2,1)S(1)} %get-tuple-element.58), channel_id=1, source_target_pairs={{0,6},{2,4},{4,2},{6,0},{1,7},{3,5},{5,3},{7,1},{8,14},{10,12},{12... | collective-permute-start | bytes 393224 | tf_op jit(solution)/shard_map/ppermute | solution.py:429
  10.3 13.0 %copy-start.1 = (bf16[336,128]{1,0:T(8,128)(2,1)S(1)}, bf16[336,128]{1,0:T(8,128)(2,1)}, u32[]{:S(2)}) copy-start(bf16[336,128]{1,0:T(8,128)(2,1)} %prepare.1) | copy-start | bytes 258052
  10.3 4.9 %collective-permute-start.4 = (bf16[336,128]{1,0:T(8,128)(2,1)}, bf16[336,128]{1,0:T(8,128)(2,1)S(1)}, u32[]{:S(2)}, u32[]{:S(2)}) collective-permute-start(bf16[336,128]{1,0:T(8,128)(2,1)} %prepare.1), channel_id=1, source_target_pairs={{0,8},{8,0},{16,24},{24,16},{1,9},{9,1},{17,25},{25,17},{2,10},{10... | collective-permute-start | bytes 258056 | tf_op jit(solution)/shard_map/ppermute | solution.py:429
  12.4 8.3 %collective-permute-start.5 = (bf16[336,128]{1,0:T(8,128)(2,1)}, bf16[336,128]{1,0:T(8,128)(2,1)S(1)}, u32[]{:S(2)}, u32[]{:S(2)}) collective-permute-start(bf16[336,128]{1,0:T(8,128)(2,1)} %prepare.1), channel_id=1, source_target_pairs={{0,16},{8,24},{16,0},{24,8},{1,17},{9,25},{17,1},{25,9},{2,18},{10... | collective-permute-start | bytes 258056 | tf_op jit(solution)/shard_map/ppermute | solution.py:429
  15.0 6.6 %collective-permute-start.6 = (bf16[336,128]{1,0:T(8,128)(2,1)}, bf16[336,128]{1,0:T(8,128)(2,1)S(1)}, u32[]{:S(2)}, u32[]{:S(2)}) collective-permute-start(bf16[336,128]{1,0:T(8,128)(2,1)} %prepare.1), channel_id=1, source_target_pairs={{0,24},{8,16},{16,8},{24,0},{1,25},{9,17},{17,9},{25,1},{2,26},{10... | collective-permute-start | bytes 258056 | tf_op jit(solution)/shard_map/ppermute | solution.py:429
  21.7 5.5 %collective-permute-start.8 = (bf16[2,336,128]{2,1,0:T(8,128)(2,1)S(1)}, bf16[2,336,128]{2,1,0:T(8,128)(2,1)S(1)}, u32[]{:S(2)}, u32[]{:S(2)}) collective-permute-start(bf16[2,336,128]{2,1,0:T(8,128)(2,1)S(1)} %pad_maximum_fusion.8), channel_id=1, source_target_pairs={{0,4},{2,6},{4,0},{6,2},{1,5},{3,7},{5,1},{7,3},{8,12},{10,14},{12... | collective-permute-start | bytes 516104 | tf_op jit(solution)/shard_map/ppermute | solution.py:429
  23.3 5.5 %collective-permute-start.7 = (bf16[2,336,128]{2,1,0:T(8,128)(2,1)S(1)}, bf16[2,336,128]{2,1,0:T(8,128)(2,1)S(1)}, u32[]{:S(2)}, u32[]{:S(2)}) collective-permute-start(bf16[2,336,128]{2,1,0:T(8,128)(2,1)S(1)} %pad_maximum_fusion.7), channel_id=1, source_target_pairs={{0,2},{2,0},{4,6},{6,4},{1,3},{3,1},{5,7},{7,5},{8,10},{10,8},{12,... | collective-permute-start | bytes 516104 | tf_op jit(solution)/shard_map/ppermute | solution.py:429
  24.8 5.0 %collective-permute-start.9 = (bf16[512,128]{1,0:T(8,128)(2,1)S(1)}, bf16[512,128]{1,0:T(8,128)(2,1)S(1)}, u32[]{:S(2)}, u32[]{:S(2)}) collective-permute-start(bf16[512,128]{1,0:T(8,128)(2,1)S(1)} %bitcast.43), channel_id=1, source_target_pairs={{0,8},{8,0},{16,24},{24,16},{1,9},{9,1},{17,25},{25,17},{2,10},{10... | collective-permute-start | bytes 393224 | tf_op jit(solution)/shard_map/ppermute | solution.py:429
  29.8 7.2 %collective-permute-start.12 = (bf16[4,336,128]{2,1,0:T(8,128)(2,1)S(1)}, bf16[4,336,128]{2,1,0:T(8,128)(2,1)S(1)}, u32[]{:S(2)}, u32[]{:S(2)}) collective-permute-start(bf16[4,336,128]{2,1,0:T(8,128)(2,1)S(1)} %pad_maximum_fusion.3), channel_id=1, source_target_pairs={{0,4},{2,6},{4,0},{6,2},{1,5},{3,7},{5,1},{7,3},{8,12},{10,14},{12... | collective-permute-start | bytes 1032200 | tf_op jit(solution)/shard_map/ppermute | solution.py:429
  30.3 7.2 %collective-permute-start.13 = (bf16[4,336,128]{2,1,0:T(8,128)(2,1)S(1)}, bf16[4,336,128]{2,1,0:T(8,128)(2,1)S(1)}, u32[]{:S(2)}, u32[]{:S(2)}) collective-permute-start(bf16[4,336,128]{2,1,0:T(8,128)(2,1)S(1)} %pad_maximum_fusion.4), channel_id=1, source_target_pairs={{0,2},{2,0},{4,6},{6,4},{1,3},{3,1},{5,7},{7,5},{8,10},{10,8},{12,... | collective-permute-start | bytes 1032200 | tf_op jit(solution)/shard_map/ppermute | solution.py:429
  30.9 9.6 %collective-permute-start.10 = (bf16[512,128]{1,0:T(8,128)(2,1)S(1)}, bf16[512,128]{1,0:T(8,128)(2,1)S(1)}, u32[]{:S(2)}, u32[]{:S(2)}) collective-permute-start(bf16[512,128]{1,0:T(8,128)(2,1)S(1)} %bitcast.44), channel_id=1, source_target_pairs={{0,16},{8,24},{16,0},{24,8},{1,17},{9,25},{17,1},{25,9},{2,18},{10... | collective-permute-start | bytes 393224 | tf_op jit(solution)/shard_map/ppermute | solution.py:429
  33.3 7.3 %collective-permute-start.11 = (bf16[512,128]{1,0:T(8,128)(2,1)S(1)}, bf16[512,128]{1,0:T(8,128)(2,1)S(1)}, u32[]{:S(2)}, u32[]{:S(2)}) collective-permute-start(bf16[512,128]{1,0:T(8,128)(2,1)S(1)} %bitcast.45), channel_id=1, source_target_pairs={{0,24},{8,16},{16,8},{24,0},{1,25},{9,17},{17,9},{25,1},{2,26},{10... | collective-permute-start | bytes 393224 | tf_op jit(solution)/shard_map/ppermute | solution.py:429
  40.5 12.5 %collective-permute-start.18 = (bf16[16,336,128]{2,1,0:T(8,128)(2,1)S(1)}, bf16[16,336,128]{2,1,0:T(8,128)(2,1)S(1)}, u32[]{:S(2)}, u32[]{:S(2)}) collective-permute-start(bf16[16,336,128]{2,1,0:T(8,128)(2,1)S(1)} %pad_maximum_fusion.mine), channel_id=1, source_target_pairs={{0,1},{1,0},{2,3},{3,2},{4,5},{5,4},{6,7},{7,6},{8,9},{9,8},{10,11... | collective-permute-start | bytes 4128776 | tf_op jit(solution)/shard_map/ppermute | solution.py:429
  40.6 8.8 %collective-permute-start.16 = (bf16[2,512,128]{2,1,0:T(8,128)(2,1)S(1)}, bf16[2,512,128]{2,1,0:T(8,128)(2,1)S(1)}, u32[]{:S(2)}, u32[]{:S(2)}) collective-permute-start(bf16[2,512,128]{2,1,0:T(8,128)(2,1)S(1)} %pad_maximum_fusion.6), channel_id=1, source_target_pairs={{0,4},{2,6},{4,0},{6,2},{1,5},{3,7},{5,1},{7,3},{8,12},{10,14},{12... | collective-permute-start | bytes 786440 | tf_op jit(solution)/shard_map/ppermute | solution.py:429
  42.3 8.5 %collective-permute-start.14 = (bf16[2,512,128]{2,1,0:T(8,128)(2,1)S(1)}, bf16[2,512,128]{2,1,0:T(8,128)(2,1)S(1)}, u32[]{:S(2)}, u32[]{:S(2)}) collective-permute-start(bf16[2,512,128]{2,1,0:T(8,128)(2,1)S(1)} %pad_maximum_fusion.5), channel_id=1, source_target_pairs={{0,2},{2,0},{4,6},{6,4},{1,3},{3,1},{5,7},{7,5},{8,10},{10,8},{12,... | collective-permute-start | bytes 786440 | tf_op jit(solution)/shard_map/ppermute | solution.py:429
  49.4 13.6 %collective-permute-start.17 = (bf16[4,512,128]{2,1,0:T(8,128)(2,1)S(1)}, bf16[4,512,128]{2,1,0:T(8,128)(2,1)S(1)}, u32[]{:S(2)}, u32[]{:S(2)}) collective-permute-start(bf16[4,512,128]{2,1,0:T(8,128)(2,1)S(1)} %pad_maximum_fusion.2.rest_8_), channel_id=1, source_target_pairs={{0,2},{2,0},{4,6},{6,4},{1,3},{3,1},{5,7},{7,5},{8,10},{10,8},{12,... | collective-permute-start | bytes 1572872 | tf_op jit(solution)/shard_map/ppermute | solution.py:429
  50.9 13.3 %collective-permute-start.15 = (bf16[4,512,128]{2,1,0:T(8,128)(2,1)S(1)}, bf16[4,512,128]{2,1,0:T(8,128)(2,1)S(1)}, u32[]{:S(2)}, u32[]{:S(2)}) collective-permute-start(bf16[4,512,128]{2,1,0:T(8,128)(2,1)S(1)} %pad_maximum_fusion.1.rest_7_), channel_id=1, source_target_pairs={{0,4},{2,6},{4,0},{6,2},{1,5},{3,7},{5,1},{7,3},{8,12},{10,14},{12... | collective-permute-start | bytes 1572872 | tf_op jit(solution)/shard_map/ppermute | solution.py:429
  52.6 12.2 %collective-permute-start.20 = (bf16[4,512,128]{2,1,0:T(8,128)(2,1)S(1)}, bf16[4,512,128]{2,1,0:T(8,128)(2,1)S(1)}, u32[]{:S(2)}, u32[]{:S(2)}) collective-permute-start(bf16[4,512,128]{2,1,0:T(8,128)(2,1)S(1)} %pad_maximum_fusion.2.rest_8_), channel_id=1, source_target_pairs={{0,1},{1,0},{2,3},{3,2},{4,5},{5,4},{6,7},{7,6},{8,9},{9,8},{10,11... | collective-permute-start | bytes 1572872 | tf_op jit(solution)/shard_map/ppermute | solution.py:429
  52.6 12.2 %collective-permute-start.19 = (bf16[4,512,128]{2,1,0:T(8,128)(2,1)S(1)}, bf16[4,512,128]{2,1,0:T(8,128)(2,1)S(1)}, u32[]{:S(2)}, u32[]{:S(2)}) collective-permute-start(bf16[4,512,128]{2,1,0:T(8,128)(2,1)S(1)} %pad_maximum_fusion.1.rest_7_), channel_id=1, source_target_pairs={{0,1},{1,0},{2,3},{3,2},{4,5},{5,4},{6,7},{7,6},{8,9},{9,8},{10,11... | collective-permute-start | bytes 1572872 | tf_op jit(solution)/shard_map/ppermute | solution.py:429
  64.2 1.9 %collective-permute-start.21 = (bf16[4,512,128]{2,1,0:T(8,128)(2,1)S(1)}, bf16[4,512,128]{2,1,0:T(8,128)(2,1)S(1)}, u32[]{:S(2)}, u32[]{:S(2)}) collective-permute-start(bf16[4,512,128]{2,1,0:T(8,128)(2,1)S(1)} %collective-permute-done.15.rest_9_), channel_id=1, source_target_pairs={{0,1},{1,0},{2,3},{3,2},{4,5},{5,4},{6,7},{7,6},{8,9},{9,8},{10,11... | collective-permute-start | bytes 1572872 | tf_op jit(solution)/shard_map/ppermute | solution.py:429
  64.2 2.7 %collective-permute-start.22 = (bf16[4,512,128]{2,1,0:T(8,128)(2,1)S(1)}, bf16[4,512,128]{2,1,0:T(8,128)(2,1)S(1)}, u32[]{:S(2)}, u32[]{:S(2)}) collective-permute-start(bf16[4,512,128]{2,1,0:T(8,128)(2,1)S(1)} %collective-permute-done.17.rest_10_), channel_id=1, source_target_pairs={{0,1},{1,0},{2,3},{3,2},{4,5},{5,4},{6,7},{7,6},{8,9},{9,8},{10,11... | collective-permute-start | bytes 1572872 | tf_op jit(solution)/shard_map/ppermute | solution.py:429
